TPU v7x, 32 devices: a whole 2x2x4 slice. The times are simulated.
32 devices in a mesh: dp: 8 (over z, x), head: 4 (over y, core).
Axes of the slice: x: 2, y: 2, z: 4, core: 2. Of those that a mesh axis runs over, the one named last changes fastest.
Arguments:
- hidden: bfloat16 [16384, 768], P(('dp', 'head')), may hold values from -6 to 6
- lengths: int32 [8, 3], P('dp'), may hold values from 1 to 1536, as said below
- norm_gain: float32 [768], replicated, may hold values from 0.5 to 1.5
- gate_proj: bfloat16 [768, 1536], P(None, 'head'), may hold values from -0.21875 to 0.21875
- value_proj: bfloat16 [768, 1536], P(None, 'head'), may hold values from -0.21875 to 0.21875
- state_proj: bfloat16 [768, 256], replicated, may hold values from -0.21875 to 0.21875
- step_proj: bfloat16 [768, 24], P(None, 'head'), may hold values from -0.21875 to 0.21875
- value_taps: float32 [4, 1536], P(None, 'head'), may hold values from -3 to 3
- value_bias: float32 [1536], P('head'), may hold values from -3 to 3
- state_taps: float32 [4, 256], replicated, may hold values from -3 to 3
- state_bias: float32 [256], replicated, may hold values from -3 to 3
- step_bias: float32 [24], P('head'), may hold values from -5 to -1
- decay_log: float32 [24], P('head'), may hold values from 0 to 2.7
- skip_gain: float32 [24], P('head'), may hold values from 0.5 to 2
- out_gain: float32 [1536], P('head'), may hold values from 0.5 to 1.5
- out_proj: bfloat16 [1536, 768], P('head'), may hold values from -0.15625 to 0.15625
- cotangent: bfloat16 [16384, 768], P(('dp', 'head')), may hold values from -6 to 6
Outputs:
- mixed: bfloat16 [16384, 768], P(('dp', 'head'))
- grad_hidden: float32 [16384, 768], P(('dp', 'head'))
- grad_norm_gain: float32 [768], replicated
- grad_gate_proj: float32 [768, 1536], P(None, 'head')
- grad_value_proj: float32 [768, 1536], P(None, 'head')
- grad_state_proj: float32 [768, 256], replicated
- grad_step_proj: float32 [768, 24], P(None, 'head')
- grad_value_taps: float32 [4, 1536], P(None, 'head')
- grad_value_bias: float32 [1536], P('head')
- grad_state_taps: float32 [4, 256], replicated
- grad_state_bias: float32 [256], replicated
- grad_step_bias: float32 [24], P('head')
- grad_decay_log: float32 [24], P('head')
- grad_skip_gain: float32 [24], P('head')
- grad_out_gain: float32 [1536], P('head')
- grad_out_proj: float32 [1536, 768], P('head')
Inputs may be any that keep to these rules, and one draw needn't show every extreme that they name: lengths[g] gives group g's three sequences in slot order: the first and the third have at most 256 tokens and fill blocks 0 and 7; the second has more than (6) * 256 - 256 // 2 tokens and fills the blocks between; slots past a sequence's length are padding.
All inputs are finite; a program needn't handle non-finite values.
Results may differ from a plain program's by a relative error of at most 0.019.
Values may be sent and summed in bfloat16 or wider, within the bound.
No kernel may reach another device: no remote copies, remote signals or barrier semaphores. Data moves between devices by JAX's collectives and lax.ppermute only.
A program may use at most 192 MiB of HBM per device.

v0:
```python
import jax
import jax.numpy as jnp
from jax import lax
from jax.sharding import PartitionSpec as P

K = 4
Q = 256


EPSILON = 1e-05


def settle(values):
    return lax.optimization_barrier(values.astype(jnp.bfloat16)).astype(jnp.float32)


def silu_slope(values):
    sigmoid_v = jax.nn.sigmoid(values)
    return sigmoid_v * (1.0 + values * (1.0 - sigmoid_v))


def layout(lengths_row, span_rows):
    slots = jnp.arange(span_rows, dtype=jnp.int32)
    starts = jnp.where(slots < Q, 0, jnp.where(slots < span_rows - Q, Q, span_rows - Q)).astype(
        jnp.int32
    )
    seq_length = jnp.where(
        slots < Q, lengths_row[0], jnp.where(slots < span_rows - Q, lengths_row[1], lengths_row[2])
    )
    places = slots - starts
    valid_rows = (places < seq_length).astype(jnp.float32)
    return (places, valid_rows)


def conv_pre(values, taps, offset, places):
    total_rows = values.shape[0]
    result = offset + taps[K - 1] * values
    for distance in range(1, K):
        earlier = jnp.pad(values, ((distance, 0), (0, 0)))[:total_rows]
        keeper = (places >= distance).astype(jnp.float32)[:, None]
        result = result + taps[K - 1 - distance] * earlier * keeper
    return result


def mixer(x_conv, b_matrix, c_matrix, step_sizes, decay_rate, skip_weight):
    total_rows, channel_count = x_conv.shape
    head_count = step_sizes.shape[1]
    head_size = channel_count // head_count
    block_count = total_rows // Q
    state_size = b_matrix.shape[1]
    x_blocks = x_conv.reshape(block_count, Q, head_count, head_size)
    x_low = x_conv.astype(jnp.bfloat16).reshape(block_count, Q, head_count, head_size)
    b_low = b_matrix.astype(jnp.bfloat16).reshape(block_count, Q, state_size)
    c_low = c_matrix.astype(jnp.bfloat16).reshape(block_count, Q, state_size)
    step_blocks = step_sizes.reshape(block_count, Q, head_count)
    log_decay = jnp.cumsum(step_blocks * decay_rate, axis=1)
    intersections = jnp.einsum("cqn,csn->cqs", c_low, b_low, preferred_element_type=jnp.float32)
    causal = jnp.arange(Q)[:, None] >= jnp.arange(Q)[None, :]

    def one_head(inputs):
        head_logs, head_steps, head_values = inputs
        spread = jnp.where(causal, head_logs[:, :, None] - head_logs[:, None, :], -jnp.inf)
        scores = (intersections * jnp.exp(spread) * head_steps[:, None, :]).astype(jnp.bfloat16)
        return jnp.einsum("cqs,csp->cqp", scores, head_values, preferred_element_type=jnp.float32)

    intra = lax.map(
        jax.checkpoint(one_head),
        (jnp.moveaxis(log_decay, 2, 0), jnp.moveaxis(step_blocks, 2, 0), jnp.moveaxis(x_low, 2, 0)),
    )
    intra = jnp.moveaxis(intra, 0, 2)
    final_log = log_decay[:, -1:, :]
    carry_weight = jnp.exp(final_log - log_decay) * step_blocks
    weighted_x = (carry_weight[..., None] * x_blocks).astype(jnp.bfloat16)
    block_state = jnp.einsum(
        "csn,cshp->chnp", b_low, weighted_x, preferred_element_type=jnp.float32
    )
    block_index = jnp.arange(block_count)
    fresh = ((block_index == 0) | (block_index == 1) | (block_index == block_count - 1)).astype(
        jnp.float32
    )

    def advance(state, item):
        local_state, fading, flag = item
        arriving = state * (1.0 - flag)
        return (fading[:, None, None] * arriving + local_state, arriving)

    start_state = jnp.zeros((head_count, state_size, head_size), jnp.float32)
    _, incoming = lax.scan(advance, start_state, (block_state, jnp.exp(final_log[:, 0, :]), fresh))
    inter = (
        jnp.einsum(
            "cqn,chnp->cqhp",
            c_low,
            incoming.astype(jnp.bfloat16),
            preferred_element_type=jnp.float32,
        )
        * jnp.exp(log_decay)[..., None]
    )
    result = intra + inter + skip_weight[:, None] * x_blocks
    return result.reshape(total_rows, channel_count)


def body(
    hidden,
    lengths,
    norm_gain,
    gate_proj,
    value_proj,
    state_proj,
    step_proj,
    value_taps,
    value_bias,
    state_taps,
    state_bias,
    step_bias,
    decay_log,
    skip_gain,
    out_gain,
    out_proj,
    cotangent,
):
    own_rows = hidden.shape[0]
    head_ways = lax.axis_size("head")
    span_rows = own_rows * head_ways
    begin = lax.axis_index("head") * own_rows
    places, valid_rows = layout(lengths[0], span_rows)
    valid_own = lax.dynamic_slice_in_dim(valid_rows, begin, own_rows, 0)
    channels = gate_proj.shape[1]
    head_share = step_proj.shape[1]
    state_size = state_proj.shape[1] // 2
    hidden_full = hidden.astype(jnp.float32)

    def norm_input(values, gain_in):
        scale_in = lax.rsqrt(jnp.mean(values * values, axis=1, keepdims=True) + EPSILON)
        return values * scale_in * gain_in

    normed_full, norm_pull = jax.vjp(norm_input, hidden_full, norm_gain)
    normed = normed_full.astype(jnp.bfloat16)
    local_cols = jnp.concatenate([gate_proj, value_proj, step_proj], axis=1)
    all_cols = jnp.concatenate([local_cols, state_proj], axis=1)
    gathered = lax.all_gather(normed, "head", axis=0, tiled=True)
    projected = jnp.dot(gathered, all_cols, preferred_element_type=jnp.float32)
    gate_in = projected[:, :channels]
    inner_x = projected[:, channels : 2 * channels]
    step_raw = projected[:, 2 * channels : 2 * channels + head_share]
    state_raw = projected[:, 2 * channels + head_share :]
    state_pre = conv_pre(state_raw, state_taps, state_bias, places)
    state_conv = jax.nn.silu(state_pre)

    def local_mix(
        gate_vals,
        inner_vals,
        step_vals,
        state_vals,
        taps_vals,
        bias_vals,
        step_offset,
        decay_vals,
        skip_vals,
    ):
        x_conv = jax.nn.silu(conv_pre(inner_vals, taps_vals, bias_vals, places))
        step_sizes = jax.nn.softplus(step_vals + step_offset)
        mix_y = mixer(
            x_conv,
            state_vals[:, :state_size],
            state_vals[:, state_size:],
            step_sizes,
            -jnp.exp(decay_vals),
            skip_vals,
        )
        return mix_y * jax.nn.silu(gate_vals)

    gated_y, mix_pull = jax.vjp(
        local_mix,
        gate_in,
        inner_x,
        step_raw,
        state_conv,
        value_taps,
        value_bias,
        step_bias,
        decay_log,
        skip_gain,
    )
    all_channels = channels * head_ways
    squares = lax.psum(jnp.sum(gated_y * gated_y, axis=1), "head")
    scale_y = lax.rsqrt(squares / all_channels + EPSILON)[:, None]
    normed_y = (gated_y * scale_y * out_gain).astype(jnp.bfloat16)
    part_rows = normed_y
    branch_own = lax.psum_scatter(
        jnp.dot(part_rows, out_proj, preferred_element_type=jnp.float32).astype(jnp.bfloat16),
        "head",
        scatter_dimension=0,
        tiled=True,
    ).astype(jnp.float32)
    mixed = (hidden_full + valid_own[:, None] * branch_own).astype(jnp.bfloat16)
    cotan_full = cotangent.astype(jnp.float32)
    d_branch = (cotan_full * valid_own[:, None]).astype(jnp.bfloat16)
    d_branch_all = lax.all_gather(d_branch, "head", axis=0, tiled=True)
    grad_out = jnp.einsum("tc,td->cd", normed_y, d_branch_all, preferred_element_type=jnp.float32)
    d_normed_y = settle(
        jnp.einsum("td,cd->tc", d_branch_all, out_proj, preferred_element_type=jnp.float32)
    )
    grad_out_gain = jnp.sum(d_normed_y * gated_y * scale_y, axis=0)
    weighted_grad = d_normed_y * out_gain
    cross = lax.psum(jnp.sum(weighted_grad * gated_y, axis=1), "head")
    d_gated = (
        weighted_grad * scale_y
        - gated_y * scale_y * scale_y * scale_y * (cross / all_channels)[:, None]
    )
    (
        d_gate,
        d_inner,
        d_step,
        d_state_conv,
        grad_vtaps,
        grad_vbias,
        grad_sbias,
        grad_decay,
        grad_skip,
    ) = mix_pull(d_gated)
    slope = silu_slope(state_pre)
    summed_all = lax.psum(d_state_conv.astype(jnp.bfloat16), "head").astype(jnp.float32)
    padded = jnp.pad(summed_all * slope, ((0, K - 1), (0, 0)))
    d_pre_ext = lax.dynamic_slice_in_dim(padded, begin, own_rows + K - 1, 0)
    place_ext = lax.dynamic_slice_in_dim(jnp.pad(places, (0, K - 1)), begin, own_rows + K - 1, 0)
    place_own = place_ext[:own_rows]
    d_pre_rows = d_pre_ext[:own_rows]
    raw_padded = jnp.pad(state_raw, ((K - 1, 0), (0, 0)))
    d_state_raw = state_taps[K - 1] * d_pre_rows
    tap_grads = []
    for index in range(K):
        distance = K - 1 - index
        earlier = lax.dynamic_slice_in_dim(raw_padded, begin + index, own_rows, 0)
        keeper = (place_own >= distance).astype(jnp.float32)[:, None]
        tap_grads.append(jnp.sum(d_pre_rows * earlier * keeper, axis=0))
    for distance in range(1, K):
        ahead = (place_ext[distance : distance + own_rows] >= distance).astype(jnp.float32)[:, None]
        d_state_raw = (
            d_state_raw
            + state_taps[K - 1 - distance] * d_pre_ext[distance : distance + own_rows] * ahead
        )
    grad_state_taps = jnp.stack(tap_grads, axis=0)
    grad_state_bias = jnp.sum(d_pre_rows, axis=0)
    d_state_low = d_state_raw.astype(jnp.bfloat16)
    grad_state = jnp.einsum("td,tk->dk", normed, d_state_low, preferred_element_type=jnp.float32)
    d_from_state = jnp.einsum(
        "tk,dk->td", d_state_low, state_proj, preferred_element_type=jnp.float32
    )
    d_proj = jnp.concatenate(
        [d_gate.astype(jnp.bfloat16), d_inner.astype(jnp.bfloat16), d_step.astype(jnp.bfloat16)],
        axis=1,
    )
    part_rows = d_proj
    d_norm_part = lax.psum_scatter(
        jnp.einsum("tk,dk->td", part_rows, local_cols, preferred_element_type=jnp.float32).astype(
            jnp.bfloat16
        ),
        "head",
        scatter_dimension=0,
        tiled=True,
    ).astype(jnp.float32)
    grad_cols = jnp.einsum("td,tk->dk", gathered, d_proj, preferred_element_type=jnp.float32)
    d_normed = settle(d_norm_part + d_from_state)
    d_hidden_norm, grad_norm = norm_pull(d_normed)
    grad_hidden = cotan_full + d_hidden_norm
    grad_gate = grad_cols[:, :channels]
    grad_value = grad_cols[:, channels : 2 * channels]
    grad_step = grad_cols[:, 2 * channels :]
    (
        grad_gate,
        grad_value,
        grad_step,
        grad_out,
        grad_vtaps,
        grad_vbias,
        grad_sbias,
        grad_decay,
        grad_skip,
        grad_out_gain,
    ) = (
        lax.psum(grad_gate.astype(jnp.bfloat16), "dp").astype(jnp.float32),
        lax.psum(grad_value.astype(jnp.bfloat16), "dp").astype(jnp.float32),
        lax.psum(grad_step.astype(jnp.bfloat16), "dp").astype(jnp.float32),
        lax.psum(grad_out.astype(jnp.bfloat16), "dp").astype(jnp.float32),
        lax.psum(grad_vtaps.astype(jnp.bfloat16), "dp").astype(jnp.float32),
        lax.psum(grad_vbias.astype(jnp.bfloat16), "dp").astype(jnp.float32),
        lax.psum(grad_sbias.astype(jnp.bfloat16), "dp").astype(jnp.float32),
        lax.psum(grad_decay.astype(jnp.bfloat16), "dp").astype(jnp.float32),
        lax.psum(grad_skip.astype(jnp.bfloat16), "dp").astype(jnp.float32),
        lax.psum(grad_out_gain.astype(jnp.bfloat16), "dp").astype(jnp.float32),
    )
    grad_norm, grad_state, grad_state_taps, grad_state_bias = lax.psum(
        (grad_norm, grad_state, grad_state_taps, grad_state_bias), ("dp", "head")
    )
    return (
        mixed,
        grad_hidden,
        grad_norm,
        grad_gate,
        grad_value,
        grad_state,
        grad_step,
        grad_vtaps,
        grad_vbias,
        grad_state_taps,
        grad_state_bias,
        grad_sbias,
        grad_decay,
        grad_skip,
        grad_out_gain,
        grad_out,
    )


def solution(mesh):
    in_specs = (
        P(("dp", "head"), None),
        P("dp", None),
        P(),
        P(None, "head"),
        P(None, "head"),
        P(),
        P(None, "head"),
        P(None, "head"),
        P("head"),
        P(),
        P(),
        P("head"),
        P("head"),
        P("head"),
        P("head"),
        P("head", None),
        P(("dp", "head"), None),
    )
    out_specs = (
        P(("dp", "head"), None),
        P(("dp", "head"), None),
        P(),
        P(None, "head"),
        P(None, "head"),
        P(),
        P(None, "head"),
        P(None, "head"),
        P("head"),
        P(),
        P(),
        P("head"),
        P("head"),
        P("head"),
        P("head"),
        P("head", None),
    )
    return jax.shard_map(body, mesh=mesh, in_specs=in_specs, out_specs=out_specs, check_vma=False)
```

profile of v0, /device:TPU:0, one launch (start us, length us, event | category | flops | bytes accessed | tf_op | source)
XLA Modules:
  0.0 739.7 jit_solution(11270393066361740462)
XLA Ops:
  23.6 18.9 %all-gather.3.cloned.1.call-done = bf16[2048,768]{1,0:T(8,128)(2,1)} async-done(((bf16[512,768]{1,0:T(8,128)(2,1)}), bf16[2048,768]{1,0:T(8,128)(2,1)}) %all-gather.3.cloned.1.call-update) | async-done | bytes 3145744 | tf_op jit(solution)/shard_map/all_gather | solution.py:140
  42.5 5.5 fusion.168
  53.5 7.2 reduce-window.14
  70.6 9.8 %fusion.161 = (bf16[2048,384]{0,1:T(8,128)(2,1)}, f32[2048,384]{0,1:T(8,128)S(1)}, f32[2048,384]{0,1:T(8,128)}) fusion(f32[2048]{0:T(1024)S(1)} %get-tuple-element.965, f32[2048,384]{0,1:T(8,128)} %slice.177, f32[384]{0:T(512)} %get-tuple-element.828, f32[2048]{0:T(1024)S(1)} %get-tuple-element.966, f32[384]{0:T(512)} %get-tuple-element.829, ...), kind=kLoop, calls=%fused_computation.281 | loop fusion | flops 12582912 | bytes 11042304 | tf_op jit(solution)/shard_map/jvp()/convert_element_type | solution.py:52
  80.5 3.1 copy.382
  83.6 3.1 multiply_convert_fusion.6
  87.6 4.2 convolution_bitcast_fusion.1
  91.8 35.4 %while.74 = (s32[]{:T(128)}, f32[6,128,64]{2,1,0:T(8,128)S(1)}, f32[8,6,128,64]{3,2,1,0:T(8,128)}, f32[8]{0:T(128)S(1)}, f32[8,6,1,1]{1,3,2,0:T(1,128)}, /*index...) while((s32[]{:T(128)}, f32[6,128,64]{2,1,0:T(8,128)S(1)}, ...), condition=%wide.region_6.7_spmd.clone.clone, body=%wide.region_5.6_spmd.clone.sunk.clone | while | flops 294916 | bytes 1968884 | solution.py:88
  143.5 23.2 %while.73 = (s32[]{:T(128)}, f32[6,8,256,64]{2,3,0,1:T(8,128)}, f32[6,8,256]{2,1,0:T(8,128)}, f32[8,256,256]{2,1,0:T(8,128)}, f32[6,8,256]{2,1,0:T(8,128)}, /*in...) while((s32[]{:T(128)}, f32[6,8,256,64]{2,3,0,1:T(8,128)}, ...), condition=%wide.region_4.5_spmd.clone.clone, body=%wide.region_3.4_spmd.clone.sunk.clone | while | flops 69730304 | bytes 3007569 | solution.py:66
  144.2 3.2 fusion.222
  148.1 3.2 fusion.222
  152.0 3.1 fusion.222
  155.8 3.2 fusion.222
  159.7 3.1 fusion.222
  163.6 3.1 fusion.222
  166.7 6.0 fusion.57
  176.0 5.9 multiply_reduce_fusion.6
  181.8 6.0 psum.119
  187.9 3.5 convolution_convert_fusion.4
  192.9 5.7 psum.120
  198.7 7.8 %multiply_reduce_fusion = (f32[384]{0:T(512)}, f32[2048,384]{0,1:T(8,128)S(1)}, bf16[2048,384]{0,1:T(8,128)(2,1)}) fusion(f32[2048,384]{0,1:T(8,128)} %copy-done.6, f32[2048,1030]{0,1:T(8,128)} %copy-done.9, f32[2048]{0:T(1024)S(1)} %broadcast_multiply_fusion, f32[2048,384]{0,1:T(8,128)} %get-tuple-element.915, f32[2048]{0:T(1024)S(1)} %add_rsqrt_fusion, ...), kind=kLoop, calls=%fused_computation.101 | loop fusion | flops 18087552 | bytes 18893824 | tf_op jit(solution)/shard_map/transpose(jvp())/reduce_sum | solution.py:98
  212.5 75.6 %while.75 = (s32[]{:T(128)}, f32[8,256,256]{2,1,0:T(8,128)S(1)}, f32[6,8,256]{2,0,1:T(8,128)}, f32[6,8,256]{2,0,1:T(8,128)}, bf16[6,8,256,64]{2,3,0,1:T(8,128)(2...) while((s32[]{:T(128)}, f32[8,256,256]{2,1,0:T(8,128)S(1)}, ...), condition=%wide.region_16.17_spmd.clone.clone, body=%wide.region_12.16_spmd.clone.sunk.clone | while | flops 144766976 | bytes 10936519 | solution.py:66
  215.6 3.0 fusion.229
  218.6 3.4 fusion.228
  228.2 3.0 fusion.229
  231.2 3.4 fusion.228
  240.8 3.0 fusion.229
  243.8 3.4 fusion.228
  256.4 3.4 fusion.228
  269.0 3.4 fusion.228
  281.6 3.4 fusion.228
  294.1 34.5 %while.76 = (s32[]{:T(128)}, f32[6,128,64]{2,1,0:T(8,128)S(1)}, bf16[8,6,128,64]{3,2,1,0:T(8,128)(2,1)S(1)}, f32[8,6]{1,0:T(8,128)S(1)}, f32[8,6,128,64]{2,3,1,0...) while((s32[]{:T(128)}, f32[6,128,64]{2,1,0:T(8,128)S(1)}, ...), condition=%wide.region_19.20_spmd.clone.clone, body=%wide.region_17.19_spmd.clone.sunk.clone | while | flops 344062 | bytes 2162976 | solution.py:88
  328.6 6.8 fusion.46
  340.1 4.9 multiply_reduce_fusion.4
  345.1 4.5 multiply_multiply_fusion
  350.2 15.1 %reduce-window.16 = f32[8,6,2,128]{3,0,1,2:T(8,128)S(1)} reduce-window(f32[8,6,2,128]{3,0,1,2:T(8,128)S(1)} %copy.287, f32[]{:T(128)} %constant.220.clone.1), window={size=1x1x1x128 pad=0_0x0_0x0_0x0_127}, to_apply=%region_23.24 | reduce-window | flops 1560576 | bytes 98308 | tf_op jit(solution)/shard_map/reduce-window.2
  366.8 3.9 fusion.108
  371.7 3.4 fusion.111
  377.5 6.1 fusion.40
  390.3 6.8 convolution_convert_fusion.2
  397.1 5.4 convolution_convert_fusion.3
  403.7 38.0 %all-reduce.19 = (bf16[768,6]{0,1:T(8,128)(2,1)S(1)}, bf16[4,384]{1,0:T(4,128)(2,1)S(1)}, bf16[384]{0:T(512)(128)(2,1)S(1)}, bf16[6]{0:T(256)(128)(2,1)S(1)}, bf...) all-reduce(bf16[768,6]{0,1:T(8,128)(2,1)S(1)} %slice-done, ...), channel_id=1, replica_groups=mesh['dp'=8,'head'=4] {'dp'}, use_global_device_ids=true, to_apply=%region_33.34 | all-reduce | flops 6930 | bytes 27720 | tf_op jit(solution)/shard_map/psum | solution.py:283
  451.2 4.2 fusion.116
  455.4 59.1 %all-reduce.29.cloned.1.call-done = (bf16[768,384]{0,1:T(8,128)(2,1)}, bf16[768,384]{0,1:T(8,128)(2,1)}, bf16[384,768]{1,0:T(8,128)(2,1)}) async-done(((bf16[768,384]{0,1:T(8,128)(2,1)}, bf16[768,384]{0,1:T(8,128)(2,1)}, bf16[384,768]{1,0:T(8,128)(2,1)}), (bf16[768,384]{0,1:T(8,128)(2,1)}, bf16[768,384]{0,1:T(8,128)(2,1)}, bf16[384,768]{1,0:T(8,128)(2,1)})) %all-reduce.29.cloned.1.call-update) | async-done | bytes 1769488 | tf_op jit(solution)/shard_map/psum | solution.py:281
  520.4 34.0 %reduce-scatter.5.cloned.1.call-done = bf16[512,768]{1,0:T(8,128)(2,1)} async-done(((bf16[2048,768]{1,0:T(8,128)(2,1)}), bf16[512,768]{1,0:T(8,128)(2,1)}) %reduce-scatter.5.cloned.1.call-update) | async-done | bytes 786448 | tf_op jit(solution)/shard_map/reduce_scatter | solution.py:254
  556.9 39.7 %all-reduce.18 = (f32[768]{0:T(1024)}, f32[4,256]{1,0:T(4,128)}, f32[256]{0:T(256)}) all-reduce(f32[768]{0:T(1024)S(1)} %get-tuple-element.824, f32[4,256]{1,0:T(4,128)S(1)} %pad_maximum_fusion.3, f32[256]{0:T(256)S(1)} %get-tuple-element.823), channel_id=1, replica_groups=mesh['dp'=8,'head'=4] {'dp','head'}, use_global_device_ids=true, to_apply=%region_29.30 | all-reduce | flops 2048 | bytes 16384 | tf_op jit(solution)/shard_map/psum | solution.py:292
  596.7 3.2 convert_add_fusion.1
  599.9 130.5 %all-reduce.27.cloned.1.call-done = f32[768,256]{1,0:T(8,128)} async-done(((f32[768,256]{1,0:T(8,128)}), f32[768,256]{1,0:T(8,128)}) %all-reduce.27.cloned.1.call-update) | async-done | bytes 786448 | tf_op jit(solution)/shard_map/psum | solution.py:292
  (531 shorter events, 222.3 us)
Async XLA Ops:
  7.2 180.7 %copy-start = (bf16[384,768]{1,0:T(8,128)(2,1)S(1)}, bf16[384,768]{1,0:T(8,128)(2,1)}, u32[]{:S(2)}) copy-start(bf16[384,768]{1,0:T(8,128)(2,1)} %param.40) | copy-start | bytes 1769476
  7.2 6.7 copy-start.27
  7.2 35.3 %all-gather.3.cloned.1.call-start = ((), (), s32[]{:S(2)}) async-start(), calls=%async_computation.2 | async-start | bytes 3932160 | tf_op jit(solution)/shard_map/all_gather | solution.py:140
  8.8 9.6 %copy-start.73 = (bf16[768,6]{0,1:T(8,128)(2,1)S(1)}, bf16[768,6]{0,1:T(8,128)(2,1)}, u32[]{:S(2)}) copy-start(bf16[768,6]{0,1:T(8,128)(2,1)} %param.31) | copy-start | bytes 27652
  8.8 10.5 %copy-start.96 = (f32[6]{0:T(128)S(1)}, f32[6]{0:T(128)}, u32[]{:S(2)}) copy-start(f32[6]{0:T(128)} %param.37) | copy-start | bytes 76
  8.8 11.0 %copy-start.83 = (f32[4,384]{1,0:T(4,128)S(1)}, f32[4,384]{1,0:T(4,128)}, u32[]{:S(2)}) copy-start(f32[4,384]{1,0:T(4,128)} %param.32) | copy-start | bytes 18436
  8.8 11.6 %copy-start.86 = (f32[4,256]{1,0:T(4,128)S(1)}, f32[4,256]{1,0:T(4,128)}, u32[]{:S(2)}) copy-start(f32[4,256]{1,0:T(4,128)} %param.34) | copy-start | bytes 12292
  8.8 12.2 %copy-start.33 = (bf16[768,256]{1,0:T(8,128)(2,1)S(1)}, bf16[768,256]{1,0:T(8,128)(2,1)}, u32[]{:S(2)}) copy-start(bf16[768,256]{1,0:T(8,128)(2,1)} %param.30) | copy-start | bytes 1179652
  11.2 176.7 %all-gather.5.cloned.1.call-start = ((), (), s32[]{:S(2)}) async-start(), calls=%async_computation.4 | async-start | bytes 3932160 | tf_op jit(solution)/shard_map/all_gather | solution.py:198
  11.8 5.0 copy-start.55
  15.0 430.6 %all-reduce.25.cloned.1.call-start = ((), (), s32[]{:S(2)}) async-start(), calls=%async_computation.6 | async-start | bytes 2097152 | tf_op jit(solution)/shard_map/psum | solution.py:222
  15.0 68.5 %copy-start.46 = (f32[2048]{0:T(1024)}, f32[2048]{0:T(1024)S(1)}, u32[]{:S(2)}) copy-start(f32[2048]{0:T(1024)S(1)} %get-tuple-element.965) | copy-start | bytes 24580
  15.0 68.5 %copy-start.48 = (f32[2048]{0:T(1024)}, f32[2048]{0:T(1024)S(1)}, u32[]{:S(2)}) copy-start(f32[2048]{0:T(1024)S(1)} %get-tuple-element.966) | copy-start | bytes 24580
  52.5 31.1 %copy-start.10 = (f32[2048,256]{0,1:T(8,128)}, f32[2048,256]{0,1:T(8,128)S(1)}, u32[]{:S(2)}) copy-start(f32[2048,256]{0,1:T(8,128)S(1)} %slice.174) | copy-start | bytes 6291460
  87.0 4.8 copy-start.23
  87.0 4.8 copy-start.72
  129.9 8.4 %copy-start.14 = (bf16[8,6,128,64]{3,2,1,0:T(8,128)(2,1)}, bf16[8,6,128,64]{3,2,1,0:T(8,128)(2,1)S(1)}, u32[]{:S(2)}) copy-start(bf16[8,6,128,64]{3,2,1,0:T(8,128)(2,1)S(1)} %convert_element_type.296) | copy-start | bytes 2359300
  133.9 7.2 copy-start.19
  143.5 23.2 %copy-start.37 = (f32[8,256,6]{1,2,0:T(8,128)S(1)}, f32[8,256,6]{1,2,0:T(8,128)}, u32[]{:S(2)}) copy-start(f32[8,256,6]{1,2,0:T(8,128)} %get-tuple-element.947) | copy-start | bytes 147460
  143.5 23.2 %copy-start.87 = (f32[6]{0:T(128)S(1)}, f32[6]{0:T(128)}, u32[]{:S(2)}) copy-start(f32[6]{0:T(128)} %param.38) | copy-start | bytes 76
  166.7 6.0 copy-start.22
  176.0 5.9 copy-start.7
  294.1 34.5 %copy-start.88 = (f32[6]{0:T(128)S(1)}, f32[6]{0:T(128)}, u32[]{:S(2)}) copy-start(f32[6]{0:T(128)} %param.38) | copy-start | bytes 76
  340.1 4.9 copy-start.68
  340.1 4.9 copy-start.69
  340.1 4.9 copy-start.70
  345.0 4.9 copy-start.59
  345.0 5.0 copy-start.42
  345.1 20.5 %copy-start.43 = (f32[6,8,256]{2,0,1:T(8,128)S(1)}, f32[6,8,256]{2,0,1:T(8,128)}, u32[]{:S(2)}) copy-start(f32[6,8,256]{2,0,1:T(8,128)} %get-tuple-element.516) | copy-start | bytes 147460
  345.1 20.5 %copy-start.92 = (f32[6]{0:T(128)S(1)}, f32[6]{0:T(128)}, u32[]{:S(2)}) copy-start(f32[6]{0:T(128)} %exponential_negate_fusion) | copy-start | bytes 76
  345.1 20.6 %copy-start.90 = (f32[6]{0:T(128)S(1)}, f32[6]{0:T(128)}, u32[]{:S(2)}) copy-start(f32[6]{0:T(128)} %param.36) | copy-start | bytes 76
  377.4 137.1 %all-reduce.29.cloned.1.call-start = ((), (), s32[]{:S(2)}) async-start(), calls=%async_computation.8 | async-start | bytes 3538944 | tf_op jit(solution)/shard_map/psum | solution.py:281
  377.5 6.2 copy-start.32
  377.5 6.2 copy-start.94
  389.9 164.5 %reduce-scatter.5.cloned.1.call-start = ((), (), s32[]{:S(2)}) async-start(), calls=%async_computation.5 | async-start | bytes 3932160 | tf_op jit(solution)/shard_map/reduce_scatter | solution.py:254
  397.1 199.6 %reduce-scatter.3.cloned.1.call-start = ((), (), s32[]{:S(2)}) async-start(), calls=%async_computation.3 | async-start | bytes 3932160 | tf_op jit(solution)/shard_map/reduce_scatter | solution.py:189
  402.6 43.0 %copy-start.17 = (f32[2048,256]{0,1:T(8,128)S(1)}, f32[2048,256]{0,1:T(8,128)}, u32[]{:S(2)}) copy-start(f32[2048,256]{0,1:T(8,128)} %get-tuple-element.920) | copy-start | bytes 6291460
  402.6 46.4 %copy-start.75 = (f32[1,256]{1,0:T(1,128)S(1)}, f32[1,256]{1,0:T(1,128)}, u32[]{:S(2)}) copy-start(f32[1,256]{1,0:T(1,128)} %get-tuple-element.958) | copy-start | bytes 3076
  402.7 46.4 %copy-start.77 = (f32[1,256]{1,0:T(1,128)S(1)}, f32[1,256]{1,0:T(1,128)}, u32[]{:S(2)}) copy-start(f32[1,256]{1,0:T(1,128)} %get-tuple-element.959) | copy-start | bytes 3076
  402.7 46.4 %copy-start.79 = (f32[1,256]{1,0:T(1,128)S(1)}, f32[1,256]{1,0:T(1,128)}, u32[]{:S(2)}) copy-start(f32[1,256]{1,0:T(1,128)} %get-tuple-element.960) | copy-start | bytes 3076
  402.7 46.4 %copy-start.81 = (f32[1,256]{1,0:T(1,128)S(1)}, f32[1,256]{1,0:T(1,128)}, u32[]{:S(2)}) copy-start(f32[1,256]{1,0:T(1,128)} %get-tuple-element.961) | copy-start | bytes 3076
  402.7 327.7 %all-reduce.27.cloned.1.call-start = ((), (), s32[]{:S(2)}) async-start(), calls=%async_computation.7 | async-start | bytes 1572864 | tf_op jit(solution)/shard_map/psum | solution.py:292
  516.8 39.4 %copy-start.15 = (bf16[512,768]{1,0:T(8,128)(2,1)S(1)}, bf16[512,768]{1,0:T(8,128)(2,1)}, u32[]{:S(2)}) copy-start(bf16[512,768]{1,0:T(8,128)(2,1)} %param.25) | copy-start | bytes 2359300
  516.8 39.4 %copy-start.57 = (f32[768]{0:T(1024)S(1)}, f32[768]{0:T(1024)}, u32[]{:S(2)}) copy-start(f32[768]{0:T(1024)} %param.27) | copy-start | bytes 9220
  516.8 39.4 %copy-start.63 = (f32[512]{0:T(512)S(1)}, f32[512]{0:T(512)}, u32[]{:S(2)}) copy-start(f32[512]{0:T(512)} %copy-done.62) | copy-start | bytes 6148
  519.2 37.8 %copy-start.67 = (f32[512]{0:T(512)S(1)}, f32[512]{0:T(512)}, u32[]{:S(2)}) copy-start(f32[512]{0:T(512)} %copy-done.66) | copy-start | bytes 6148
  519.2 77.5 %copy-start.28 = (bf16[512,768]{1,0:T(8,128)(2,1)S(1)}, bf16[512,768]{1,0:T(8,128)(2,1)}, u32[]{:S(2)}) copy-start(bf16[512,768]{1,0:T(8,128)(2,1)} %param.41) | copy-start | bytes 2359300
  519.2 77.5 %copy-start.65 = (f32[512]{0:T(512)S(1)}, f32[512]{0:T(512)}, u32[]{:S(2)}) copy-start(f32[512]{0:T(512)} %copy-done.64) | copy-start | bytes 6148
  (71 other events, 179.2 us)
Sparse Core Ops, SparseCore 0:
  11.3 31.2 all-gather.2
  44.7 28.5 all-gather.4
  377.6 37.2 all-reduce.24
  419.6 94.8 all-reduce.28
  516.9 37.4 reduce-scatter.4
  557.0 38.1 reduce-scatter.2
  600.9 129.3 all-reduce.26
where the time goes:
time: 753 us; the launch traced here: 740 us
  waiting for transfers between devices  243 us (32%)
  other arithmetic  147 us (20%)
  local copies, waits for them, and re-layouts  129 us (17%)
  matrix products  115 us (15%)
  blocking collectives  89.4 us (12%)
  between operations  15.9 us (2%)
    psum x1, waiting for transfers between devices, body(): lax.psum((grad_norm, grad_state, grad_state_taps, grad_state_bias), ('dp'...  131 us
    psum x1, waiting for transfers between devices, body(): lax.psum(grad_gate.astype(jnp.bfloat16), 'dp').astype(jnp.float32)  59.1 us
    dot_general x18, matrix products, one_head(): jnp.einsum('cqs,csp->cqp', scores, head_values, preferred_element_type=jn...  57.6 us
    psum x1, blocking collectives, body(): lax.psum((grad_norm, grad_state, grad_state_taps, grad_state_bias), ('dp'...  39.7 us
    psum x1, blocking collectives, body(): lax.psum(grad_step.astype(jnp.bfloat16), 'dp').astype(jnp.float32)  38 us
    reduce_scatter x1, waiting for transfers between devices, body(): lax.psum_scatter(jnp.einsum('tk,dk->td', part_rows, local_cols, preferred...  34 us
    another operation x10, other arithmetic  28.4 us
    unnamed x212, local copies, waits for them, and re-layouts  25.3 us
  transfers between devices with their start and end apart: 7, of which 4 were waited for; matrix products, arithmetic and copies ran while one was open for 26% of the time, Pallas kernels for 0%

commit v1 on v0

v1 whole, which is shorter than its diff:
```python
import functools

import jax
import jax.numpy as jnp
from jax import lax
from jax.experimental import pallas as pl
from jax.experimental.pallas import tpu as pltpu
from jax.sharding import PartitionSpec as P

K = 4
Q = 256
HALO = 16
LANES = 128
EPSILON = 1e-05
F32 = jnp.float32
BF16 = jnp.bfloat16
HIGHEST = lax.Precision.HIGHEST


def mm(left, right, lc=1, rc=0, precision=None):
    return lax.dot_general(
        left,
        right,
        (((lc,), (rc,)), ((), ())),
        preferred_element_type=F32,
        precision=precision,
    )


def call(kernel, outs, args, scratch=(), flops=0, moved=0):
    specs = [pl.BlockSpec(memory_space=pltpu.SMEM)] + [
        pl.BlockSpec(memory_space=pltpu.VMEM) for _ in args[1:]
    ]
    return pl.pallas_call(
        kernel,
        out_shape=[jax.ShapeDtypeStruct(s, d) for s, d in outs],
        in_specs=specs,
        out_specs=[pl.BlockSpec(memory_space=pltpu.VMEM) for _ in outs],
        scratch_shapes=list(scratch),
        compiler_params=pltpu.CompilerParams(vmem_limit_bytes=60 * 1024 * 1024),
        cost_estimate=pl.CostEstimate(flops=flops, bytes_accessed=moved, transcendentals=0),
    )(*args)


def keeps_of(s_ref, block, blocks):
    place = s_ref[0] * blocks + block
    fresh = (place == 0) | (place == 1) | (place == s_ref[1] - 1)
    return fresh, jnp.where(fresh, 0.0, 1.0).astype(F32)


def row_keep(fresh, distance):
    rows = lax.broadcasted_iota(jnp.int32, (Q, 1), 0)
    return (rows >= jnp.where(fresh, distance, 0)).astype(F32)


def conv_block(ref, base, cols, taps, fresh):
    total = taps[K : K + 1] + taps[K - 1 : K] * ref[pl.ds(base, Q), cols]
    for distance in range(1, K):
        earlier = ref[pl.ds(base - distance, Q), cols]
        total = total + taps[K - 1 - distance : K - distance] * (earlier * row_keep(fresh, distance))
    return total


def silu_slope(values, sig):
    return sig * (1.0 + values * (1.0 - sig))


def first_lanes():
    return lax.broadcasted_iota(jnp.int32, (1, LANES), 1) < LANES // 2


def spread(cols, quantity):
    return jnp.where(
        first_lanes(), cols[:, 2 * quantity : 2 * quantity + 1], cols[:, 2 * quantity + 1 : 2 * quantity + 2]
    )


def head_lanes(rows, heads_first, head_size):
    lane = lax.broadcasted_iota(jnp.int32, rows, 1 if heads_first else 0)
    head = lax.broadcasted_iota(jnp.int32, rows, 0 if heads_first else 1)
    return (lane >= head * head_size) & (lane < (head + 1) * head_size)


def pre_kernel(blocks, s_ref, hid_ref, halo_ref, gain_ref, proj_ref, taps_ref,
               nx_ref, nt_ref, raw_ref, pre_ref, b_ref, c_ref, bt_ref, ct_ref, cb_ref, cbt_ref):
    gain = gain_ref[...]
    rows = blocks * Q

    def norm(v):
        v = v.astype(F32)
        return v * lax.rsqrt(jnp.mean(v * v, axis=1, keepdims=True) + EPSILON) * gain

    halo = norm(halo_ref[...])
    own = norm(hid_ref[...])
    nx_ref[0:HALO] = halo.astype(BF16)
    nx_ref[HALO:] = own.astype(BF16)
    nt_ref[:, 0:rows] = own.T.astype(BF16)
    raw_ref[...] = mm(nx_ref[...], proj_ref[...])
    taps = taps_ref[...]
    state = b_ref.shape[1]
    for block in range(blocks):
        fresh, _ = keeps_of(s_ref, block, blocks)
        pre = conv_block(raw_ref, HALO + block * Q, slice(None), taps, fresh)
        at = pl.ds(block * Q, Q)
        pre_ref[at] = pre
        conv = pre * jax.nn.sigmoid(pre)
        b_mat = conv[:, :state]
        c_mat = conv[:, state:]
        b_low = b_mat.astype(BF16)
        c_low = c_mat.astype(BF16)
        b_ref[at] = b_low
        c_ref[at] = c_low
        bt_ref[:, at] = b_mat.T.astype(BF16)
        ct_ref[:, at] = c_mat.T.astype(BF16)
        cb_ref[block] = mm(c_low, b_low, 1, 1)
        cbt_ref[block] = mm(b_low, c_low, 1, 1)


def step_kernel(blocks, head_size, s_ref, nx_ref, hp_ref, rowp_ref, colp_ref, step_ref, ratio_ref, sig_ref, chan_ref):
    rows = blocks * Q
    depth = nx_ref.shape[1]
    hp = hp_ref[...]
    raw = mm(hp[:, :depth].astype(BF16), nx_ref[HALO:], 1, 1)
    u = raw + hp[:, depth : depth + 1]
    step = jnp.maximum(u, 0.0) + jnp.log1p(jnp.exp(-jnp.abs(u)))
    sig = jax.nn.sigmoid(u)
    step_ref[...] = step
    sig_ref[...] = sig
    ratio_ref[...] = jnp.where(step > 1e-30, sig / jnp.maximum(step, 1e-30), 1.0)
    rate = -jnp.exp(hp[:, depth + 1 : depth + 2])
    move = step * rate
    upto = (
        lax.broadcasted_iota(jnp.int32, (Q, Q), 0) <= lax.broadcasted_iota(jnp.int32, (Q, Q), 1)
    ).astype(F32)
    heads = hp.shape[0]
    lane = lax.broadcasted_iota(jnp.int32, (heads, LANES), 1)
    last_cols = jnp.zeros((heads, LANES), F32)
    lstep = jnp.log(step)
    product = jnp.ones((heads, 1), F32)
    pairs = rowp_ref.shape[0]
    for block in range(blocks):
        at = slice(block * Q, (block + 1) * Q)
        logd = mm(move[:, at], upto, precision=HIGHEST)
        less = logd - lstep[:, at]
        last = logd[:, Q - 1 : Q]
        grown = jnp.exp(logd)
        carry = jnp.exp(last - less)
        final = jnp.exp(last)
        _, kept = keeps_of(s_ref, block, blocks)
        product = product * final * kept
        last_cols = jnp.where(lane == block, final, last_cols)
        for pair in range(pairs):
            for index, values in enumerate((logd, less, grown, carry)):
                rowp_ref[pair, 2 * index : 2 * index + 2, at] = values[2 * pair : 2 * pair + 2]
    last_cols = jnp.where(lane == 6, product, last_cols)
    last_cols = jnp.where(lane == 7, hp[:, depth + 2 : depth + 3], last_cols)
    spots = head_lanes((heads, chan_ref.shape[1]), True, head_size).astype(F32)
    chan_ref[...] = mm(last_cols.T[0:8], spots, precision=HIGHEST)
    for pair in range(pairs):
        colp_ref[pair] = rowp_ref[pair].T


def front_kernel(blocks, group, pieces, s_ref, nx_ref, par_ref, bt_ref, colp_ref, chan_ref, *refs):
    gates, values = refs[:pieces], refs[pieces : 2 * pieces]
    gate_ref, inner_ref, pre_ref, x_ref, s_out, carry_ref = refs[2 * pieces :]
    wide = gates[0].shape[1]
    for p in range(pieces):
        inner_ref[:, p * wide : (p + 1) * wide] = mm(nx_ref[...], values[p][...])
        gate_ref[:, p * wide : (p + 1) * wide] = mm(nx_ref[HALO:], gates[p][...])
    tiles = gate_ref.shape[1] // LANES

    def tile(i, none):
        cols = pl.ds(pl.multiple_of(i * LANES, LANES), LANES)
        far = pl.ds(pl.multiple_of((i + group * tiles) * LANES, LANES), LANES)
        taps = par_ref[:, far]
        for block in range(blocks):
            at = pl.ds(block * Q, Q)
            fresh, kept = keeps_of(s_ref, block, blocks)
            pre = conv_block(inner_ref, HALO + block * Q, cols, taps, fresh)
            pre_ref[at, cols] = pre
            x = pre * jax.nn.sigmoid(pre)
            x_ref[at, cols] = x
            weighted = (spread(colp_ref[i + group * tiles, at, :], 3) * x).astype(BF16)
            state = mm(bt_ref[:, at], weighted)
            s_out[block, :, cols] = state
            if block == 0:
                carry = state
            else:
                carry = chan_ref[block : block + 1, far] * (kept * carry) + state
        carry_ref[:, cols] = carry.astype(BF16)
        return none

    lax.fori_loop(0, tiles, tile, 0)


def intra_kernel(blocks, s_ref, rowp_ref, colp_ref, cb_ref, x0_ref, x1_ref, y_ref):
    half = Q // 2
    first = first_lanes()
    tri = lax.broadcasted_iota(jnp.int32, (half, half), 0) >= lax.broadcasted_iota(
        jnp.int32, (half, half), 1
    )
    for group, x_ref in enumerate((x0_ref, x1_ref)):
        tiles = x_ref.shape[1] // LANES

        def tile(i, none, group=group, x_ref=x_ref, tiles=tiles):
            cols = pl.ds(pl.multiple_of(i * LANES, LANES), LANES)
            pair = i + group * tiles
            far = pl.ds(pl.multiple_of(pair * LANES, LANES), LANES)
            for block in range(blocks):
                at = pl.ds(block * Q, Q)
                x = x_ref[at, cols].astype(BF16)
                both = [jnp.where(first, x, 0), jnp.where(first, 0, x)]
                cp = colp_ref[pair, at, :]
                rp = rowp_ref[pair, :, at]
                tops, bots = [], []
                for k in range(2):
                    ld, ls = cp[:, k : k + 1], rp[2 + k : 3 + k, :]
                    arg = jnp.where(tri, ld[:half] - ls[:, :half], -1e30)
                    tops.append((cb_ref[block, 0:half, 0:half] * jnp.exp(arg)).astype(BF16))
                    arg = ld[half:] - ls[:, :half]
                    bots.append((cb_ref[block, half:, 0:half] * jnp.exp(arg)).astype(BF16))
                    arg = jnp.where(tri, ld[half:] - ls[:, half:], -1e30)
                    bots.append((cb_ref[block, half:, half:] * jnp.exp(arg)).astype(BF16))
                top = mm(jnp.concatenate(tops, 1), jnp.concatenate([b[:half] for b in both], 0))
                bot = mm(jnp.concatenate(bots, 1), jnp.concatenate(both, 0))
                y_ref[pl.ds(block * Q, half), far] = top
                y_ref[pl.ds(block * Q + half, half), far] = bot
            return none

        lax.fori_loop(0, tiles, tile, 0)


def arrive(chan_ref, s_tiles, incoming, kept, far):
    result = []
    for block, state in enumerate(s_tiles):
        incoming = kept[block] * incoming
        result.append(incoming)
        incoming = chan_ref[block : block + 1, far] * incoming + state
    return result


def valid_of(s_ref, blocks, block):
    place = s_ref[0] * blocks + block
    last = place == s_ref[1] - 1
    length = jnp.where(place == 0, s_ref[2], jnp.where(last, s_ref[4], s_ref[3]))
    start = jnp.where(place == 0, 0, jnp.where(last, s_ref[1] - 1, 1))
    rows = lax.broadcasted_iota(jnp.int32, (Q, 1), 0) + (place - start) * Q
    return (rows < length).astype(F32)


def middle_kernel(blocks, pieces, head_size, s_ref, cot_ref, inc_in, colp_ref, chan_ref, par_ref, c_ref, ct_ref,
                  y_ref, *refs):
    outs_w = refs[:pieces]
    g_refs = refs[pieces : pieces + 2]
    x_refs = refs[pieces + 2 : pieces + 4]
    st_refs = refs[pieces + 4 : pieces + 6]
    (ny_ref, dgate_ref, dy_ref, di_ref, carry_ref, dc_ref, rowpart_ref, rows_ref,
     db_ref, dny_ref, mix_ref, sq_ref, cr_ref, inc_ref, dye_ref, hi_ref, lo_ref) = refs[pieces + 6 :]
    for block in range(blocks):
        at = slice(block * Q, (block + 1) * Q)
        db_ref[at] = (cot_ref[at].astype(F32) * valid_of(s_ref, blocks, block)).astype(BF16)
    wide = outs_w[0].shape[0]
    for p in range(pieces):
        dny_ref[:, p * wide : (p + 1) * wide] = mm(db_ref[...], outs_w[p][...], 1, 1).astype(BF16)
    sq_ref[...] = jnp.zeros_like(sq_ref)
    cr_ref[...] = jnp.zeros_like(cr_ref)
    kept = [keeps_of(s_ref, block, blocks)[1] for block in range(blocks)]
    for group in range(2):
        gate_ref, x_ref, st_ref = g_refs[group], x_refs[group], st_refs[group]
        tiles = x_ref.shape[1] // LANES

        def tile(i, none, group=group, gate_ref=gate_ref, x_ref=x_ref, st_ref=st_ref, tiles=tiles):
            cols = pl.ds(pl.multiple_of(i * LANES, LANES), LANES)
            pair = i + group * tiles
            far = pl.ds(pl.multiple_of(pair * LANES, LANES), LANES)
            incs = arrive(chan_ref, [st_ref[b, :, cols] for b in range(blocks)], inc_in[:, far], kept, far)
            gain = par_ref[5:6, far]
            for block in range(blocks):
                at = pl.ds(block * Q, Q)
                inc_low = incs[block].astype(BF16)
                inc_ref[block, :, far] = inc_low
                inter = mm(c_ref[at], inc_low) * spread(colp_ref[pair, at, :], 2)
                mix = y_ref[at, far] + inter + chan_ref[7:8, far] * x_ref[at, cols]
                mix_ref[at, far] = mix
                gate = gate_ref[at, cols]
                gated = mix * (gate * jax.nn.sigmoid(gate))
                sq_ref[at] += gated * gated
                cr_ref[at] += dny_ref[at, far].astype(F32) * gain * gated
            return none

        lax.fori_loop(0, tiles, tile, 0)
    total = 2 * x_refs[0].shape[1]
    scale = lax.rsqrt(jnp.sum(sq_ref[...], axis=1, keepdims=True) / total + EPSILON)
    coef = scale * scale * scale * (jnp.sum(cr_ref[...], axis=1, keepdims=True) / total)
    sq_ref[...] = jnp.broadcast_to(scale, sq_ref.shape)
    cr_ref[...] = jnp.broadcast_to(coef, cr_ref.shape)
    rows_ref[...] = jnp.zeros_like(rows_ref)
    for group in range(2):
        gate_ref, x_ref = g_refs[group], x_refs[group]
        tiles = x_ref.shape[1] // LANES

        def tile(i, none, group=group, gate_ref=gate_ref, x_ref=x_ref, tiles=tiles):
            cols = pl.ds(pl.multiple_of(i * LANES, LANES), LANES)
            pair = i + group * tiles
            far = pl.ds(pl.multiple_of(pair * LANES, LANES), LANES)
            gain = par_ref[5:6, far]
            skip = chan_ref[7:8, far]
            gain_row = jnp.zeros((1, LANES), F32)
            skip_row = jnp.zeros((1, LANES), F32)
            dis = []
            for block in range(blocks):
                at = pl.ds(block * Q, Q)
                gate, mix, x = gate_ref[at, cols], mix_ref[at, far], x_ref[at, cols]
                sig = jax.nn.sigmoid(gate)
                act = gate * sig
                gated = mix * act
                normed = gated * sq_ref[at]
                dny = dny_ref[at, far].astype(F32)
                ny_ref[at, far] = (normed * gain).astype(BF16)
                gain_row += jnp.sum(dny * normed, axis=0, keepdims=True)
                d_gated = dny * gain * sq_ref[at] - gated * cr_ref[at]
                dgate_ref[at, far] = (d_gated * mix * silu_slope(gate, sig)).astype(BF16)
                dy = d_gated * act
                dy_ref[at, far] = dy
                skip_row += jnp.sum(dy * x, axis=0, keepdims=True)
                part = dy.astype(BF16).astype(F32) * (mix - skip * x)
                high = part.astype(BF16)
                hi_ref[at, far] = high
                lo_ref[at, far] = (part - high.astype(F32)).astype(BF16)
                dye = (dy * spread(colp_ref[pair, at, :], 2)).astype(BF16)
                dye_ref[at, far] = dye
                di = mm(ct_ref[:, at], dye)
                di_ref[block, :, far] = di
                dis.append(di)
            rows_ref[0:1, far] = gain_row
            rows_ref[1:2, far] = skip_row
            back = jnp.zeros_like(dis[0])
            for block in reversed(range(blocks)):
                back = kept[block] * (dis[block] + chan_ref[block : block + 1, far] * back)
            carry_ref[:, far] = back.astype(BF16)
            return none

        lax.fori_loop(0, tiles, tile, 0)
    spots = head_lanes((rowpart_ref.shape[0], total), True, head_size).astype(F32).astype(BF16)
    rowpart_ref[...] = mm(spots, hi_ref[...], 1, 1) + mm(spots, lo_ref[...], 1, 1)
    for block in range(blocks):
        at = slice(block * Q, (block + 1) * Q)
        dc_ref[at] = mm(dye_ref[at], inc_ref[block], 1, 1)


def out_kernel(blocks, pieces, s_ref, hid_ref, cot_ref, nt_ref, ny_ref, dgate_ref, *refs):
    outs_w = refs[:pieces]
    mixed_ref = refs[pieces]
    g_outs = refs[pieces + 1 : 2 * pieces + 1]
    g_gates = refs[2 * pieces + 1 : 3 * pieces + 1]
    db_ref = refs[3 * pieces + 1]
    wide = outs_w[0].shape[0]
    rows = blocks * Q
    for block in range(blocks):
        at = slice(block * Q, (block + 1) * Q)
        db_ref[at] = (cot_ref[at].astype(F32) * valid_of(s_ref, blocks, block)).astype(BF16)
    for p in range(pieces):
        span = slice(p * wide, (p + 1) * wide)
        g_outs[p][...] = mm(ny_ref[:, span], db_ref[...], 0, 0).astype(BF16)
        g_gates[p][...] = mm(nt_ref[:, 0:rows], dgate_ref[:, span]).astype(BF16)
    for block in range(blocks):
        at = slice(block * Q, (block + 1) * Q)
        branch = mm(ny_ref[at, 0:wide], outs_w[0][...])
        for p in range(1, pieces):
            branch += mm(ny_ref[at, p * wide : (p + 1) * wide], outs_w[p][...])
        mixed_ref[at] = (hid_ref[at].astype(F32) + valid_of(s_ref, blocks, block) * branch).astype(BF16)


def back_kernel(blocks, s_ref, rowp_ref, colp_ref, cbt_ref, b_ref, c_ref, dy_ref, x0_ref, x1_ref,
                dx_ref, db_ref, dc_ref, acc_ref):
    half = Q // 2
    first = first_lanes()
    tri = lax.broadcasted_iota(jnp.int32, (half, half), 0) <= lax.broadcasted_iota(
        jnp.int32, (half, half), 1
    )
    acc_ref[...] = jnp.zeros_like(acc_ref)
    for group, x_ref in enumerate((x0_ref, x1_ref)):
        tiles = x_ref.shape[1] // LANES

        def tile(i, none, group=group, x_ref=x_ref, tiles=tiles):
            cols = pl.ds(pl.multiple_of(i * LANES, LANES), LANES)
            pair = i + group * tiles
            far = pl.ds(pl.multiple_of(pair * LANES, LANES), LANES)
            for block in range(blocks):
                at = pl.ds(block * Q, Q)
                x = x_ref[at, cols].astype(BF16)
                dy = dy_ref[at, far].astype(BF16)
                dys = [jnp.where(first, dy, 0), jnp.where(first, 0, dy)]
                xs = [jnp.where(first, x, 0), jnp.where(first, 0, x)]
                cp = colp_ref[pair, at, :]
                rp = rowp_ref[pair, :, at]
                tops, bots = [], []
                w00 = w01 = w11 = 0.0
                for k in range(2):
                    ls, ld = cp[:, 2 + k : 3 + k], rp[k : k + 1, :]
                    ds_top = mm(xs[k][:half], dy, 1, 1)
                    ds_bot = mm(xs[k][half:], dy[half:], 1, 1)
                    e00 = jnp.exp(jnp.where(tri, ld[:, :half] - ls[:half], -1e30))
                    e01 = jnp.exp(ld[:, half:] - ls[:half])
                    e11 = jnp.exp(jnp.where(tri, ld[:, half:] - ls[half:], -1e30))
                    tops.append((cbt_ref[block, 0:half, 0:half] * e00).astype(BF16))
                    tops.append((cbt_ref[block, 0:half, half:] * e01).astype(BF16))
                    bots.append((cbt_ref[block, half:, half:] * e11).astype(BF16))
                    w00 += ds_top[:, :half] * e00
                    w01 += ds_top[:, half:] * e01
                    w11 += ds_bot * e11
                acc_ref[block, 0:half, 0:half] += w00
                acc_ref[block, 0:half, half:] += w01
                acc_ref[block, half:, half:] += w11
                dx_ref[pl.ds(block * Q, half), far] = mm(jnp.concatenate(tops, 1), jnp.concatenate(dys, 0))
                dx_ref[pl.ds(block * Q + half, half), far] = mm(
                    jnp.concatenate(bots, 1), jnp.concatenate([d[half:] for d in dys], 0)
                )
            return none

        lax.fori_loop(0, tiles, tile, 0)
    for block in range(blocks):
        at = slice(block * Q, (block + 1) * Q)
        acc = acc_ref[block].astype(BF16)
        db_ref[at] = mm(acc, c_ref[at])
        dc_ref[at] = mm(acc, b_ref[at], 0, 0)


def tail_kernel(blocks, head_size, s_ref, back_in, inc_in, colp_ref, chan_ref, par_ref, b_ref, dx_ref, dy_ref, di_ref,
                dbin_ref, dcin_ref, dcx_ref, rowpart_ref, step_ref, ratio_ref, sig_ref, hp_ref, rows_ref,
                raw_ref, spre_ref, staps_ref, x0_ref, x1_ref, p0_ref, p1_ref, n0_ref, n1_ref, st0_ref, st1_ref,
                dinner_ref, dstate_ref, dstep_ref, vgrad_ref, sgrad_ref, hgrad_ref,
                wx_ref, gs_ref, hi_ref, lo_ref, last_ref, d_ref, e_ref):
    rows = blocks * Q
    kept = [keeps_of(s_ref, block, blocks)[1] for block in range(blocks)]
    total = dx_ref.shape[1]
    last_ref[...] = jnp.zeros_like(last_ref)
    d_ref[...] = jnp.zeros_like(d_ref)
    e_ref[...] = jnp.zeros_like(e_ref)
    vgrad_ref[...] = jnp.zeros_like(vgrad_ref)
    sgrad_ref[...] = jnp.zeros_like(sgrad_ref)

    def conv_back(work, taps, values_of, slope_of, store, grads, cols, grad_cols):
        sums = [0.0] * (K + 1)
        for block in range(blocks):
            at = pl.ds(block * Q, Q)
            fresh, _ = keeps_of(s_ref, block, blocks)
            d_pre = slope_of(block)
            work[0, pl.ds(HALO + block * Q, Q)] = d_pre
            sums[K] += jnp.sum(d_pre, axis=0, keepdims=True)
            sums[K - 1] += jnp.sum(d_pre * values_of(HALO + block * Q), axis=0, keepdims=True)
            for distance in range(1, K):
                held = d_pre * row_keep(fresh, distance)
                work[distance, pl.ds(HALO + block * Q, Q)] = held
                sums[K - 1 - distance] += jnp.sum(
                    held * values_of(HALO + block * Q - distance), axis=0, keepdims=True
                )
        for index in range(K + 1):
            grads[index : index + 1, grad_cols] = sums[index]
        for begin, count in [(0, HALO)] + [(HALO + b * Q, Q) for b in range(blocks)]:
            out = taps[K - 1 : K] * work[0, pl.ds(begin, count)]
            for distance in range(1, K):
                out = out + taps[K - 1 - distance : K - distance] * work[distance, pl.ds(begin + distance, count)]
            store(begin, count, out.astype(BF16))

    for group in range(2):
        x_ref, p_ref, n_ref, st_ref = (
            (x0_ref, x1_ref)[group], (p0_ref, p1_ref)[group], (n0_ref, n1_ref)[group], (st0_ref, st1_ref)[group],
        )
        tiles = x_ref.shape[1] // LANES

        def tile(i, none, group=group, x_ref=x_ref, p_ref=p_ref, n_ref=n_ref, st_ref=st_ref, tiles=tiles):
            cols = pl.ds(pl.multiple_of(i * LANES, LANES), LANES)
            pair = i + group * tiles
            far = pl.ds(pl.multiple_of(pair * LANES, LANES), LANES)
            taps = par_ref[:, far]
            skip = chan_ref[7:8, far]
            incs = arrive(chan_ref, [st_ref[b, :, cols] for b in range(blocks)], inc_in[:, far], kept, far)
            back = back_in[:, far]
            for block in reversed(range(blocks)):
                fade = chan_ref[block : block + 1, far]
                gs_ref[block, :, far] = back.astype(BF16)
                last_ref[block : block + 1, far] = fade * jnp.sum(incs[block] * back, axis=0, keepdims=True)
                back = kept[block] * (di_ref[block, :, far] + fade * back)

            def slope_of(block):
                at = pl.ds(block * Q, Q)
                x = x_ref[at, cols]
                carry = spread(colp_ref[pair, at, :], 3)
                weighted = carry * x
                wx_ref[at, far] = weighted.astype(BF16)
                d_weighted = mm(b_ref[at], gs_ref[block, :, far])
                dx = dx_ref[at, far]
                moved = weighted * d_weighted
                last_ref[block : block + 1, far] += jnp.sum(moved, axis=0, keepdims=True)
                part = x.astype(BF16).astype(F32) * dx + moved
                high = part.astype(BF16)
                hi_ref[at, far] = high
                lo_ref[at, far] = (part - high.astype(F32)).astype(BF16)
                d_x = dx + carry * d_weighted + skip * dy_ref[at, far]
                pre = p_ref[at, cols]
                return d_x * silu_slope(pre, jax.nn.sigmoid(pre))

            def store(begin, count, value):
                dinner_ref[pl.ds(begin, count), far] = value

            conv_back(d_ref, taps, lambda at: n_ref[pl.ds(at, Q), cols], slope_of, store, vgrad_ref, None, far)
            return none

        lax.fori_loop(0, tiles, tile, 0)

    wide = raw_ref.shape[1]
    state = wide // 2
    d_states = []
    for block in range(blocks):
        at = slice(block * Q, (block + 1) * Q)
        d_b = dbin_ref[at] + mm(wx_ref[at], gs_ref[block], 1, 1)
        d_c = dcin_ref[at] + dcx_ref[at]
        d_states.append(jnp.concatenate([d_b, d_c], 1))

    def state_slope(block):
        pre = spre_ref[pl.ds(block * Q, Q), :]
        return d_states[block] * silu_slope(pre, jax.nn.sigmoid(pre))

    def state_store(begin, count, value):
        dstate_ref[pl.ds(begin, count), :] = value

    conv_back(e_ref, staps_ref[...], lambda at: raw_ref[pl.ds(at, Q), :], state_slope, state_store, sgrad_ref, None, slice(None))

    heads = hp_ref.shape[0]
    depth = hp_ref.shape[1] - LANES
    spots = head_lanes((heads, total), True, head_size).astype(F32)
    low_spots = spots.astype(BF16)
    cols = mm(low_spots, hi_ref[...], 1, 1) + mm(low_spots, lo_ref[...], 1, 1)
    lasts = mm(spots, last_ref[...], 1, 1, precision=HIGHEST)
    skips = mm(spots, rows_ref[...], 1, 1, precision=HIGHEST)[:, 1:2]
    rate = -jnp.exp(hp_ref[:, depth + 1 : depth + 2])
    lane = lax.broadcasted_iota(jnp.int32, (heads, Q), 1)
    upto = (
        lax.broadcasted_iota(jnp.int32, (Q, Q), 0) >= lax.broadcasted_iota(jnp.int32, (Q, Q), 1)
    ).astype(F32)
    grad_bias = jnp.zeros((heads, 1), F32)
    grad_decay = jnp.zeros((heads, 1), F32)
    for block in range(blocks):
        at = slice(block * Q, (block + 1) * Q)
        d_log = rowpart_ref[:, at] - cols[:, at]
        d_log = d_log + jnp.where(lane == Q - 1, lasts[:, block : block + 1], 0.0)
        d_move = mm(d_log, upto, precision=HIGHEST)
        d_raw = cols[:, at] * ratio_ref[:, at] + rate * d_move * sig_ref[:, at]
        grad_bias += jnp.sum(d_raw, axis=1, keepdims=True)
        grad_decay += rate * jnp.sum(step_ref[:, at] * d_move, axis=1, keepdims=True)
        dstep_ref[:, at] = d_raw.astype(BF16)
    wide_lane = lax.broadcasted_iota(jnp.int32, (heads, LANES), 1)
    hgrad_ref[...] = jnp.where(
        wide_lane == 0, grad_bias, jnp.where(wide_lane == 1, grad_decay, jnp.where(wide_lane == 2, skips, 0.0))
    )


def value_kernel(pieces, s_ref, nx_ref, nt_ref, dinner_ref, dstep_ref, *refs):
    wide = refs[0].shape[1]
    rows = dinner_ref.shape[0] - HALO
    for p in range(pieces):
        span = slice(p * wide, (p + 1) * wide)
        total = mm(nt_ref[:, 0:rows], dinner_ref[HALO:, span])
        refs[p][...] = (total + mm(nx_ref[0:HALO], dinner_ref[0:HALO, span], 0, 0)).astype(BF16)
    refs[pieces][...] = mm(dstep_ref[...], nx_ref[HALO:])


def norm_kernel(pieces, s_ref, hid_ref, halo_ref, cot_ref, gain_ref, nx_ref, nt_ref, dgate_ref, dinner_ref, dstate_ref,
                dstep_ref, hp_ref, sproj_ref, sgrad_ref, *refs):
    gates, values = refs[:pieces], refs[pieces : 2 * pieces]
    grad_ref, extra_ref, d_ref = refs[2 * pieces :]
    wide = gates[0].shape[1]
    rows = hid_ref.shape[0]
    depth = hid_ref.shape[1]
    gain = gain_ref[...]
    gain_sum = jnp.zeros((1, depth), F32)

    def finish(values_in, d_normed):
        h = values_in.astype(F32)
        scale = lax.rsqrt(jnp.mean(h * h, axis=1, keepdims=True) + EPSILON)
        weighted = gain * d_normed
        inner = jnp.mean(weighted * h, axis=1, keepdims=True)
        return scale * weighted - h * (scale * scale * scale * inner), jnp.sum(d_normed * h * scale, axis=0, keepdims=True)

    total = mm(dinner_ref[0:HALO, 0:wide], values[0][...], 1, 1)
    for p in range(1, pieces):
        total += mm(dinner_ref[0:HALO, p * wide : (p + 1) * wide], values[p][...], 1, 1)
    total += mm(dstate_ref[0:HALO], sproj_ref[...], 1, 1)
    extra_ref[...], part = finish(halo_ref[...], total)
    gain_sum += part
    for begin in range(0, rows, Q):
        at = slice(begin, begin + Q)
        ext = slice(begin + HALO, begin + HALO + Q)
        total = mm(dstate_ref[ext], sproj_ref[...], 1, 1)
        total += mm(dstep_ref[:, at], hp_ref[:, 0:depth].astype(BF16), 0, 0)
        for p in range(pieces):
            span = slice(p * wide, (p + 1) * wide)
            total += mm(dgate_ref[at, span], gates[p][...], 1, 1)
            total += mm(dinner_ref[ext, span], values[p][...], 1, 1)
        d_hidden, part = finish(hid_ref[at], total.astype(BF16).astype(F32))
        gain_sum += part
        grad_ref[at] = cot_ref[at].astype(F32) + d_hidden
    state = mm(nt_ref[:, 0:rows], dstate_ref[HALO:]) + mm(nx_ref[0:HALO], dstate_ref[0:HALO], 0, 0)
    side = sgrad_ref.shape[1]
    d_ref[...] = jnp.zeros_like(d_ref)
    d_ref[0:depth] = state
    d_ref[depth : depth + 5] = sgrad_ref[0:5]
    for part_at in range(depth // side):
        d_ref[depth + 8 + part_at : depth + 9 + part_at] = gain_sum[:, part_at * side : (part_at + 1) * side]


def swap(value, axis, mask):
    size = lax.axis_size(axis)
    return lax.ppermute(value, axis, [(i, i ^ mask) for i in range(size)])


def pick(value, index):
    return lax.dynamic_index_in_dim(value, index, 0, keepdims=False)


def reduce_dp(value):
    size = lax.axis_size("dp")
    index = lax.axis_index("dp")
    rows, columns = value.shape
    side, deep = index & 1, (index >> 1) & 3
    halves = value.reshape(2, rows // 2, columns)
    got = swap(pick(halves, 1 - side).astype(BF16), "dp", 1)
    half = pick(halves, side).astype(F32) + got.astype(F32)
    quarters = half.astype(BF16).reshape(4, rows // 8, columns)
    sent = [swap(pick(quarters, deep ^ m), "dp", 2 * m) for m in (1, 2, 3)]
    own = pick(half.reshape(4, rows // 8, columns), deep)
    for part in sent:
        own = own + part.astype(F32)
    own = own.astype(BF16)
    bit = 8
    while bit < size:
        own = (own.astype(F32) + swap(own, "dp", bit).astype(F32)).astype(BF16)
        bit *= 2
    parts = jnp.stack([own] + [swap(own, "dp", 2 * m) for m in (1, 2, 3)])
    half = jnp.concatenate([pick(parts, deep ^ a) for a in range(4)], axis=0)
    other = swap(half, "dp", 1)
    return jnp.concatenate([jnp.where(side == 0, half, other), jnp.where(side == 0, other, half)], axis=0)


def gather_pieces(value):
    ways = lax.axis_size("head")
    pieces = {0: value}
    order = [1 << b for b in range(ways.bit_length() - 1)]
    far = order[1:] + order[:1]
    for mask in far[:-1]:
        for p in list(pieces):
            pieces[p | mask] = swap(pieces[p], "head", mask)
    for p in list(pieces):
        pieces[p | 1] = swap(pieces[p], "head", 1)
    return [pieces[p] for p in range(ways)]


def reduce_pieces(pieces):
    ways = len(pieces)
    mask = 1
    live = {p: v for p, v in enumerate(pieces)}
    order = [1 << b for b in range(ways.bit_length() - 1)]
    for mask in order:
        got = {p ^ mask: swap(live[p].astype(BF16), "head", mask) for p in live if p & mask}
        live = {p: live[p].astype(F32) + got[p].astype(F32) for p in live if not p & mask}
    return live[0]


def body(hidden, lengths, norm_gain, gate_proj, value_proj, state_proj, step_proj, value_taps, value_bias,
         state_taps, state_bias, step_bias, decay_log, skip_gain, out_gain, out_proj, cotangent):
    rows, depth = hidden.shape
    ways = lax.axis_size("head")
    me = lax.axis_index("head")
    blocks = rows // Q
    wide = gate_proj.shape[1]
    share = step_proj.shape[1]
    total = wide * ways
    heads = share * ways
    head_size = wide // share
    pairs = heads // 2
    side = state_proj.shape[1]
    state = side // 2
    group = total // 2
    padded = -(-heads // 32) * 32
    scalars = jnp.concatenate(
        [jnp.stack([me, blocks * ways]).astype(jnp.int32), lengths[0], jnp.zeros((3,), jnp.int32)]
    )

    halo = lax.ppermute(hidden[rows - HALO :], "head", [(i, i + 1) for i in range(ways - 1)])
    top = jnp.concatenate(
        [step_proj.T.astype(F32), step_bias[:, None], decay_log[:, None], skip_gain[:, None], jnp.zeros((share, LANES - 3), F32)],
        axis=1,
    )
    low = jnp.concatenate([value_taps, value_bias[None], out_gain[None]], axis=0)
    pack = jnp.concatenate(
        [
            jnp.pad(top, ((0, 8 - share), (0, 0))),
            jnp.pad(low, ((0, 2), (0, depth + LANES - wide))),
        ],
        axis=0,
    )
    packs = gather_pieces(pack)
    gates = gather_pieces(gate_proj)
    values = gather_pieces(value_proj)
    outs = gather_pieces(out_proj)

    def merged(parts, axis):
        if wide % LANES == 0:
            return parts
        return [jnp.concatenate(parts[i : i + 2], axis=axis) for i in range(0, len(parts), 2)]

    gates_m, values_m, outs_m = merged(gates, 1), merged(values, 1), merged(outs, 0)
    pieces = len(gates_m)
    half = pieces // 2
    hp = jnp.pad(jnp.concatenate([p[:share] for p in packs], axis=0), ((0, padded - heads), (0, 0)))
    par = jnp.concatenate([p[8:, :wide] for p in packs], axis=1)
    gain_in = norm_gain[None]
    staps = jnp.pad(jnp.concatenate([state_taps, state_bias[None]], axis=0), ((0, 3), (0, 0)))

    ext = rows + HALO
    (nx, nt, state_raw, state_pre, b_low, c_low, b_t, c_t, cb, cbt) = call(
        functools.partial(pre_kernel, blocks),
        [((ext, depth), BF16), ((depth, rows), BF16), ((ext, side), F32), ((rows, side), F32),
         ((rows, state), BF16), ((rows, state), BF16), ((state, rows), BF16), ((state, rows), BF16),
         ((blocks, Q, Q), F32), ((blocks, Q, Q), F32)],
        [scalars, hidden, halo, gain_in, state_proj, staps],
        flops=2 * ext * depth * side,
        moved=8 << 20,
    )
    rowp, colp, step, ratio, sig, chan = call(
        functools.partial(step_kernel, blocks, head_size),
        [((pairs, 8, rows), F32), ((pairs, rows, 8), F32), ((padded, rows), F32), ((padded, rows), F32),
         ((padded, rows), F32), ((8, total), F32)],
        [scalars, nx, hp],
        flops=2 * rows * depth * padded,
        moved=4 << 20,
    )
    fronts = []
    for g in range(2):
        fronts.append(
            call(
                functools.partial(front_kernel, blocks, g, half),
                [((rows, group), F32), ((ext, group), F32), ((rows, group), F32), ((rows, group), F32),
                 ((blocks, state, group), F32), ((state, group), BF16)],
                [scalars, nx, par, b_t, colp, chan, *gates_m[g * half : (g + 1) * half], *values_m[g * half : (g + 1) * half]],
                flops=4 * rows * depth * group,
                moved=12 << 20,
            )
        )
    (gate0, inner0, pre0, x0, st0, car0), (gate1, inner1, pre1, x1, st1, car1) = fronts
    (y_intra,) = call(
        functools.partial(intra_kernel, blocks),
        [((rows, total), F32)],
        [scalars, rowp, colp, cb, x0, x1],
        flops=2 * heads * rows * Q * LANES,
        moved=10 << 20,
    )

    fades = {0: chan[6:7]}

    def turned(value, mask):
        parts = [value[..., (p ^ mask) * wide : ((p ^ mask) + 1) * wide] for p in range(ways)]
        return jnp.concatenate(parts, axis=-1)

    order = [1 << b for b in range(ways.bit_length() - 1)]
    for mask in order:
        for p in list(fades):
            fades[p | mask] = turned(swap(fades[p], "head", mask), mask)

    def scan(own, forward):
        run, run_fade = own, fades[0]
        before = jnp.zeros_like(own, dtype=F32)
        before_fade = jnp.ones_like(run_fade)
        for mask in order:
            got = turned(swap(run.astype(BF16), "head", mask), mask).astype(F32)
            got_fade = functools.reduce(jnp.multiply, [fades[mask ^ low] for low in range(mask)])
            later = ((me & mask) != 0) if forward else ((me & mask) == 0)
            before = jnp.where(later, before_fade * got + before, before)
            before_fade = jnp.where(later, before_fade * got_fade, before_fade)
            if mask != order[-1]:
                mine = run.astype(F32)
                run = jnp.where(later, run_fade * got + mine, got_fade * mine + got)
                run_fade = run_fade * got_fade
        return before

    inc_in = scan(jnp.concatenate([car0, car1], axis=1), True)
    big = pltpu.VMEM
    (ny, d_gate, d_y, d_inc, back_car, dc_inter, rowpart, rows_sum) = call(
        functools.partial(middle_kernel, blocks, pieces, head_size),
        [((rows, total), BF16), ((rows, total), BF16), ((rows, total), F32), ((blocks, state, total), F32),
         ((state, total), BF16), ((rows, state), F32), ((padded, rows), F32), ((8, total), F32)],
        [scalars, cotangent, inc_in, colp, chan, par, c_low, c_t, y_intra, *outs_m, gate0, gate1, x0, x1, st0, st1],
        scratch=[big((rows, depth), BF16), big((rows, total), BF16), big((rows, total), F32), big((rows, LANES), F32),
                 big((rows, LANES), F32), big((blocks, state, total), BF16), big((rows, total), BF16),
                 big((rows, total), BF16), big((rows, total), BF16)],
        flops=2 * rows * depth * total,
        moved=30 << 20,
    )
    back_in = scan(back_car, False)
    res = call(
        functools.partial(out_kernel, blocks, pieces),
        [((rows, depth), BF16)] + [((total // pieces, depth), BF16)] * pieces + [((depth, total // pieces), BF16)] * pieces,
        [scalars, hidden, cotangent, nt, ny, d_gate, *outs_m],
        scratch=[big((rows, depth), BF16)],
        flops=6 * rows * depth * total,
        moved=12 << 20,
    )
    mixed, g_out, g_gate = res[0], res[1 : pieces + 1], res[pieces + 1 :]

    def split(parts, axis):
        if wide % LANES == 0:
            return list(parts)
        return [h for p in parts for h in jnp.split(p, 2, axis=axis)]

    grad_out = reduce_dp(reduce_pieces(split(g_out, 0)))
    grad_gate = reduce_dp(reduce_pieces(split(g_gate, 1)))

    (dx, db_in, dc_in) = call(
        functools.partial(back_kernel, blocks),
        [((rows, total), F32), ((rows, state), F32), ((rows, state), F32)],
        [scalars, rowp, colp, cbt, b_low, c_low, d_y, x0, x1],
        scratch=[big((blocks, Q, Q), F32)],
        flops=6 * heads * rows * Q * LANES,
        moved=14 << 20,
    )
    (d_inner, d_state, d_step, vgrad, sgrad, hgrad) = call(
        functools.partial(tail_kernel, blocks, head_size),
        [((ext, total), BF16), ((ext, side), BF16), ((padded, rows), BF16), ((8, total), F32), ((8, side), F32),
         ((padded, LANES), F32)],
        [scalars, back_in, inc_in, colp, chan, par, b_low, dx, d_y, d_inc, db_in, dc_in, dc_inter, rowpart, step, ratio,
         sig, hp, rows_sum, state_raw, state_pre, staps, x0, x1, pre0, pre1, inner0, inner1, st0, st1],
        scratch=[big((rows, total), BF16), big((blocks, state, total), BF16), big((rows, total), BF16),
                 big((rows, total), BF16), big((8, total), F32), big((K, rows + 2 * HALO, LANES), F32),
                 big((K, rows + 2 * HALO, side), F32)],
        flops=6 * rows * state * total,
        moved=30 << 20,
    )
    res = call(
        functools.partial(value_kernel, pieces),
        [((depth, total // pieces), BF16)] * pieces + [((padded, depth), F32)],
        [scalars, nx, nt, d_inner, d_step],
        flops=2 * rows * depth * total,
        moved=6 << 20,
    )
    g_value, g_step = res[:pieces], res[pieces]
    grad_value = reduce_dp(reduce_pieces(split(g_value, 1)))
    extra_rows = 832
    (grad_hidden, extra, d_pack) = call(
        functools.partial(norm_kernel, pieces),
        [((rows, depth), F32), ((HALO, depth), F32), ((extra_rows, side), F32)],
        [scalars, hidden, halo, cotangent, gain_in, nx, nt, d_gate, d_inner, d_state, d_step, hp, state_proj, sgrad,
         *gates_m, *values_m],
        flops=4 * rows * depth * total,
        moved=12 << 20,
    )
    extra = lax.ppermute(extra, "head", [(i + 1, i) for i in range(ways - 1)])
    grad_hidden = grad_hidden.at[rows - HALO :].add(extra)

    smalls = []
    for p in range(ways):
        span = slice(p * wide, (p + 1) * wide)
        some = slice(p * share, (p + 1) * share)
        flat = jnp.concatenate(
            [vgrad[0:5, span].reshape(-1), rows_sum[0, span], g_step[some].reshape(-1), hgrad[some, 0:3].reshape(-1)]
        )
        smalls.append(jnp.pad(flat, (0, 32 * side - flat.shape[0])).reshape(32, side))
    core = me & 1
    low_half, high_half = d_pack[: extra_rows // 2], d_pack[extra_rows // 2 :]
    got = swap(jnp.where(core == 0, high_half, low_half).astype(BF16), "head", 1)
    common = jnp.where(core == 0, low_half, high_half) + got.astype(F32)
    for mask in order[1:]:
        low_common = common.astype(BF16)
        common = low_common.astype(F32) + swap(low_common, "head", mask).astype(F32)
    own_small = reduce_pieces(smalls)
    both = reduce_dp(jnp.concatenate([common, own_small], axis=0))
    own_half = both[: extra_rows // 2]
    other = swap(own_half, "head", 1)
    d_all = jnp.concatenate(
        [jnp.where(core == 0, own_half, other), jnp.where(core == 0, other, own_half)], axis=0
    ).astype(F32)
    flat = both[extra_rows // 2 :].astype(F32).reshape(-1)
    grad_vtaps = flat[: 4 * wide].reshape(4, wide)
    grad_vbias = flat[4 * wide : 5 * wide]
    grad_gain = flat[5 * wide : 6 * wide]
    grad_step = flat[6 * wide : 6 * wide + share * depth].reshape(share, depth).T
    rest = flat[6 * wide + share * depth : 6 * wide + share * depth + 3 * share].reshape(share, 3)
    return (
        mixed,
        grad_hidden,
        d_all[depth + 8 : depth + 8 + depth // side].reshape(-1),
        grad_gate.astype(F32),
        grad_value.astype(F32),
        d_all[:depth],
        grad_step,
        grad_vtaps,
        grad_vbias,
        d_all[depth : depth + 4],
        d_all[depth + 4],
        rest[:, 0],
        rest[:, 1],
        rest[:, 2],
        grad_gain,
        grad_out.astype(F32),
    )


def solution(mesh):
    rows = P(("dp", "head"), None)
    in_specs = (
        rows, P("dp", None), P(), P(None, "head"), P(None, "head"), P(), P(None, "head"), P(None, "head"),
        P("head"), P(), P(), P("head"), P("head"), P("head"), P("head"), P("head", None), rows,
    )
    out_specs = (
        rows, rows, P(), P(None, "head"), P(None, "head"), P(), P(None, "head"), P(None, "head"),
        P("head"), P(), P(), P("head"), P("head"), P("head"), P("head"), P("head", None),
    )
    return jax.shard_map(body, mesh=mesh, in_specs=in_specs, out_specs=out_specs, check_vma=False)
```

time: 753 us -> 333 us (0.44); the launches traced: 740 us -> 332 us
  waiting for transfers between devices: 243 us -> 76.6 us
  other arithmetic: 147 us -> 26.5 us
  Pallas kernels: 0 us -> 119 us
  matrix products: 115 us -> 0 us
  local copies, waits for them, and re-layouts: 129 us -> 20.3 us
  blocking collectives: 89.4 us -> 0 us
  starting transfers between devices: 0.54 us -> 87.6 us
  between operations: 15.9 us -> 1.55 us
    psum x3 -> x0, waiting for transfers between devices: 190 us -> none  [the longest x1 131 us: body(): lax.psum((grad_norm, grad_state, grad_state_taps, grad_state_bias), ('dp'...]
    pallas_call x0 -> x11, Pallas kernels: none -> 119 us  [call(): pl.pallas_call(kernel, out_shape=[jax.ShapeDtypeStruct(s, d) for s, d in...]
    dot_general x34 -> x0, matrix products: 113 us -> none  [the longest x18 57.6 us: one_head(): jnp.einsum('cqs,csp->cqp', scores, head_values, preferred_element_type=jn...]
    psum x4 -> x0, blocking collectives: 89.4 us -> none  [the longest x1 39.7 us: body(): lax.psum((grad_norm, grad_state, grad_state_taps, grad_state_bias), ('dp'...]
    ppermute x0 -> x66, starting transfers between devices: none -> 87.6 us  [the longest x64 84.2 us: swap(): return lax.ppermute(value, axis, [(i, i ^ mask) for i in range(size)])]
    ppermute x0 -> x66, waiting for transfers between devices: none -> 76.6 us  [the longest x64 75 us: swap(): return lax.ppermute(value, axis, [(i, i ^ mask) for i in range(size)])]
    reduce_sum x19 -> x0, other arithmetic: 42.4 us -> none  [the longest x8 14.4 us: advance(): return (fading[:, None, None] * arriving + local_state, arriving)]
    reduce_scatter x2 -> x0, waiting for transfers between devices: 34.1 us -> none  [the longest x1 34 us: body(): lax.psum_scatter(jnp.einsum('tk,dk->td', part_rows, local_cols, preferred...]
  transfers between devices with their start and end apart: 7 -> 66, of which waited for: 4 -> 24; matrix products, arithmetic and copies ran while one was open for 26% -> 12% of each run, Pallas kernels for 0% -> 24%
where the time goes in v1:
time: 333 us; the launch traced here: 332 us
  Pallas kernels  119 us (36%)
  starting transfers between devices  87.6 us (26%)
  waiting for transfers between devices  76.6 us (23%)
  other arithmetic  26.5 us (8%)
  local copies, waits for them, and re-layouts  20.3 us (6%)
    pallas_call x11, Pallas kernels, call(): pl.pallas_call(kernel, out_shape=[jax.ShapeDtypeStruct(s, d) for s, d in...  119 us
    ppermute x64, starting transfers between devices, swap(): return lax.ppermute(value, axis, [(i, i ^ mask) for i in range(size)])  84.2 us
    ppermute x64, waiting for transfers between devices, swap(): return lax.ppermute(value, axis, [(i, i ^ mask) for i in range(size)])  75 us
  transfers between devices with their start and end apart: 66, of which 24 were waited for; matrix products, arithmetic and copies ran while one was open for 12% of the time, Pallas kernels for 24%

profile of v1, /device:TPU:0, one launch (start us, length us, event | category | flops | bytes accessed | tf_op | source)
XLA Modules:
  0.0 331.6 jit_solution(11968715453229438879)
XLA Ops:
  0.6 3.0 collective-permute-start.9
  8.9 2.0 collective-permute-start.2
  11.6 1.9 collective-permute-start
  13.9 15.9 %collective-permute-start.6 = (bf16[768,384]{1,0:T(8,128)(2,1)}, bf16[768,384]{1,0:T(8,128)(2,1)S(1)}, u32[]{:S(2)}, u32[]{:S(2)}) collective-permute-start(bf16[768,384]{1,0:T(8,128)(2,1)} %refs_4_.1), channel_id=1, source_target_pairs={{0,1},{1,0},{2,3},{3,2},{4,5},{5,4},{6,7},{7,6},{8,9},{9,8},{10,11... | collective-permute-start | bytes 1769480 | tf_op jit(solution)/shard_map/ppermute | solution.py:615
  36.1 4.2 %shard_map.288 = (bf16[528,768]{1,0:T(8,128)(2,1)}, bf16[768,512]{1,0:T(8,128)(2,1)}, f32[528,256]{1,0:T(8,128)}, f32[512,256]{1,0:T(8,128)}, bf16[512,128]{1,0:...) custom-call(s32[8]{0:T(128)} %pad_add_fusion.s_ref, ...), custom_call_target="tpu_custom_call" | custom-call | flops 207618048 | bytes 8388608 | tf_op jit(solution)/shard_map/pallas_call | solution.py:34
  42.5 4.7 %shard_map.289 = (f32[12,8,512]{2,1,0:T(8,128)}, f32[12,512,8]{2,1,0:T(8,128)}, f32[32,512]{1,0:T(8,128)}, f32[32,512]{1,0:T(8,128)}, f32[32,512]{1,0:T(8,128)}, /*index=5*/f32[8,1536]{1,0:T(8,128)}) custom-call(s32[8]{0:T(128)} %pad_add_fusion.s_ref, bf16[528,768]{1,0:T(8,128)(2,1)} %get-tuple-element.91.nx_ref, f32[32,896]{1,0:T(8,128)} %select_maximum_fusion.hp_ref), custom_call_target="tpu_custom_call" | custom-call | flops 25165824 | bytes 4194304 | tf_op jit(solution)/shard_map/pallas_call | solution.py:34
  48.8 10.7 %shard_map.290 = (f32[512,768]{1,0:T(8,128)}, f32[528,768]{1,0:T(8,128)}, f32[512,768]{1,0:T(8,128)}, f32[512,768]{1,0:T(8,128)}, f32[2,128,768]{2,1,0:T(8,128)}, /*index=5*/bf16[128,768]{1,0:T(8,128)(2,1)}) custom-call(s32[8]{0:T(128)} %pad_add_fusion.s_ref, bf16[528,768]{1,0:T(8,128)(2,1)} %get-tuple-element.91.nx_ref, ...), custom_call_target="tpu_custom_call" | custom-call | flops 1207959552 | bytes 12582912 | tf_op jit(solution)/shard_map/pallas_call | solution.py:34
  62.2 10.6 %shard_map.291 = (f32[512,768]{1,0:T(8,128)}, f32[528,768]{1,0:T(8,128)}, f32[512,768]{1,0:T(8,128)}, f32[512,768]{1,0:T(8,128)}, f32[2,128,768]{2,1,0:T(8,128)}, /*index=5*/bf16[128,768]{1,0:T(8,128)(2,1)}) custom-call(s32[8]{0:T(128)} %pad_add_fusion.s_ref, bf16[528,768]{1,0:T(8,128)(2,1)} %get-tuple-element.91.nx_ref, ...), custom_call_target="tpu_custom_call" | custom-call | flops 1207959552 | bytes 12582912 | tf_op jit(solution)/shard_map/pallas_call | solution.py:34
  75.2 2.0 collective-permute-start.14
  79.1 12.2 %collective-permute-done.14.refs_2_ = bf16[384,768]{1,0:T(8,128)(2,1)S(1)} collective-permute-done((bf16[384,768]{1,0:T(8,128)(2,1)S(1)}, bf16[384,768]{1,0:T(8,128)(2,1)S(1)}, u32[]{:S(2)}, u32[]{:S(2)}) %collective-permute-start.14) | collective-permute-done | bytes 589856 | tf_op jit(solution)/shard_map/ppermute | solution.py:615
  91.3 9.9 %shard_map.292.y_ref = f32[512,1536]{1,0:T(8,128)} custom-call(s32[8]{0:T(128)} %pad_add_fusion.s_ref, f32[12,8,512]{2,1,0:T(8,128)} %get-tuple-element.99.rowp_ref, f32[12,512,8]{2,1,0:T(8,128)} %get-tuple-element.94.colp_ref, f32[2,256,256]{2,1,0:T(8,128)} %get-tuple-element.100.cb_ref, f32[512,768]{1,0:T(8,128)} %get-tuple-element.101.x0_ref.refs_6_, ...), custom_call_target="tpu_custom_call" | custom-call | flops 805306368 | bytes 10485760 | tf_op jit(solution)/shard_map/pallas_call | solution.py:34
  103.4 21.2 %shard_map.293 = (bf16[512,1536]{1,0:T(8,128)(2,1)}, bf16[512,1536]{1,0:T(8,128)(2,1)}, f32[512,1536]{1,0:T(8,128)}, f32[2,128,1536]{2,1,0:T(8,128)}, bf16[128,1...) custom-call(s32[8]{0:T(128)} %pad_add_fusion.s_ref, bf16[512,768]{1,0:T(8,128)(2,1)} %cot_ref.5, ...), custom_call_target="tpu_custom_call" | custom-call | flops 1207959552 | bytes 31457280 | tf_op jit(solution)/shard_map/pallas_call | solution.py:34
  124.6 8.9 %shard_map.294 = (bf16[512,768]{1,0:T(8,128)(2,1)}, bf16[384,768]{1,0:T(8,128)(2,1)}, bf16[384,768]{1,0:T(8,128)(2,1)}, bf16[384,768]{1,0:T(8,128)(2,1)}, bf16[3...) custom-call(s32[8]{0:T(128)} %pad_add_fusion.s_ref, ...), custom_call_target="tpu_custom_call" | custom-call | flops 3623878656 | bytes 12582912 | tf_op jit(solution)/shard_map/pallas_call | solution.py:34
  135.0 11.4 %shard_map.295 = (f32[512,1536]{1,0:T(8,128)}, f32[512,128]{1,0:T(8,128)}, f32[512,128]{1,0:T(8,128)}) custom-call(s32[8]{0:T(128)} %pad_add_fusion.s_ref, f32[12,8,512]{2,1,0:T(8,128)} %get-tuple-element.99.rowp_ref, f32[12,512,8]{2,1,0:T(8,128)} %get-tuple-element.94.colp_ref, f32[2,256,256]{2,1,0:T(8,128)} %get-tuple-element.112.cbt_ref, ...), custom_call_target="tpu_custom_call" | custom-call | flops 2415919104 | bytes 14680064 | tf_op jit(solution)/shard_map/pallas_call | solution.py:34
  146.7 2.1 collective-permute-start.17
  149.9 8.8 %collective-permute-done.17 = bf16[128,1536]{1,0:T(8,128)(2,1)S(1)} collective-permute-done((bf16[128,1536]{1,0:T(8,128)(2,1)S(1)}, bf16[128,1536]{1,0:T(8,128)(2,1)S(1)}, u32[]{:S(2)}, u32[]{:S(2)}) %collective-permute-start.17) | collective-permute-done | bytes 393248 | tf_op jit(solution)/shard_map/ppermute | solution.py:615
  159.8 21.4 %shard_map.296 = (bf16[528,1536]{1,0:T(8,128)(2,1)}, bf16[528,256]{1,0:T(8,128)(2,1)}, bf16[32,512]{1,0:T(8,128)(2,1)}, f32[8,1536]{1,0:T(8,128)}, f32[8,256]{1,0:T(8,128)}, /*index=5*/f32[32,128]{1,0:T(8,128)}) custom-call(s32[8]{0:T(128)} %pad_add_fusion.s_ref, f32[128,1536]{1,0:T(8,128)} %add_select_fusion.back_in, f32[128,1536]{1,0:T(8,128)} %add_select_fusion.1.inc_in, ...), custom_call_target="tpu_custom_call" | custom-call | flops 603979776 | bytes 31457280 | tf_op jit(solution)/shard_map/pallas_call | solution.py:34
  181.1 5.3 %shard_map.298 = (bf16[768,384]{1,0:T(8,128)(2,1)}, bf16[768,384]{1,0:T(8,128)(2,1)}, bf16[768,384]{1,0:T(8,128)(2,1)}, bf16[768,384]{1,0:T(8,128)(2,1)}, f32[32,768]{1,0:T(8,128)}) custom-call(s32[8]{0:T(128)} %pad_add_fusion.s_ref, bf16[528,768]{1,0:T(8,128)(2,1)} %get-tuple-element.91.nx_ref, bf16[768,512]{1,0:T(8,128)(2,1)} %get-tuple-element.90.nt_ref, ...), custom_call_target="tpu_custom_call" | custom-call | flops 1207959552 | bytes 6291456 | tf_op jit(solution)/shard_map/pallas_call | solution.py:34
  188.2 10.8 %shard_map.297 = (f32[512,768]{1,0:T(8,128)}, f32[16,768]{1,0:T(8,128)}, f32[832,256]{1,0:T(8,128)}) custom-call(s32[8]{0:T(128)} %pad_add_fusion.s_ref, bf16[512,768]{1,0:T(8,128)(2,1)} %hid_ref.5, bf16[16,768]{1,0:T(8,128)(2,1)} %collective-permute-done.halo_ref, bf16[512,768]{1,0:T(8,128)(2,1)} %cot_ref.5, f32[1,768]{1,0:T(1,128)} %broadcast_in_dim.24.gain_ref, ...), custom_call_target="tpu_custom_call" | custom-call | flops 2415919104 | bytes 12582912 | tf_op jit(solution)/shard_map/pallas_call | solution.py:34
  202.2 2.1 collective-permute-start.23
  204.4 1.6 collective-permute-done.23
  207.6 1.5 collective-permute-done.18
  209.1 10.9 %collective-permute-start.19 = (bf16[416,256]{1,0:T(8,128)(2,1)S(1)}, bf16[416,256]{1,0:T(8,128)(2,1)S(1)}, u32[]{:S(2)}, u32[]{:S(2)}) collective-permute-start(bf16[416,256]{1,0:T(8,128)(2,1)S(1)} %select_convert_fusion), channel_id=1, source_target_pairs={{0,1},{1,0},{2,3},{3,2},{4,5},{5,4},{6,7},{7,6},{8,9},{9,8},{10,11... | collective-permute-start | bytes 638984 | tf_op jit(solution)/shard_map/ppermute | solution.py:615
  224.9 4.4 %collective-permute-done.20 = bf16[416,256]{1,0:T(8,128)(2,1)S(1)} collective-permute-done((bf16[416,256]{1,0:T(8,128)(2,1)S(1)}, bf16[416,256]{1,0:T(8,128)(2,1)S(1)}, u32[]{:S(2)}, u32[]{:S(2)}) %collective-permute-start.20) | collective-permute-done | bytes 213024 | tf_op jit(solution)/shard_map/ppermute | solution.py:615
  229.5 1.5 collective-permute-start.24
  231.1 3.3 collective-permute-done.24
  234.4 1.6 collective-permute-start.25
  236.0 2.6 collective-permute-start.26
  241.3 3.0 collective-permute-done.27
  245.3 3.5 %collective-permute-start.30 = (bf16[56,256]{1,0:T(8,128)(2,1)S(1)}, bf16[56,256]{1,0:T(8,128)(2,1)S(1)}, u32[]{:S(2)}, u32[]{:S(2)}) collective-permute-start(bf16[56,256]{1,0:T(8,128)(2,1)S(1)} %fusion.19), channel_id=1, source_target_pairs={{0,24},{4,28},{8,16},{12,20},{16,8},{20,12},{24,0},{28,4},{1,25},{... | collective-permute-start | bytes 86024 | tf_op jit(solution)/shard_map/ppermute | solution.py:615
  248.9 1.6 collective-permute-start.36
  251.1 1.7 collective-permute-start.31
  253.8 1.9 collective-permute-done.36
  255.7 1.6 collective-permute-start.60
  257.5 1.9 collective-permute-start.61
  262.2 2.5 collective-permute-done.60
  264.7 1.8 collective-permute-start.39
  267.5 1.7 collective-permute-start.62
  269.2 4.0 %collective-permute-done.38 = bf16[96,384]{1,0:T(8,128)(2,1)S(1)} collective-permute-done((bf16[96,384]{1,0:T(8,128)(2,1)S(1)}, bf16[96,384]{1,0:T(8,128)(2,1)S(1)}, u32[]{:S(2)}, u32[]{:S(2)}) %collective-permute-start.38) | collective-permute-done | bytes 73760 | tf_op jit(solution)/shard_map/ppermute | solution.py:615
  273.4 3.3 %collective-permute-start.40 = (bf16[96,384]{1,0:T(8,128)(2,1)S(1)}, bf16[96,384]{1,0:T(8,128)(2,1)S(1)}, u32[]{:S(2)}, u32[]{:S(2)}) collective-permute-start(bf16[96,384]{1,0:T(8,128)(2,1)S(1)} %fusion.15), channel_id=1, source_target_pairs={{0,8},{4,12},{8,0},{12,4},{16,24},{20,28},{24,16},{28,20},{1,9},{5... | collective-permute-start | bytes 221192 | tf_op jit(solution)/shard_map/ppermute | solution.py:615
  276.8 3.4 %collective-permute-done.63 = bf16[48,768]{1,0:T(8,128)(2,1)S(1)} collective-permute-done((bf16[48,768]{1,0:T(8,128)(2,1)S(1)}, bf16[48,768]{1,0:T(8,128)(2,1)S(1)}, u32[]{:S(2)}, u32[]{:S(2)}) %collective-permute-start.63) | collective-permute-done | bytes 73760 | tf_op jit(solution)/shard_map/ppermute | solution.py:615
  282.2 3.2 collective-permute-done.41
  292.9 11.5 %collective-permute-done.47 = bf16[384,384]{1,0:T(8,128)(2,1)S(1)} collective-permute-done((bf16[384,384]{1,0:T(8,128)(2,1)S(1)}, bf16[384,384]{1,0:T(8,128)(2,1)S(1)}, u32[]{:S(2)}, u32[]{:S(2)}) %collective-permute-start.47) | collective-permute-done | bytes 294944 | tf_op jit(solution)/shard_map/ppermute | solution.py:615
  304.6 2.4 collective-permute-start.48
  309.9 4.5 %collective-permute-done.49 = bf16[96,384]{1,0:T(8,128)(2,1)S(1)} collective-permute-done((bf16[96,384]{1,0:T(8,128)(2,1)S(1)}, bf16[96,384]{1,0:T(8,128)(2,1)S(1)}, u32[]{:S(2)}, u32[]{:S(2)}) %collective-permute-start.49) | collective-permute-done | bytes 73760 | tf_op jit(solution)/shard_map/ppermute | solution.py:615
  316.5 2.4 collective-permute-start.53
  320.5 2.9 collective-permute-done.52
  327.6 2.8 collective-permute-done.54
  (284 shorter events, 71.7 us)
Async XLA Ops:
  0.6 34.9 %collective-permute-start.9 = (bf16[768,384]{1,0:T(8,128)(2,1)}, bf16[768,384]{1,0:T(8,128)(2,1)S(1)}, u32[]{:S(2)}, u32[]{:S(2)}) collective-permute-start(bf16[768,384]{1,0:T(8,128)(2,1)} %refs_4_.1), channel_id=1, source_target_pairs={{0,2},{1,3},{2,0},{3,1},{4,6},{5,7},{6,4},{7,5},{8,10},{9,11},{10,... | collective-permute-start | bytes 1769480 | tf_op jit(solution)/shard_map/ppermute | solution.py:615
  3.7 31.9 %collective-permute-start.7 = (bf16[768,384]{1,0:T(8,128)(2,1)}, bf16[768,384]{1,0:T(8,128)(2,1)S(1)}, u32[]{:S(2)}, u32[]{:S(2)}) collective-permute-start(bf16[768,384]{1,0:T(8,128)(2,1)} %refs_0_.7), channel_id=1, source_target_pairs={{0,2},{1,3},{2,0},{3,1},{4,6},{5,7},{6,4},{7,5},{8,10},{9,11},{10,... | collective-permute-start | bytes 1769480 | tf_op jit(solution)/shard_map/ppermute | solution.py:615
  8.9 22.3 %collective-permute-start.2 = (f32[16,896]{1,0:T(8,128)S(1)}, f32[16,896]{1,0:T(8,128)}, u32[]{:S(2)}, u32[]{:S(2)}) collective-permute-start(f32[16,896]{1,0:T(8,128)S(1)} %select_maximum_fusion.3), channel_id=1, source_target_pairs={{0,2},{1,3},{2,0},{3,1},{4,6},{5,7},{6,4},{7,5},{8,10},{9,11},{10,... | collective-permute-start | bytes 172040 | tf_op jit(solution)/shard_map/ppermute | solution.py:615
  13.5 34.3 %collective-permute-start.5 = (bf16[768,384]{1,0:T(8,128)(2,1)}, bf16[768,384]{1,0:T(8,128)(2,1)S(1)}, u32[]{:S(2)}, u32[]{:S(2)}) collective-permute-start(bf16[768,384]{1,0:T(8,128)(2,1)} %refs_0_.7), channel_id=1, source_target_pairs={{0,1},{1,0},{2,3},{3,2},{4,5},{5,4},{6,7},{7,6},{8,9},{9,8},{10,11... | collective-permute-start | bytes 1769480 | tf_op jit(solution)/shard_map/ppermute | solution.py:615
  13.9 33.9 %collective-permute-start.6 = (bf16[768,384]{1,0:T(8,128)(2,1)}, bf16[768,384]{1,0:T(8,128)(2,1)S(1)}, u32[]{:S(2)}, u32[]{:S(2)}) collective-permute-start(bf16[768,384]{1,0:T(8,128)(2,1)} %refs_4_.1), channel_id=1, source_target_pairs={{0,1},{1,0},{2,3},{3,2},{4,5},{5,4},{6,7},{7,6},{8,9},{9,8},{10,11... | collective-permute-start | bytes 1769480 | tf_op jit(solution)/shard_map/ppermute | solution.py:615
  32.5 9.3 %collective-permute-start.3 = (f32[16,896]{1,0:T(8,128)}, f32[16,896]{1,0:T(8,128)S(1)}, u32[]{:S(2)}, u32[]{:S(2)}) collective-permute-start(f32[16,896]{1,0:T(8,128)} %collective-permute-done.2), channel_id=1, source_target_pairs={{0,1},{1,0},{2,3},{3,2},{4,5},{5,4},{6,7},{7,6},{8,9},{9,8},{10,11... | collective-permute-start | bytes 172040 | tf_op jit(solution)/shard_map/ppermute | solution.py:615
  35.5 25.0 %collective-permute-start.10 = (bf16[768,384]{1,0:T(8,128)(2,1)S(1)}, bf16[768,384]{1,0:T(8,128)(2,1)S(1)}, u32[]{:S(2)}, u32[]{:S(2)}) collective-permute-start(bf16[768,384]{1,0:T(8,128)(2,1)S(1)} %collective-permute-done.9.refs_2_.refs_6_), channel_id=1, source_target_pairs={{0,1},{1,0},{2,3},{3,2},{4,5},{5,4},{6,7},{7,6},{8,9},{9,8},{10,11... | collective-permute-start | bytes 1769480 | tf_op jit(solution)/shard_map/ppermute | solution.py:615
  35.6 24.9 %collective-permute-start.8 = (bf16[768,384]{1,0:T(8,128)(2,1)S(1)}, bf16[768,384]{1,0:T(8,128)(2,1)S(1)}, u32[]{:S(2)}, u32[]{:S(2)}) collective-permute-start(bf16[768,384]{1,0:T(8,128)(2,1)S(1)} %collective-permute-done.7.refs_0_.refs_2_), channel_id=1, source_target_pairs={{0,1},{1,0},{2,3},{3,2},{4,5},{5,4},{6,7},{7,6},{8,9},{9,8},{10,11... | collective-permute-start | bytes 1769480 | tf_op jit(solution)/shard_map/ppermute | solution.py:615
  75.2 16.1 %collective-permute-start.14 = (bf16[384,768]{1,0:T(8,128)(2,1)S(1)}, bf16[384,768]{1,0:T(8,128)(2,1)S(1)}, u32[]{:S(2)}, u32[]{:S(2)}) collective-permute-start(bf16[384,768]{1,0:T(8,128)(2,1)S(1)} %copy-done.13), channel_id=1, source_target_pairs={{0,2},{1,3},{2,0},{3,1},{4,6},{5,7},{6,4},{7,5},{8,10},{9,11},{10,... | collective-permute-start | bytes 1769480 | tf_op jit(solution)/shard_map/ppermute | solution.py:615
  77.5 23.7 %collective-permute-start.12 = (bf16[128,1536]{1,0:T(8,128)(2,1)S(1)}, bf16[128,1536]{1,0:T(8,128)(2,1)S(1)}, u32[]{:S(2)}, u32[]{:S(2)}) collective-permute-start(bf16[128,1536]{1,0:T(8,128)(2,1)S(1)} %fusion.1), channel_id=1, source_target_pairs={{0,2},{1,3},{2,0},{3,1},{4,6},{5,7},{6,4},{7,5},{8,10},{9,11},{10,... | collective-permute-start | bytes 1179656 | tf_op jit(solution)/shard_map/ppermute | solution.py:615
  78.5 23.9 %collective-permute-start.13 = (bf16[384,768]{1,0:T(8,128)(2,1)S(1)}, bf16[384,768]{1,0:T(8,128)(2,1)S(1)}, u32[]{:S(2)}, u32[]{:S(2)}) collective-permute-start(bf16[384,768]{1,0:T(8,128)(2,1)S(1)} %copy-done.13), channel_id=1, source_target_pairs={{0,1},{1,0},{2,3},{3,2},{4,5},{5,4},{6,7},{7,6},{8,9},{9,8},{10,11... | collective-permute-start | bytes 1769480 | tf_op jit(solution)/shard_map/ppermute | solution.py:615
  91.3 11.0 %collective-permute-start.15 = (bf16[384,768]{1,0:T(8,128)(2,1)S(1)}, bf16[384,768]{1,0:T(8,128)(2,1)S(1)}, u32[]{:S(2)}, u32[]{:S(2)}) collective-permute-start(bf16[384,768]{1,0:T(8,128)(2,1)S(1)} %collective-permute-done.14.refs_2_), channel_id=1, source_target_pairs={{0,1},{1,0},{2,3},{3,2},{4,5},{5,4},{6,7},{7,6},{8,9},{9,8},{10,11... | collective-permute-start | bytes 1769480 | tf_op jit(solution)/shard_map/ppermute | solution.py:615
  133.5 15.3 %collective-permute-start.56 = (bf16[384,768]{1,0:T(8,128)(2,1)}, bf16[384,768]{1,0:T(8,128)(2,1)S(1)}, u32[]{:S(2)}, u32[]{:S(2)}) collective-permute-start(bf16[384,768]{1,0:T(8,128)(2,1)} %get-tuple-element.151), channel_id=1, source_target_pairs={{0,1},{1,0},{2,3},{3,2},{4,5},{5,4},{6,7},{7,6},{8,9},{9,8},{10,11... | collective-permute-start | bytes 1769480 | tf_op jit(solution)/shard_map/ppermute | solution.py:615
  133.9 87.7 %collective-permute-start.55 = (bf16[384,768]{1,0:T(8,128)(2,1)}, bf16[384,768]{1,0:T(8,128)(2,1)}, u32[]{:S(2)}, u32[]{:S(2)}) collective-permute-start(bf16[384,768]{1,0:T(8,128)(2,1)} %get-tuple-element.149), channel_id=1, source_target_pairs={{0,1},{1,0},{2,3},{3,2},{4,5},{5,4},{6,7},{7,6},{8,9},{9,8},{10,11... | collective-permute-start | bytes 1769480 | tf_op jit(solution)/shard_map/ppermute | solution.py:615
  134.1 12.3 %collective-permute-start.16 = (bf16[128,1536]{1,0:T(8,128)(2,1)S(1)}, bf16[128,1536]{1,0:T(8,128)(2,1)S(1)}, u32[]{:S(2)}, u32[]{:S(2)}) collective-permute-start(bf16[128,1536]{1,0:T(8,128)(2,1)S(1)} %copy-done.17), channel_id=1, source_target_pairs={{0,1},{1,0},{2,3},{3,2},{4,5},{5,4},{6,7},{7,6},{8,9},{9,8},{10,11... | collective-permute-start | bytes 1179656 | tf_op jit(solution)/shard_map/ppermute | solution.py:615
  134.4 15.3 %collective-permute-start.34 = (bf16[768,384]{1,0:T(8,128)(2,1)}, bf16[768,384]{1,0:T(8,128)(2,1)S(1)}, u32[]{:S(2)}, u32[]{:S(2)}) collective-permute-start(bf16[768,384]{1,0:T(8,128)(2,1)} %get-tuple-element.143), channel_id=1, source_target_pairs={{0,1},{1,0},{2,3},{3,2},{4,5},{5,4},{6,7},{7,6},{8,9},{9,8},{10,11... | collective-permute-start | bytes 1769480 | tf_op jit(solution)/shard_map/ppermute | solution.py:615
  134.7 88.9 %collective-permute-start.33 = (bf16[768,384]{1,0:T(8,128)(2,1)}, bf16[768,384]{1,0:T(8,128)(2,1)}, u32[]{:S(2)}, u32[]{:S(2)}) collective-permute-start(bf16[768,384]{1,0:T(8,128)(2,1)} %get-tuple-element.141), channel_id=1, source_target_pairs={{0,1},{1,0},{2,3},{3,2},{4,5},{5,4},{6,7},{7,6},{8,9},{9,8},{10,11... | collective-permute-start | bytes 1769480 | tf_op jit(solution)/shard_map/ppermute | solution.py:615
  146.7 12.0 %collective-permute-start.17 = (bf16[128,1536]{1,0:T(8,128)(2,1)S(1)}, bf16[128,1536]{1,0:T(8,128)(2,1)S(1)}, u32[]{:S(2)}, u32[]{:S(2)}) collective-permute-start(bf16[128,1536]{1,0:T(8,128)(2,1)S(1)} %fusion.3), channel_id=1, source_target_pairs={{0,2},{1,3},{2,0},{3,1},{4,6},{5,7},{6,4},{7,5},{8,10},{9,11},{10,... | collective-permute-start | bytes 1179656 | tf_op jit(solution)/shard_map/ppermute | solution.py:615
  148.9 73.2 %collective-permute-start.57 = (bf16[384,768]{1,0:T(8,128)(2,1)S(1)}, bf16[384,768]{1,0:T(8,128)(2,1)}, u32[]{:S(2)}, u32[]{:S(2)}) collective-permute-start(bf16[384,768]{1,0:T(8,128)(2,1)S(1)} %add_convert_fusion), channel_id=1, source_target_pairs={{0,2},{1,3},{2,0},{3,1},{4,6},{5,7},{6,4},{7,5},{8,10},{9,11},{10,... | collective-permute-start | bytes 1769480 | tf_op jit(solution)/shard_map/ppermute | solution.py:615
  204.3 19.3 %collective-permute-start.35 = (bf16[768,384]{1,0:T(8,128)(2,1)S(1)}, bf16[768,384]{1,0:T(8,128)(2,1)S(1)}, u32[]{:S(2)}, u32[]{:S(2)}) collective-permute-start(bf16[768,384]{1,0:T(8,128)(2,1)S(1)} %add_convert_fusion.2), channel_id=1, source_target_pairs={{0,2},{1,3},{2,0},{3,1},{4,6},{5,7},{6,4},{7,5},{8,10},{9,11},{10,... | collective-permute-start | bytes 1769480 | tf_op jit(solution)/shard_map/ppermute | solution.py:615
  209.1 12.3 %collective-permute-start.19 = (bf16[416,256]{1,0:T(8,128)(2,1)S(1)}, bf16[416,256]{1,0:T(8,128)(2,1)S(1)}, u32[]{:S(2)}, u32[]{:S(2)}) collective-permute-start(bf16[416,256]{1,0:T(8,128)(2,1)S(1)} %select_convert_fusion), channel_id=1, source_target_pairs={{0,1},{1,0},{2,3},{3,2},{4,5},{5,4},{6,7},{7,6},{8,9},{9,8},{10,11... | collective-permute-start | bytes 638984 | tf_op jit(solution)/shard_map/ppermute | solution.py:615
  221.4 23.9 %collective-permute-start.45 = (bf16[768,384]{1,0:T(8,128)(2,1)}, bf16[768,384]{1,0:T(8,128)(2,1)S(1)}, u32[]{:S(2)}, u32[]{:S(2)}) collective-permute-start(bf16[768,384]{1,0:T(8,128)(2,1)} %get-tuple-element.147), channel_id=1, source_target_pairs={{0,1},{1,0},{2,3},{3,2},{4,5},{5,4},{6,7},{7,6},{8,9},{9,8},{10,11... | collective-permute-start | bytes 1769480 | tf_op jit(solution)/shard_map/ppermute | solution.py:615
  221.6 66.8 %collective-permute-start.44 = (bf16[768,384]{1,0:T(8,128)(2,1)}, bf16[768,384]{1,0:T(8,128)(2,1)S(1)}, u32[]{:S(2)}, u32[]{:S(2)}) collective-permute-start(bf16[768,384]{1,0:T(8,128)(2,1)} %get-tuple-element.145), channel_id=1, source_target_pairs={{0,1},{1,0},{2,3},{3,2},{4,5},{5,4},{6,7},{7,6},{8,9},{9,8},{10,11... | collective-permute-start | bytes 1769480 | tf_op jit(solution)/shard_map/ppermute | solution.py:615
  222.1 7.2 %collective-permute-start.20 = (bf16[416,256]{1,0:T(8,128)(2,1)S(1)}, bf16[416,256]{1,0:T(8,128)(2,1)S(1)}, u32[]{:S(2)}, u32[]{:S(2)}) collective-permute-start(bf16[416,256]{1,0:T(8,128)(2,1)S(1)} %add_convert_fusion.3), channel_id=1, source_target_pairs={{0,2},{1,3},{2,0},{3,1},{4,6},{5,7},{6,4},{7,5},{8,10},{9,11},{10,... | collective-permute-start | bytes 638984 | tf_op jit(solution)/shard_map/ppermute | solution.py:615
  238.9 13.8 %collective-permute-start.58 = (bf16[192,768]{1,0:T(8,128)(2,1)S(1)}, bf16[192,768]{1,0:T(8,128)(2,1)S(1)}, u32[]{:S(2)}, u32[]{:S(2)}) collective-permute-start(bf16[192,768]{1,0:T(8,128)(2,1)S(1)} %fusion.6), channel_id=1, source_target_pairs={{0,4},{4,0},{8,12},{12,8},{16,20},{20,16},{24,28},{28,24},{1,5},{5... | collective-permute-start | bytes 884744 | tf_op jit(solution)/shard_map/ppermute | solution.py:615
  244.4 6.1 %collective-permute-start.29 = (bf16[56,256]{1,0:T(8,128)(2,1)S(1)}, bf16[56,256]{1,0:T(8,128)(2,1)S(1)}, u32[]{:S(2)}, u32[]{:S(2)}) collective-permute-start(bf16[56,256]{1,0:T(8,128)(2,1)S(1)} %fusion.19), channel_id=1, source_target_pairs={{0,16},{4,20},{8,24},{12,28},{16,0},{20,4},{24,8},{28,12},{1,17},{... | collective-permute-start | bytes 86024 | tf_op jit(solution)/shard_map/ppermute | solution.py:615
  248.9 6.8 %collective-permute-start.36 = (bf16[384,384]{1,0:T(8,128)(2,1)S(1)}, bf16[384,384]{1,0:T(8,128)(2,1)S(1)}, u32[]{:S(2)}, u32[]{:S(2)}) collective-permute-start(bf16[384,384]{1,0:T(8,128)(2,1)S(1)} %fusion.4), channel_id=1, source_target_pairs={{0,4},{4,0},{8,12},{12,8},{16,20},{20,16},{24,28},{28,24},{1,5},{5... | collective-permute-start | bytes 884744 | tf_op jit(solution)/shard_map/ppermute | solution.py:615
  250.5 37.8 %collective-permute-start.46 = (bf16[768,384]{1,0:T(8,128)(2,1)S(1)}, bf16[768,384]{1,0:T(8,128)(2,1)}, u32[]{:S(2)}, u32[]{:S(2)}) collective-permute-start(bf16[768,384]{1,0:T(8,128)(2,1)S(1)} %add_convert_fusion.1), channel_id=1, source_target_pairs={{0,2},{1,3},{2,0},{3,1},{4,6},{5,7},{6,4},{7,5},{8,10},{9,11},{10,... | collective-permute-start | bytes 1769480 | tf_op jit(solution)/shard_map/ppermute | solution.py:615
  251.1 6.4 %collective-permute-start.31 = (bf16[224,256]{1,0:T(8,128)(2,1)S(1)}, bf16[224,256]{1,0:T(8,128)(2,1)S(1)}, u32[]{:S(2)}, u32[]{:S(2)}) collective-permute-start(bf16[224,256]{1,0:T(8,128)(2,1)S(1)} %pad_maximum_fusion.11), channel_id=1, source_target_pairs={{0,4},{4,0},{8,12},{12,8},{16,20},{20,16},{24,28},{28,24},{1,5},{5... | collective-permute-start | bytes 344072 | tf_op jit(solution)/shard_map/ppermute | solution.py:615
  253.5 8.7 %collective-permute-start.59 = (bf16[48,768]{1,0:T(8,128)(2,1)}, bf16[48,768]{1,0:T(8,128)(2,1)S(1)}, u32[]{:S(2)}, u32[]{:S(2)}) collective-permute-start(bf16[48,768]{1,0:T(8,128)(2,1)} %get-tuple-element.195), channel_id=1, source_target_pairs={{0,8},{4,12},{8,0},{12,4},{16,24},{20,28},{24,16},{28,20},{1,9},{5... | collective-permute-start | bytes 221192 | tf_op jit(solution)/shard_map/ppermute | solution.py:615
  255.7 9.0 %collective-permute-start.60 = (bf16[48,768]{1,0:T(8,128)(2,1)S(1)}, bf16[48,768]{1,0:T(8,128)(2,1)S(1)}, u32[]{:S(2)}, u32[]{:S(2)}) collective-permute-start(bf16[48,768]{1,0:T(8,128)(2,1)S(1)} %get-tuple-element.197), channel_id=1, source_target_pairs={{0,16},{4,20},{8,24},{12,28},{16,0},{20,4},{24,8},{28,12},{1,17},{... | collective-permute-start | bytes 221192 | tf_op jit(solution)/shard_map/ppermute | solution.py:615
  257.5 7.2 %collective-permute-start.61 = (bf16[48,768]{1,0:T(8,128)(2,1)S(1)}, bf16[48,768]{1,0:T(8,128)(2,1)}, u32[]{:S(2)}, u32[]{:S(2)}) collective-permute-start(bf16[48,768]{1,0:T(8,128)(2,1)S(1)} %get-tuple-element.196), channel_id=1, source_target_pairs={{0,24},{4,28},{8,16},{12,20},{16,8},{20,12},{24,0},{28,4},{1,25},{... | collective-permute-start | bytes 221192 | tf_op jit(solution)/shard_map/ppermute | solution.py:615
  264.7 8.5 %collective-permute-start.38 = (bf16[96,384]{1,0:T(8,128)(2,1)S(1)}, bf16[96,384]{1,0:T(8,128)(2,1)S(1)}, u32[]{:S(2)}, u32[]{:S(2)}) collective-permute-start(bf16[96,384]{1,0:T(8,128)(2,1)S(1)} %get-tuple-element.211), channel_id=1, source_target_pairs={{0,16},{4,20},{8,24},{12,28},{16,0},{20,4},{24,8},{28,12},{1,17},{... | collective-permute-start | bytes 221192 | tf_op jit(solution)/shard_map/ppermute | solution.py:615
  264.7 8.5 %collective-permute-start.39 = (bf16[96,384]{1,0:T(8,128)(2,1)S(1)}, bf16[96,384]{1,0:T(8,128)(2,1)S(1)}, u32[]{:S(2)}, u32[]{:S(2)}) collective-permute-start(bf16[96,384]{1,0:T(8,128)(2,1)S(1)} %get-tuple-element.210), channel_id=1, source_target_pairs={{0,24},{4,28},{8,16},{12,20},{16,8},{20,12},{24,0},{28,4},{1,25},{... | collective-permute-start | bytes 221192 | tf_op jit(solution)/shard_map/ppermute | solution.py:615
  273.2 7.0 %collective-permute-start.63 = (bf16[48,768]{1,0:T(8,128)(2,1)S(1)}, bf16[48,768]{1,0:T(8,128)(2,1)S(1)}, u32[]{:S(2)}, u32[]{:S(2)}) collective-permute-start(bf16[48,768]{1,0:T(8,128)(2,1)S(1)} %fusion.9), channel_id=1, source_target_pairs={{0,16},{4,20},{8,24},{12,28},{16,0},{20,4},{24,8},{28,12},{1,17},{... | collective-permute-start | bytes 221192 | tf_op jit(solution)/shard_map/ppermute | solution.py:615
  273.2 7.0 %collective-permute-start.64 = (bf16[48,768]{1,0:T(8,128)(2,1)S(1)}, bf16[48,768]{1,0:T(8,128)(2,1)S(1)}, u32[]{:S(2)}, u32[]{:S(2)}) collective-permute-start(bf16[48,768]{1,0:T(8,128)(2,1)S(1)} %fusion.9), channel_id=1, source_target_pairs={{0,24},{4,28},{8,16},{12,20},{16,8},{20,12},{24,0},{28,4},{1,25},{... | collective-permute-start | bytes 221192 | tf_op jit(solution)/shard_map/ppermute | solution.py:615
  273.4 8.7 %collective-permute-start.40 = (bf16[96,384]{1,0:T(8,128)(2,1)S(1)}, bf16[96,384]{1,0:T(8,128)(2,1)S(1)}, u32[]{:S(2)}, u32[]{:S(2)}) collective-permute-start(bf16[96,384]{1,0:T(8,128)(2,1)S(1)} %fusion.15), channel_id=1, source_target_pairs={{0,8},{4,12},{8,0},{12,4},{16,24},{20,28},{24,16},{28,20},{1,9},{5... | collective-permute-start | bytes 221192 | tf_op jit(solution)/shard_map/ppermute | solution.py:615
  280.2 6.3 %collective-permute-start.42 = (bf16[96,384]{1,0:T(8,128)(2,1)S(1)}, bf16[96,384]{1,0:T(8,128)(2,1)S(1)}, u32[]{:S(2)}, u32[]{:S(2)}) collective-permute-start(bf16[96,384]{1,0:T(8,128)(2,1)S(1)} %fusion.15), channel_id=1, source_target_pairs={{0,24},{4,28},{8,16},{12,20},{16,8},{20,12},{24,0},{28,4},{1,25},{... | collective-permute-start | bytes 221192 | tf_op jit(solution)/shard_map/ppermute | solution.py:615
  282.2 6.1 %collective-permute-start.32 = (bf16[416,256]{1,0:T(8,128)(2,1)S(1)}, bf16[416,256]{1,0:T(8,128)(2,1)S(1)}, u32[]{:S(2)}, u32[]{:S(2)}) collective-permute-start(bf16[416,256]{1,0:T(8,128)(2,1)S(1)} %pad_maximum_fusion.9), channel_id=1, source_target_pairs={{0,1},{1,0},{2,3},{3,2},{4,5},{5,4},{6,7},{7,6},{8,9},{9,8},{10,11... | collective-permute-start | bytes 638984 | tf_op jit(solution)/shard_map/ppermute | solution.py:615
  285.4 33.6 %collective-permute-start.65 = (bf16[192,768]{1,0:T(8,128)(2,1)}, bf16[192,768]{1,0:T(8,128)(2,1)}, u32[]{:S(2)}, u32[]{:S(2)}) collective-permute-start(bf16[192,768]{1,0:T(8,128)(2,1)} %pad_maximum_fusion.8), channel_id=1, source_target_pairs={{0,4},{4,0},{8,12},{12,8},{16,20},{20,16},{24,28},{28,24},{1,5},{5... | collective-permute-start | bytes 884744 | tf_op jit(solution)/shard_map/ppermute | solution.py:615
  287.3 37.0 %collective-permute-start.43 = (bf16[384,384]{1,0:T(8,128)(2,1)}, bf16[384,384]{1,0:T(8,128)(2,1)}, u32[]{:S(2)}, u32[]{:S(2)}) collective-permute-start(bf16[384,384]{1,0:T(8,128)(2,1)} %pad_maximum_fusion.4), channel_id=1, source_target_pairs={{0,4},{4,0},{8,12},{12,8},{16,20},{20,16},{24,28},{28,24},{1,5},{5... | collective-permute-start | bytes 884744 | tf_op jit(solution)/shard_map/ppermute | solution.py:615
  289.7 14.8 %collective-permute-start.47 = (bf16[384,384]{1,0:T(8,128)(2,1)S(1)}, bf16[384,384]{1,0:T(8,128)(2,1)S(1)}, u32[]{:S(2)}, u32[]{:S(2)}) collective-permute-start(bf16[384,384]{1,0:T(8,128)(2,1)S(1)} %fusion.5), channel_id=1, source_target_pairs={{0,4},{4,0},{8,12},{12,8},{16,20},{20,16},{24,28},{28,24},{1,5},{5... | collective-permute-start | bytes 884744 | tf_op jit(solution)/shard_map/ppermute | solution.py:615
  306.9 7.5 %collective-permute-start.49 = (bf16[96,384]{1,0:T(8,128)(2,1)S(1)}, bf16[96,384]{1,0:T(8,128)(2,1)S(1)}, u32[]{:S(2)}, u32[]{:S(2)}) collective-permute-start(bf16[96,384]{1,0:T(8,128)(2,1)S(1)} %get-tuple-element.204), channel_id=1, source_target_pairs={{0,16},{4,20},{8,24},{12,28},{16,0},{20,4},{24,8},{28,12},{1,17},{... | collective-permute-start | bytes 221192 | tf_op jit(solution)/shard_map/ppermute | solution.py:615
  307.8 6.6 %collective-permute-start.50 = (bf16[96,384]{1,0:T(8,128)(2,1)S(1)}, bf16[96,384]{1,0:T(8,128)(2,1)S(1)}, u32[]{:S(2)}, u32[]{:S(2)}) collective-permute-start(bf16[96,384]{1,0:T(8,128)(2,1)S(1)} %get-tuple-element.203), channel_id=1, source_target_pairs={{0,24},{4,28},{8,16},{12,20},{16,8},{20,12},{24,0},{28,4},{1,25},{... | collective-permute-start | bytes 221192 | tf_op jit(solution)/shard_map/ppermute | solution.py:615
  314.5 6.0 %collective-permute-start.51 = (bf16[96,384]{1,0:T(8,128)(2,1)S(1)}, bf16[96,384]{1,0:T(8,128)(2,1)S(1)}, u32[]{:S(2)}, u32[]{:S(2)}) collective-permute-start(bf16[96,384]{1,0:T(8,128)(2,1)S(1)} %fusion.12), channel_id=1, source_target_pairs={{0,8},{4,12},{8,0},{12,4},{16,24},{20,28},{24,16},{28,20},{1,9},{5... | collective-permute-start | bytes 221192 | tf_op jit(solution)/shard_map/ppermute | solution.py:615
  315.9 7.5 %collective-permute-start.52 = (bf16[96,384]{1,0:T(8,128)(2,1)S(1)}, bf16[96,384]{1,0:T(8,128)(2,1)S(1)}, u32[]{:S(2)}, u32[]{:S(2)}) collective-permute-start(bf16[96,384]{1,0:T(8,128)(2,1)S(1)} %fusion.12), channel_id=1, source_target_pairs={{0,16},{4,20},{8,24},{12,28},{16,0},{20,4},{24,8},{28,12},{1,17},{... | collective-permute-start | bytes 221192 | tf_op jit(solution)/shard_map/ppermute | solution.py:615
  316.5 6.9 %collective-permute-start.53 = (bf16[96,384]{1,0:T(8,128)(2,1)S(1)}, bf16[96,384]{1,0:T(8,128)(2,1)S(1)}, u32[]{:S(2)}, u32[]{:S(2)}) collective-permute-start(bf16[96,384]{1,0:T(8,128)(2,1)S(1)} %fusion.12), channel_id=1, source_target_pairs={{0,24},{4,28},{8,16},{12,20},{16,8},{20,12},{24,0},{28,4},{1,25},{... | collective-permute-start | bytes 221192 | tf_op jit(solution)/shard_map/ppermute | solution.py:615
  323.6 6.8 %collective-permute-start.54 = (bf16[384,384]{1,0:T(8,128)(2,1)S(1)}, bf16[384,384]{1,0:T(8,128)(2,1)S(1)}, u32[]{:S(2)}, u32[]{:S(2)}) collective-permute-start(bf16[384,384]{1,0:T(8,128)(2,1)S(1)} %pad_maximum_fusion.6), channel_id=1, source_target_pairs={{0,4},{4,0},{8,12},{12,8},{16,20},{20,16},{24,28},{28,24},{1,5},{5... | collective-permute-start | bytes 884744 | tf_op jit(solution)/shard_map/ppermute | solution.py:615
  (45 other events, 302.6 us)

commit v2 on v1

v2 whole, which is shorter than its diff:
```python
import functools

import jax
import jax.numpy as jnp
from jax import lax
from jax.experimental import pallas as pl
from jax.experimental.pallas import tpu as pltpu
from jax.sharding import PartitionSpec as P

K = 4
Q = 256
HALO = 16
LANES = 128
EPSILON = 1e-05
F32 = jnp.float32
BF16 = jnp.bfloat16
HIGHEST = lax.Precision.HIGHEST


def mm(left, right, lc=1, rc=0, precision=None):
    return lax.dot_general(
        left,
        right,
        (((lc,), (rc,)), ((), ())),
        preferred_element_type=F32,
        precision=precision,
    )


MIB = 1024 * 1024
PRE, FRONT, INTRA, MIDDLE, BACK, TAIL, STATE, FINAL = 12, 14, 12, 21, 12, 16, 12, 24


def whole(shape):
    return pl.BlockSpec(shape, lambda *_: (0,) * len(shape))


def call(kernel, outs, args, scratch=(), grid=(), ins=None, out_specs=None, aliases=None, mib=48, cost=0, pin=pltpu.VMEM, kinds=None):
    ins, out_specs, kinds = ins or {}, out_specs or {}, kinds or {}
    specs = [pl.BlockSpec(memory_space=pltpu.SMEM)]
    for at, value in enumerate(args[1:], 1):
        specs.append(ins[at] if at in ins else whole(value.shape))
    outs_specs = [out_specs[at] if at in out_specs else whole(o[0]) for at, o in enumerate(outs)]
    return pl.pallas_call(
        kernel,
        grid=grid,
        out_shape=[kinds[at](s, d) if at in kinds else pin(s, d) for at, (s, d) in enumerate(outs)],
        in_specs=specs,
        out_specs=outs_specs,
        scratch_shapes=list(scratch),
        input_output_aliases=aliases or {},
        compiler_params=pltpu.CompilerParams(vmem_limit_bytes=mib * MIB),
        cost_estimate=pl.CostEstimate(flops=int(cost * 4e8), bytes_accessed=int(cost * 3e5), transcendentals=0),
    )(*args)


def keeps_of(s_ref, block, blocks):
    place = s_ref[0] * blocks + block
    fresh = (place == 0) | (place == 1) | (place == s_ref[1] - 1)
    return fresh, jnp.where(fresh, 0.0, 1.0).astype(F32)


def row_keep(fresh, distance):
    rows = lax.broadcasted_iota(jnp.int32, (Q, 1), 0)
    return (rows >= jnp.where(fresh, distance, 0)).astype(F32)


def conv_block(ref, base, cols, taps, fresh):
    total = taps[K : K + 1] + taps[K - 1 : K] * ref[pl.ds(base, Q), cols]
    for distance in range(1, K):
        earlier = ref[pl.ds(base - distance, Q), cols]
        total = total + taps[K - 1 - distance : K - distance] * (earlier * row_keep(fresh, distance))
    return total


def silu_slope(values, sig):
    return sig * (1.0 + values * (1.0 - sig))


def first_lanes():
    return lax.broadcasted_iota(jnp.int32, (1, LANES), 1) < LANES // 2


def spread(cols, quantity):
    return jnp.where(
        first_lanes(), cols[:, 2 * quantity : 2 * quantity + 1], cols[:, 2 * quantity + 1 : 2 * quantity + 2]
    )


def head_lanes(rows, heads_first, head_size):
    lane = lax.broadcasted_iota(jnp.int32, rows, 1 if heads_first else 0)
    head = lax.broadcasted_iota(jnp.int32, rows, 0 if heads_first else 1)
    return (lane >= head * head_size) & (lane < (head + 1) * head_size)


def pre_kernel(blocks, s_ref, hid_ref, halo_ref, gain_ref, proj_ref, taps_ref,
               nx_ref, nt_ref, raw_ref, pre_ref, b_ref, c_ref, bt_ref, ct_ref, cb_ref, cbt_ref):
    gain = gain_ref[...]
    rows = blocks * Q

    def norm(v):
        v = v.astype(F32)
        return v * lax.rsqrt(jnp.mean(v * v, axis=1, keepdims=True) + EPSILON) * gain

    halo = norm(halo_ref[...])
    own = norm(hid_ref[...])
    nx_ref[0:HALO] = halo.astype(BF16)
    nx_ref[HALO:] = own.astype(BF16)
    nt_ref[:, 0:rows] = own.T.astype(BF16)
    raw_ref[...] = mm(nx_ref[...], proj_ref[...])
    taps = taps_ref[...]
    state = b_ref.shape[1]
    for block in range(blocks):
        fresh, _ = keeps_of(s_ref, block, blocks)
        pre = conv_block(raw_ref, HALO + block * Q, slice(None), taps, fresh)
        at = pl.ds(block * Q, Q)
        pre_ref[at] = pre
        conv = pre * jax.nn.sigmoid(pre)
        b_mat = conv[:, :state]
        c_mat = conv[:, state:]
        b_low = b_mat.astype(BF16)
        c_low = c_mat.astype(BF16)
        b_ref[at] = b_low
        c_ref[at] = c_low
        bt_ref[:, at] = b_mat.T.astype(BF16)
        ct_ref[:, at] = c_mat.T.astype(BF16)
        cb_ref[block] = mm(c_low, b_low, 1, 1)
        cbt_ref[block] = mm(b_low, c_low, 1, 1)


def step_kernel(blocks, head_size, s_ref, nx_ref, hp_ref, rowp_ref, colp_ref, step_ref, ratio_ref, sig_ref, chan_ref):
    depth = nx_ref.shape[1]
    hp = hp_ref[...]
    u = mm(hp[:, :depth].astype(BF16), nx_ref[HALO:], 1, 1) + hp[:, depth : depth + 1]
    step = jnp.maximum(u, 0.0) + jnp.log1p(jnp.exp(-jnp.abs(u)))
    sig = jax.nn.sigmoid(u)
    step_ref[...] = step
    sig_ref[...] = sig
    ratio_ref[...] = jnp.where(step > 1e-30, sig / jnp.maximum(step, 1e-30), 1.0)
    rate = -jnp.exp(hp[:, depth + 1 : depth + 2])
    move = step * rate
    upto = (
        lax.broadcasted_iota(jnp.int32, (Q, Q), 0) <= lax.broadcasted_iota(jnp.int32, (Q, Q), 1)
    ).astype(F32)
    heads = hp.shape[0]
    lane = lax.broadcasted_iota(jnp.int32, (heads, LANES), 1)
    last_cols = jnp.zeros((heads, LANES), F32)
    lstep = jnp.log(step)
    product = jnp.ones((heads, 1), F32)
    pairs = rowp_ref.shape[0]
    for block in range(blocks):
        at = slice(block * Q, (block + 1) * Q)
        logd = mm(move[:, at], upto, precision=HIGHEST)
        less = logd - lstep[:, at]
        last = logd[:, Q - 1 : Q]
        grown = jnp.exp(logd)
        carry = jnp.exp(last - less)
        final = jnp.exp(last)
        _, kept = keeps_of(s_ref, block, blocks)
        product = product * final * kept
        last_cols = jnp.where(lane == block, final, last_cols)
        for pair in range(pairs):
            for index, values in enumerate((logd, less, grown, carry)):
                rowp_ref[pair, 2 * index : 2 * index + 2, at] = values[2 * pair : 2 * pair + 2]
    last_cols = jnp.where(lane == 6, product, last_cols)
    last_cols = jnp.where(lane == 7, hp[:, depth + 2 : depth + 3], last_cols)
    spots = head_lanes((heads, chan_ref.shape[1]), True, head_size).astype(F32)
    chan_ref[...] = mm(last_cols.T[0:8], spots, precision=HIGHEST)
    for pair in range(pairs):
        colp_ref[pair] = rowp_ref[pair].T


def carry_block(ref, cols, carry, fades):
    state = carry.shape[0]
    ref[0:state, cols] = carry.astype(BF16)
    high = fades.astype(BF16).astype(F32)
    row = lax.broadcasted_iota(jnp.int32, (HALO, LANES), 0)
    ref[state:, cols] = jnp.where(row == 0, high, jnp.where(row == 1, fades - high, 0.0)).astype(BF16)


def tile_at(index):
    return pl.ds(pl.multiple_of(index * LANES, LANES), LANES)


def front_kernel(blocks, first_piece, pieces, s_ref, nx_ref, par_ref, bt_ref, colp_ref, chan_ref, *refs):
    weights = refs[:pieces]
    (gate_out, inner_out, pre_out, s_out, x_ref, carry_ref, turned_ref,
     gate_ref, inner_ref, pre_ref, st_ref, work, sems) = refs[-13:]
    done = refs[pieces:-13]
    wide = weights[0].shape[1] // 2
    for old, new in zip(done[4:], (x_ref, carry_ref, turned_ref)):
        new[:, 0 : first_piece * wide] = old[:, 0 : first_piece * wide]
    own = slice(first_piece * wide, (first_piece + pieces) * wide)
    moves = [(gate_ref, gate_out), (inner_ref, inner_out), (pre_ref, pre_out), (st_ref, s_out)]
    for p in range(pieces):
        here = slice(p * wide, (p + 1) * wide)
        work[:, here] = mm(nx_ref[...], weights[p][:, wide:])
        gate_ref[:, here] = mm(nx_ref[HALO:], weights[p][:, :wide]).astype(BF16)
    tiles = wide // LANES

    def tile(i, none):
        here = tile_at(i)
        pair = i + first_piece * tiles
        far = tile_at(pair)
        turned = tile_at(jnp.bitwise_xor(pair // tiles, 1) * tiles + pair % tiles)
        taps = par_ref[:, far]
        inner_ref[:, here] = work[:, here].astype(BF16)
        for block in range(blocks):
            at = pl.ds(block * Q, Q)
            fresh, kept = keeps_of(s_ref, block, blocks)
            pre = conv_block(work, HALO + block * Q, here, taps, fresh)
            pre_ref[at, here] = pre.astype(BF16)
            x = pre * jax.nn.sigmoid(pre)
            x_ref[at, far] = x.astype(BF16)
            weighted = (spread(colp_ref[pair, at, :], 3) * x).astype(BF16)
            state = mm(bt_ref[:, at], weighted)
            st_ref[block, :, here] = state
            if block == 0:
                carry = state
            else:
                carry = chan_ref[block : block + 1, far] * (kept * carry) + state
        carry_block(carry_ref, far, carry, chan_ref[6:7, far])
        carry_block(turned_ref, turned, carry, chan_ref[6:7, far])
        for index, (held, out) in enumerate(moves):
            pltpu.make_async_copy(held.at[..., here], out.at[..., far], sems.at[index]).start()
        return none

    lax.fori_loop(0, pieces * tiles, tile, 0)
    for index, (held, out) in enumerate(moves):
        pltpu.make_async_copy(held, out.at[..., own], sems.at[index]).wait()


def unpack_carry(ref):
    state = ref.shape[0] - HALO
    return ref[0:state].astype(F32), ref[state : state + 1].astype(F32) + ref[state + 1 : state + 2].astype(F32)


def join_kernel(forward, s_ref, own_ref, got_ref, out_ref):
    mine, my_fade = unpack_carry(own_ref)
    his, his_fade = unpack_carry(got_ref)
    later = (jnp.bitwise_and(s_ref[0], 1) == 1) == forward
    state = mine.shape[0]
    total = jnp.where(later, my_fade * his + mine, his_fade * mine + his)
    fade = my_fade * his_fade
    high = fade.astype(BF16).astype(F32)
    row = lax.broadcasted_iota(jnp.int32, (HALO, total.shape[1]), 0)
    out_ref[0:state] = total.astype(BF16)
    out_ref[state:] = jnp.where(row == 0, high, jnp.where(row == 1, fade - high, 0.0)).astype(BF16)


def arrive_kernel(forward, s_ref, near_ref, far_ref, out_ref):
    near, near_fade = unpack_carry(near_ref)
    wide = near.shape[1] // 2
    later = (jnp.bitwise_and(s_ref[0], 1) == 1) == forward
    far_later = (jnp.bitwise_and(s_ref[0], 2) == 2) == forward
    near = jnp.where(later, near, 0.0)
    fade = jnp.where(far_later, jnp.where(later, near_fade, 1.0), 0.0)
    for half in range(2):
        here, there = slice(half * wide, (half + 1) * wide), slice((1 - half) * wide, (2 - half) * wide)
        out_ref[:, here] = near[:, here] + fade[:, here] * far_ref[0 : near.shape[0], there].astype(F32)


def masked_cotangent(s_ref, cot_ref, blocks, block):
    at = slice(block * Q, (block + 1) * Q)
    return cot_ref[at].astype(F32) * valid_of(s_ref, blocks, block)


def intra_kernel(blocks, pieces, s_ref, rowp_ref, colp_ref, cb_ref, x_ref, cot_ref, *refs):
    outs_w = refs[:pieces]
    y_ref, dny_ref, db_ref = refs[pieces:]
    for block in range(blocks):
        db_ref[block * Q : (block + 1) * Q] = masked_cotangent(s_ref, cot_ref, blocks, block).astype(BF16)
    wide = outs_w[0].shape[0]
    for p in range(pieces):
        dny_ref[:, p * wide : (p + 1) * wide] = mm(db_ref[...], outs_w[p][...], 1, 1).astype(BF16)
    half = Q // 2
    first = first_lanes()
    tri = lax.broadcasted_iota(jnp.int32, (half, half), 0) >= lax.broadcasted_iota(
        jnp.int32, (half, half), 1
    )

    def work(pair):
        far = tile_at(pair)
        for block in range(blocks):
            at = pl.ds(block * Q, Q)
            x = x_ref[at, far]
            both = [jnp.where(first, x, 0), jnp.where(first, 0, x)]
            rp = rowp_ref[pair, :, at]
            cp = colp_ref[pair, at, :]
            tops, bots = [], []
            for k in range(2):
                ld, ls = cp[:, k : k + 1], rp[2 + k : 3 + k, :]
                arg = jnp.where(tri, ld[:half] - ls[:, :half], -1e30)
                tops.append((cb_ref[block, 0:half, 0:half] * jnp.exp(arg)).astype(BF16))
                arg = ld[half:] - ls[:, :half]
                bots.append((cb_ref[block, half:, 0:half] * jnp.exp(arg)).astype(BF16))
                arg = jnp.where(tri, ld[half:] - ls[:, half:], -1e30)
                bots.append((cb_ref[block, half:, half:] * jnp.exp(arg)).astype(BF16))
            y_ref[pl.ds(block * Q, half), far] = mm(jnp.concatenate(tops, 1), jnp.concatenate([b[:half] for b in both], 0))
            y_ref[pl.ds(block * Q + half, half), far] = mm(jnp.concatenate(bots, 1), jnp.concatenate(both, 0))

    def two(i, none):
        work(2 * i)
        work(2 * i + 1)
        return none

    lax.fori_loop(0, x_ref.shape[1] // (2 * LANES), two, 0)


def split_store(hi_ref, lo_ref, at, cols, part):
    high = part.astype(BF16)
    hi_ref[at, cols] = high
    lo_ref[at, cols] = (part - high.astype(F32)).astype(BF16)


def head_sums(heads, head_size, hi_ref, lo_ref):
    spots = head_lanes((heads, hi_ref.shape[1]), True, head_size).astype(F32).astype(BF16)
    return mm(spots, hi_ref[...], 1, 1) + mm(spots, lo_ref[...], 1, 1)


def valid_of(s_ref, blocks, block):
    place = s_ref[0] * blocks + block
    last = place == s_ref[1] - 1
    length = jnp.where(place == 0, s_ref[2], jnp.where(last, s_ref[4], s_ref[3]))
    start = jnp.where(place == 0, 0, jnp.where(last, s_ref[1] - 1, 1))
    rows = lax.broadcasted_iota(jnp.int32, (Q, 1), 0) + (place - start) * Q
    return (rows < length).astype(F32)


def piece_loop(total_tiles, tiles, work, store, keep_ref, send_ref):
    half = total_tiles // 2

    for odd, ref in ((1, send_ref), (0, keep_ref)):
        def place(i, odd=odd):
            return (2 * (i // tiles) + odd) * tiles + i % tiles

        def turn(i, none, place=place, ref=ref):
            before = jnp.maximum(2 * i - 2, 0)
            store([before, before + 1], [place(before), place(before + 1)], ref)
            work(place(2 * i))
            work(place(2 * i + 1))
            return none

        lax.fori_loop(0, half // 2, turn, 0)
        store([half - 2, half - 1], [place(half - 2), place(half - 1)], ref)


def store_grad(ref, at, tiles, rows_at, value):
    for j in range(2):
        slot, lane = at[j] // tiles, at[j] % tiles
        cols = tile_at(lane) if not isinstance(lane, int) else slice(lane * LANES, (lane + 1) * LANES)
        ref[slot, rows_at, cols] = value[:, j * LANES : (j + 1) * LANES]


def middle_kernel(blocks, tiles, head_size, s_ref, cot_ref, inc_in, colp_ref, chan_ref, par_ref, c_ref, ct_ref, nt_ref,
                  y_ref, dny_ref, gate_ref, x_ref, st_ref,
                  ny_out, dgate_out, keep_out, send_out, inc_ref, di_ref, dy_ref, carry_ref, turned_ref, dc_ref, rowpart_ref,
                  rows_ref, ny_ref, dgate_ref, keep_ref, send_ref,
                  dbt_ref, mix_ref, sq_ref, cr_ref, dye_ref, hi_ref, lo_ref, sems):
    moves = [(ny_ref, ny_out), (dgate_ref, dgate_out), (keep_ref, keep_out), (send_ref, send_out)]

    def move(index, *where):
        held, out = moves[index]
        pltpu.make_async_copy(held.at[where], out.at[where], sems.at[index]).start()

    depth = cot_ref.shape[1]
    total = chan_ref.shape[1]
    kept = [keeps_of(s_ref, block, blocks)[1] for block in range(blocks)]
    for block in range(blocks):
        at = slice(block * Q, (block + 1) * Q)
        dbt_ref[:, at] = masked_cotangent(s_ref, cot_ref, blocks, block).T.astype(BF16)
    sq_ref[...] = jnp.zeros_like(sq_ref)
    cr_ref[...] = jnp.zeros_like(cr_ref)

    def forward(i, none):
        for pair in (2 * i, 2 * i + 1):
            far = tile_at(pair)
            incoming = inc_in[:, far]
            for block in range(blocks):
                at = pl.ds(block * Q, Q)
                incoming = kept[block] * incoming
                inc_low = incoming.astype(BF16)
                inc_ref[block, :, far] = inc_low
                incoming = chan_ref[block : block + 1, far] * incoming + st_ref[block, :, far]
                inter = mm(c_ref[at], inc_low) * spread(colp_ref[pair, at, :], 2)
                mix = y_ref[at, far] + inter + chan_ref[7:8, far] * x_ref[at, far].astype(F32)
                mix_ref[at, far] = mix
                gate = gate_ref[at, far].astype(F32)
                gated = mix * (gate * jax.nn.sigmoid(gate))
                sq_ref[at] += gated * gated
                cr_ref[at] += dny_ref[at, far].astype(F32) * par_ref[5:6, far] * gated
        return none

    lax.fori_loop(0, total // (2 * LANES), forward, 0)
    scale = lax.rsqrt(jnp.sum(sq_ref[...], axis=1, keepdims=True) / total + EPSILON)
    coef = scale * scale * scale * (jnp.sum(cr_ref[...], axis=1, keepdims=True) / total)
    sq_ref[...] = jnp.broadcast_to(scale, sq_ref.shape)
    cr_ref[...] = jnp.broadcast_to(coef, cr_ref.shape)
    rows_ref[...] = jnp.zeros_like(rows_ref)

    def backward(pair):
        far = tile_at(pair)
        gain = par_ref[5:6, far]
        skip = chan_ref[7:8, far]
        gain_row = jnp.zeros((1, LANES), F32)
        skip_row = jnp.zeros((1, LANES), F32)
        dis = []
        for block in range(blocks):
            at = pl.ds(block * Q, Q)
            gate, mix, x = gate_ref[at, far].astype(F32), mix_ref[at, far], x_ref[at, far].astype(F32)
            sig = jax.nn.sigmoid(gate)
            act = gate * sig
            gated = mix * act
            normed = gated * sq_ref[at]
            dny = dny_ref[at, far].astype(F32)
            ny_ref[at, far] = (normed * gain).astype(BF16)
            gain_row += jnp.sum(dny * normed, axis=0, keepdims=True)
            d_gated = dny * gain * sq_ref[at] - gated * cr_ref[at]
            dgate_ref[at, far] = (d_gated * mix * silu_slope(gate, sig)).astype(BF16)
            dy = d_gated * act
            dy_low = dy.astype(BF16)
            dy_ref[at, far] = dy_low
            skip_row += jnp.sum(dy * x, axis=0, keepdims=True)
            split_store(hi_ref, lo_ref, at, far, dy_low.astype(F32) * (mix - skip * x))
            dye = (dy * spread(colp_ref[pair, at, :], 2)).astype(BF16)
            dye_ref[at, far] = dye
            di = mm(ct_ref[:, at], dye).astype(BF16)
            di_ref[block, :, far] = di
            dis.append(di.astype(F32))
        rows_ref[0:1, far] = gain_row
        rows_ref[1:2, far] = skip_row
        back = jnp.zeros_like(dis[0])
        for block in reversed(range(blocks)):
            back = kept[block] * (dis[block] + chan_ref[block : block + 1, far] * back)
        carry_block(carry_ref, far, back, chan_ref[6:7, far])
        turned = tile_at(jnp.bitwise_xor(pair // tiles, 1) * tiles + pair % tiles)
        carry_block(turned_ref, turned, back, chan_ref[6:7, far])
        move(0, slice(None), far)
        move(1, slice(None), far)

    def store(at, places, ref):
        cols = [tile_at(place) for place in places]
        normed = jnp.concatenate([ny_ref[:, c] for c in cols], 1)
        store_grad(ref, at, tiles, slice(0, depth), mm(dbt_ref[...], normed).astype(BF16))
        gates = jnp.concatenate([dgate_ref[:, c] for c in cols], 1)
        store_grad(ref, at, tiles, slice(depth, 2 * depth), mm(nt_ref[...], gates).astype(BF16))

    piece_loop(total // LANES, tiles, backward, store, keep_ref, send_ref)
    move(2)
    move(3)
    rowpart_ref[...] = head_sums(rowpart_ref.shape[0], head_size, hi_ref, lo_ref)
    for block in range(blocks):
        at = slice(block * Q, (block + 1) * Q)
        dc_ref[at] = mm(dye_ref[at], inc_ref[block], 1, 1)
    for index, (held, out) in enumerate(moves):
        pltpu.make_async_copy(held, out, sems.at[index]).wait()


def back_kernel(blocks, head_size, s_ref, rowp_ref, colp_ref, cbt_ref, b_ref, c_ref, dy_ref, x_ref,
                dx_ref, part_ref, db_ref, dc_ref, acc_ref, hi_ref, lo_ref):
    half = Q // 2
    first = first_lanes()
    tri = lax.broadcasted_iota(jnp.int32, (half, half), 0) <= lax.broadcasted_iota(
        jnp.int32, (half, half), 1
    )
    acc_ref[...] = jnp.zeros_like(acc_ref)

    def two(i, none):
        for block in range(blocks):
            at = pl.ds(block * Q, Q)
            w00 = w01 = w11 = 0.0
            for pair in (2 * i, 2 * i + 1):
                far = tile_at(pair)
                x, dy = x_ref[at, far], dy_ref[at, far]
                dys = [jnp.where(first, dy, 0), jnp.where(first, 0, dy)]
                xs = [jnp.where(first, x, 0), jnp.where(first, 0, x)]
                rp = rowp_ref[pair, :, at]
                cp = colp_ref[pair, at, :]
                tops, bots = [], []
                for k in range(2):
                    ls, ld = cp[:, 2 + k : 3 + k], rp[k : k + 1, :]
                    ds_top = mm(xs[k][:half], dy, 1, 1)
                    ds_bot = mm(xs[k][half:], dy[half:], 1, 1)
                    e00 = jnp.exp(jnp.where(tri, ld[:, :half] - ls[:half], -1e30))
                    e01 = jnp.exp(ld[:, half:] - ls[:half])
                    e11 = jnp.exp(jnp.where(tri, ld[:, half:] - ls[half:], -1e30))
                    tops.append((cbt_ref[block, 0:half, 0:half] * e00).astype(BF16))
                    tops.append((cbt_ref[block, 0:half, half:] * e01).astype(BF16))
                    bots.append((cbt_ref[block, half:, half:] * e11).astype(BF16))
                    w00 += ds_top[:, :half] * e00
                    w01 += ds_top[:, half:] * e01
                    w11 += ds_bot * e11
                dx_top = mm(jnp.concatenate(tops, 1), jnp.concatenate(dys, 0))
                dx_bot = mm(jnp.concatenate(bots, 1), jnp.concatenate([d[half:] for d in dys], 0))
                dx = jnp.concatenate([dx_top, dx_bot], 0)
                dx_ref[at, far] = dx.astype(BF16)
                split_store(hi_ref, lo_ref, at, far, x.astype(F32) * dx)
            acc_ref[block, 0:half, 0:half] += w00
            acc_ref[block, 0:half, half:] += w01
            acc_ref[block, half:, half:] += w11
        return none

    lax.fori_loop(0, x_ref.shape[1] // (2 * LANES), two, 0)
    part_ref[...] = head_sums(part_ref.shape[0], head_size, hi_ref, lo_ref)
    for block in range(blocks):
        at = slice(block * Q, (block + 1) * Q)
        acc = acc_ref[block].astype(BF16)
        db_ref[at] = mm(acc, c_ref[at])
        dc_ref[at] = mm(acc, b_ref[at], 0, 0)


def conv_back(s_ref, blocks, work, taps, values_of, slope_of, store):
    sums = [0.0] * (K + 1)
    for block in range(blocks):
        fresh, _ = keeps_of(s_ref, block, blocks)
        d_pre = slope_of(block)
        work[0, pl.ds(HALO + block * Q, Q)] = d_pre
        sums[K] += jnp.sum(d_pre, axis=0, keepdims=True)
        sums[K - 1] += jnp.sum(d_pre * values_of(HALO + block * Q), axis=0, keepdims=True)
        for distance in range(1, K):
            held = d_pre * row_keep(fresh, distance)
            work[distance, pl.ds(HALO + block * Q, Q)] = held
            sums[K - 1 - distance] += jnp.sum(
                held * values_of(HALO + block * Q - distance), axis=0, keepdims=True
            )
    for begin, count in [(0, HALO)] + [(HALO + b * Q, Q) for b in range(blocks)]:
        out = taps[K - 1 : K] * work[0, pl.ds(begin, count)]
        for distance in range(1, K):
            out = out + taps[K - 1 - distance : K - distance] * work[distance, pl.ds(begin + distance, count)]
        store(begin, count, out.astype(BF16))
    return sums


def tail_kernel(blocks, tiles, head_size, s_ref, back_in, colp_ref, chan_ref, par_ref, b_ref, nt_ref, nx_ref,
                inc_ref, dx_ref, dy_ref, di_ref, x_ref, pre_ref, inner_ref,
                dinner_ref, vgrad_ref, part_ref, lasts_ref, db_ref, keep_ref, send_ref,
                d_ref, in_ref, wx_ref, gs_ref, hi_ref, lo_ref):
    total = chan_ref.shape[1]
    kept = [keeps_of(s_ref, block, blocks)[1] for block in range(blocks)]
    d_ref[...] = jnp.zeros_like(d_ref)
    vgrad_ref[...] = jnp.zeros_like(vgrad_ref)
    lasts_ref[...] = jnp.zeros_like(lasts_ref)

    def work(pair):
        far = tile_at(pair)
        in_ref[...] = inner_ref[:, far].astype(F32)
        skip = chan_ref[7:8, far]
        back = back_in[:, far]
        lasts = [None] * blocks
        for block in reversed(range(blocks)):
            fade = chan_ref[block : block + 1, far]
            gs_ref[block, :, far] = back.astype(BF16)
            lasts[block] = fade * jnp.sum(inc_ref[block, :, far].astype(F32) * back, axis=0, keepdims=True)
            back = kept[block] * (di_ref[block, :, far].astype(F32) + fade * back)

        def slope_of(block):
            at = pl.ds(block * Q, Q)
            carry = spread(colp_ref[pair, at, :], 3)
            weighted = carry * x_ref[at, far].astype(F32)
            wx_ref[at, far] = weighted.astype(BF16)
            d_weighted = mm(b_ref[at], gs_ref[block, :, far])
            moved = weighted * d_weighted
            lasts_ref[block : block + 1, far] = lasts[block] + jnp.sum(moved, axis=0, keepdims=True)
            split_store(hi_ref, lo_ref, at, far, moved)
            d_x = dx_ref[at, far].astype(F32) + carry * d_weighted + skip * dy_ref[at, far].astype(F32)
            pre = pre_ref[at, far].astype(F32)
            return d_x * silu_slope(pre, jax.nn.sigmoid(pre))

        def store(begin, count, value):
            dinner_ref[pl.ds(begin, count), far] = value

        sums = conv_back(s_ref, blocks, d_ref, par_ref[:, far], lambda at: in_ref[pl.ds(at, Q)], slope_of, store)
        for index in range(K + 1):
            vgrad_ref[index : index + 1, far] = sums[index]

    def store_two(at, places, ref):
        cols = [tile_at(place) for place in places]
        own = jnp.concatenate([dinner_ref[HALO:, c] for c in cols], 1)
        halo = jnp.concatenate([dinner_ref[0:HALO, c] for c in cols], 1)
        grad = mm(nt_ref[...], own) + mm(nx_ref[0:HALO], halo, 0, 0)
        store_grad(ref, at, tiles, slice(None), grad.astype(BF16))

    piece_loop(total // LANES, tiles, work, store_two, keep_ref, send_ref)
    part_ref[...] = head_sums(part_ref.shape[0], head_size, hi_ref, lo_ref)
    for block in range(blocks):
        at = slice(block * Q, (block + 1) * Q)
        db_ref[at] = mm(wx_ref[at], gs_ref[block], 1, 1)


def state_kernel(blocks, head_size, shares, s_ref, dbx_ref, dbin_ref, dcin_ref, dcx_ref, raw_ref, spre_ref, staps_ref,
                 rowpart_ref, part_a, part_b, step_ref, ratio_ref, sig_ref, hp_ref, rows_ref, lasts_ref, vgrad_ref,
                 nt_ref, nx_ref, dstate_ref, dstep_ref, *refs):
    e_ref, all_ref, step_grad_ref = refs[-3:]
    outs = refs[:-3]
    e_ref[...] = jnp.zeros_like(e_ref)
    d_states = []
    for block in range(blocks):
        at = slice(block * Q, (block + 1) * Q)
        d_states.append(jnp.concatenate([dbin_ref[at] + dbx_ref[at], dcin_ref[at] + dcx_ref[at]], 1))

    def slope_of(block):
        pre = spre_ref[pl.ds(block * Q, Q), :]
        return d_states[block] * silu_slope(pre, jax.nn.sigmoid(pre))

    def store(begin, count, value):
        dstate_ref[pl.ds(begin, count), :] = value

    sgrad = conv_back(s_ref, blocks, e_ref, staps_ref[...], lambda at: raw_ref[pl.ds(at, Q), :], slope_of, store)
    heads = hp_ref.shape[0]
    total = lasts_ref.shape[1]
    depth = hp_ref.shape[1] - LANES
    spots = head_lanes((heads, total), True, head_size).astype(F32)
    lasts = mm(spots, lasts_ref[...], 1, 1, precision=HIGHEST)
    skips = mm(spots, rows_ref[...], 1, 1, precision=HIGHEST)[:, 1:2]
    rate = -jnp.exp(hp_ref[:, depth + 1 : depth + 2])
    lane = lax.broadcasted_iota(jnp.int32, (heads, Q), 1)
    upto = (
        lax.broadcasted_iota(jnp.int32, (Q, Q), 0) >= lax.broadcasted_iota(jnp.int32, (Q, Q), 1)
    ).astype(F32)
    grad_bias = jnp.zeros((heads, 1), F32)
    grad_decay = jnp.zeros((heads, 1), F32)
    for block in range(blocks):
        at = slice(block * Q, (block + 1) * Q)
        cols = part_a[:, at] + part_b[:, at]
        d_log = rowpart_ref[:, at] - cols + jnp.where(lane == Q - 1, lasts[:, block : block + 1], 0.0)
        d_move = mm(d_log, upto, precision=HIGHEST)
        d_raw = cols * ratio_ref[:, at] + rate * d_move * sig_ref[:, at]
        grad_bias += jnp.sum(d_raw, axis=1, keepdims=True)
        grad_decay += rate * jnp.sum(step_ref[:, at] * d_move, axis=1, keepdims=True)
        dstep_ref[:, at] = d_raw.astype(BF16)
    wide_lane = lax.broadcasted_iota(jnp.int32, (heads, LANES), 1)
    per_head = jnp.where(
        wide_lane == 0, grad_bias, jnp.where(wide_lane == 1, grad_decay, jnp.where(wide_lane == 2, skips, 0.0))
    )
    step_grad_ref[...] = mm(dstep_ref[...], nx_ref[HALO:])
    all_ref[...] = jnp.zeros_like(all_ref)
    all_ref[0:depth] = mm(nt_ref[...], dstate_ref[HALO:]) + mm(nx_ref[0:HALO], dstate_ref[0:HALO], 0, 0)
    for index in range(K + 1):
        all_ref[depth + index : depth + index + 1] = sgrad[index]
    if not shares:
        outs[0][...] = all_ref[...]
        outs[1][...] = step_grad_ref[...]
        outs[2][...] = per_head
        return
    ways, share, wide = shares
    quarter = all_ref.shape[0] // ways
    work = outs[-1]
    for p in range(ways):
        span = slice(p * wide, (p + 1) * wide)
        some = slice(p * share, (p + 1) * share)
        work[...] = jnp.zeros_like(work)
        work[0 : K + 1] = vgrad_ref[0 : K + 1, span]
        work[K + 1 : K + 2] = rows_ref[0:1, span]
        for part in range(depth // wide):
            begin = 8 + part * share
            work[begin : begin + share] = step_grad_ref[some, part * wide : (part + 1) * wide]
        work[24 : 24 + share, 0:LANES] = per_head[some]
        owner = jnp.bitwise_xor(s_ref[0], p)
        work[32 : 32 + quarter, 0 : all_ref.shape[1]] = all_ref[pl.ds(pl.multiple_of(owner * quarter, 8), quarter)]
        outs[p % 2][p // 2] = work[...].astype(BF16)


def final_kernel(pieces, blocks, s_ref, hid_ref, halo_ref, cot_ref, gain_ref, ny_ref, dgate_ref, dinner_ref, dstate_ref,
                 dstep_ref, hp_ref, sproj_ref, *refs):
    both, outs_w = refs[:pieces], refs[pieces : 2 * pieces]
    mixed_ref, grad_ref, extra_ref, gain_out = refs[2 * pieces :]
    wide = outs_w[0].shape[0]
    depth = hid_ref.shape[1]
    gain = gain_ref[...]
    gain_sum = jnp.zeros((1, depth), F32)

    def finish(values_in, d_normed):
        h = values_in.astype(F32)
        scale = lax.rsqrt(jnp.mean(h * h, axis=1, keepdims=True) + EPSILON)
        weighted = gain * d_normed
        inner = jnp.mean(weighted * h, axis=1, keepdims=True)
        return scale * weighted - h * (scale * scale * scale * inner), jnp.sum(d_normed * h * scale, axis=0, keepdims=True)

    total = mm(dstate_ref[0:HALO], sproj_ref[...], 1, 1)
    for p in range(pieces):
        total += mm(dinner_ref[0:HALO, p * wide : (p + 1) * wide], both[p][:, wide:], 1, 1)
    extra_ref[...], part = finish(halo_ref[...], total)
    gain_sum += part
    for block in range(blocks):
        at = slice(block * Q, (block + 1) * Q)
        ext = slice(HALO + block * Q, HALO + (block + 1) * Q)
        total = mm(dstate_ref[ext], sproj_ref[...], 1, 1)
        total += mm(dstep_ref[:, at], hp_ref[:, 0:depth].astype(BF16), 0, 0)
        branch = mm(ny_ref[at, 0:wide], outs_w[0][...])
        for p in range(pieces):
            span = slice(p * wide, (p + 1) * wide)
            total += mm(dgate_ref[at, span], both[p][:, :wide], 1, 1)
            total += mm(dinner_ref[ext, span], both[p][:, wide:], 1, 1)
            if p:
                branch += mm(ny_ref[at, span], outs_w[p][...])
        mixed_ref[at] = (hid_ref[at].astype(F32) + valid_of(s_ref, blocks, block) * branch).astype(BF16)
        d_hidden, part = finish(hid_ref[at], total.astype(BF16).astype(F32))
        gain_sum += part
        grad_ref[at] = cot_ref[at].astype(F32) + d_hidden
    gain_out[...] = jnp.zeros_like(gain_out)
    side = gain_out.shape[1]
    for index in range(depth // side):
        gain_out[index : index + 1] = gain_sum[:, index * side : (index + 1) * side]


def gather_far(value, ahead):
    ways = lax.axis_size("head")
    pieces = {0: value}
    far = {0: after(value, ahead)}
    mask = 2
    while mask < ways:
        for p in list(far):
            far[p | mask] = swap(far[p], "head", mask)
        mask *= 2
    return [value] + [far[p] for p in range(2, ways, 2)]


def near_pair(value, ahead):
    return value, swap(after(value, ahead) if len(ahead) else value, "head", 1)


def swap(value, axis, mask):
    size = lax.axis_size(axis)
    return lax.ppermute(value, axis, [(i, i ^ mask) for i in range(size)])


def pick(value, index):
    return lax.dynamic_index_in_dim(value, index, 0, keepdims=False)


def reduce_dp(own):
    size = lax.axis_size("dp")
    index = lax.axis_index("dp")
    masks = [1 << b for b in range(size.bit_length() - 1)]
    for mask in masks[1:3]:
        side = jnp.where((index & mask) != 0, 1, 0)
        parts = own.reshape(2, own.shape[0] // 2, own.shape[1])
        got = swap(pick(parts, 1 - side).astype(BF16), "dp", mask)
        own = pick(parts, side).astype(F32) + got.astype(F32)
    low = own.astype(BF16)
    for mask in masks[3:]:
        low = (low.astype(F32) + swap(low, "dp", mask).astype(F32)).astype(BF16)
    for mask in reversed(masks[1:3]):
        upper = (index & mask) != 0
        other = swap(low, "dp", mask)
        low = jnp.concatenate([jnp.where(upper, other, low), jnp.where(upper, low, other)], axis=0)
    return low


def after(value, *others):
    return lax.optimization_barrier((value, others))[0]


def gather_pieces(value, ahead=()):
    ways = lax.axis_size("head")
    pieces = {0: value, 1: swap(value, "head", 1)}
    far = {0: after(value, ahead) if ahead else value}
    mask = 2
    while mask < ways:
        for p in list(far):
            far[p | mask] = swap(far[p], "head", mask)
        mask *= 2
    for p in far:
        if p:
            pieces[p] = far[p]
            pieces[p | 1] = swap(far[p], "head", 1)
    return [pieces[p] for p in range(ways)]


def reduce_pieces(pieces):
    ways = len(pieces)
    mask = 1
    live = {p: v for p, v in enumerate(pieces)}
    order = [1 << b for b in range(ways.bit_length() - 1)]
    for mask in order:
        got = {p ^ mask: swap(live[p].astype(BF16), "head", mask) for p in live if p & mask}
        live = {p: live[p].astype(F32) + got[p].astype(F32) for p in live if not p & mask}
    return live[0]


def body(hidden, lengths, norm_gain, gate_proj, value_proj, state_proj, step_proj, value_taps, value_bias,
         state_taps, state_bias, step_bias, decay_log, skip_gain, out_gain, out_proj, cotangent):
    rows, depth = hidden.shape
    ways = lax.axis_size("head")
    me = lax.axis_index("head")
    blocks = rows // Q
    wide = gate_proj.shape[1]
    share = step_proj.shape[1]
    total = wide * ways
    heads = share * ways
    head_size = wide // share
    pairs = heads // 2
    side = state_proj.shape[1]
    state = side // 2
    padded = -(-heads // 32) * 32
    plain = wide % LANES == 0
    order = [1 << b for b in range(ways.bit_length() - 1)]
    scalars = jnp.concatenate(
        [jnp.stack([me, blocks * ways]).astype(jnp.int32), lengths[0], jnp.zeros((3,), jnp.int32)]
    )

    top = jnp.concatenate(
        [step_proj.T.astype(F32), step_bias[:, None], decay_log[:, None], skip_gain[:, None], jnp.zeros((share, LANES - 3), F32)],
        axis=1,
    )
    low = jnp.concatenate([value_taps, value_bias[None], out_gain[None]], axis=0)
    pack = jnp.concatenate(
        [
            jnp.pad(top, ((0, 8 - share), (0, 0))),
            jnp.pad(low, ((0, 2), (0, depth + LANES - wide))),
            jnp.pad(hidden[rows - HALO :].astype(F32), ((0, 0), (0, LANES))),
        ],
        axis=0,
    )
    packs = gather_pieces(pack)
    halo = jnp.zeros((HALO, depth), F32)
    for p in range(1, ways):
        halo = jnp.where((me ^ p) == me - 1, packs[p][16:, :depth], halo)
    halo = halo.astype(BF16)
    both = gather_far(jnp.concatenate([gate_proj, value_proj], axis=1), (packs[1],))
    outs = gather_far(out_proj, (packs, both[0]))

    def both_merged(pair):
        if plain:
            return list(pair)
        a, b = pair
        return [jnp.concatenate([a[:, :wide], b[:, :wide], a[:, wide:], b[:, wide:]], axis=1)]

    def outs_merged(pair):
        return list(pair) if plain else [jnp.concatenate(pair, axis=0)]

    pieces = ways if plain else ways // 2
    span = total // pieces
    tiles = span // LANES
    hp = jnp.pad(jnp.concatenate([p[:share] for p in packs], axis=0), ((0, padded - heads), (0, 0)))
    par = jnp.concatenate([p[8:16, :wide] for p in packs], axis=1)
    gain_in = norm_gain[None]
    staps = jnp.pad(jnp.concatenate([state_taps, state_bias[None]], axis=0), ((0, 3), (0, 0)))

    ext = rows + HALO
    (nx, nt, state_raw, state_pre, b_low, c_low, b_t, c_t, cb, cbt) = call(
        functools.partial(pre_kernel, blocks),
        [((ext, depth), BF16), ((depth, rows), BF16), ((ext, side), F32), ((rows, side), F32),
         ((rows, state), BF16), ((rows, state), BF16), ((state, rows), BF16), ((state, rows), BF16),
         ((blocks, Q, Q), F32), ((blocks, Q, Q), F32)],
        [scalars, hidden, halo, gain_in, state_proj, staps],
        cost=2, mib=PRE,
    )
    rowp, colp, step, ratio, sig, chan = call(
        functools.partial(step_kernel, blocks, head_size),
        [((pairs, 8, rows), F32), ((pairs, rows, 8), F32), ((padded, rows), F32), ((padded, rows), F32),
         ((padded, rows), F32), ((8, total), F32)],
        [scalars, nx, hp],
        cost=2,
        mib=PRE,
    )
    vmem = pltpu.VMEM
    hbm = pl.BlockSpec(memory_space=pltpu.HBM)
    front_outs = [((rows, total), BF16), ((ext, total), BF16), ((rows, total), BF16), ((blocks, state, total), F32),
                  ((rows, total), BF16), ((state + HALO, total), BF16), ((state + HALO, total), BF16)]
    fronts, all_both = [], []
    half = pieces // 2
    for begin in (0, half):
        pairs_of = range(begin // 2, begin // 2 + ways // 4) if plain else range(begin, begin + half)
        weights = [w for at in pairs_of for w in both_merged(near_pair(both[at], fronts))]
        all_both += weights
        args = [scalars, nx, par, b_t, colp, chan, *weights]
        aliases = {len(args) + at: at for at in range(len(fronts))}
        fronts = call(
            functools.partial(front_kernel, blocks, begin, half), front_outs, [*args, *fronts], aliases=aliases,
            ins={len(args) + at: hbm for at in range(min(4, len(fronts)))}, out_specs={at: hbm for at in range(4)},
            kinds={at: pltpu.HBM for at in range(4)},
            scratch=[vmem((rows, half * span), BF16), vmem((ext, half * span), BF16), vmem((rows, half * span), BF16),
                     vmem((blocks, state, half * span), F32), vmem((ext, half * span), F32), pltpu.SemaphoreType.DMA((4,))],
            cost=6, mib=FRONT,
        )
    gate, inner, pre, st, x, carry, carry_turned = fronts

    def turned(value, mask):
        parts = [value[..., (p ^ mask) * wide : ((p ^ mask) + 1) * wide] for p in range(ways)]
        return jnp.concatenate(parts, axis=-1)

    def scan(own, own_turned, forward):
        def fade_of(value):
            return value[state : state + 1].astype(F32) + value[state + 1 : state + 2].astype(F32)

        if plain and ways == 4:
            near = swap(own_turned, "head", 1)
            (run,) = call(functools.partial(join_kernel, forward), [(own.shape, BF16)], [scalars, own, near], mib=8)
            far = swap(run, "head", 2)
            return call(functools.partial(arrive_kernel, forward), [((state, total), F32)], [scalars, near, far], mib=8)[0]
        before = before_fade = None
        run = own
        for mask in order:
            if mask == 1 and plain:
                got = swap(own_turned, "head", 1)
            else:
                got = turned(swap(run, "head", mask), mask)
            got_fade, run_fade = fade_of(got), fade_of(run)
            got, mine = got[:state].astype(F32), run[:state].astype(F32)
            later = ((me & mask) != 0) if forward else ((me & mask) == 0)
            if before is None:
                before = jnp.where(later, got, 0.0)
                before_fade = jnp.where(later, got_fade, 1.0)
            else:
                before = jnp.where(later, before_fade * got + before, before)
                before_fade = jnp.where(later, before_fade * got_fade, before_fade)
            if mask != order[-1]:
                both_maps = jnp.where(later, run_fade * got + mine, got_fade * mine + got)
                fades = run_fade * got_fade
                high = fades.astype(BF16)
                low_part = (fades - high.astype(F32)).astype(BF16)
                run = jnp.concatenate(
                    [both_maps.astype(BF16), high, low_part, jnp.zeros((HALO - 2, total), BF16)], axis=0
                )
        return before

    inc_in = scan(carry, carry_turned, True)
    all_outs = [w for value in outs for w in outs_merged(near_pair(value, x))]
    y_intra, dny = call(
        functools.partial(intra_kernel, blocks, pieces),
        [((rows, total), F32), ((rows, total), BF16)],
        [scalars, rowp, colp, cb, x, cotangent, *all_outs],
        scratch=[vmem((rows, depth), BF16)],
        cost=7,
        mib=INTRA,
    )
    wide_bf = vmem((rows, total), BF16)
    held_outs = [((rows, total), BF16), ((rows, total), BF16),
                 ((pieces // 2, 2 * depth, span), BF16), ((pieces // 2, 2 * depth, span), BF16)]
    (ny, d_gate, a_keep, a_send, inc, d_inc, d_y, back_carry, back_turned, dc_inter, rowpart, rows_sum) = call(
        functools.partial(middle_kernel, blocks, tiles, head_size),
        [*held_outs, ((blocks, state, total), BF16), ((blocks, state, total), BF16),
         ((rows, total), BF16), ((state + HALO, total), BF16), ((state + HALO, total), BF16), ((rows, state), F32),
         ((padded, rows), F32), ((8, total), F32)],
        [scalars, cotangent, inc_in, colp, chan, par, c_low, c_t, nt, y_intra, dny, gate, x, st],
        out_specs={at: hbm for at in range(len(held_outs))}, kinds={at: pltpu.HBM for at in range(len(held_outs))},
        scratch=[*[vmem(*o) for o in held_outs], vmem((depth, rows), BF16), vmem((rows, total), F32), vmem((rows, LANES), F32),
                 vmem((rows, LANES), F32), wide_bf, wide_bf, wide_bf, pltpu.SemaphoreType.DMA((len(held_outs),))],
        cost=14, mib=MIDDLE,
    )
    back_in = scan(back_carry, back_turned, False)

    def over_head(keep, send):
        if not plain:
            parts = [None] * ways
            for m in range(pieces):
                merged = (keep, send)[m % 2][m // 2]
                parts[2 * m], parts[2 * m + 1] = merged[:, :wide], merged[:, wide:]
            return reduce_pieces(parts)
        got = swap(send, "head", 1)
        live = [keep[i].astype(F32) + got[i].astype(F32) for i in range(pieces // 2)]
        return live

    def finish_head(live):
        if not plain:
            return live
        return live[0] + swap(live[1].astype(BF16), "head", 2).astype(F32)

    def halve(value, axis_at=0):
        side = lax.axis_index("dp") & 1
        cut = value.shape[:axis_at] + (2, value.shape[axis_at] // 2) + value.shape[axis_at + 1 :]
        parts = jnp.moveaxis(value.reshape(cut), axis_at, 0)
        got = swap(pick(parts, 1 - side).astype(BF16), "dp", 1)
        return pick(parts, side).astype(F32) + got.astype(F32)

    a_live = over_head(a_keep, a_send)
    if plain:
        a_out = finish_head([v[:depth] for v in a_live])
        a_gate = halve(jnp.stack([v[depth:] for v in a_live]), 1)
        gates = (a_out, a_gate)
    else:
        gates = a_live
    dx, part_a, db_in, dc_in = call(
        functools.partial(back_kernel, blocks, head_size),
        [((rows, total), BF16), ((padded, rows), F32), ((rows, state), F32), ((rows, state), F32)],
        [scalars, rowp, colp, cbt, b_low, c_low, d_y, x],
        scratch=[vmem((blocks, Q, Q), F32), wide_bf, wide_bf],
        cost=8,
        mib=BACK,
    )
    (d_inner, vgrad, part_b, lasts, db_x, b_keep, b_send) = call(
        functools.partial(tail_kernel, blocks, tiles, head_size),
        [((ext, total), BF16), ((8, total), F32), ((padded, rows), F32), ((8, total), F32), ((rows, state), F32),
         ((pieces // 2, depth, span), BF16), ((pieces // 2, depth, span), BF16)],
        [scalars, after(back_in, a_live), colp, chan, par, b_low, nt, nx, inc, dx, d_y, d_inc, x, pre, inner],
        scratch=[vmem((K, rows + 2 * HALO, LANES), F32), vmem((ext, LANES), F32), wide_bf, vmem((blocks, state, total), BF16),
                 wide_bf, wide_bf],
        cost=10, mib=TAIL,
    )
    small_rows, all_rows = 256, 832
    if plain:
        small_outs = [((pieces // 2, small_rows, span), BF16)] * 2
        shares = (ways, share, wide)
        work = [vmem((small_rows, span), F32)]
    else:
        small_outs = [((all_rows, side), F32), ((padded, depth), F32), ((padded, LANES), F32)]
        shares = None
        work = []
    d_state, d_step, *smalls = call(
        functools.partial(state_kernel, blocks, head_size, shares),
        [((ext, side), BF16), ((padded, rows), BF16)] + small_outs,
        [scalars, after(db_x, gates), db_in, dc_in, dc_inter, state_raw, state_pre, staps, rowpart, part_a, part_b, step, ratio, sig, hp,
         rows_sum, lasts, vgrad, nt, nx],
        scratch=work + [vmem((K, rows + 2 * HALO, side), F32), vmem((all_rows, side), F32), vmem((padded, depth), F32)],
        cost=4, mib=STATE,
    )
    share_rows = all_rows // ways
    if not plain:
        all_grad, step_grad, per_head = smalls
        parts = []
        for p in range(ways):
            cols, some = slice(p * wide, (p + 1) * wide), slice(p * share, (p + 1) * share)
            flat = step_grad[some].reshape(share, depth // wide, wide).swapaxes(0, 1).reshape(-1, wide)
            own = lax.dynamic_slice_in_dim(all_grad, (me ^ p) * share_rows, share_rows, 0).reshape(-1)
            count = -(-own.shape[0] // wide)
            own = jnp.pad(own, (0, count * wide - own.shape[0])).reshape(count, wide)
            part = jnp.concatenate(
                [vgrad[0:5, cols], rows_sum[0:1, cols], jnp.zeros((2, wide), F32), flat, jnp.zeros((16 - flat.shape[0], wide), F32),
                 jnp.pad(per_head[some], ((0, 8 - share), (0, wide - LANES))), own], axis=0)
            parts.append(jnp.pad(part, ((0, small_rows - part.shape[0]), (0, 0))))
        c_live = reduce_pieces(parts)
    else:
        c_live = over_head(smalls[0], smalls[1])
    b_live = over_head(b_keep, after(b_send, gates))
    if plain:
        a_part = jnp.concatenate([halve(a_out), finish_head([a_gate[0], a_gate[1]])], axis=0)
    else:
        a_part = halve(a_live)
    mixed, grad_hidden, extra, gain_part = call(
        functools.partial(final_kernel, pieces, blocks),
        [((rows, depth), BF16), ((rows, depth), F32), ((HALO, depth), F32), ((8, span), F32)],
        [scalars, hidden, halo, cotangent, gain_in, after(ny, a_part), d_gate, d_inner, d_state, d_step, hp, state_proj, *all_both, *all_outs],
        cost=9,
        mib=FINAL,
        pin=jax.ShapeDtypeStruct,
    )
    extra = lax.ppermute(extra, "head", [(i + 1, i) for i in range(ways - 1)])
    grad_hidden = grad_hidden.at[rows - HALO :].add(extra)
    a_all = reduce_dp(a_part)
    if plain:
        b_whole = [jnp.concatenate([b, c], axis=0) for b, c in zip(b_live, c_live)]
        cut = b_whole[0].shape[0] // 2
        one = finish_head([v[:cut] for v in b_whole])
        two = halve(jnp.stack([v[cut:] for v in b_whole]), 1)
        b_part = jnp.concatenate([halve(one), finish_head([two[0], two[1]])], axis=0)
    else:
        b_part = halve(jnp.concatenate([b_live, c_live], axis=0))
    gain_rows = gain_part[: depth // span].reshape(depth // wide, wide)
    b_part = jnp.concatenate([b_part, gain_rows, jnp.zeros((32 - gain_rows.shape[0], wide), F32)], axis=0)
    b_all = reduce_dp(b_part)

    def unhalve(value, cuts):
        upper = (lax.axis_index("dp") & 1) != 0
        other = swap(value, "dp", 1)
        rows_out, begin = [], 0
        for count in cuts:
            mine, his = value[begin : begin + count], other[begin : begin + count]
            rows_out.append(jnp.concatenate([jnp.where(upper, his, mine), jnp.where(upper, mine, his)], axis=0))
            begin += count
        return rows_out

    a_out, a_gate = unhalve(a_all, [depth // 2, depth // 2]) if plain else jnp.split(unhalve(a_all, [depth])[0], 2)
    grad_out = a_out.T.astype(F32)
    grad_gate = a_gate.astype(F32)
    *b_rows, gain_all = unhalve(b_all, ([256, 256] if plain else [512]) + [32])
    b_all = jnp.concatenate(b_rows, axis=0)
    gain_all = (gain_all[:32].astype(F32) + gain_all[32:].astype(F32))[: depth // wide].reshape(1, depth)
    gain_all = jnp.pad(gain_all.reshape(-1, side), ((0, 16 - depth // side), (0, 0)))
    grad_value = b_all[:depth].astype(F32)
    small = b_all[depth:].astype(F32)
    grad_step = jnp.concatenate([small[8 + j * share : 8 + (j + 1) * share].T for j in range(depth // wide)], axis=0)
    if plain:
        own = b_all[depth + 32 : depth + 32 + share_rows, :side]
    else:
        own = b_all[depth + 32 : depth + 240].reshape(-1)[: share_rows * side].reshape(share_rows, side)
    stacked = own
    for mask in order:
        gain_low = gain_all.astype(BF16)
        got = swap(jnp.concatenate([stacked, gain_low], axis=0), "head", mask)
        stacked = jnp.concatenate([stacked, got[: stacked.shape[0]]], axis=0)
        gain_all = gain_low.astype(F32) + got[-16:].astype(F32)
    stacked = stacked.reshape(ways, share_rows, side)
    full = jnp.concatenate([pick(stacked, me ^ q) for q in range(ways)], axis=0).astype(F32)
    return (
        mixed,
        grad_hidden,
        gain_all[: depth // side].reshape(-1),
        grad_gate,
        grad_value,
        full[:depth],
        grad_step,
        small[0:4],
        small[4],
        full[depth : depth + 4],
        full[depth + 4],
        small[24 : 24 + share, 0],
        small[24 : 24 + share, 1],
        small[24 : 24 + share, 2],
        small[5],
        grad_out,
    )


def solution(mesh):
    rows = P(("dp", "head"), None)
    in_specs = (
        rows, P("dp", None), P(), P(None, "head"), P(None, "head"), P(), P(None, "head"), P(None, "head"),
        P("head"), P(), P(), P("head"), P("head"), P("head"), P("head"), P("head", None), rows,
    )
    out_specs = (
        rows, rows, P(), P(None, "head"), P(None, "head"), P(), P(None, "head"), P(None, "head"),
        P("head"), P(), P(), P("head"), P("head"), P("head"), P("head"), P("head", None),
    )
    return jax.shard_map(body, mesh=mesh, in_specs=in_specs, out_specs=out_specs, check_vma=False)
```

time: 333 us -> 227 us (0.68)
  starting transfers between devices: 87.6 us -> 33.7 us
  Pallas kernels: 119 us -> 79.1 us
  other arithmetic: 26.5 us -> 11.2 us
  waiting for transfers between devices: 76.6 us -> 80.4 us
    ppermute x64 -> x36, starting transfers between devices: 84.2 us -> 32.2 us  [swap(): return lax.ppermute(value, axis, [(i, i ^ mask) for i in range(size)])]
    pallas_call x11 -> x14, Pallas kernels: 119 us -> 79.1 us  [call(): pl.pallas_call(kernel, grid=grid, out_shape=[kinds[at](s, d) if at in kin...]
    unnamed x54 -> x144, local copies, waits for them, and re-layouts: 4.7 us -> 14.6 us
    ppermute x64 -> x36, waiting for transfers between devices: 75 us -> 80.4 us  [swap(): return lax.ppermute(value, axis, [(i, i ^ mask) for i in range(size)])]
    select_n x8 -> x6, other arithmetic: 5.09 us -> 0.52 us  [the longest x2 0.27 us: unhalve(): jnp.where(upper, his, mine)]
    convert_element_type x20 -> x9, other arithmetic: 6.75 us -> 2.59 us  [the longest x1 1.17 us: body(): grad_out = a_out.T.astype(F32)]
  transfers between devices with their start and end apart: 66 -> 37, of which waited for: 24 -> 22; matrix products, arithmetic and copies ran while one was open for 12% -> 6% of each run, Pallas kernels for 24% -> 27%
where the time goes in v2:
time: 227 us; the launch traced here: 226 us
  waiting for transfers between devices  80.4 us (35%)
  Pallas kernels  79.1 us (35%)
  starting transfers between devices  33.7 us (15%)
  local copies, waits for them, and re-layouts  20.1 us (9%)
  other arithmetic  11.2 us (5%)
    ppermute x36, waiting for transfers between devices, swap(): return lax.ppermute(value, axis, [(i, i ^ mask) for i in range(size)])  80.4 us
    pallas_call x14, Pallas kernels, call(): pl.pallas_call(kernel, grid=grid, out_shape=[kinds[at](s, d) if at in kin...  79.1 us
    ppermute x36, starting transfers between devices, swap(): return lax.ppermute(value, axis, [(i, i ^ mask) for i in range(size)])  32.2 us
    unnamed x144, local copies, waits for them, and re-layouts  14.6 us
  transfers between devices with their start and end apart: 37, of which 22 were waited for; matrix products, arithmetic and copies ran while one was open for 6% of the time, Pallas kernels for 27%

profile of v2, /device:TPU:0, one launch (start us, length us, event | category | flops | bytes accessed | tf_op | source)
XLA Modules:
  0.0 226.5 jit_solution(4260512060540859093)
XLA Ops:
  0.8 2.0 constant_dynamic-update-slice_fusion.1
  4.7 3.0 %collective-permute-start = (f32[32,896]{1,0:T(8,128)S(1)}, f32[32,896]{1,0:T(8,128)S(1)}, u32[]{:S(2)}, u32[]{:S(2)}) collective-permute-start(f32[32,896]{1,0:T(8,128)S(1)} %fusion.28), channel_id=1, source_target_pairs={{0,2},{1,3},{2,0},{3,1},{4,6},{5,7},{6,4},{7,5},{8,10},{9,11},{10,... | collective-permute-start | bytes 344072 | tf_op jit(solution)/shard_map/ppermute | solution.py:724
  7.7 1.9 collective-permute-start.3
  9.6 1.6 collective-permute-done
  12.6 2.0 shard_map.288
  17.0 2.3 %shard_map.289 = (f32[12,8,512]{2,1,0:T(8,128)S(1)}, f32[12,512,8]{2,1,0:T(8,128)S(1)}, f32[32,512]{1,0:T(8,128)S(1)}, f32[32,512]{1,0:T(8,128)S(1)}, f32[32,512]{1,0:T(8,128)S(1)}, /*index=5*/f32[8,1536]{1,0:T(8,128)S(1)}) custom-call(s32[8]{0:T(128)S(1)} %pad_add_fusion.s_ref, bf16[528,768]{1,0:T(8,128)(2,1)S(1)} %get-tuple-element.99.nx_ref, ...), custom_call_target="tpu_custom_call" | custom-call | flops 800000000 | bytes 600000 | tf_op jit(solution)/shard_map/pallas_call | solution.py:44
  19.4 7.7 %shard_map.290 = (bf16[512,1536]{1,0:T(8,128)(2,1)}, bf16[528,1536]{1,0:T(8,128)(2,1)}, bf16[512,1536]{1,0:T(8,128)(2,1)}, f32[2,128,1536]{2,1,0:T(8,128)}, bf16...) custom-call(s32[8]{0:T(128)S(1)} %pad_add_fusion.s_ref, ...), custom_call_target="tpu_custom_call" | custom-call | flops 2400000000 | bytes 1800000 | tf_op jit(solution)/shard_map/pallas_call | solution.py:44
  27.1 9.3 %collective-permute-done.3.refs_0_.refs_2_ = bf16[768,768]{1,0:T(8,128)(2,1)} collective-permute-done((bf16[768,768]{1,0:T(8,128)(2,1)}, bf16[768,768]{1,0:T(8,128)(2,1)}, u32[]{:S(2)}, u32[]{:S(2)}) %collective-permute-start.3) | collective-permute-done | bytes 1179680 | tf_op jit(solution)/shard_map/ppermute | solution.py:724
  36.5 1.7 collective-permute-start.9
  38.2 1.3 collective-permute-done.5.refs_1_.refs_3_
  39.5 7.6 %shard_map.291 = (bf16[512,1536]{1,0:T(8,128)(2,1)}, bf16[528,1536]{1,0:T(8,128)(2,1)}, bf16[512,1536]{1,0:T(8,128)(2,1)}, f32[2,128,1536]{2,1,0:T(8,128)}, bf16...) custom-call(s32[8]{0:T(128)S(1)} %pad_add_fusion.s_ref, ...), custom_call_target="tpu_custom_call", output_to_operand_aliasing={{0}: (8, {}), {1}: (9, {}), {2}: (10, {}), {3}: (11, {}), {... | custom-call | flops 2400000000 | bytes 1800000 | tf_op jit(solution)/shard_map/pallas_call | solution.py:44
  47.4 4.8 %collective-permute-done.9.refs_2_.refs_6_ = bf16[384,768]{1,0:T(8,128)(2,1)S(1)} collective-permute-done((bf16[384,768]{1,0:T(8,128)(2,1)S(1)}, bf16[384,768]{1,0:T(8,128)(2,1)S(1)}, u32[]{:S(2)}, u32[]{:S(2)}) %collective-permute-start.9) | collective-permute-done | bytes 589856 | tf_op jit(solution)/shard_map/ppermute | solution.py:724
  53.5 1.8 collective-permute-start.7
  55.4 5.9 %shard_map.294 = (f32[512,1536]{1,0:T(8,128)S(1)}, bf16[512,1536]{1,0:T(8,128)(2,1)S(1)}) custom-call(s32[8]{0:T(128)S(1)} %pad_add_fusion.s_ref, f32[12,8,512]{2,1,0:T(8,128)S(1)} %get-tuple-element.117.rowp_ref, f32[12,512,8]{2,1,0:T(8,128)S(1)} %get-tuple-element.101.colp_ref, f32[2,256,256]{2,1,0:T(8,128)S(1)} %get-tuple-element.118.cb_ref, ...), custom_call_target="tpu_custom_call" | custom-call | flops 2800000000 | bytes 2100000 | tf_op jit(solution)/shard_map/pallas_call | solution.py:44
  61.3 4.4 %collective-permute-done.7.far_ref = bf16[144,1536]{1,0:T(8,128)(2,1)S(1)} collective-permute-done((bf16[144,1536]{1,0:T(8,128)(2,1)S(1)}, bf16[144,1536]{1,0:T(8,128)(2,1)S(1)}, u32[]{:S(2)}, u32[]{:S(2)}) %collective-permute-start.7) | collective-permute-done | bytes 442400 | tf_op jit(solution)/shard_map/ppermute | solution.py:724
  66.4 17.5 %shard_map.295 = (bf16[512,1536]{1,0:T(8,128)(2,1)}, bf16[512,1536]{1,0:T(8,128)(2,1)}, bf16[2,1536,384]{2,1,0:T(8,128)(2,1)}, bf16[2,1536,384]{2,1,0:T(8,128)(2...) custom-call(s32[8]{0:T(128)S(1)} %pad_add_fusion.s_ref, ...), custom_call_target="tpu_custom_call" | custom-call | flops 5600000000 | bytes 4200000 | tf_op jit(solution)/shard_map/pallas_call | solution.py:44
  90.1 4.9 %collective-permute-done.16.got_ref.near_ref = bf16[144,1536]{1,0:T(8,128)(2,1)} collective-permute-done((bf16[144,1536]{1,0:T(8,128)(2,1)}, bf16[144,1536]{1,0:T(8,128)(2,1)}, u32[]{:S(2)}, u32[]{:S(2)}) %collective-permute-start.16) | collective-permute-done | bytes 442400 | tf_op jit(solution)/shard_map/ppermute | solution.py:724
  96.0 1.2 shard_map.296
  97.3 1.8 collective-permute-start.17
  99.1 2.9 %convert_add_fusion = (f32[1,1536,384]{2,1,0:T(8,128)S(1)}, f32[1,1536,384]{2,1,0:T(8,128)S(1)}) fusion(bf16[2,1536,384]{2,1,0:T(8,128)(2,1)} %collective-permute-done.11, bf16[2,1536,384]{2,1,0:T(8,128)(2,1)} %get-tuple-element.128), kind=kLoop, calls=%fused_computation.4 | loop fusion | flops 3538944 | bytes 9437184 | tf_op jit(solution)/shard_map/add | solution.py:952
  103.2 7.5 %shard_map.298 = (bf16[512,1536]{1,0:T(8,128)(2,1)S(1)}, f32[32,512]{1,0:T(8,128)S(1)}, f32[512,128]{1,0:T(8,128)S(1)}, f32[512,128]{1,0:T(8,128)S(1)}) custom-call(s32[8]{0:T(128)S(1)} %pad_add_fusion.s_ref, f32[12,8,512]{2,1,0:T(8,128)S(1)} %copy-done.45, f32[12,512,8]{2,1,0:T(8,128)S(1)} %get-tuple-element.101.colp_ref, f32[2,256,256]{2,1,0:T(8,128)S(1)} %copy-done.41, ...), custom_call_target="tpu_custom_call" | custom-call | flops 3200000000 | bytes 2400000 | tf_op jit(solution)/shard_map/pallas_call | solution.py:44
  110.8 1.2 shard_map.297.back_in
  112.3 1.6 collective-permute-start.14
  114.8 12.5 %shard_map.299 = (bf16[528,1536]{1,0:T(8,128)(2,1)S(1)}, f32[8,1536]{1,0:T(8,128)S(1)}, f32[32,512]{1,0:T(8,128)S(1)}, f32[8,1536]{1,0:T(8,128)S(1)}, f32[512,12...) custom-call(s32[8]{0:T(128)S(1)} %pad_add_fusion.s_ref, ...), custom_call_target="tpu_custom_call" | custom-call | flops 4000000000 | bytes 3000000 | tf_op jit(solution)/shard_map/pallas_call | solution.py:44
  127.9 1.6 collective-permute-start.13
  129.4 1.4 collective-permute-start.15
  130.9 2.6 %shard_map.300 = (bf16[528,256]{1,0:T(8,128)(2,1)S(1)}, bf16[32,512]{1,0:T(8,128)(2,1)S(1)}, bf16[2,256,384]{2,1,0:T(8,128)(2,1)S(1)}, bf16[2,256,384]{2,1,0:T(8,128)(2,1)S(1)}) custom-call(s32[8]{0:T(128)S(1)} %pad_add_fusion.s_ref, f32[512,128]{1,0:T(8,128)S(1)} %get-tuple-element.144.dbx_ref, f32[512,128]{1,0:T(8,128)S(1)} %get-tuple-element.145.dbin_ref, ...), custom_call_target="tpu_custom_call" | custom-call | flops 1600000000 | bytes 1200000 | tf_op jit(solution)/shard_map/pallas_call | solution.py:44
  133.6 3.7 %collective-permute-done.13 = bf16[384,384]{1,0:T(8,128)(2,1)S(1)} collective-permute-done((bf16[384,384]{1,0:T(8,128)(2,1)S(1)}, bf16[384,384]{1,0:T(8,128)(2,1)S(1)}, u32[]{:S(2)}, u32[]{:S(2)}) %collective-permute-start.13) | collective-permute-done | bytes 294944 | tf_op jit(solution)/shard_map/ppermute | solution.py:724
  137.4 1.3 collective-permute-done.15
  138.9 1.6 collective-permute-start.32
  140.9 9.7 %shard_map.301 = (bf16[512,768]{1,0:T(8,128)(2,1)}, f32[512,768]{1,0:T(8,128)}, f32[16,768]{1,0:T(8,128)S(1)}, f32[8,384]{1,0:T(8,128)S(1)}) custom-call(s32[8]{0:T(128)S(1)} %pad_add_fusion.s_ref, bf16[512,768]{1,0:T(8,128)(2,1)S(1)} %copy-done.15, bf16[16,768]{1,0:T(8,128)(2,1)S(1)} %fusion.32.halo_ref, bf16[512,768]{1,0:T(8,128)(2,1)S(1)} %copy-done.23, ...), custom_call_target="tpu_custom_call" | custom-call | flops 3600000000 | bytes 2700000 | tf_op jit(solution)/shard_map/pallas_call | solution.py:44
  150.6 1.5 collective-permute-start.18
  152.3 2.7 %collective-permute-start.33 = (bf16[192,384]{1,0:T(8,128)(2,1)S(1)}, bf16[192,384]{1,0:T(8,128)(2,1)S(1)}, u32[]{:S(2)}, u32[]{:S(2)}) collective-permute-start(bf16[192,384]{1,0:T(8,128)(2,1)S(1)} %fusion.27), channel_id=1, source_target_pairs={{0,16},{4,20},{8,24},{12,28},{16,0},{20,4},{24,8},{28,12},{1,17},{... | collective-permute-start | bytes 442376 | tf_op jit(solution)/shard_map/ppermute | solution.py:724
  155.2 2.0 collective-permute-start.20
  158.4 4.6 %collective-permute-done.33 = bf16[192,384]{1,0:T(8,128)(2,1)S(1)} collective-permute-done((bf16[192,384]{1,0:T(8,128)(2,1)S(1)}, bf16[192,384]{1,0:T(8,128)(2,1)S(1)}, u32[]{:S(2)}, u32[]{:S(2)}) %collective-permute-start.33) | collective-permute-done | bytes 147488 | tf_op jit(solution)/shard_map/ppermute | solution.py:724
  163.1 4.0 %collective-permute-done.20 = bf16[512,384]{1,0:T(8,128)(2,1)S(1)} collective-permute-done((bf16[512,384]{1,0:T(8,128)(2,1)S(1)}, bf16[512,384]{1,0:T(8,128)(2,1)S(1)}, u32[]{:S(2)}, u32[]{:S(2)}) %collective-permute-start.20) | collective-permute-done | bytes 393248 | tf_op jit(solution)/shard_map/ppermute | solution.py:724
  169.5 4.6 %collective-permute-done.21 = bf16[256,384]{1,0:T(8,128)(2,1)S(1)} collective-permute-done((bf16[256,384]{1,0:T(8,128)(2,1)S(1)}, bf16[256,384]{1,0:T(8,128)(2,1)S(1)}, u32[]{:S(2)}, u32[]{:S(2)}) %collective-permute-start.21) | collective-permute-done | bytes 196640 | tf_op jit(solution)/shard_map/ppermute | solution.py:724
  175.0 1.6 collective-permute-start.25
  177.2 7.0 %collective-permute-done.25 = bf16[272,384]{1,0:T(8,128)(2,1)S(1)} collective-permute-done((bf16[272,384]{1,0:T(8,128)(2,1)S(1)}, bf16[272,384]{1,0:T(8,128)(2,1)S(1)}, u32[]{:S(2)}, u32[]{:S(2)}) %collective-permute-start.25) | collective-permute-done | bytes 208928 | tf_op jit(solution)/shard_map/ppermute | solution.py:724
  184.4 3.7 %collective-permute-done.35 = bf16[384,384]{1,0:T(8,128)(2,1)S(1)} collective-permute-done((bf16[384,384]{1,0:T(8,128)(2,1)S(1)}, bf16[384,384]{1,0:T(8,128)(2,1)S(1)}, u32[]{:S(2)}, u32[]{:S(2)}) %collective-permute-start.35) | collective-permute-done | bytes 294944 | tf_op jit(solution)/shard_map/ppermute | solution.py:724
  188.2 4.9 %collective-permute-done.26 = bf16[136,384]{1,0:T(8,128)(2,1)S(1)} collective-permute-done((bf16[136,384]{1,0:T(8,128)(2,1)S(1)}, bf16[136,384]{1,0:T(8,128)(2,1)S(1)}, u32[]{:S(2)}, u32[]{:S(2)}) %collective-permute-start.26) | collective-permute-done | bytes 104480 | tf_op jit(solution)/shard_map/ppermute | solution.py:724
  194.2 4.7 %collective-permute-done.27 = bf16[136,384]{1,0:T(8,128)(2,1)S(1)} collective-permute-done((bf16[136,384]{1,0:T(8,128)(2,1)S(1)}, bf16[136,384]{1,0:T(8,128)(2,1)S(1)}, u32[]{:S(2)}, u32[]{:S(2)}) %collective-permute-start.27) | collective-permute-done | bytes 104480 | tf_op jit(solution)/shard_map/ppermute | solution.py:724
  199.1 1.4 add_dynamic-update-slice_fusion
  200.5 4.3 %collective-permute-done.28 = bf16[272,384]{1,0:T(8,128)(2,1)S(1)} collective-permute-done((bf16[272,384]{1,0:T(8,128)(2,1)S(1)}, bf16[272,384]{1,0:T(8,128)(2,1)S(1)}, u32[]{:S(2)}, u32[]{:S(2)}) %collective-permute-start.28) | collective-permute-done | bytes 208928 | tf_op jit(solution)/shard_map/ppermute | solution.py:724
  207.4 1.4 copy.47
  208.8 4.4 %collective-permute-done.29 = bf16[544,384]{1,0:T(8,128)(2,1)S(1)} collective-permute-done((bf16[544,384]{1,0:T(8,128)(2,1)S(1)}, bf16[544,384]{1,0:T(8,128)(2,1)S(1)}, u32[]{:S(2)}, u32[]{:S(2)}) %collective-permute-start.29) | collective-permute-done | bytes 417824 | tf_op jit(solution)/shard_map/ppermute | solution.py:724
  215.4 2.2 collective-permute-start.31
  219.4 4.3 %collective-permute-done.31 = bf16[432,256]{1,0:T(8,128)(2,1)S(1)} collective-permute-done((bf16[432,256]{1,0:T(8,128)(2,1)S(1)}, bf16[432,256]{1,0:T(8,128)(2,1)S(1)}, u32[]{:S(2)}, u32[]{:S(2)}) %collective-permute-start.31) | collective-permute-done | bytes 221216 | tf_op jit(solution)/shard_map/ppermute | solution.py:724
  (287 shorter events, 34.9 us)
Async XLA Ops:
  0.7 10.5 %copy-start.70 = (s32[1,3]{1,0:T(1,128)S(1)}, s32[1,3]{1,0:T(1,128)}, u32[]{:S(2)}) copy-start(s32[1,3]{1,0:T(1,128)} %param.20) | copy-start | bytes 40
  0.8 10.6 %copy-start.62 = (f32[768]{0:T(1024)S(1)}, f32[768]{0:T(1024)}, u32[]{:S(2)}) copy-start(f32[768]{0:T(1024)} %param.21) | copy-start | bytes 9220
  2.8 9.8 %copy-start.14 = (bf16[512,768]{1,0:T(8,128)(2,1)S(1)}, bf16[512,768]{1,0:T(8,128)(2,1)}, u32[]{:S(2)}) copy-start(bf16[512,768]{1,0:T(8,128)(2,1)} %hid_ref.3) | copy-start | bytes 2359300
  2.8 9.8 %copy-start.34 = (bf16[768,256]{1,0:T(8,128)(2,1)S(1)}, bf16[768,256]{1,0:T(8,128)(2,1)}, u32[]{:S(2)}) copy-start(bf16[768,256]{1,0:T(8,128)(2,1)} %sproj_ref.1) | copy-start | bytes 1179652
  3.7 15.8 %collective-permute-start.4 = (bf16[768,768]{1,0:T(8,128)(2,1)}, bf16[768,768]{1,0:T(8,128)(2,1)}, u32[]{:S(2)}, u32[]{:S(2)}) collective-permute-start(bf16[768,768]{1,0:T(8,128)(2,1)} %constant_dynamic-update-slice_fusion.refs_0_), channel_id=1, source_target_pairs={{0,1},{1,0},{2,3},{3,2},{4,5},{5,4},{6,7},{7,6},{8,9},{9,8},{10,11... | collective-permute-start | bytes 3538952 | tf_op jit(solution)/shard_map/ppermute | solution.py:724
  4.6 3.1 %collective-permute-start.2 = (f32[32,896]{1,0:T(8,128)S(1)}, f32[32,896]{1,0:T(8,128)S(1)}, u32[]{:S(2)}, u32[]{:S(2)}) collective-permute-start(f32[32,896]{1,0:T(8,128)S(1)} %fusion.28), channel_id=1, source_target_pairs={{0,1},{1,0},{2,3},{3,2},{4,5},{5,4},{6,7},{7,6},{8,9},{9,8},{10,11... | collective-permute-start | bytes 344072 | tf_op jit(solution)/shard_map/ppermute | solution.py:724
  4.7 6.5 %collective-permute-start = (f32[32,896]{1,0:T(8,128)S(1)}, f32[32,896]{1,0:T(8,128)S(1)}, u32[]{:S(2)}, u32[]{:S(2)}) collective-permute-start(f32[32,896]{1,0:T(8,128)S(1)} %fusion.28), channel_id=1, source_target_pairs={{0,2},{1,3},{2,0},{3,1},{4,6},{5,7},{6,4},{7,5},{8,10},{9,11},{10,... | collective-permute-start | bytes 344072 | tf_op jit(solution)/shard_map/ppermute | solution.py:724
  7.7 28.8 %collective-permute-start.3 = (bf16[768,768]{1,0:T(8,128)(2,1)}, bf16[768,768]{1,0:T(8,128)(2,1)}, u32[]{:S(2)}, u32[]{:S(2)}) collective-permute-start(bf16[768,768]{1,0:T(8,128)(2,1)} %constant_dynamic-update-slice_fusion.refs_0_), channel_id=1, source_target_pairs={{0,2},{1,3},{2,0},{3,1},{4,6},{5,7},{6,4},{7,5},{8,10},{9,11},{10,... | collective-permute-start | bytes 3538952 | tf_op jit(solution)/shard_map/ppermute | solution.py:724
  11.3 1.3 collective-permute-start.1
  17.0 22.5 %copy-start.6 = (bf16[528,768]{1,0:T(8,128)(2,1)}, bf16[528,768]{1,0:T(8,128)(2,1)S(1)}, u32[]{:S(2)}) copy-start(bf16[528,768]{1,0:T(8,128)(2,1)S(1)} %get-tuple-element.99.nx_ref) | copy-start | bytes 2433028
  17.0 49.3 %copy-start.16 = (bf16[768,512]{1,0:T(8,128)(2,1)}, bf16[768,512]{1,0:T(8,128)(2,1)S(1)}, u32[]{:S(2)}) copy-start(bf16[768,512]{1,0:T(8,128)(2,1)S(1)} %get-tuple-element.116.nt_ref) | copy-start | bytes 2359300
  17.0 49.3 %copy-start.46 = (bf16[512,128]{1,0:T(8,128)(2,1)}, bf16[512,128]{1,0:T(8,128)(2,1)S(1)}, u32[]{:S(2)}) copy-start(bf16[512,128]{1,0:T(8,128)(2,1)S(1)} %get-tuple-element.114.c_ref) | copy-start | bytes 393220
  19.4 35.9 %copy-start.44 = (f32[12,8,512]{2,1,0:T(8,128)}, f32[12,8,512]{2,1,0:T(8,128)S(1)}, u32[]{:S(2)}) copy-start(f32[12,8,512]{2,1,0:T(8,128)S(1)} %get-tuple-element.117.rowp_ref) | copy-start | bytes 589828
  19.4 17.1 %copy-start.24 = (bf16[384,768]{1,0:T(8,128)(2,1)S(1)}, bf16[384,768]{1,0:T(8,128)(2,1)}, u32[]{:S(2)}) copy-start(bf16[384,768]{1,0:T(8,128)(2,1)} %refs_4_.1) | copy-start | bytes 1769476
  36.5 3.1 %collective-permute-start.5 = (bf16[768,768]{1,0:T(8,128)(2,1)}, bf16[768,768]{1,0:T(8,128)(2,1)S(1)}, u32[]{:S(2)}, u32[]{:S(2)}) collective-permute-start(bf16[768,768]{1,0:T(8,128)(2,1)} %collective-permute-done.3.refs_0_.refs_2_), channel_id=1, source_target_pairs={{0,1},{1,0},{2,3},{3,2},{4,5},{5,4},{6,7},{7,6},{8,9},{9,8},{10,11... | collective-permute-start | bytes 3538952 | tf_op jit(solution)/shard_map/ppermute | solution.py:724
  36.5 15.7 %collective-permute-start.9 = (bf16[384,768]{1,0:T(8,128)(2,1)S(1)}, bf16[384,768]{1,0:T(8,128)(2,1)S(1)}, u32[]{:S(2)}, u32[]{:S(2)}) collective-permute-start(bf16[384,768]{1,0:T(8,128)(2,1)S(1)} %copy-done.24), channel_id=1, source_target_pairs={{0,2},{1,3},{2,0},{3,1},{4,6},{5,7},{6,4},{7,5},{8,10},{9,11},{10,... | collective-permute-start | bytes 1769480 | tf_op jit(solution)/shard_map/ppermute | solution.py:724
  47.1 19.2 %copy-start.2 = (bf16[512,1536]{1,0:T(8,128)(2,1)}, bf16[512,1536]{1,0:T(8,128)(2,1)S(1)}, u32[]{:S(2)}) copy-start(bf16[512,1536]{1,0:T(8,128)(2,1)S(1)} %get-tuple-element.119.x_ref) | copy-start | bytes 4718596
  47.2 5.6 %collective-permute-start.6 = (bf16[144,1536]{1,0:T(8,128)(2,1)S(1)}, bf16[144,1536]{1,0:T(8,128)(2,1)S(1)}, u32[]{:S(2)}, u32[]{:S(2)}) collective-permute-start(bf16[144,1536]{1,0:T(8,128)(2,1)S(1)} %get-tuple-element.112), channel_id=1, source_target_pairs={{0,1},{1,0},{2,3},{3,2},{4,5},{5,4},{6,7},{7,6},{8,9},{9,8},{10,11... | collective-permute-start | bytes 1327112 | tf_op jit(solution)/shard_map/ppermute | solution.py:724
  52.2 3.1 %collective-permute-start.10 = (bf16[384,768]{1,0:T(8,128)(2,1)S(1)}, bf16[384,768]{1,0:T(8,128)(2,1)S(1)}, u32[]{:S(2)}, u32[]{:S(2)}) collective-permute-start(bf16[384,768]{1,0:T(8,128)(2,1)S(1)} %collective-permute-done.9.refs_2_.refs_6_), channel_id=1, source_target_pairs={{0,1},{1,0},{2,3},{3,2},{4,5},{5,4},{6,7},{7,6},{8,9},{9,8},{10,11... | collective-permute-start | bytes 1769480 | tf_op jit(solution)/shard_map/ppermute | solution.py:724
  52.2 3.1 %collective-permute-start.8 = (bf16[384,768]{1,0:T(8,128)(2,1)S(1)}, bf16[384,768]{1,0:T(8,128)(2,1)S(1)}, u32[]{:S(2)}, u32[]{:S(2)}) collective-permute-start(bf16[384,768]{1,0:T(8,128)(2,1)S(1)} %copy-done.24), channel_id=1, source_target_pairs={{0,1},{1,0},{2,3},{3,2},{4,5},{5,4},{6,7},{7,6},{8,9},{9,8},{10,11... | collective-permute-start | bytes 1769480 | tf_op jit(solution)/shard_map/ppermute | solution.py:724
  53.5 12.1 %collective-permute-start.7 = (bf16[144,1536]{1,0:T(8,128)(2,1)S(1)}, bf16[144,1536]{1,0:T(8,128)(2,1)S(1)}, u32[]{:S(2)}, u32[]{:S(2)}) collective-permute-start(bf16[144,1536]{1,0:T(8,128)(2,1)S(1)} %shard_map.292), channel_id=1, source_target_pairs={{0,2},{1,3},{2,0},{3,1},{4,6},{5,7},{6,4},{7,5},{8,10},{9,11},{10,... | collective-permute-start | bytes 1327112 | tf_op jit(solution)/shard_map/ppermute | solution.py:724
  55.3 11.0 %copy-start.13 = (f32[2,128,1536]{2,1,0:T(8,128)S(1)}, f32[2,128,1536]{2,1,0:T(8,128)}, u32[]{:S(2)}) copy-start(f32[2,128,1536]{2,1,0:T(8,128)} %get-tuple-element.126.st_ref) | copy-start | bytes 4718596
  89.5 9.6 %collective-permute-start.11 = (bf16[2,1536,384]{2,1,0:T(8,128)(2,1)}, bf16[2,1536,384]{2,1,0:T(8,128)(2,1)}, u32[]{:S(2)}, u32[]{:S(2)}) collective-permute-start(bf16[2,1536,384]{2,1,0:T(8,128)(2,1)} %get-tuple-element.129), channel_id=1, source_target_pairs={{0,1},{1,0},{2,3},{3,2},{4,5},{5,4},{6,7},{7,6},{8,9},{9,8},{10,11... | collective-permute-start | bytes 7077896 | tf_op jit(solution)/shard_map/ppermute | solution.py:724
  89.5 5.5 %collective-permute-start.16 = (bf16[144,1536]{1,0:T(8,128)(2,1)}, bf16[144,1536]{1,0:T(8,128)(2,1)}, u32[]{:S(2)}, u32[]{:S(2)}) collective-permute-start(bf16[144,1536]{1,0:T(8,128)(2,1)} %get-tuple-element.132), channel_id=1, source_target_pairs={{0,1},{1,0},{2,3},{3,2},{4,5},{5,4},{6,7},{7,6},{8,9},{9,8},{10,11... | collective-permute-start | bytes 1327112 | tf_op jit(solution)/shard_map/ppermute | solution.py:724
  97.3 13.5 %collective-permute-start.17 = (bf16[144,1536]{1,0:T(8,128)(2,1)S(1)}, bf16[144,1536]{1,0:T(8,128)(2,1)S(1)}, u32[]{:S(2)}, u32[]{:S(2)}) collective-permute-start(bf16[144,1536]{1,0:T(8,128)(2,1)S(1)} %shard_map.296), channel_id=1, source_target_pairs={{0,2},{1,3},{2,0},{3,1},{4,6},{5,7},{6,4},{7,5},{8,10},{9,11},{10,... | collective-permute-start | bytes 1327112 | tf_op jit(solution)/shard_map/ppermute | solution.py:724
  102.1 25.2 %collective-permute-start.12 = (bf16[768,384]{1,0:T(8,128)(2,1)S(1)}, bf16[768,384]{1,0:T(8,128)(2,1)S(1)}, u32[]{:S(2)}, u32[]{:S(2)}) collective-permute-start(bf16[768,384]{1,0:T(8,128)(2,1)S(1)} %fusion.12), channel_id=1, source_target_pairs={{0,2},{1,3},{2,0},{3,1},{4,6},{5,7},{6,4},{7,5},{8,10},{9,11},{10,... | collective-permute-start | bytes 1769480 | tf_op jit(solution)/shard_map/ppermute | solution.py:724
  112.3 15.2 %collective-permute-start.14 = (bf16[2,384,384]{2,1,0:T(8,128)(2,1)S(1)}, bf16[2,384,384]{2,1,0:T(8,128)(2,1)S(1)}, u32[]{:S(2)}, u32[]{:S(2)}) collective-permute-start(bf16[2,384,384]{2,1,0:T(8,128)(2,1)S(1)} %fusion.13), channel_id=1, source_target_pairs={{0,4},{4,0},{8,12},{12,8},{16,20},{20,16},{24,28},{28,24},{1,5},{5... | collective-permute-start | bytes 1769480 | tf_op jit(solution)/shard_map/ppermute | solution.py:724
  127.7 27.3 %collective-permute-start.19 = (bf16[2,768,384]{2,1,0:T(8,128)(2,1)S(1)}, bf16[2,768,384]{2,1,0:T(8,128)(2,1)S(1)}, u32[]{:S(2)}, u32[]{:S(2)}) collective-permute-start(bf16[2,768,384]{2,1,0:T(8,128)(2,1)S(1)} %get-tuple-element.166), channel_id=1, source_target_pairs={{0,1},{1,0},{2,3},{3,2},{4,5},{5,4},{6,7},{7,6},{8,9},{9,8},{10,11... | collective-permute-start | bytes 3538952 | tf_op jit(solution)/shard_map/ppermute | solution.py:724
  127.9 9.5 %collective-permute-start.13 = (bf16[384,384]{1,0:T(8,128)(2,1)S(1)}, bf16[384,384]{1,0:T(8,128)(2,1)S(1)}, u32[]{:S(2)}, u32[]{:S(2)}) collective-permute-start(bf16[384,384]{1,0:T(8,128)(2,1)S(1)} %fusion.18), channel_id=1, source_target_pairs={{0,4},{4,0},{8,12},{12,8},{16,20},{20,16},{24,28},{28,24},{1,5},{5... | collective-permute-start | bytes 884744 | tf_op jit(solution)/shard_map/ppermute | solution.py:724
  129.4 9.2 %collective-permute-start.15 = (bf16[384,384]{1,0:T(8,128)(2,1)S(1)}, bf16[384,384]{1,0:T(8,128)(2,1)S(1)}, u32[]{:S(2)}, u32[]{:S(2)}) collective-permute-start(bf16[384,384]{1,0:T(8,128)(2,1)S(1)} %fusion.20), channel_id=1, source_target_pairs={{0,2},{1,3},{2,0},{3,1},{4,6},{5,7},{6,4},{7,5},{8,10},{9,11},{10,... | collective-permute-start | bytes 884744 | tf_op jit(solution)/shard_map/ppermute | solution.py:724
  133.6 18.6 %collective-permute-start.22 = (bf16[2,256,384]{2,1,0:T(8,128)(2,1)S(1)}, bf16[2,256,384]{2,1,0:T(8,128)(2,1)S(1)}, u32[]{:S(2)}, u32[]{:S(2)}) collective-permute-start(bf16[2,256,384]{2,1,0:T(8,128)(2,1)S(1)} %get-tuple-element.168), channel_id=1, source_target_pairs={{0,1},{1,0},{2,3},{3,2},{4,5},{5,4},{6,7},{7,6},{8,9},{9,8},{10,11... | collective-permute-start | bytes 1179656 | tf_op jit(solution)/shard_map/ppermute | solution.py:724
  138.9 13.4 %collective-permute-start.32 = (bf16[384,384]{1,0:T(8,128)(2,1)S(1)}, bf16[384,384]{1,0:T(8,128)(2,1)S(1)}, u32[]{:S(2)}, u32[]{:S(2)}) collective-permute-start(bf16[384,384]{1,0:T(8,128)(2,1)S(1)} %fusion.19), channel_id=1, source_target_pairs={{0,8},{4,12},{8,0},{12,4},{16,24},{20,28},{24,16},{28,20},{1,9},{5... | collective-permute-start | bytes 884744 | tf_op jit(solution)/shard_map/ppermute | solution.py:724
  150.6 48.5 %collective-permute-start.18 = (f32[16,768]{1,0:T(8,128)S(1)}, f32[16,768]{1,0:T(8,128)S(1)}, u32[]{:S(2)}, u32[]{:S(2)}) collective-permute-start(f32[16,768]{1,0:T(8,128)S(1)} %get-tuple-element.163), channel_id=1, source_target_pairs={{1,0},{2,1},{3,2},{5,4},{6,5},{7,6},{9,8},{10,9},{11,10},{13,12},{... | collective-permute-start | bytes 147464 | tf_op jit(solution)/shard_map/ppermute | solution.py:1038
  152.3 10.7 %collective-permute-start.33 = (bf16[192,384]{1,0:T(8,128)(2,1)S(1)}, bf16[192,384]{1,0:T(8,128)(2,1)S(1)}, u32[]{:S(2)}, u32[]{:S(2)}) collective-permute-start(bf16[192,384]{1,0:T(8,128)(2,1)S(1)} %fusion.27), channel_id=1, source_target_pairs={{0,16},{4,20},{8,24},{12,28},{16,0},{20,4},{24,8},{28,12},{1,17},{... | collective-permute-start | bytes 442376 | tf_op jit(solution)/shard_map/ppermute | solution.py:724
  155.2 11.9 %collective-permute-start.20 = (bf16[512,384]{1,0:T(8,128)(2,1)S(1)}, bf16[512,384]{1,0:T(8,128)(2,1)S(1)}, u32[]{:S(2)}, u32[]{:S(2)}) collective-permute-start(bf16[512,384]{1,0:T(8,128)(2,1)S(1)} %fusion.15), channel_id=1, source_target_pairs={{0,2},{1,3},{2,0},{3,1},{4,6},{5,7},{6,4},{7,5},{8,10},{9,11},{10,... | collective-permute-start | bytes 1179656 | tf_op jit(solution)/shard_map/ppermute | solution.py:724
  157.6 11.0 %collective-permute-start.23 = (bf16[2,256,384]{2,1,0:T(8,128)(2,1)S(1)}, bf16[2,256,384]{2,1,0:T(8,128)(2,1)S(1)}, u32[]{:S(2)}, u32[]{:S(2)}) collective-permute-start(bf16[2,256,384]{2,1,0:T(8,128)(2,1)S(1)} %fusion.16), channel_id=1, source_target_pairs={{0,4},{4,0},{8,12},{12,8},{16,20},{20,16},{24,28},{28,24},{1,5},{5... | collective-permute-start | bytes 1179656 | tf_op jit(solution)/shard_map/ppermute | solution.py:724
  163.0 13.6 %collective-permute-start.34 = (bf16[192,384]{1,0:T(8,128)(2,1)S(1)}, bf16[192,384]{1,0:T(8,128)(2,1)S(1)}, u32[]{:S(2)}, u32[]{:S(2)}) collective-permute-start(bf16[192,384]{1,0:T(8,128)(2,1)S(1)} %fusion.21), channel_id=1, source_target_pairs={{0,16},{4,20},{8,24},{12,28},{16,0},{20,4},{24,8},{28,12},{1,17},{... | collective-permute-start | bytes 442376 | tf_op jit(solution)/shard_map/ppermute | solution.py:724
  167.3 6.9 %collective-permute-start.21 = (bf16[256,384]{1,0:T(8,128)(2,1)S(1)}, bf16[256,384]{1,0:T(8,128)(2,1)S(1)}, u32[]{:S(2)}, u32[]{:S(2)}) collective-permute-start(bf16[256,384]{1,0:T(8,128)(2,1)S(1)} %fusion.24), channel_id=1, source_target_pairs={{0,4},{4,0},{8,12},{12,8},{16,20},{20,16},{24,28},{28,24},{1,5},{5... | collective-permute-start | bytes 589832 | tf_op jit(solution)/shard_map/ppermute | solution.py:724
  168.7 6.0 %collective-permute-start.24 = (bf16[256,384]{1,0:T(8,128)(2,1)S(1)}, bf16[256,384]{1,0:T(8,128)(2,1)S(1)}, u32[]{:S(2)}, u32[]{:S(2)}) collective-permute-start(bf16[256,384]{1,0:T(8,128)(2,1)S(1)} %fusion.25), channel_id=1, source_target_pairs={{0,2},{1,3},{2,0},{3,1},{4,6},{5,7},{6,4},{7,5},{8,10},{9,11},{10,... | collective-permute-start | bytes 589832 | tf_op jit(solution)/shard_map/ppermute | solution.py:724
  175.0 9.3 %collective-permute-start.25 = (bf16[272,384]{1,0:T(8,128)(2,1)S(1)}, bf16[272,384]{1,0:T(8,128)(2,1)S(1)}, u32[]{:S(2)}, u32[]{:S(2)}) collective-permute-start(bf16[272,384]{1,0:T(8,128)(2,1)S(1)} %fusion.22), channel_id=1, source_target_pairs={{0,8},{4,12},{8,0},{12,4},{16,24},{20,28},{24,16},{28,20},{1,9},{5... | collective-permute-start | bytes 626696 | tf_op jit(solution)/shard_map/ppermute | solution.py:724
  176.7 11.4 %collective-permute-start.35 = (bf16[384,384]{1,0:T(8,128)(2,1)S(1)}, bf16[384,384]{1,0:T(8,128)(2,1)S(1)}, u32[]{:S(2)}, u32[]{:S(2)}) collective-permute-start(bf16[384,384]{1,0:T(8,128)(2,1)S(1)} %pad_maximum_fusion.6), channel_id=1, source_target_pairs={{0,8},{4,12},{8,0},{12,4},{16,24},{20,28},{24,16},{28,20},{1,9},{5... | collective-permute-start | bytes 884744 | tf_op jit(solution)/shard_map/ppermute | solution.py:724
  184.4 8.8 %collective-permute-start.26 = (bf16[136,384]{1,0:T(8,128)(2,1)S(1)}, bf16[136,384]{1,0:T(8,128)(2,1)S(1)}, u32[]{:S(2)}, u32[]{:S(2)}) collective-permute-start(bf16[136,384]{1,0:T(8,128)(2,1)S(1)} %fusion.29), channel_id=1, source_target_pairs={{0,16},{4,20},{8,24},{12,28},{16,0},{20,4},{24,8},{28,12},{1,17},{... | collective-permute-start | bytes 313352 | tf_op jit(solution)/shard_map/ppermute | solution.py:724
  193.2 5.8 %collective-permute-start.27 = (bf16[136,384]{1,0:T(8,128)(2,1)S(1)}, bf16[136,384]{1,0:T(8,128)(2,1)S(1)}, u32[]{:S(2)}, u32[]{:S(2)}) collective-permute-start(bf16[136,384]{1,0:T(8,128)(2,1)S(1)} %fusion.23), channel_id=1, source_target_pairs={{0,16},{4,20},{8,24},{12,28},{16,0},{20,4},{24,8},{28,12},{1,17},{... | collective-permute-start | bytes 313352 | tf_op jit(solution)/shard_map/ppermute | solution.py:724
  193.3 12.8 %collective-permute-start.36 = (bf16[768,384]{1,0:T(8,128)(2,1)S(1)}, bf16[768,384]{1,0:T(8,128)(2,1)S(1)}, u32[]{:S(2)}, u32[]{:S(2)}) collective-permute-start(bf16[768,384]{1,0:T(8,128)(2,1)S(1)} %pad_maximum_fusion.3), channel_id=1, source_target_pairs={{0,4},{4,0},{8,12},{12,8},{16,20},{20,16},{24,28},{28,24},{1,5},{5... | collective-permute-start | bytes 1769480 | tf_op jit(solution)/shard_map/ppermute | solution.py:724
  199.0 5.9 %collective-permute-start.28 = (bf16[272,384]{1,0:T(8,128)(2,1)S(1)}, bf16[272,384]{1,0:T(8,128)(2,1)S(1)}, u32[]{:S(2)}, u32[]{:S(2)}) collective-permute-start(bf16[272,384]{1,0:T(8,128)(2,1)S(1)} %pad_maximum_fusion.8), channel_id=1, source_target_pairs={{0,8},{4,12},{8,0},{12,4},{16,24},{20,28},{24,16},{28,20},{1,9},{5... | collective-permute-start | bytes 626696 | tf_op jit(solution)/shard_map/ppermute | solution.py:724
  205.0 8.2 %collective-permute-start.29 = (bf16[544,384]{1,0:T(8,128)(2,1)S(1)}, bf16[544,384]{1,0:T(8,128)(2,1)S(1)}, u32[]{:S(2)}, u32[]{:S(2)}) collective-permute-start(bf16[544,384]{1,0:T(8,128)(2,1)S(1)} %pad_maximum_fusion.4), channel_id=1, source_target_pairs={{0,4},{4,0},{8,12},{12,8},{16,20},{20,16},{24,28},{28,24},{1,5},{5... | collective-permute-start | bytes 1253384 | tf_op jit(solution)/shard_map/ppermute | solution.py:724
  213.4 1.9 collective-permute-start.30
  215.4 8.2 %collective-permute-start.31 = (bf16[432,256]{1,0:T(8,128)(2,1)S(1)}, bf16[432,256]{1,0:T(8,128)(2,1)S(1)}, u32[]{:S(2)}, u32[]{:S(2)}) collective-permute-start(bf16[432,256]{1,0:T(8,128)(2,1)S(1)} %pad_maximum_fusion.7), channel_id=1, source_target_pairs={{0,2},{1,3},{2,0},{3,1},{4,6},{5,7},{6,4},{7,5},{8,10},{9,11},{10,... | collective-permute-start | bytes 663560 | tf_op jit(solution)/shard_map/ppermute | solution.py:724
  (62 other events, 242.1 us)

commit v3 on v2

--- a/solution.py
+++ b/solution.py
@@ -28,7 +28,7 @@
 
 
 MIB = 1024 * 1024
-PRE, FRONT, INTRA, MIDDLE, BACK, TAIL, STATE, FINAL = 12, 14, 12, 21, 12, 16, 12, 24
+PRE, FRONT, INTRA, MIDDLE, BACK, TAIL, STATE, FINAL = 12, 14, 12, 18, 12, 14, 12, 56
 
 
 def whole(shape):
@@ -166,8 +166,8 @@
     last_cols = jnp.where(lane == 7, hp[:, depth + 2 : depth + 3], last_cols)
     spots = head_lanes((heads, chan_ref.shape[1]), True, head_size).astype(F32)
     chan_ref[...] = mm(last_cols.T[0:8], spots, precision=HIGHEST)
-    for pair in range(pairs):
-        colp_ref[pair] = rowp_ref[pair].T
+    for pair in range(0, pairs, 2):
+        colp_ref[pair // 2] = jnp.concatenate([rowp_ref[pair], rowp_ref[pair + 1]], 0).T
 
 
 def carry_block(ref, cols, carry, fades):
@@ -198,7 +198,7 @@
         gate_ref[:, here] = mm(nx_ref[HALO:], weights[p][:, :wide]).astype(BF16)
     tiles = wide // LANES
 
-    def tile(i, none):
+    def tile(i, cols_of):
         here = tile_at(i)
         pair = i + first_piece * tiles
         far = tile_at(pair)
@@ -212,7 +212,7 @@
             pre_ref[at, here] = pre.astype(BF16)
             x = pre * jax.nn.sigmoid(pre)
             x_ref[at, far] = x.astype(BF16)
-            weighted = (spread(colp_ref[pair, at, :], 3) * x).astype(BF16)
+            weighted = (spread(cols_of(at), 3) * x).astype(BF16)
             state = mm(bt_ref[:, at], weighted)
             st_ref[block, :, here] = state
             if block == 0:
@@ -223,9 +223,13 @@
         carry_block(turned_ref, turned, carry, chan_ref[6:7, far])
         for index, (held, out) in enumerate(moves):
             pltpu.make_async_copy(held.at[..., here], out.at[..., far], sems.at[index]).start()
+
+    def turn(i, none):
+        for k in range(2):
+            tile(2 * i + k, lambda at, k=k: colp_ref[i + first_piece * tiles // 2, at, 8 * k : 8 * k + 8])
         return none
 
-    lax.fori_loop(0, pieces * tiles, tile, 0)
+    lax.fori_loop(0, pieces * tiles // 2, turn, 0)
     for index, (held, out) in enumerate(moves):
         pltpu.make_async_copy(held, out.at[..., own], sems.at[index]).wait()
 
@@ -265,31 +269,38 @@
     return cot_ref[at].astype(F32) * valid_of(s_ref, blocks, block)
 
 
-def intra_kernel(blocks, pieces, s_ref, rowp_ref, colp_ref, cb_ref, x_ref, cot_ref, *refs):
+def masked_kernel(blocks, pieces, s_ref, cot_ref, *refs):
     outs_w = refs[:pieces]
-    y_ref, dny_ref, db_ref = refs[pieces:]
+    dny_ref, dbt_ref, db_ref = refs[pieces:]
     for block in range(blocks):
-        db_ref[block * Q : (block + 1) * Q] = masked_cotangent(s_ref, cot_ref, blocks, block).astype(BF16)
+        at = slice(block * Q, (block + 1) * Q)
+        masked = masked_cotangent(s_ref, cot_ref, blocks, block)
+        db_ref[at] = masked.astype(BF16)
+        dbt_ref[:, at] = masked.T.astype(BF16)
     wide = outs_w[0].shape[0]
     for p in range(pieces):
         dny_ref[:, p * wide : (p + 1) * wide] = mm(db_ref[...], outs_w[p][...], 1, 1).astype(BF16)
+
+
+def intra_kernel(blocks, s_ref, rowp_ref, colp_ref, cb_ref, x_ref, y_ref):
     half = Q // 2
     first = first_lanes()
     tri = lax.broadcasted_iota(jnp.int32, (half, half), 0) >= lax.broadcasted_iota(
         jnp.int32, (half, half), 1
     )
 
-    def work(pair):
+    def work(i, k):
+        pair = 2 * i + k
         far = tile_at(pair)
         for block in range(blocks):
             at = pl.ds(block * Q, Q)
             x = x_ref[at, far]
             both = [jnp.where(first, x, 0), jnp.where(first, 0, x)]
             rp = rowp_ref[pair, :, at]
-            cp = colp_ref[pair, at, :]
+            cp = colp_ref[i, at, 8 * k : 8 * k + 8]
             tops, bots = [], []
-            for k in range(2):
-                ld, ls = cp[:, k : k + 1], rp[2 + k : 3 + k, :]
+            for h in range(2):
+                ld, ls = cp[:, h : h + 1], rp[2 + h : 3 + h, :]
                 arg = jnp.where(tri, ld[:half] - ls[:, :half], -1e30)
                 tops.append((cb_ref[block, 0:half, 0:half] * jnp.exp(arg)).astype(BF16))
                 arg = ld[half:] - ls[:, :half]
@@ -300,8 +311,8 @@
             y_ref[pl.ds(block * Q + half, half), far] = mm(jnp.concatenate(bots, 1), jnp.concatenate(both, 0))
 
     def two(i, none):
-        work(2 * i)
-        work(2 * i + 1)
+        work(i, 0)
+        work(i, 1)
         return none
 
     lax.fori_loop(0, x_ref.shape[1] // (2 * LANES), two, 0)
@@ -327,54 +338,78 @@
     return (rows < length).astype(F32)
 
 
-def piece_loop(total_tiles, tiles, work, store, keep_ref, send_ref):
-    half = total_tiles // 2
-
-    for odd, ref in ((1, send_ref), (0, keep_ref)):
-        def place(i, odd=odd):
-            return (2 * (i // tiles) + odd) * tiles + i % tiles
-
-        def turn(i, none, place=place, ref=ref):
-            before = jnp.maximum(2 * i - 2, 0)
-            store([before, before + 1], [place(before), place(before + 1)], ref)
-            work(place(2 * i))
-            work(place(2 * i + 1))
-            return none
-
-        lax.fori_loop(0, half // 2, turn, 0)
-        store([half - 2, half - 1], [place(half - 2), place(half - 1)], ref)
-
-
-def store_grad(ref, at, tiles, rows_at, value):
-    for j in range(2):
-        slot, lane = at[j] // tiles, at[j] % tiles
-        cols = tile_at(lane) if not isinstance(lane, int) else slice(lane * LANES, (lane + 1) * LANES)
-        ref[slot, rows_at, cols] = value[:, j * LANES : (j + 1) * LANES]
-
-
-def middle_kernel(blocks, tiles, head_size, s_ref, cot_ref, inc_in, colp_ref, chan_ref, par_ref, c_ref, ct_ref, nt_ref,
+class Outbound:
+    def __init__(self, held, sems, keep, send, tiles):
+        self.held, self.sems, self.keep, self.send, self.tiles = held, sems, keep, send, tiles
+
+    def wait(self, slot):
+        for k in range(2):
+            held = self.held.at[slot, :, k * LANES : (k + 1) * LANES]
+            pltpu.make_async_copy(held, self.keep.at[0, :, 0:LANES], self.sems.at[slot, k]).wait()
+
+    def start(self, turn, slot):
+        for k in range(2):
+            at = 2 * turn + k
+            piece, lane = at // self.tiles, at % self.tiles
+            held = self.held.at[slot, :, k * LANES : (k + 1) * LANES]
+            cols = slice(lane * LANES, (lane + 1) * LANES) if isinstance(lane, int) else tile_at(lane)
+            for odd, ref in enumerate((self.keep, self.send)):
+
+                @pl.when(piece % 2 == odd)
+                def _(ref=ref, held=held, piece=piece, cols=cols, k=k):
+                    pltpu.make_async_copy(held, ref.at[piece // 2, :, cols], self.sems.at[slot, k]).start()
+
+
+def turns_with_grads(turns, work, grads, out):
+    def turn(i, none):
+        before = jnp.maximum(i - 1, 0)
+        slot = before % 2
+
+        @pl.when(i >= 3)
+        def _():
+            out.wait(slot)
+
+        grads(before, slot)
+        work(i, 0)
+        work(i, 1)
+
+        @pl.when(i >= 1)
+        def _():
+            out.start(before, slot)
+
+        return none
+
+    lax.fori_loop(0, turns, turn, 0)
+    last = turns - 1
+    if last >= 2:
+        out.wait(last % 2)
+    grads(last, last % 2)
+    out.start(jnp.int32(last), last % 2)
+    for slot in range(min(2, turns)):
+        out.wait(slot)
+
+
+def middle_kernel(blocks, tiles, head_size, s_ref, dbt_ref, inc_in, colp_ref, chan_ref, par_ref, c_ref, ct_ref, nt_ref,
                   y_ref, dny_ref, gate_ref, x_ref, st_ref,
-                  ny_out, dgate_out, keep_out, send_out, inc_ref, di_ref, dy_ref, carry_ref, turned_ref, dc_ref, rowpart_ref,
-                  rows_ref, ny_ref, dgate_ref, keep_ref, send_ref,
-                  dbt_ref, mix_ref, sq_ref, cr_ref, dye_ref, hi_ref, lo_ref, sems):
-    moves = [(ny_ref, ny_out), (dgate_ref, dgate_out), (keep_ref, keep_out), (send_ref, send_out)]
+                  ny_out, dgate_out, keep_out, send_out, inc_out, di_out, dc_out, rowpart_out, rows_out,
+                  dy_ref, carry_ref, turned_ref,
+                  ny_ref, dgate_ref, inc_ref, di_ref, dc_ref, rowpart_ref, rows_ref, grad_ref,
+                  mix_ref, sq_ref, cr_ref, hi_ref, lo_ref, sems, grad_sems):
+    moves = [(ny_ref, ny_out), (dgate_ref, dgate_out), (inc_ref, inc_out), (di_ref, di_out), (dc_ref, dc_out), (rowpart_ref, rowpart_out), (rows_ref, rows_out)]
 
     def move(index, *where):
         held, out = moves[index]
         pltpu.make_async_copy(held.at[where], out.at[where], sems.at[index]).start()
 
-    depth = cot_ref.shape[1]
+    depth = dbt_ref.shape[0]
     total = chan_ref.shape[1]
     kept = [keeps_of(s_ref, block, blocks)[1] for block in range(blocks)]
-    for block in range(blocks):
-        at = slice(block * Q, (block + 1) * Q)
-        dbt_ref[:, at] = masked_cotangent(s_ref, cot_ref, blocks, block).T.astype(BF16)
     sq_ref[...] = jnp.zeros_like(sq_ref)
     cr_ref[...] = jnp.zeros_like(cr_ref)
 
     def forward(i, none):
-        for pair in (2 * i, 2 * i + 1):
-            far = tile_at(pair)
+        for k in range(2):
+            far = tile_at(2 * i + k)
             incoming = inc_in[:, far]
             for block in range(blocks):
                 at = pl.ds(block * Q, Q)
@@ -382,7 +417,7 @@
                 inc_low = incoming.astype(BF16)
                 inc_ref[block, :, far] = inc_low
                 incoming = chan_ref[block : block + 1, far] * incoming + st_ref[block, :, far]
-                inter = mm(c_ref[at], inc_low) * spread(colp_ref[pair, at, :], 2)
+                inter = mm(c_ref[at], inc_low) * spread(colp_ref[i, at, 8 * k : 8 * k + 8], 2)
                 mix = y_ref[at, far] + inter + chan_ref[7:8, far] * x_ref[at, far].astype(F32)
                 mix_ref[at, far] = mix
                 gate = gate_ref[at, far].astype(F32)
@@ -398,7 +433,8 @@
     cr_ref[...] = jnp.broadcast_to(coef, cr_ref.shape)
     rows_ref[...] = jnp.zeros_like(rows_ref)
 
-    def backward(pair):
+    def backward(i, k):
+        pair = 2 * i + k
         far = tile_at(pair)
         gain = par_ref[5:6, far]
         skip = chan_ref[7:8, far]
@@ -422,8 +458,8 @@
             dy_ref[at, far] = dy_low
             skip_row += jnp.sum(dy * x, axis=0, keepdims=True)
             split_store(hi_ref, lo_ref, at, far, dy_low.astype(F32) * (mix - skip * x))
-            dye = (dy * spread(colp_ref[pair, at, :], 2)).astype(BF16)
-            dye_ref[at, far] = dye
+            dye = (dy * spread(colp_ref[i, at, 8 * k : 8 * k + 8], 2)).astype(BF16)
+            dc_ref[at] += mm(dye, inc_ref[block, :, far], 1, 1)
             di = mm(ct_ref[:, at], dye).astype(BF16)
             di_ref[block, :, far] = di
             dis.append(di.astype(F32))
@@ -438,20 +474,17 @@
         move(0, slice(None), far)
         move(1, slice(None), far)
 
-    def store(at, places, ref):
-        cols = [tile_at(place) for place in places]
-        normed = jnp.concatenate([ny_ref[:, c] for c in cols], 1)
-        store_grad(ref, at, tiles, slice(0, depth), mm(dbt_ref[...], normed).astype(BF16))
-        gates = jnp.concatenate([dgate_ref[:, c] for c in cols], 1)
-        store_grad(ref, at, tiles, slice(depth, 2 * depth), mm(nt_ref[...], gates).astype(BF16))
-
-    piece_loop(total // LANES, tiles, backward, store, keep_ref, send_ref)
-    move(2)
-    move(3)
+    def grads(turn, slot):
+        cols = pl.ds(pl.multiple_of(turn * 2 * LANES, 2 * LANES), 2 * LANES)
+        grad_ref[slot, 0:depth] = mm(dbt_ref[...], ny_ref[:, cols]).astype(BF16)
+        grad_ref[slot, depth:] = mm(nt_ref[...], dgate_ref[:, cols]).astype(BF16)
+
+    dc_ref[...] = jnp.zeros_like(dc_ref)
+    turns_with_grads(total // (2 * LANES), backward, grads, Outbound(grad_ref, grad_sems, keep_out, send_out, tiles))
+    for index in (2, 3, 4, 6):
+        move(index)
     rowpart_ref[...] = head_sums(rowpart_ref.shape[0], head_size, hi_ref, lo_ref)
-    for block in range(blocks):
-        at = slice(block * Q, (block + 1) * Q)
-        dc_ref[at] = mm(dye_ref[at], inc_ref[block], 1, 1)
+    move(5)
     for index, (held, out) in enumerate(moves):
         pltpu.make_async_copy(held, out, sems.at[index]).wait()
 
@@ -469,18 +502,19 @@
         for block in range(blocks):
             at = pl.ds(block * Q, Q)
             w00 = w01 = w11 = 0.0
-            for pair in (2 * i, 2 * i + 1):
+            for k in range(2):
+                pair = 2 * i + k
                 far = tile_at(pair)
                 x, dy = x_ref[at, far], dy_ref[at, far]
                 dys = [jnp.where(first, dy, 0), jnp.where(first, 0, dy)]
                 xs = [jnp.where(first, x, 0), jnp.where(first, 0, x)]
                 rp = rowp_ref[pair, :, at]
-                cp = colp_ref[pair, at, :]
+                cp = colp_ref[i, at, 8 * k : 8 * k + 8]
                 tops, bots = [], []
-                for k in range(2):
-                    ls, ld = cp[:, 2 + k : 3 + k], rp[k : k + 1, :]
-                    ds_top = mm(xs[k][:half], dy, 1, 1)
-                    ds_bot = mm(xs[k][half:], dy[half:], 1, 1)
+                for h in range(2):
+                    ls, ld = cp[:, 2 + h : 3 + h], rp[h : h + 1, :]
+                    ds_top = mm(xs[h][:half], dy, 1, 1)
+                    ds_bot = mm(xs[h][half:], dy[half:], 1, 1)
                     e00 = jnp.exp(jnp.where(tri, ld[:, :half] - ls[:half], -1e30))
                     e01 = jnp.exp(ld[:, half:] - ls[:half])
                     e11 = jnp.exp(jnp.where(tri, ld[:, half:] - ls[half:], -1e30))
@@ -533,32 +567,33 @@
 
 def tail_kernel(blocks, tiles, head_size, s_ref, back_in, colp_ref, chan_ref, par_ref, b_ref, nt_ref, nx_ref,
                 inc_ref, dx_ref, dy_ref, di_ref, x_ref, pre_ref, inner_ref,
-                dinner_ref, vgrad_ref, part_ref, lasts_ref, db_ref, keep_ref, send_ref,
-                d_ref, in_ref, wx_ref, gs_ref, hi_ref, lo_ref):
+                dinner_ref, vgrad_ref, part_ref, lasts_ref, db_ref, keep_out, send_out,
+                d_ref, in_ref, hi_ref, lo_ref, grad_ref, grad_sems):
     total = chan_ref.shape[1]
     kept = [keeps_of(s_ref, block, blocks)[1] for block in range(blocks)]
     d_ref[...] = jnp.zeros_like(d_ref)
     vgrad_ref[...] = jnp.zeros_like(vgrad_ref)
     lasts_ref[...] = jnp.zeros_like(lasts_ref)
-
-    def work(pair):
-        far = tile_at(pair)
-        in_ref[...] = inner_ref[:, far].astype(F32)
+    db_ref[...] = jnp.zeros_like(db_ref)
+
+    def work(i, k):
+        far = tile_at(2 * i + k)
+        in_ref[k] = inner_ref[:, far].astype(F32)
         skip = chan_ref[7:8, far]
         back = back_in[:, far]
-        lasts = [None] * blocks
+        lasts, lows = [None] * blocks, [None] * blocks
         for block in reversed(range(blocks)):
             fade = chan_ref[block : block + 1, far]
-            gs_ref[block, :, far] = back.astype(BF16)
+            lows[block] = back.astype(BF16)
             lasts[block] = fade * jnp.sum(inc_ref[block, :, far].astype(F32) * back, axis=0, keepdims=True)
             back = kept[block] * (di_ref[block, :, far].astype(F32) + fade * back)
 
         def slope_of(block):
             at = pl.ds(block * Q, Q)
-            carry = spread(colp_ref[pair, at, :], 3)
+            carry = spread(colp_ref[i, at, 8 * k : 8 * k + 8], 3)
             weighted = carry * x_ref[at, far].astype(F32)
-            wx_ref[at, far] = weighted.astype(BF16)
-            d_weighted = mm(b_ref[at], gs_ref[block, :, far])
+            db_ref[at] += mm(weighted.astype(BF16), lows[block], 1, 1)
+            d_weighted = mm(b_ref[at], lows[block])
             moved = weighted * d_weighted
             lasts_ref[block : block + 1, far] = lasts[block] + jnp.sum(moved, axis=0, keepdims=True)
             split_store(hi_ref, lo_ref, at, far, moved)
@@ -569,22 +604,19 @@
         def store(begin, count, value):
             dinner_ref[pl.ds(begin, count), far] = value
 
-        sums = conv_back(s_ref, blocks, d_ref, par_ref[:, far], lambda at: in_ref[pl.ds(at, Q)], slope_of, store)
+        sums = conv_back(
+            s_ref, blocks, d_ref.at[k], par_ref[:, far], lambda at: in_ref[k, pl.ds(at, Q)], slope_of, store
+        )
         for index in range(K + 1):
             vgrad_ref[index : index + 1, far] = sums[index]
 
-    def store_two(at, places, ref):
-        cols = [tile_at(place) for place in places]
-        own = jnp.concatenate([dinner_ref[HALO:, c] for c in cols], 1)
-        halo = jnp.concatenate([dinner_ref[0:HALO, c] for c in cols], 1)
-        grad = mm(nt_ref[...], own) + mm(nx_ref[0:HALO], halo, 0, 0)
-        store_grad(ref, at, tiles, slice(None), grad.astype(BF16))
-
-    piece_loop(total // LANES, tiles, work, store_two, keep_ref, send_ref)
+    def grads(turn, slot):
+        cols = pl.ds(pl.multiple_of(turn * 2 * LANES, 2 * LANES), 2 * LANES)
+        grad = mm(nt_ref[...], dinner_ref[HALO:, cols]) + mm(nx_ref[0:HALO], dinner_ref[0:HALO, cols], 0, 0)
+        grad_ref[slot] = grad.astype(BF16)
+
+    turns_with_grads(total // (2 * LANES), work, grads, Outbound(grad_ref, grad_sems, keep_out, send_out, tiles))
     part_ref[...] = head_sums(part_ref.shape[0], head_size, hi_ref, lo_ref)
-    for block in range(blocks):
-        at = slice(block * Q, (block + 1) * Q)
-        db_ref[at] = mm(wx_ref[at], gs_ref[block], 1, 1)
 
 
 def state_kernel(blocks, head_size, shares, s_ref, dbx_ref, dbin_ref, dcin_ref, dcx_ref, raw_ref, spre_ref, staps_ref,
@@ -660,12 +692,33 @@
         outs[p % 2][p // 2] = work[...].astype(BF16)
 
 
-def final_kernel(pieces, blocks, s_ref, hid_ref, halo_ref, cot_ref, gain_ref, ny_ref, dgate_ref, dinner_ref, dstate_ref,
-                 dstep_ref, hp_ref, sproj_ref, *refs):
-    both, outs_w = refs[:pieces], refs[pieces : 2 * pieces]
-    mixed_ref, grad_ref, extra_ref, gain_out = refs[2 * pieces :]
+def mixed_kernel(pieces, blocks, s_ref, hid_ref, ny_ref, *refs):
+    outs_w, mixed_ref = refs[:pieces], refs[pieces]
     wide = outs_w[0].shape[0]
+    for block in range(blocks):
+        at = slice(block * Q, (block + 1) * Q)
+        branch = mm(ny_ref[at, 0:wide], outs_w[0][...])
+        for p in range(1, pieces):
+            branch += mm(ny_ref[at, p * wide : (p + 1) * wide], outs_w[p][...])
+        mixed_ref[at] = (hid_ref[at].astype(F32) + valid_of(s_ref, blocks, block) * branch).astype(BF16)
+
+
+def final_kernel(pieces, blocks, mine, s_ref, hid_ref, halo_ref, cot_ref, gain_ref, dgate_ref, dinner_ref,
+                 dstate_ref, dstep_ref, hp_ref, sproj_ref, *refs):
+    both_in = refs[:pieces]
+    grad_out, extra_ref, gain_out, grad_ref, sems, both, dgate_here, dinner_here, in_sems = refs[-9:]
+    wide = both.shape[2] // 2
     depth = hid_ref.shape[1]
+    own = pl.ds(mine[0] * Q, len(mine) * Q)
+    waits = [
+        pltpu.make_async_copy(dinner_ref.at[pl.ds(mine[0] * Q, len(mine) * Q + HALO)], dinner_here, in_sems.at[0]),
+        pltpu.make_async_copy(dgate_ref.at[own], dgate_here, in_sems.at[1]),
+    ]
+    for copy in waits:
+        copy.start()
+    loads = [pltpu.make_async_copy(both_in[p], both.at[p], in_sems.at[2 + p]) for p in range(pieces)]
+    for copy in loads:
+        copy.start()
     gain = gain_ref[...]
     gain_sum = jnp.zeros((1, depth), F32)
 
@@ -676,31 +729,43 @@
         inner = jnp.mean(weighted * h, axis=1, keepdims=True)
         return scale * weighted - h * (scale * scale * scale * inner), jnp.sum(d_normed * h * scale, axis=0, keepdims=True)
 
-    total = mm(dstate_ref[0:HALO], sproj_ref[...], 1, 1)
+    moves = []
+    totals = [mm(dstate_ref[0:HALO], sproj_ref[...], 1, 1)]
+    for block in mine:
+        ext = slice(HALO + block * Q, HALO + (block + 1) * Q)
+        part = mm(dstate_ref[ext], sproj_ref[...], 1, 1)
+        totals.append(part + mm(dstep_ref[:, block * Q : (block + 1) * Q], hp_ref[:, 0:depth].astype(BF16), 0, 0))
+    for copy in waits:
+        copy.wait()
     for p in range(pieces):
-        total += mm(dinner_ref[0:HALO, p * wide : (p + 1) * wide], both[p][:, wide:], 1, 1)
-    extra_ref[...], part = finish(halo_ref[...], total)
-    gain_sum += part
-    for block in range(blocks):
+        loads[p].wait()
+        span = slice(p * wide, (p + 1) * wide)
+        if mine[0] == 0:
+            totals[0] += mm(dinner_here[0:HALO, span], both[p, :, wide:], 1, 1)
+        for index in range(len(mine)):
+            here = slice(index * Q, (index + 1) * Q)
+            ext = slice(HALO + index * Q, HALO + (index + 1) * Q)
+            totals[index + 1] += mm(dgate_here[here, span], both[p, :, :wide], 1, 1)
+            totals[index + 1] += mm(dinner_here[ext, span], both[p, :, wide:], 1, 1)
+    if mine[0] == 0:
+        extra_ref[...], part = finish(halo_ref[...], totals[0])
+        gain_sum += part
+    else:
+        extra_ref[...] = jnp.zeros_like(extra_ref)
+    for index, block in enumerate(mine):
         at = slice(block * Q, (block + 1) * Q)
-        ext = slice(HALO + block * Q, HALO + (block + 1) * Q)
-        total = mm(dstate_ref[ext], sproj_ref[...], 1, 1)
-        total += mm(dstep_ref[:, at], hp_ref[:, 0:depth].astype(BF16), 0, 0)
-        branch = mm(ny_ref[at, 0:wide], outs_w[0][...])
-        for p in range(pieces):
-            span = slice(p * wide, (p + 1) * wide)
-            total += mm(dgate_ref[at, span], both[p][:, :wide], 1, 1)
-            total += mm(dinner_ref[ext, span], both[p][:, wide:], 1, 1)
-            if p:
-                branch += mm(ny_ref[at, span], outs_w[p][...])
-        mixed_ref[at] = (hid_ref[at].astype(F32) + valid_of(s_ref, blocks, block) * branch).astype(BF16)
-        d_hidden, part = finish(hid_ref[at], total.astype(BF16).astype(F32))
+        here = slice(index * Q, (index + 1) * Q)
+        d_hidden, part = finish(hid_ref[at], totals[index + 1].astype(BF16).astype(F32))
         gain_sum += part
-        grad_ref[at] = cot_ref[at].astype(F32) + d_hidden
+        grad_ref[here] = cot_ref[at].astype(F32) + d_hidden
+        moves.append(pltpu.make_async_copy(grad_ref.at[here], grad_out.at[at], sems.at[index]))
+        moves[-1].start()
     gain_out[...] = jnp.zeros_like(gain_out)
     side = gain_out.shape[1]
     for index in range(depth // side):
         gain_out[index : index + 1] = gain_sum[:, index * side : (index + 1) * side]
+    for copy in moves:
+        copy.wait()
 
 
 def gather_far(value, ahead):
@@ -728,23 +793,21 @@
     return lax.dynamic_index_in_dim(value, index, 0, keepdims=False)
 
 
-def reduce_dp(own):
-    size = lax.axis_size("dp")
-    index = lax.axis_index("dp")
-    masks = [1 << b for b in range(size.bit_length() - 1)]
-    for mask in masks[1:3]:
-        side = jnp.where((index & mask) != 0, 1, 0)
-        parts = own.reshape(2, own.shape[0] // 2, own.shape[1])
-        got = swap(pick(parts, 1 - side).astype(BF16), "dp", mask)
-        own = pick(parts, side).astype(F32) + got.astype(F32)
-    low = own.astype(BF16)
-    for mask in masks[3:]:
-        low = (low.astype(F32) + swap(low, "dp", mask).astype(F32)).astype(BF16)
-    for mask in reversed(masks[1:3]):
-        upper = (index & mask) != 0
-        other = swap(low, "dp", mask)
-        low = jnp.concatenate([jnp.where(upper, other, low), jnp.where(upper, low, other)], axis=0)
+def half_of(value, mask):
+    side = jnp.where((lax.axis_index("dp") & mask) != 0, 1, 0)
+    parts = value.reshape(2, value.shape[0] // 2, value.shape[1])
+    return pick(parts, side).astype(F32), pick(parts, 1 - side).astype(BF16)
+
+
+def whole_dp(low):
+    for bit in range(3, lax.axis_size("dp").bit_length() - 1):
+        low = (low.astype(F32) + swap(low, "dp", 1 << bit).astype(F32)).astype(BF16)
     return low
+
+
+def both_of(low, mask, other):
+    upper = (lax.axis_index("dp") & mask) != 0
+    return jnp.concatenate([jnp.where(upper, other, low), jnp.where(upper, low, other)], axis=0)
 
 
 def after(value, *others):
@@ -848,7 +911,7 @@
     )
     rowp, colp, step, ratio, sig, chan = call(
         functools.partial(step_kernel, blocks, head_size),
-        [((pairs, 8, rows), F32), ((pairs, rows, 8), F32), ((padded, rows), F32), ((padded, rows), F32),
+        [((pairs, 8, rows), F32), ((pairs // 2, rows, 16), F32), ((padded, rows), F32), ((padded, rows), F32),
          ((padded, rows), F32), ((8, total), F32)],
         [scalars, nx, hp],
         cost=2,
@@ -888,7 +951,8 @@
             near = swap(own_turned, "head", 1)
             (run,) = call(functools.partial(join_kernel, forward), [(own.shape, BF16)], [scalars, own, near], mib=8)
             far = swap(run, "head", 2)
-            return call(functools.partial(arrive_kernel, forward), [((state, total), F32)], [scalars, near, far], mib=8)[0]
+            (result,) = call(functools.partial(arrive_kernel, forward), [((state, total), F32)], [scalars, near, far], mib=8)
+            return result, run
         before = before_fade = None
         run = own
         for mask in order:
@@ -913,33 +977,41 @@
                 run = jnp.concatenate(
                     [both_maps.astype(BF16), high, low_part, jnp.zeros((HALO - 2, total), BF16)], axis=0
                 )
-        return before
-
-    inc_in = scan(carry, carry_turned, True)
-    all_outs = [w for value in outs for w in outs_merged(near_pair(value, x))]
-    y_intra, dny = call(
-        functools.partial(intra_kernel, blocks, pieces),
-        [((rows, total), F32), ((rows, total), BF16)],
-        [scalars, rowp, colp, cb, x, cotangent, *all_outs],
+        return before, run
+
+    inc_in, run = scan(carry, carry_turned, True)
+    (y_intra,) = call(
+        functools.partial(intra_kernel, blocks),
+        [((rows, total), F32)],
+        [scalars, rowp, colp, cb, after(x, run)],
+        cost=5,
+        mib=INTRA,
+    )
+    all_outs = [w for value in outs for w in outs_merged(near_pair(value, run))]
+    dny, dbt = call(
+        functools.partial(masked_kernel, blocks, pieces),
+        [((rows, total), BF16), ((depth, rows), BF16)],
+        [scalars, cotangent, *all_outs],
         scratch=[vmem((rows, depth), BF16)],
-        cost=7,
+        cost=3,
         mib=INTRA,
     )
     wide_bf = vmem((rows, total), BF16)
     held_outs = [((rows, total), BF16), ((rows, total), BF16),
-                 ((pieces // 2, 2 * depth, span), BF16), ((pieces // 2, 2 * depth, span), BF16)]
-    (ny, d_gate, a_keep, a_send, inc, d_inc, d_y, back_carry, back_turned, dc_inter, rowpart, rows_sum) = call(
+                 ((pieces // 2, 2 * depth, span), BF16), ((pieces // 2, 2 * depth, span), BF16),
+                 ((blocks, state, total), BF16), ((blocks, state, total), BF16), ((rows, state), F32),
+                 ((padded, rows), F32), ((8, total), F32)]
+    (ny, d_gate, a_keep, a_send, inc, d_inc, dc_inter, rowpart, rows_sum, d_y, back_carry, back_turned) = call(
         functools.partial(middle_kernel, blocks, tiles, head_size),
-        [*held_outs, ((blocks, state, total), BF16), ((blocks, state, total), BF16),
-         ((rows, total), BF16), ((state + HALO, total), BF16), ((state + HALO, total), BF16), ((rows, state), F32),
-         ((padded, rows), F32), ((8, total), F32)],
-        [scalars, cotangent, inc_in, colp, chan, par, c_low, c_t, nt, y_intra, dny, gate, x, st],
+        [*held_outs, ((rows, total), BF16), ((state + HALO, total), BF16), ((state + HALO, total), BF16)],
+        [scalars, dbt, inc_in, colp, chan, par, c_low, c_t, nt, y_intra, dny, gate, x, st],
         out_specs={at: hbm for at in range(len(held_outs))}, kinds={at: pltpu.HBM for at in range(len(held_outs))},
-        scratch=[*[vmem(*o) for o in held_outs], vmem((depth, rows), BF16), vmem((rows, total), F32), vmem((rows, LANES), F32),
-                 vmem((rows, LANES), F32), wide_bf, wide_bf, wide_bf, pltpu.SemaphoreType.DMA((len(held_outs),))],
+        scratch=[*[vmem(*o) for at, o in enumerate(held_outs) if at not in (2, 3)], vmem((2, 2 * depth, 2 * LANES), BF16), vmem((rows, total), F32), vmem((rows, LANES), F32),
+                 vmem((rows, LANES), F32), wide_bf, wide_bf, pltpu.SemaphoreType.DMA((len(held_outs) - 2,)),
+                 pltpu.SemaphoreType.DMA((2, 2))],
         cost=14, mib=MIDDLE,
     )
-    back_in = scan(back_carry, back_turned, False)
+    back_in, back_run = scan(back_carry, back_turned, False)
 
     def over_head(keep, send):
         if not plain:
@@ -964,7 +1036,7 @@
         got = swap(pick(parts, 1 - side).astype(BF16), "dp", 1)
         return pick(parts, side).astype(F32) + got.astype(F32)
 
-    a_live = over_head(a_keep, a_send)
+    a_live = over_head(a_keep, after(a_send, back_run))
     if plain:
         a_out = finish_head([v[:depth] for v in a_live])
         a_gate = halve(jnp.stack([v[depth:] for v in a_live]), 1)
@@ -984,8 +1056,9 @@
         [((ext, total), BF16), ((8, total), F32), ((padded, rows), F32), ((8, total), F32), ((rows, state), F32),
          ((pieces // 2, depth, span), BF16), ((pieces // 2, depth, span), BF16)],
         [scalars, after(back_in, a_live), colp, chan, par, b_low, nt, nx, inc, dx, d_y, d_inc, x, pre, inner],
-        scratch=[vmem((K, rows + 2 * HALO, LANES), F32), vmem((ext, LANES), F32), wide_bf, vmem((blocks, state, total), BF16),
-                 wide_bf, wide_bf],
+        out_specs={5: hbm, 6: hbm}, kinds={5: pltpu.HBM, 6: pltpu.HBM},
+        scratch=[vmem((2, K, rows + 2 * HALO, LANES), F32), vmem((2, ext, LANES), F32), wide_bf, wide_bf,
+                 vmem((2, depth, 2 * LANES), BF16), pltpu.SemaphoreType.DMA((2, 2))],
         cost=10, mib=TAIL,
     )
     small_rows, all_rows = 256, 832
@@ -1027,32 +1100,72 @@
         a_part = jnp.concatenate([halve(a_out), finish_head([a_gate[0], a_gate[1]])], axis=0)
     else:
         a_part = halve(a_live)
-    mixed, grad_hidden, extra, gain_part = call(
-        functools.partial(final_kernel, pieces, blocks),
-        [((rows, depth), BF16), ((rows, depth), F32), ((HALO, depth), F32), ((8, span), F32)],
-        [scalars, hidden, halo, cotangent, gain_in, after(ny, a_part), d_gate, d_inner, d_state, d_step, hp, state_proj, *all_both, *all_outs],
-        cost=9,
-        mib=FINAL,
-        pin=jax.ShapeDtypeStruct,
-    )
-    extra = lax.ppermute(extra, "head", [(i + 1, i) for i in range(ways - 1)])
-    grad_hidden = grad_hidden.at[rows - HALO :].add(extra)
-    a_all = reduce_dp(a_part)
+    a_keep_z, a_send_z = half_of(a_part, 2)
     if plain:
         b_whole = [jnp.concatenate([b, c], axis=0) for b, c in zip(b_live, c_live)]
         cut = b_whole[0].shape[0] // 2
-        one = finish_head([v[:cut] for v in b_whole])
-        two = halve(jnp.stack([v[cut:] for v in b_whole]), 1)
-        b_part = jnp.concatenate([halve(one), finish_head([two[0], two[1]])], axis=0)
+        side_x = lax.axis_index("dp") & 1
+        low, high = [v[:cut] for v in b_whole], jnp.stack([v[cut:] for v in b_whole])
+        high = jnp.moveaxis(high.reshape(2, 2, cut // 2, wide), 1, 0)
+        b_sends = low[1].astype(BF16), pick(high, 1 - side_x).astype(BF16)
+    else:
+        b_sends = ()
+    a_got_z = swap(after(a_send_z, b_sends), "dp", 2)
+    if plain:
+        b_got = swap(b_sends[0], "head", 2), swap(b_sends[1], "dp", 1)
+    mine = list(range(blocks))
+    args = [scalars, hidden, halo, cotangent, gain_in, after(d_gate, b_sends, a_send_z), d_inner, d_state, d_step, hp, state_proj,
+            *all_both]
+    results = call(
+        functools.partial(final_kernel, pieces, blocks, mine),
+        [((rows, depth), F32), ((HALO, depth), F32), ((8, span), F32)],
+        args,
+        ins={at: hbm for at in (5, 6, *range(len(args) - pieces, len(args)))},
+        out_specs={0: hbm},
+        kinds={0: pltpu.HBM},
+        scratch=[vmem((rows, depth), F32), pltpu.SemaphoreType.DMA((blocks,)), vmem((pieces, depth, 2 * span), BF16),
+                 vmem((rows, total), BF16), vmem((ext, total), BF16), pltpu.SemaphoreType.DMA((2 + pieces,))],
+        cost=9,
+        mib=FINAL,
+    )
+    grad_hidden, extra, gain_part = results
+    extra = lax.ppermute(extra, "head", [(i + 1, i) for i in range(ways - 1)])
+    grad_hidden = grad_hidden.at[rows - HALO :].add(extra)
+    if plain:
+        one = low[0] + after(b_got[0], results).astype(F32)
+        two = pick(high, side_x) + after(b_got[1], results).astype(F32)
+        one_keep, one_send = half_of(one, 1)
+        b_sends = one_send, two[1].astype(BF16)
+        b_part = [one_keep + swap(one_send, "dp", 1).astype(F32), two[0] + swap(b_sends[1], "head", 2).astype(F32)]
+        b_part = jnp.concatenate(b_part, axis=0)
     else:
         b_part = halve(jnp.concatenate([b_live, c_live], axis=0))
     gain_rows = gain_part[: depth // span].reshape(depth // wide, wide)
     b_part = jnp.concatenate([b_part, gain_rows, jnp.zeros((32 - gain_rows.shape[0], wide), F32)], axis=0)
-    b_all = reduce_dp(b_part)
-
-    def unhalve(value, cuts):
+    a_low = (a_keep_z + after(a_got_z, results).astype(F32)).astype(BF16)
+    a_got_y = swap(a_low, "dp", 4)
+    a_low = whole_dp((a_low.astype(F32) + after(a_got_y, b_sends).astype(F32)).astype(BF16))
+    b_keep_z, b_send_z = half_of(b_part, 2)
+    b_got_z = swap(after(b_send_z, a_low), "dp", 2)
+    a_got_z = swap(a_low, "dp", 2)
+    (mixed,) = call(
+        functools.partial(mixed_kernel, pieces, blocks),
+        [((rows, depth), BF16)],
+        [scalars, hidden, after(ny, a_low, b_send_z), *all_outs],
+        pin=jax.ShapeDtypeStruct,
+        cost=4,
+        mib=FINAL,
+    )
+    b_low = (b_keep_z + after(b_got_z, a_low, mixed).astype(F32)).astype(BF16)
+    b_got_y = swap(b_low, "dp", 4)
+    a_all = both_of(a_low, 2, a_got_z)
+    a_other = swap(a_all, "dp", 1)
+    b_low = whole_dp((b_low.astype(F32) + after(b_got_y, a_all).astype(F32)).astype(BF16))
+    b_all = both_of(b_low, 2, swap(b_low, "dp", 2))
+
+    def unhalve(value, cuts, other=None):
         upper = (lax.axis_index("dp") & 1) != 0
-        other = swap(value, "dp", 1)
+        other = swap(value, "dp", 1) if other is None else other
         rows_out, begin = [], 0
         for count in cuts:
             mine, his = value[begin : begin + count], other[begin : begin + count]
@@ -1060,10 +1173,16 @@
             begin += count
         return rows_out
 
-    a_out, a_gate = unhalve(a_all, [depth // 2, depth // 2]) if plain else jnp.split(unhalve(a_all, [depth])[0], 2)
+    b_all = after(b_all, a_other)
+    a_cuts = [depth // 2, depth // 2] if plain else [depth]
+    a_out, a_gate = unhalve(a_all, a_cuts, a_other) if plain else jnp.split(unhalve(a_all, a_cuts, a_other)[0], 2)
     grad_out = a_out.T.astype(F32)
     grad_gate = a_gate.astype(F32)
-    *b_rows, gain_all = unhalve(b_all, ([256, 256] if plain else [512]) + [32])
+    cut = b_all.shape[0] - 32 - 256
+    *b_rows, gain_all = unhalve(b_all[cut:], [256, 32])
+    b_rows = unhalve(b_all[:cut], [cut]) + b_rows
+    if not plain:
+        *b_rows, gain_all = unhalve(b_all, [cut + 256, 32])
     b_all = jnp.concatenate(b_rows, axis=0)
     gain_all = (gain_all[:32].astype(F32) + gain_all[32:].astype(F32))[: depth // wide].reshape(1, depth)
     gain_all = jnp.pad(gain_all.reshape(-1, side), ((0, 16 - depth // side), (0, 0)))
@@ -1074,13 +1193,16 @@
         own = b_all[depth + 32 : depth + 32 + share_rows, :side]
     else:
         own = b_all[depth + 32 : depth + 240].reshape(-1)[: share_rows * side].reshape(share_rows, side)
-    stacked = own
-    for mask in order:
+    stacked, members = own, [0]
+    for mask in reversed(order):
+        members += [p | mask for p in members]
         gain_low = gain_all.astype(BF16)
-        got = swap(jnp.concatenate([stacked, gain_low], axis=0), "head", mask)
+        sent = jnp.concatenate([stacked, gain_low], axis=0)
+        got = swap(after(sent, grad_value) if mask == 1 else sent, "head", mask)
         stacked = jnp.concatenate([stacked, got[: stacked.shape[0]]], axis=0)
         gain_all = gain_low.astype(F32) + got[-16:].astype(F32)
     stacked = stacked.reshape(ways, share_rows, side)
+    stacked = jnp.stack([stacked[members.index(p)] for p in range(ways)])
     full = jnp.concatenate([pick(stacked, me ^ q) for q in range(ways)], axis=0).astype(F32)
     return (
         mixed,

time: 227 us -> 215 us (0.947)
  waiting for transfers between devices: 80.4 us -> 69.1 us
    ppermute x36 -> x35, waiting for transfers between devices: 80.4 us -> 69.1 us  [swap(): return lax.ppermute(value, axis, [(i, i ^ mask) for i in range(size)])]
    ppermute x36 -> x35, starting transfers between devices: 32.2 us -> 31.1 us  [swap(): return lax.ppermute(value, axis, [(i, i ^ mask) for i in range(size)])]
    unnamed x144 -> x138, local copies, waits for them, and re-layouts: 14.6 us -> 15.3 us
    pallas_call x14 -> x16, Pallas kernels: 79.1 us -> 79.7 us  [call(): pl.pallas_call(kernel, grid=grid, out_shape=[kinds[at](s, d) if at in kin...]
  transfers between devices with their start and end apart: 37 -> 36, of which waited for: 22 -> 17; matrix products, arithmetic and copies ran while one was open for 6% -> 5% of each run, Pallas kernels for 27% -> 29%
where the time goes in v3:
time: 215 us
  Pallas kernels  79.7 us (37%)
  waiting for transfers between devices  69.1 us (32%)
  starting transfers between devices  32.7 us (15%)
  local copies, waits for them, and re-layouts  20.8 us (10%)
  other arithmetic  10.2 us (5%)
    pallas_call x16, Pallas kernels, call(): pl.pallas_call(kernel, grid=grid, out_shape=[kinds[at](s, d) if at in kin...  79.7 us
    ppermute x35, waiting for transfers between devices, swap(): return lax.ppermute(value, axis, [(i, i ^ mask) for i in range(size)])  69.1 us
    ppermute x35, starting transfers between devices, swap(): return lax.ppermute(value, axis, [(i, i ^ mask) for i in range(size)])  31.1 us
    unnamed x138, local copies, waits for them, and re-layouts  15.3 us
  transfers between devices with their start and end apart: 36, of which 17 were waited for; matrix products, arithmetic and copies ran while one was open for 5% of the time, Pallas kernels for 29%

profile of v3, /device:TPU:0, one launch (start us, length us, event | category | flops | bytes accessed | tf_op | source)
XLA Modules:
  0.0 214.6 jit_solution(16217890676170648791)
XLA Ops:
  0.8 2.0 constant_dynamic-update-slice_fusion.1
  4.7 3.0 %collective-permute-start = (f32[32,896]{1,0:T(8,128)S(1)}, f32[32,896]{1,0:T(8,128)S(1)}, u32[]{:S(2)}, u32[]{:S(2)}) collective-permute-start(f32[32,896]{1,0:T(8,128)S(1)} %fusion.26), channel_id=1, source_target_pairs={{0,2},{1,3},{2,0},{3,1},{4,6},{5,7},{6,4},{7,5},{8,10},{9,11},{10,... | collective-permute-start | bytes 344072 | tf_op jit(solution)/shard_map/ppermute | solution.py:789
  7.7 1.9 collective-permute-start.3
  9.6 1.6 collective-permute-done
  11.4 1.1 collective-permute-done.1
  12.6 2.0 shard_map.288
  16.2 1.9 shard_map.289
  18.2 7.4 %shard_map.290 = (bf16[512,1536]{1,0:T(8,128)(2,1)}, bf16[528,1536]{1,0:T(8,128)(2,1)}, bf16[512,1536]{1,0:T(8,128)(2,1)}, f32[2,128,1536]{2,1,0:T(8,128)}, bf16...) custom-call(s32[8]{0:T(128)S(1)} %pad_add_fusion.s_ref, ...), custom_call_target="tpu_custom_call" | custom-call | flops 2400000000 | bytes 1800000 | tf_op jit(solution)/shard_map/pallas_call | solution.py:44
  25.6 10.7 %collective-permute-done.3.refs_0_.refs_2_ = bf16[768,768]{1,0:T(8,128)(2,1)S(1)} collective-permute-done((bf16[768,768]{1,0:T(8,128)(2,1)}, bf16[768,768]{1,0:T(8,128)(2,1)S(1)}, u32[]{:S(2)}, u32[]{:S(2)}) %collective-permute-start.3) | collective-permute-done | bytes 1179680 | tf_op jit(solution)/shard_map/ppermute | solution.py:789
  36.4 1.8 collective-permute-start.8
  39.2 6.2 %shard_map.291 = (bf16[512,1536]{1,0:T(8,128)(2,1)}, bf16[528,1536]{1,0:T(8,128)(2,1)}, bf16[512,1536]{1,0:T(8,128)(2,1)}, f32[2,128,1536]{2,1,0:T(8,128)}, bf16...) custom-call(s32[8]{0:T(128)S(1)} %pad_add_fusion.s_ref, ...), custom_call_target="tpu_custom_call", output_to_operand_aliasing={{0}: (8, {}), {1}: (9, {}), {2}: (10, {}), {3}: (11, {}), {... | custom-call | flops 2400000000 | bytes 1800000 | tf_op jit(solution)/shard_map/pallas_call | solution.py:44
  45.7 1.7 collective-permute-done.6.got_ref.near_ref
  48.1 4.0 %collective-permute-done.8.refs_2_ = bf16[384,768]{1,0:T(8,128)(2,1)S(1)} collective-permute-done((bf16[384,768]{1,0:T(8,128)(2,1)S(1)}, bf16[384,768]{1,0:T(8,128)(2,1)S(1)}, u32[]{:S(2)}, u32[]{:S(2)}) %collective-permute-start.8) | collective-permute-done | bytes 589856 | tf_op jit(solution)/shard_map/ppermute | solution.py:789
  52.6 1.7 collective-permute-start.10
  54.4 4.0 %shard_map.295.y_ref = f32[512,1536]{1,0:T(8,128)S(1)} custom-call(s32[8]{0:T(128)S(1)} %pad_add_fusion.s_ref, f32[12,8,512]{2,1,0:T(8,128)S(1)} %get-tuple-element.133.rowp_ref, f32[6,512,16]{2,1,0:T(8,128)S(1)} %get-tuple-element.113.colp_ref, f32[2,256,256]{2,1,0:T(8,128)S(1)} %get-tuple-element.134.cb_ref, bf16[512,1536]{1,0:T(8,128)(2,1)S(1)} %get-tuple-element.136.x_ref), custom_call_target="tpu_custom_call" | custom-call | flops 2000000000 | bytes 1500000 | tf_op jit(solution)/shard_map/pallas_call | solution.py:44
  58.4 6.3 %collective-permute-done.10.far_ref = bf16[144,1536]{1,0:T(8,128)(2,1)S(1)} collective-permute-done((bf16[144,1536]{1,0:T(8,128)(2,1)S(1)}, bf16[144,1536]{1,0:T(8,128)(2,1)S(1)}, u32[]{:S(2)}, u32[]{:S(2)}) %collective-permute-start.10) | collective-permute-done | bytes 442400 | tf_op jit(solution)/shard_map/ppermute | solution.py:789
  65.5 2.4 %shard_map.293 = (bf16[512,1536]{1,0:T(8,128)(2,1)S(1)}, bf16[768,512]{1,0:T(8,128)(2,1)S(1)}) custom-call(s32[8]{0:T(128)S(1)} %pad_add_fusion.s_ref, bf16[512,768]{1,0:T(8,128)(2,1)S(1)} %copy-done.16, bf16[384,768]{1,0:T(8,128)(2,1)S(1)} %copy-done.17, bf16[384,768]{1,0:T(8,128)(2,1)S(1)} %collective-permute-done.7.refs_1_, ...), custom_call_target="tpu_custom_call" | custom-call | flops 1200000000 | bytes 900000 | tf_op jit(solution)/shard_map/pallas_call | solution.py:44
  67.9 14.7 %shard_map.296 = (bf16[512,1536]{1,0:T(8,128)(2,1)}, bf16[512,1536]{1,0:T(8,128)(2,1)}, bf16[2,1536,384]{2,1,0:T(8,128)(2,1)}, bf16[2,1536,384]{2,1,0:T(8,128)(2...) custom-call(s32[8]{0:T(128)S(1)} %pad_add_fusion.s_ref, ...), custom_call_target="tpu_custom_call" | custom-call | flops 5600000000 | bytes 4200000 | tf_op jit(solution)/shard_map/pallas_call | solution.py:44
  82.6 1.1 copy-done.25
  83.8 1.8 collective-permute-done.11.got_ref.near_ref
  86.5 1.7 collective-permute-start.17
  88.4 1.4 copy-done.5
  89.8 1.4 copy-done.26
  94.0 7.4 %shard_map.299 = (bf16[512,1536]{1,0:T(8,128)(2,1)S(1)}, f32[32,512]{1,0:T(8,128)S(1)}, f32[512,128]{1,0:T(8,128)S(1)}, f32[512,128]{1,0:T(8,128)S(1)}) custom-call(s32[8]{0:T(128)S(1)} %pad_add_fusion.s_ref, f32[12,8,512]{2,1,0:T(8,128)S(1)} %copy-done.23, f32[6,512,16]{2,1,0:T(8,128)S(1)} %get-tuple-element.113.colp_ref, f32[2,256,256]{2,1,0:T(8,128)S(1)} %copy-done.37, ...), custom_call_target="tpu_custom_call" | custom-call | flops 3200000000 | bytes 2400000 | tf_op jit(solution)/shard_map/pallas_call | solution.py:44
  102.2 2.2 %convert_add_fusion = (f32[1,1536,384]{2,1,0:T(8,128)S(1)}, f32[1,1536,384]{2,1,0:T(8,128)S(1)}) fusion(bf16[2,1536,384]{2,1,0:T(8,128)(2,1)} %collective-permute-done.12, bf16[2,1536,384]{2,1,0:T(8,128)(2,1)S(1)} %copy-done.53), kind=kLoop, calls=%fused_computation.4 | loop fusion | flops 3538944 | bytes 9437184 | tf_op jit(solution)/shard_map/add | solution.py:1024
  104.8 1.6 collective-permute-start.15
  107.9 13.5 %shard_map.300 = (bf16[528,1536]{1,0:T(8,128)(2,1)S(1)}, f32[8,1536]{1,0:T(8,128)S(1)}, f32[32,512]{1,0:T(8,128)S(1)}, f32[8,1536]{1,0:T(8,128)S(1)}, f32[512,12...) custom-call(s32[8]{0:T(128)S(1)} %pad_add_fusion.s_ref, ...), custom_call_target="tpu_custom_call" | custom-call | flops 4000000000 | bytes 3000000 | tf_op jit(solution)/shard_map/pallas_call | solution.py:44
  124.0 1.6 collective-permute-start.14
  125.6 2.7 %shard_map.301 = (bf16[528,256]{1,0:T(8,128)(2,1)S(1)}, bf16[32,512]{1,0:T(8,128)(2,1)S(1)}, bf16[2,256,384]{2,1,0:T(8,128)(2,1)S(1)}, bf16[2,256,384]{2,1,0:T(8,128)(2,1)S(1)}) custom-call(s32[8]{0:T(128)S(1)} %pad_add_fusion.s_ref, f32[512,128]{1,0:T(8,128)S(1)} %get-tuple-element.158.dbx_ref, f32[512,128]{1,0:T(8,128)S(1)} %get-tuple-element.159.dbin_ref, ...), custom_call_target="tpu_custom_call" | custom-call | flops 1600000000 | bytes 1200000 | tf_op jit(solution)/shard_map/pallas_call | solution.py:44
  128.6 3.2 %collective-permute-done.16 = bf16[384,384]{1,0:T(8,128)(2,1)S(1)} collective-permute-done((bf16[384,384]{1,0:T(8,128)(2,1)S(1)}, bf16[384,384]{1,0:T(8,128)(2,1)S(1)}, u32[]{:S(2)}, u32[]{:S(2)}) %collective-permute-start.16) | collective-permute-done | bytes 294944 | tf_op jit(solution)/shard_map/ppermute | solution.py:789
  131.8 1.6 collective-permute-done.14
  135.5 1.6 collective-permute-start.23
  138.1 1.6 collective-permute-start.20
  139.7 9.7 %shard_map.302 = (f32[512,768]{1,0:T(8,128)}, f32[16,768]{1,0:T(8,128)S(1)}, f32[8,384]{1,0:T(8,128)S(1)}) custom-call(s32[8]{0:T(128)} %copy-done.13, bf16[512,768]{1,0:T(8,128)(2,1)} %hid_ref.5, bf16[16,768]{1,0:T(8,128)(2,1)} %copy-done.12, bf16[512,768]{1,0:T(8,128)(2,1)} %cot_ref.3, f32[1,768]{1,0:T(1,128)} %copy-done.14, ...), custom_call_target="tpu_custom_call" | custom-call | flops 3600000000 | bytes 2700000 | tf_op jit(solution)/shard_map/pallas_call | solution.py:44
  149.5 2.6 %collective-permute-start.21 = (bf16[384,384]{1,0:T(8,128)(2,1)S(1)}, bf16[384,384]{1,0:T(8,128)(2,1)S(1)}, u32[]{:S(2)}, u32[]{:S(2)}) collective-permute-start(bf16[384,384]{1,0:T(8,128)(2,1)S(1)} %fusion.15), channel_id=1, source_target_pairs={{0,16},{4,20},{8,24},{12,28},{16,0},{20,4},{24,8},{28,12},{1,17},{... | collective-permute-start | bytes 884744 | tf_op jit(solution)/shard_map/ppermute | solution.py:789
  154.0 10.4 %collective-permute-done.21 = bf16[384,384]{1,0:T(8,128)(2,1)S(1)} collective-permute-done((bf16[384,384]{1,0:T(8,128)(2,1)S(1)}, bf16[384,384]{1,0:T(8,128)(2,1)S(1)}, u32[]{:S(2)}, u32[]{:S(2)}) %collective-permute-start.21) | collective-permute-done | bytes 294944 | tf_op jit(solution)/shard_map/ppermute | solution.py:789
  165.0 1.6 collective-permute-start.26
  166.5 2.0 collective-permute-start.29
  168.6 5.0 %shard_map.303 = bf16[512,768]{1,0:T(8,128)(2,1)} custom-call(s32[8]{0:T(128)} %copy-done.13, bf16[512,768]{1,0:T(8,128)(2,1)} %hid_ref.5, bf16[512,1536]{1,0:T(8,128)(2,1)} %get-tuple-element.188.ny_ref, bf16[384,768]{1,0:T(8,128)(2,1)} %refs_0_.3, bf16[384,768]{1,0:T(8,128)(2,1)} %copy-done.20, bf16[384,768]{1,0:T(8,128)(2,1)} %copy-done.18, ...), custom_call_target="tpu_custom_call" | custom-call | flops 1600000000 | bytes 1200000 | tf_op jit(solution)/shard_map/pallas_call | solution.py:44
  173.6 1.2 collective-permute-start.28
  174.8 4.6 %collective-permute-done.29 = bf16[384,384]{1,0:T(8,128)(2,1)S(1)} collective-permute-done((bf16[384,384]{1,0:T(8,128)(2,1)S(1)}, bf16[384,384]{1,0:T(8,128)(2,1)S(1)}, u32[]{:S(2)}, u32[]{:S(2)}) %collective-permute-start.29) | collective-permute-done | bytes 294944 | tf_op jit(solution)/shard_map/ppermute | solution.py:789
  180.2 6.8 %collective-permute-done.28 = bf16[272,384]{1,0:T(8,128)(2,1)S(1)} collective-permute-done((bf16[272,384]{1,0:T(8,128)(2,1)S(1)}, bf16[272,384]{1,0:T(8,128)(2,1)S(1)}, u32[]{:S(2)}, u32[]{:S(2)}) %collective-permute-start.28) | collective-permute-done | bytes 208928 | tf_op jit(solution)/shard_map/ppermute | solution.py:789
  187.1 1.4 add_dynamic-update-slice_fusion
  188.5 5.6 %collective-permute-done.30 = bf16[272,384]{1,0:T(8,128)(2,1)S(1)} collective-permute-done((bf16[272,384]{1,0:T(8,128)(2,1)S(1)}, bf16[272,384]{1,0:T(8,128)(2,1)S(1)}, u32[]{:S(2)}, u32[]{:S(2)}) %collective-permute-start.30) | collective-permute-done | bytes 208928 | tf_op jit(solution)/shard_map/ppermute | solution.py:789
  194.9 1.5 collective-permute-start.34
  196.6 1.4 copy.53
  199.1 6.0 %collective-permute-done.34 = bf16[256,384]{1,0:T(8,128)(2,1)S(1)} collective-permute-done((bf16[256,384]{1,0:T(8,128)(2,1)S(1)}, bf16[256,384]{1,0:T(8,128)(2,1)S(1)}, u32[]{:S(2)}, u32[]{:S(2)}) %collective-permute-start.34) | collective-permute-done | bytes 196640 | tf_op jit(solution)/shard_map/ppermute | solution.py:789
  207.7 2.5 %collective-permute-done.33 = bf16[224,256]{1,0:T(8,128)(2,1)S(1)} collective-permute-done((bf16[224,256]{1,0:T(8,128)(2,1)S(1)}, bf16[224,256]{1,0:T(8,128)(2,1)S(1)}, u32[]{:S(2)}, u32[]{:S(2)}) %collective-permute-start.33) | collective-permute-done | bytes 114720 | tf_op jit(solution)/shard_map/ppermute | solution.py:789
  (278 shorter events, 31.5 us)
Async XLA Ops:
  0.7 10.5 %copy-start.66 = (s32[1,3]{1,0:T(1,128)S(1)}, s32[1,3]{1,0:T(1,128)}, u32[]{:S(2)}) copy-start(s32[1,3]{1,0:T(1,128)} %param.20) | copy-start | bytes 40
  0.8 10.6 %copy-start.58 = (f32[768]{0:T(1024)S(1)}, f32[768]{0:T(1024)}, u32[]{:S(2)}) copy-start(f32[768]{0:T(1024)} %param.21) | copy-start | bytes 9220
  3.7 14.5 %collective-permute-start.4 = (bf16[768,768]{1,0:T(8,128)(2,1)}, bf16[768,768]{1,0:T(8,128)(2,1)}, u32[]{:S(2)}, u32[]{:S(2)}) collective-permute-start(bf16[768,768]{1,0:T(8,128)(2,1)} %constant_dynamic-update-slice_fusion.refs_0_), channel_id=1, source_target_pairs={{0,1},{1,0},{2,3},{3,2},{4,5},{5,4},{6,7},{7,6},{8,9},{9,8},{10,11... | collective-permute-start | bytes 3538952 | tf_op jit(solution)/shard_map/ppermute | solution.py:789
  4.5 10.1 %copy-start.55 = (f32[8,896]{1,0:T(8,128)}, f32[8,896]{1,0:T(8,128)S(1)}, u32[]{:S(2)}) copy-start(f32[8,896]{1,0:T(8,128)S(1)} %select_maximum_fusion.4) | copy-start | bytes 86020
  4.6 3.1 %collective-permute-start.2 = (f32[32,896]{1,0:T(8,128)S(1)}, f32[32,896]{1,0:T(8,128)S(1)}, u32[]{:S(2)}, u32[]{:S(2)}) collective-permute-start(f32[32,896]{1,0:T(8,128)S(1)} %fusion.26), channel_id=1, source_target_pairs={{0,1},{1,0},{2,3},{3,2},{4,5},{5,4},{6,7},{7,6},{8,9},{9,8},{10,11... | collective-permute-start | bytes 344072 | tf_op jit(solution)/shard_map/ppermute | solution.py:789
  4.7 6.5 %collective-permute-start = (f32[32,896]{1,0:T(8,128)S(1)}, f32[32,896]{1,0:T(8,128)S(1)}, u32[]{:S(2)}, u32[]{:S(2)}) collective-permute-start(f32[32,896]{1,0:T(8,128)S(1)} %fusion.26), channel_id=1, source_target_pairs={{0,2},{1,3},{2,0},{3,1},{4,6},{5,7},{6,4},{7,5},{8,10},{9,11},{10,... | collective-permute-start | bytes 344072 | tf_op jit(solution)/shard_map/ppermute | solution.py:789
  7.7 28.7 %collective-permute-start.3 = (bf16[768,768]{1,0:T(8,128)(2,1)}, bf16[768,768]{1,0:T(8,128)(2,1)S(1)}, u32[]{:S(2)}, u32[]{:S(2)}) collective-permute-start(bf16[768,768]{1,0:T(8,128)(2,1)} %constant_dynamic-update-slice_fusion.refs_0_), channel_id=1, source_target_pairs={{0,2},{1,3},{2,0},{3,1},{4,6},{5,7},{6,4},{7,5},{8,10},{9,11},{10,... | collective-permute-start | bytes 3538952 | tf_op jit(solution)/shard_map/ppermute | solution.py:789
  11.3 1.3 collective-permute-start.1
  11.3 114.2 %copy-start.13 = (s32[8]{0:T(128)}, s32[8]{0:T(128)S(1)}, u32[]{:S(2)}) copy-start(s32[8]{0:T(128)S(1)} %pad_add_fusion.s_ref) | copy-start | bytes 100
  16.1 23.1 %copy-start.9 = (bf16[528,768]{1,0:T(8,128)(2,1)}, bf16[528,768]{1,0:T(8,128)(2,1)S(1)}, u32[]{:S(2)}) copy-start(bf16[528,768]{1,0:T(8,128)(2,1)S(1)} %get-tuple-element.111.nx_ref) | copy-start | bytes 2433028
  16.1 51.7 %copy-start.28 = (bf16[768,512]{1,0:T(8,128)(2,1)}, bf16[768,512]{1,0:T(8,128)(2,1)S(1)}, u32[]{:S(2)}) copy-start(bf16[768,512]{1,0:T(8,128)(2,1)S(1)} %get-tuple-element.132.nt_ref) | copy-start | bytes 2359300
  16.1 51.7 %copy-start.43 = (bf16[512,128]{1,0:T(8,128)(2,1)}, bf16[512,128]{1,0:T(8,128)(2,1)S(1)}, u32[]{:S(2)}) copy-start(bf16[512,128]{1,0:T(8,128)(2,1)S(1)} %get-tuple-element.130.c_ref) | copy-start | bytes 393220
  16.2 109.4 %copy-start.11 = (f32[32,896]{1,0:T(8,128)}, f32[32,896]{1,0:T(8,128)S(1)}, u32[]{:S(2)}) copy-start(f32[32,896]{1,0:T(8,128)S(1)} %select_maximum_fusion.hp_ref) | copy-start | bytes 344068
  18.1 36.2 %copy-start.22 = (f32[12,8,512]{2,1,0:T(8,128)}, f32[12,8,512]{2,1,0:T(8,128)S(1)}, u32[]{:S(2)}) copy-start(f32[12,8,512]{2,1,0:T(8,128)S(1)} %get-tuple-element.133.rowp_ref) | copy-start | bytes 589828
  18.2 18.2 %copy-start.17 = (bf16[384,768]{1,0:T(8,128)(2,1)S(1)}, bf16[384,768]{1,0:T(8,128)(2,1)}, u32[]{:S(2)}) copy-start(bf16[384,768]{1,0:T(8,128)(2,1)} %refs_0_.3) | copy-start | bytes 1769476
  36.4 2.8 %collective-permute-start.5 = (bf16[768,768]{1,0:T(8,128)(2,1)S(1)}, bf16[768,768]{1,0:T(8,128)(2,1)S(1)}, u32[]{:S(2)}, u32[]{:S(2)}) collective-permute-start(bf16[768,768]{1,0:T(8,128)(2,1)S(1)} %collective-permute-done.3.refs_0_.refs_2_), channel_id=1, source_target_pairs={{0,1},{1,0},{2,3},{3,2},{4,5},{5,4},{6,7},{7,6},{8,9},{9,8},{10,11... | collective-permute-start | bytes 3538952 | tf_op jit(solution)/shard_map/ppermute | solution.py:789
  36.4 15.7 %collective-permute-start.8 = (bf16[384,768]{1,0:T(8,128)(2,1)S(1)}, bf16[384,768]{1,0:T(8,128)(2,1)S(1)}, u32[]{:S(2)}, u32[]{:S(2)}) collective-permute-start(bf16[384,768]{1,0:T(8,128)(2,1)S(1)} %copy-done.17), channel_id=1, source_target_pairs={{0,2},{1,3},{2,0},{3,1},{4,6},{5,7},{6,4},{7,5},{8,10},{9,11},{10,... | collective-permute-start | bytes 1769480 | tf_op jit(solution)/shard_map/ppermute | solution.py:789
  45.5 22.4 %copy-start.4 = (bf16[512,1536]{1,0:T(8,128)(2,1)}, bf16[512,1536]{1,0:T(8,128)(2,1)S(1)}, u32[]{:S(2)}) copy-start(bf16[512,1536]{1,0:T(8,128)(2,1)S(1)} %get-tuple-element.136.x_ref) | copy-start | bytes 4718596
  45.5 1.9 collective-permute-start.6
  52.1 13.3 %copy-start.18 = (bf16[384,768]{1,0:T(8,128)(2,1)}, bf16[384,768]{1,0:T(8,128)(2,1)S(1)}, u32[]{:S(2)}) copy-start(bf16[384,768]{1,0:T(8,128)(2,1)S(1)} %collective-permute-done.8.refs_2_) | copy-start | bytes 1769476
  52.1 13.3 %collective-permute-start.9 = (bf16[384,768]{1,0:T(8,128)(2,1)S(1)}, bf16[384,768]{1,0:T(8,128)(2,1)S(1)}, u32[]{:S(2)}, u32[]{:S(2)}) collective-permute-start(bf16[384,768]{1,0:T(8,128)(2,1)S(1)} %collective-permute-done.8.refs_2_), channel_id=1, source_target_pairs={{0,1},{1,0},{2,3},{3,2},{4,5},{5,4},{6,7},{7,6},{8,9},{9,8},{10,11... | collective-permute-start | bytes 1769480 | tf_op jit(solution)/shard_map/ppermute | solution.py:789
  52.1 13.3 %collective-permute-start.7 = (bf16[384,768]{1,0:T(8,128)(2,1)S(1)}, bf16[384,768]{1,0:T(8,128)(2,1)S(1)}, u32[]{:S(2)}, u32[]{:S(2)}) collective-permute-start(bf16[384,768]{1,0:T(8,128)(2,1)S(1)} %copy-done.17), channel_id=1, source_target_pairs={{0,1},{1,0},{2,3},{3,2},{4,5},{5,4},{6,7},{7,6},{8,9},{9,8},{10,11... | collective-permute-start | bytes 1769480 | tf_op jit(solution)/shard_map/ppermute | solution.py:789
  52.6 12.1 %collective-permute-start.10 = (bf16[144,1536]{1,0:T(8,128)(2,1)S(1)}, bf16[144,1536]{1,0:T(8,128)(2,1)S(1)}, u32[]{:S(2)}, u32[]{:S(2)}) collective-permute-start(bf16[144,1536]{1,0:T(8,128)(2,1)S(1)} %shard_map.292), channel_id=1, source_target_pairs={{0,2},{1,3},{2,0},{3,1},{4,6},{5,7},{6,4},{7,5},{8,10},{9,11},{10,... | collective-permute-start | bytes 1327112 | tf_op jit(solution)/shard_map/ppermute | solution.py:789
  83.8 1.8 collective-permute-start.11
  86.3 15.9 %collective-permute-start.12 = (bf16[2,1536,384]{2,1,0:T(8,128)(2,1)}, bf16[2,1536,384]{2,1,0:T(8,128)(2,1)}, u32[]{:S(2)}, u32[]{:S(2)}) collective-permute-start(bf16[2,1536,384]{2,1,0:T(8,128)(2,1)} %get-tuple-element.145), channel_id=1, source_target_pairs={{0,1},{1,0},{2,3},{3,2},{4,5},{5,4},{6,7},{7,6},{8,9},{9,8},{10,11... | collective-permute-start | bytes 7077896 | tf_op jit(solution)/shard_map/ppermute | solution.py:789
  86.5 15.0 %collective-permute-start.17 = (bf16[144,1536]{1,0:T(8,128)(2,1)S(1)}, bf16[144,1536]{1,0:T(8,128)(2,1)S(1)}, u32[]{:S(2)}, u32[]{:S(2)}) collective-permute-start(bf16[144,1536]{1,0:T(8,128)(2,1)S(1)} %shard_map.297), channel_id=1, source_target_pairs={{0,2},{1,3},{2,0},{3,1},{4,6},{5,7},{6,4},{7,5},{8,10},{9,11},{10,... | collective-permute-start | bytes 1327112 | tf_op jit(solution)/shard_map/ppermute | solution.py:789
  104.8 16.7 %collective-permute-start.15 = (bf16[2,384,384]{2,1,0:T(8,128)(2,1)S(1)}, bf16[2,384,384]{2,1,0:T(8,128)(2,1)S(1)}, u32[]{:S(2)}, u32[]{:S(2)}) collective-permute-start(bf16[2,384,384]{2,1,0:T(8,128)(2,1)S(1)} %fusion.13), channel_id=1, source_target_pairs={{0,4},{4,0},{8,12},{12,8},{16,20},{20,16},{24,28},{28,24},{1,5},{5... | collective-permute-start | bytes 1769480 | tf_op jit(solution)/shard_map/ppermute | solution.py:789
  106.4 17.0 %collective-permute-start.13 = (bf16[768,384]{1,0:T(8,128)(2,1)S(1)}, bf16[768,384]{1,0:T(8,128)(2,1)S(1)}, u32[]{:S(2)}, u32[]{:S(2)}) collective-permute-start(bf16[768,384]{1,0:T(8,128)(2,1)S(1)} %fusion.12), channel_id=1, source_target_pairs={{0,2},{1,3},{2,0},{3,1},{4,6},{5,7},{6,4},{7,5},{8,10},{9,11},{10,... | collective-permute-start | bytes 1769480 | tf_op jit(solution)/shard_map/ppermute | solution.py:789
  122.7 9.1 %collective-permute-start.16 = (bf16[384,384]{1,0:T(8,128)(2,1)S(1)}, bf16[384,384]{1,0:T(8,128)(2,1)S(1)}, u32[]{:S(2)}, u32[]{:S(2)}) collective-permute-start(bf16[384,384]{1,0:T(8,128)(2,1)S(1)} %fusion.22), channel_id=1, source_target_pairs={{0,2},{1,3},{2,0},{3,1},{4,6},{5,7},{6,4},{7,5},{8,10},{9,11},{10,... | collective-permute-start | bytes 884744 | tf_op jit(solution)/shard_map/ppermute | solution.py:789
  123.9 9.9 %collective-permute-start.18 = (bf16[2,768,384]{2,1,0:T(8,128)(2,1)S(1)}, bf16[2,768,384]{2,1,0:T(8,128)(2,1)S(1)}, u32[]{:S(2)}, u32[]{:S(2)}) collective-permute-start(bf16[2,768,384]{2,1,0:T(8,128)(2,1)S(1)} %copy-done.67), channel_id=1, source_target_pairs={{0,1},{1,0},{2,3},{3,2},{4,5},{5,4},{6,7},{7,6},{8,9},{9,8},{10,11... | collective-permute-start | bytes 3538952 | tf_op jit(solution)/shard_map/ppermute | solution.py:789
  124.0 9.4 %collective-permute-start.14 = (bf16[384,384]{1,0:T(8,128)(2,1)S(1)}, bf16[384,384]{1,0:T(8,128)(2,1)S(1)}, u32[]{:S(2)}, u32[]{:S(2)}) collective-permute-start(bf16[384,384]{1,0:T(8,128)(2,1)S(1)} %fusion.20), channel_id=1, source_target_pairs={{0,4},{4,0},{8,12},{12,8},{16,20},{20,16},{24,28},{28,24},{1,5},{5... | collective-permute-start | bytes 884744 | tf_op jit(solution)/shard_map/ppermute | solution.py:789
  128.3 5.3 %collective-permute-start.19 = (bf16[2,256,384]{2,1,0:T(8,128)(2,1)S(1)}, bf16[2,256,384]{2,1,0:T(8,128)(2,1)S(1)}, u32[]{:S(2)}, u32[]{:S(2)}) collective-permute-start(bf16[2,256,384]{2,1,0:T(8,128)(2,1)S(1)} %get-tuple-element.174), channel_id=1, source_target_pairs={{0,1},{1,0},{2,3},{3,2},{4,5},{5,4},{6,7},{7,6},{8,9},{9,8},{10,11... | collective-permute-start | bytes 1179656 | tf_op jit(solution)/shard_map/ppermute | solution.py:789
  135.5 16.7 %collective-permute-start.23 = (bf16[2,256,384]{2,1,0:T(8,128)(2,1)S(1)}, bf16[2,256,384]{2,1,0:T(8,128)(2,1)S(1)}, u32[]{:S(2)}, u32[]{:S(2)}) collective-permute-start(bf16[2,256,384]{2,1,0:T(8,128)(2,1)S(1)} %fusion.18), channel_id=1, source_target_pairs={{0,4},{4,0},{8,12},{12,8},{16,20},{20,16},{24,28},{28,24},{1,5},{5... | collective-permute-start | bytes 1179656 | tf_op jit(solution)/shard_map/ppermute | solution.py:789
  137.1 15.2 %collective-permute-start.22 = (bf16[512,384]{1,0:T(8,128)(2,1)S(1)}, bf16[512,384]{1,0:T(8,128)(2,1)S(1)}, u32[]{:S(2)}, u32[]{:S(2)}) collective-permute-start(bf16[512,384]{1,0:T(8,128)(2,1)S(1)} %fusion.17), channel_id=1, source_target_pairs={{0,2},{1,3},{2,0},{3,1},{4,6},{5,7},{6,4},{7,5},{8,10},{9,11},{10,... | collective-permute-start | bytes 1179656 | tf_op jit(solution)/shard_map/ppermute | solution.py:789
  138.1 11.3 %collective-permute-start.20 = (bf16[384,384]{1,0:T(8,128)(2,1)S(1)}, bf16[384,384]{1,0:T(8,128)(2,1)S(1)}, u32[]{:S(2)}, u32[]{:S(2)}) collective-permute-start(bf16[384,384]{1,0:T(8,128)(2,1)S(1)} %fusion.21), channel_id=1, source_target_pairs={{0,8},{4,12},{8,0},{12,4},{16,24},{20,28},{24,16},{28,20},{1,9},{5... | collective-permute-start | bytes 884744 | tf_op jit(solution)/shard_map/ppermute | solution.py:789
  149.5 14.9 %collective-permute-start.21 = (bf16[384,384]{1,0:T(8,128)(2,1)S(1)}, bf16[384,384]{1,0:T(8,128)(2,1)S(1)}, u32[]{:S(2)}, u32[]{:S(2)}) collective-permute-start(bf16[384,384]{1,0:T(8,128)(2,1)S(1)} %fusion.15), channel_id=1, source_target_pairs={{0,16},{4,20},{8,24},{12,28},{16,0},{20,4},{24,8},{28,12},{1,17},{... | collective-permute-start | bytes 884744 | tf_op jit(solution)/shard_map/ppermute | solution.py:789
  152.4 12.2 %collective-permute-start.24 = (bf16[256,384]{1,0:T(8,128)(2,1)S(1)}, bf16[256,384]{1,0:T(8,128)(2,1)S(1)}, u32[]{:S(2)}, u32[]{:S(2)}) collective-permute-start(bf16[256,384]{1,0:T(8,128)(2,1)S(1)} %fusion.24), channel_id=1, source_target_pairs={{0,4},{4,0},{8,12},{12,8},{16,20},{20,16},{24,28},{28,24},{1,5},{5... | collective-permute-start | bytes 589832 | tf_op jit(solution)/shard_map/ppermute | solution.py:789
  153.0 11.6 %collective-permute-start.25 = (bf16[256,384]{1,0:T(8,128)(2,1)S(1)}, bf16[256,384]{1,0:T(8,128)(2,1)S(1)}, u32[]{:S(2)}, u32[]{:S(2)}) collective-permute-start(bf16[256,384]{1,0:T(8,128)(2,1)S(1)} %fusion.25), channel_id=1, source_target_pairs={{0,2},{1,3},{2,0},{3,1},{4,6},{5,7},{6,4},{7,5},{8,10},{9,11},{10,... | collective-permute-start | bytes 589832 | tf_op jit(solution)/shard_map/ppermute | solution.py:789
  164.9 8.7 %collective-permute-start.27 = (bf16[272,384]{1,0:T(8,128)(2,1)S(1)}, bf16[272,384]{1,0:T(8,128)(2,1)S(1)}, u32[]{:S(2)}, u32[]{:S(2)}) collective-permute-start(bf16[272,384]{1,0:T(8,128)(2,1)S(1)} %fusion.23), channel_id=1, source_target_pairs={{0,8},{4,12},{8,0},{12,4},{16,24},{20,28},{24,16},{28,20},{1,9},{5... | collective-permute-start | bytes 626696 | tf_op jit(solution)/shard_map/ppermute | solution.py:789
  165.0 22.1 %collective-permute-start.26 = (f32[16,768]{1,0:T(8,128)S(1)}, f32[16,768]{1,0:T(8,128)S(1)}, u32[]{:S(2)}, u32[]{:S(2)}) collective-permute-start(f32[16,768]{1,0:T(8,128)S(1)} %get-tuple-element.182), channel_id=1, source_target_pairs={{1,0},{2,1},{3,2},{5,4},{6,5},{7,6},{9,8},{10,9},{11,10},{13,12},{... | collective-permute-start | bytes 147464 | tf_op jit(solution)/shard_map/ppermute | solution.py:1132
  166.5 12.9 %collective-permute-start.29 = (bf16[384,384]{1,0:T(8,128)(2,1)S(1)}, bf16[384,384]{1,0:T(8,128)(2,1)S(1)}, u32[]{:S(2)}, u32[]{:S(2)}) collective-permute-start(bf16[384,384]{1,0:T(8,128)(2,1)S(1)} %add_convert_fusion), channel_id=1, source_target_pairs={{0,8},{4,12},{8,0},{12,4},{16,24},{20,28},{24,16},{28,20},{1,9},{5... | collective-permute-start | bytes 884744 | tf_op jit(solution)/shard_map/ppermute | solution.py:789
  173.6 13.4 %collective-permute-start.28 = (bf16[272,384]{1,0:T(8,128)(2,1)S(1)}, bf16[272,384]{1,0:T(8,128)(2,1)S(1)}, u32[]{:S(2)}, u32[]{:S(2)}) collective-permute-start(bf16[272,384]{1,0:T(8,128)(2,1)S(1)} %fusion.16), channel_id=1, source_target_pairs={{0,16},{4,20},{8,24},{12,28},{16,0},{20,4},{24,8},{28,12},{1,17},{... | collective-permute-start | bytes 626696 | tf_op jit(solution)/shard_map/ppermute | solution.py:789
  179.6 14.7 %collective-permute-start.31 = (bf16[768,384]{1,0:T(8,128)(2,1)S(1)}, bf16[768,384]{1,0:T(8,128)(2,1)S(1)}, u32[]{:S(2)}, u32[]{:S(2)}) collective-permute-start(bf16[768,384]{1,0:T(8,128)(2,1)S(1)} %pad_maximum_fusion.3), channel_id=1, source_target_pairs={{0,4},{4,0},{8,12},{12,8},{16,20},{20,16},{24,28},{28,24},{1,5},{5... | collective-permute-start | bytes 1769480 | tf_op jit(solution)/shard_map/ppermute | solution.py:789
  187.0 7.1 %collective-permute-start.30 = (bf16[272,384]{1,0:T(8,128)(2,1)S(1)}, bf16[272,384]{1,0:T(8,128)(2,1)S(1)}, u32[]{:S(2)}, u32[]{:S(2)}) collective-permute-start(bf16[272,384]{1,0:T(8,128)(2,1)S(1)} %add_convert_fusion.1), channel_id=1, source_target_pairs={{0,8},{4,12},{8,0},{12,4},{16,24},{20,28},{24,16},{28,20},{1,9},{5... | collective-permute-start | bytes 626696 | tf_op jit(solution)/shard_map/ppermute | solution.py:789
  194.3 10.8 %collective-permute-start.32 = (bf16[288,384]{1,0:T(8,128)(2,1)S(1)}, bf16[288,384]{1,0:T(8,128)(2,1)S(1)}, u32[]{:S(2)}, u32[]{:S(2)}) collective-permute-start(bf16[288,384]{1,0:T(8,128)(2,1)S(1)} %slice.284), channel_id=1, source_target_pairs={{0,4},{4,0},{8,12},{12,8},{16,20},{20,16},{24,28},{28,24},{1,5},{5... | collective-permute-start | bytes 663560 | tf_op jit(solution)/shard_map/ppermute | solution.py:789
  194.9 10.2 %collective-permute-start.34 = (bf16[256,384]{1,0:T(8,128)(2,1)S(1)}, bf16[256,384]{1,0:T(8,128)(2,1)S(1)}, u32[]{:S(2)}, u32[]{:S(2)}) collective-permute-start(bf16[256,384]{1,0:T(8,128)(2,1)S(1)} %slice.293), channel_id=1, source_target_pairs={{0,4},{4,0},{8,12},{12,8},{16,20},{20,16},{24,28},{28,24},{1,5},{5... | collective-permute-start | bytes 589832 | tf_op jit(solution)/shard_map/ppermute | solution.py:789
  205.3 4.9 %collective-permute-start.33 = (bf16[224,256]{1,0:T(8,128)(2,1)S(1)}, bf16[224,256]{1,0:T(8,128)(2,1)S(1)}, u32[]{:S(2)}, u32[]{:S(2)}) collective-permute-start(bf16[224,256]{1,0:T(8,128)(2,1)S(1)} %pad_maximum_fusion.7), channel_id=1, source_target_pairs={{0,2},{1,3},{2,0},{3,1},{4,6},{5,7},{6,4},{7,5},{8,10},{9,11},{10,... | collective-permute-start | bytes 344072 | tf_op jit(solution)/shard_map/ppermute | solution.py:789
  210.2 1.5 collective-permute-start.35
  (58 other events, 209.2 us)

commit v4 on v3

--- a/solution.py
+++ b/solution.py
@@ -28,7 +28,7 @@
 
 
 MIB = 1024 * 1024
-PRE, FRONT, INTRA, MIDDLE, BACK, TAIL, STATE, FINAL = 12, 14, 12, 18, 12, 14, 12, 56
+PRE, FRONT, INTRA, MIDDLE, BACK, TAIL, STATE, FINAL = 12, 14, 12, 18, 56, 14, 12, 56
 
 
 def whole(shape):
@@ -943,7 +943,7 @@
         parts = [value[..., (p ^ mask) * wide : ((p ^ mask) + 1) * wide] for p in range(ways)]
         return jnp.concatenate(parts, axis=-1)
 
-    def scan(own, own_turned, forward):
+    def scan(own, own_turned, forward, beside=lambda run: ()):
         def fade_of(value):
             return value[state : state + 1].astype(F32) + value[state + 1 : state + 2].astype(F32)
 
@@ -951,8 +951,10 @@
             near = swap(own_turned, "head", 1)
             (run,) = call(functools.partial(join_kernel, forward), [(own.shape, BF16)], [scalars, own, near], mib=8)
             far = swap(run, "head", 2)
+            between = beside(run)
+            far = after(far, between[1]) if between else far
             (result,) = call(functools.partial(arrive_kernel, forward), [((state, total), F32)], [scalars, near, far], mib=8)
-            return result, run
+            return result, between
         before = before_fade = None
         run = own
         for mask in order:
@@ -977,25 +979,28 @@
                 run = jnp.concatenate(
                     [both_maps.astype(BF16), high, low_part, jnp.zeros((HALO - 2, total), BF16)], axis=0
                 )
-        return before, run
-
-    inc_in, run = scan(carry, carry_turned, True)
-    (y_intra,) = call(
-        functools.partial(intra_kernel, blocks),
-        [((rows, total), F32)],
-        [scalars, rowp, colp, cb, after(x, run)],
-        cost=5,
-        mib=INTRA,
-    )
-    all_outs = [w for value in outs for w in outs_merged(near_pair(value, run))]
-    dny, dbt = call(
-        functools.partial(masked_kernel, blocks, pieces),
-        [((rows, total), BF16), ((depth, rows), BF16)],
-        [scalars, cotangent, *all_outs],
-        scratch=[vmem((rows, depth), BF16)],
-        cost=3,
-        mib=INTRA,
-    )
+        return before, beside(run)
+
+    def within(run):
+        (y_intra,) = call(
+            functools.partial(intra_kernel, blocks),
+            [((rows, total), F32)],
+            [scalars, rowp, colp, cb, after(x, run)],
+            cost=5,
+            mib=INTRA,
+        )
+        all_outs = [w for value in outs for w in outs_merged(near_pair(value, run))]
+        dny, dbt = call(
+            functools.partial(masked_kernel, blocks, pieces),
+            [((rows, total), BF16), ((depth, rows), BF16)],
+            [scalars, cotangent, *all_outs],
+            scratch=[vmem((rows, depth), BF16)],
+            cost=3,
+            mib=INTRA,
+        )
+        return y_intra, dny, dbt, all_outs
+
+    inc_in, (y_intra, dny, dbt, all_outs) = scan(carry, carry_turned, True, within)
     wide_bf = vmem((rows, total), BF16)
     held_outs = [((rows, total), BF16), ((rows, total), BF16),
                  ((pieces // 2, 2 * depth, span), BF16), ((pieces // 2, 2 * depth, span), BF16),
@@ -1011,7 +1016,8 @@
                  pltpu.SemaphoreType.DMA((2, 2))],
         cost=14, mib=MIDDLE,
     )
-    back_in, back_run = scan(back_carry, back_turned, False)
+    back_runs = []
+    back_in, _ = scan(back_carry, back_turned, False, lambda run: back_runs.append(run))
 
     def over_head(keep, send):
         if not plain:
@@ -1036,7 +1042,7 @@
         got = swap(pick(parts, 1 - side).astype(BF16), "dp", 1)
         return pick(parts, side).astype(F32) + got.astype(F32)
 
-    a_live = over_head(a_keep, after(a_send, back_run))
+    a_live = over_head(a_keep, after(a_send, *back_runs))
     if plain:
         a_out = finish_head([v[:depth] for v in a_live])
         a_gate = halve(jnp.stack([v[depth:] for v in a_live]), 1)
@@ -1193,12 +1199,13 @@
         own = b_all[depth + 32 : depth + 32 + share_rows, :side]
     else:
         own = b_all[depth + 32 : depth + 240].reshape(-1)[: share_rows * side].reshape(share_rows, side)
+    smaller = (grad_value, grad_step, small[0:4], small[4], small[5], *[small[24 : 24 + share, at] for at in range(3)])
     stacked, members = own, [0]
     for mask in reversed(order):
         members += [p | mask for p in members]
         gain_low = gain_all.astype(BF16)
         sent = jnp.concatenate([stacked, gain_low], axis=0)
-        got = swap(after(sent, grad_value) if mask == 1 else sent, "head", mask)
+        got = swap(after(sent, smaller if mask == 1 else (grad_out, grad_gate, grad_hidden)), "head", mask)
         stacked = jnp.concatenate([stacked, got[: stacked.shape[0]]], axis=0)
         gain_all = gain_low.astype(F32) + got[-16:].astype(F32)
     stacked = stacked.reshape(ways, share_rows, side)
@@ -1209,17 +1216,17 @@
         grad_hidden,
         gain_all[: depth // side].reshape(-1),
         grad_gate,
-        grad_value,
+        smaller[0],
         full[:depth],
-        grad_step,
-        small[0:4],
-        small[4],
+        smaller[1],
+        smaller[2],
+        smaller[3],
         full[depth : depth + 4],
         full[depth + 4],
-        small[24 : 24 + share, 0],
-        small[24 : 24 + share, 1],
-        small[24 : 24 + share, 2],
-        small[5],
+        smaller[5],
+        smaller[6],
+        smaller[7],
+        smaller[4],
         grad_out,
     )
 

time: 215 us -> 212 us (0.986)
  local copies, waits for them, and re-layouts: 20.8 us -> 15.2 us
  waiting for transfers between devices: 69.1 us -> 66 us
  Pallas kernels: 79.7 us -> 82.3 us
    unnamed x138 -> x130, local copies, waits for them, and re-layouts: 15.3 us -> 9.72 us
    ppermute x35, waiting for transfers between devices: 69.1 us -> 66 us  [swap(): return lax.ppermute(value, axis, [(i, i ^ mask) for i in range(size)])]
    pallas_call x16, Pallas kernels: 79.7 us -> 82.3 us  [call(): pl.pallas_call(kernel, grid=grid, out_shape=[kinds[at](s, d) if at in kin...]
  transfers between devices with their start and end apart: 36 -> 36, of which waited for: 17 -> 18; matrix products, arithmetic and copies ran while one was open for 5% -> 5% of each run, Pallas kernels for 29% -> 31%
where the time goes in v4:
time: 212 us; the launch traced here: 211 us
  Pallas kernels  82.3 us (39%)
  waiting for transfers between devices  66 us (31%)
  starting transfers between devices  34.8 us (16%)
  local copies, waits for them, and re-layouts  15.2 us (7%)
  other arithmetic  11.1 us (5%)
    pallas_call x16, Pallas kernels, call(): pl.pallas_call(kernel, grid=grid, out_shape=[kinds[at](s, d) if at in kin...  82.3 us
    ppermute x35, waiting for transfers between devices, swap(): return lax.ppermute(value, axis, [(i, i ^ mask) for i in range(size)])  66 us
    ppermute x35, starting transfers between devices, swap(): return lax.ppermute(value, axis, [(i, i ^ mask) for i in range(size)])  33.2 us
    unnamed x130, local copies, waits for them, and re-layouts  9.72 us
  transfers between devices with their start and end apart: 36, of which 18 were waited for; matrix products, arithmetic and copies ran while one was open for 5% of the time, Pallas kernels for 31%

profile of v4, /device:TPU:0, one launch (start us, length us, event | category | flops | bytes accessed | tf_op | source)
XLA Modules:
  0.0 211.4 jit_solution(9596411178551569271)
XLA Ops:
  0.8 2.0 constant_dynamic-update-slice_fusion.1
  4.7 3.0 %collective-permute-start = (f32[32,896]{1,0:T(8,128)S(1)}, f32[32,896]{1,0:T(8,128)S(1)}, u32[]{:S(2)}, u32[]{:S(2)}) collective-permute-start(f32[32,896]{1,0:T(8,128)S(1)} %fusion.26), channel_id=1, source_target_pairs={{0,2},{1,3},{2,0},{3,1},{4,6},{5,7},{6,4},{7,5},{8,10},{9,11},{10,... | collective-permute-start | bytes 344072 | tf_op jit(solution)/shard_map/ppermute | solution.py:789
  7.7 1.9 collective-permute-start.3
  9.6 1.6 collective-permute-done
  12.6 2.0 shard_map.288
  17.0 1.9 shard_map.289
  19.5 8.0 %shard_map.290 = (bf16[512,1536]{1,0:T(8,128)(2,1)}, bf16[528,1536]{1,0:T(8,128)(2,1)}, bf16[512,1536]{1,0:T(8,128)(2,1)}, f32[2,128,1536]{2,1,0:T(8,128)}, bf16...) custom-call(s32[8]{0:T(128)S(1)} %pad_add_fusion.s_ref, ...), custom_call_target="tpu_custom_call" | custom-call | flops 2400000000 | bytes 1800000 | tf_op jit(solution)/shard_map/pallas_call | solution.py:44
  27.5 8.9 %collective-permute-done.3.refs_0_.refs_2_ = bf16[768,768]{1,0:T(8,128)(2,1)S(1)} collective-permute-done((bf16[768,768]{1,0:T(8,128)(2,1)}, bf16[768,768]{1,0:T(8,128)(2,1)S(1)}, u32[]{:S(2)}, u32[]{:S(2)}) %collective-permute-start.3) | collective-permute-done | bytes 1179680 | tf_op jit(solution)/shard_map/ppermute | solution.py:789
  36.4 1.8 collective-permute-start.8
  39.2 6.2 %shard_map.291 = (bf16[512,1536]{1,0:T(8,128)(2,1)}, bf16[528,1536]{1,0:T(8,128)(2,1)}, bf16[512,1536]{1,0:T(8,128)(2,1)}, f32[2,128,1536]{2,1,0:T(8,128)}, bf16...) custom-call(s32[8]{0:T(128)S(1)} %pad_add_fusion.s_ref, ...), custom_call_target="tpu_custom_call", output_to_operand_aliasing={{0}: (8, {}), {1}: (9, {}), {2}: (10, {}), {3}: (11, {}), {... | custom-call | flops 2400000000 | bytes 1800000 | tf_op jit(solution)/shard_map/pallas_call | solution.py:44
  45.7 1.7 collective-permute-done.6.got_ref.near_ref
  48.1 4.0 %collective-permute-done.8.refs_2_ = bf16[384,768]{1,0:T(8,128)(2,1)S(1)} collective-permute-done((bf16[384,768]{1,0:T(8,128)(2,1)S(1)}, bf16[384,768]{1,0:T(8,128)(2,1)S(1)}, u32[]{:S(2)}, u32[]{:S(2)}) %collective-permute-start.8) | collective-permute-done | bytes 589856 | tf_op jit(solution)/shard_map/ppermute | solution.py:789
  52.6 1.7 collective-permute-start.10
  54.4 4.0 %shard_map.295.y_ref = f32[512,1536]{1,0:T(8,128)S(1)} custom-call(s32[8]{0:T(128)S(1)} %pad_add_fusion.s_ref, f32[12,8,512]{2,1,0:T(8,128)S(1)} %get-tuple-element.137.rowp_ref, f32[6,512,16]{2,1,0:T(8,128)S(1)} %get-tuple-element.115.colp_ref, f32[2,256,256]{2,1,0:T(8,128)S(1)} %get-tuple-element.138.cb_ref, bf16[512,1536]{1,0:T(8,128)(2,1)S(1)} %get-tuple-element.140.x_ref), custom_call_target="tpu_custom_call" | custom-call | flops 2000000000 | bytes 1500000 | tf_op jit(solution)/shard_map/pallas_call | solution.py:44
  58.5 2.4 %shard_map.293 = (bf16[512,1536]{1,0:T(8,128)(2,1)S(1)}, bf16[768,512]{1,0:T(8,128)(2,1)S(1)}) custom-call(s32[8]{0:T(128)S(1)} %pad_add_fusion.s_ref, bf16[512,768]{1,0:T(8,128)(2,1)S(1)} %copy-done.18, bf16[384,768]{1,0:T(8,128)(2,1)S(1)} %copy-done.19, bf16[384,768]{1,0:T(8,128)(2,1)S(1)} %collective-permute-done.7.refs_1_, ...), custom_call_target="tpu_custom_call" | custom-call | flops 1200000000 | bytes 900000 | tf_op jit(solution)/shard_map/pallas_call | solution.py:44
  60.9 3.8 %collective-permute-done.10.far_ref = bf16[144,1536]{1,0:T(8,128)(2,1)S(1)} collective-permute-done((bf16[144,1536]{1,0:T(8,128)(2,1)S(1)}, bf16[144,1536]{1,0:T(8,128)(2,1)S(1)}, u32[]{:S(2)}, u32[]{:S(2)}) %collective-permute-start.10) | collective-permute-done | bytes 442400 | tf_op jit(solution)/shard_map/ppermute | solution.py:789
  65.4 14.8 %shard_map.296 = (bf16[512,1536]{1,0:T(8,128)(2,1)}, bf16[512,1536]{1,0:T(8,128)(2,1)}, bf16[2,1536,384]{2,1,0:T(8,128)(2,1)}, bf16[2,1536,384]{2,1,0:T(8,128)(2...) custom-call(s32[8]{0:T(128)S(1)} %pad_add_fusion.s_ref, ...), custom_call_target="tpu_custom_call" | custom-call | flops 5600000000 | bytes 4200000 | tf_op jit(solution)/shard_map/pallas_call | solution.py:44
  81.4 1.8 collective-permute-done.11.got_ref.near_ref
  84.1 1.8 collective-permute-start.17
  86.0 9.3 %shard_map.299 = (bf16[512,1536]{1,0:T(8,128)(2,1)S(1)}, f32[32,512]{1,0:T(8,128)S(1)}, f32[512,128]{1,0:T(8,128)S(1)}, f32[512,128]{1,0:T(8,128)S(1)}) custom-call(s32[8]{0:T(128)} %copy-done.14, f32[12,8,512]{2,1,0:T(8,128)} %copy-done.24, f32[6,512,16]{2,1,0:T(8,128)} %copy-done.1, f32[2,256,256]{2,1,0:T(8,128)} %copy-done.36, ...), custom_call_target="tpu_custom_call" | custom-call | flops 3200000000 | bytes 2400000 | tf_op jit(solution)/shard_map/pallas_call | solution.py:44
  95.3 1.3 collective-permute-done.17.far_ref
  97.3 2.9 %convert_add_fusion = (f32[1,1536,384]{2,1,0:T(8,128)S(1)}, f32[1,1536,384]{2,1,0:T(8,128)S(1)}) fusion(bf16[2,1536,384]{2,1,0:T(8,128)(2,1)} %collective-permute-done.12, bf16[2,1536,384]{2,1,0:T(8,128)(2,1)} %get-tuple-element.144), kind=kLoop, calls=%fused_computation.4 | loop fusion | flops 3538944 | bytes 9437184 | tf_op jit(solution)/shard_map/add | solution.py:1030
  100.6 1.8 collective-permute-start.15
  102.5 1.6 collective-permute-start.13
  104.1 13.6 %shard_map.300 = (bf16[528,1536]{1,0:T(8,128)(2,1)S(1)}, f32[8,1536]{1,0:T(8,128)S(1)}, f32[32,512]{1,0:T(8,128)S(1)}, f32[8,1536]{1,0:T(8,128)S(1)}, f32[512,12...) custom-call(s32[8]{0:T(128)S(1)} %copy-done.15, f32[128,1536]{1,0:T(8,128)S(1)} %shard_map.298.back_in, ...), custom_call_target="tpu_custom_call" | custom-call | flops 4000000000 | bytes 3000000 | tf_op jit(solution)/shard_map/pallas_call | solution.py:44
  119.0 1.5 collective-permute-start.16
  120.8 1.6 collective-permute-start.14
  122.4 2.6 %shard_map.301 = (bf16[528,256]{1,0:T(8,128)(2,1)S(1)}, bf16[32,512]{1,0:T(8,128)(2,1)S(1)}, bf16[2,256,384]{2,1,0:T(8,128)(2,1)S(1)}, bf16[2,256,384]{2,1,0:T(8,128)(2,1)S(1)}) custom-call(s32[8]{0:T(128)S(1)} %copy-done.15, f32[512,128]{1,0:T(8,128)S(1)} %get-tuple-element.161.dbx_ref, f32[512,128]{1,0:T(8,128)S(1)} %get-tuple-element.162.dbin_ref, ...), custom_call_target="tpu_custom_call" | custom-call | flops 1600000000 | bytes 1200000 | tf_op jit(solution)/shard_map/pallas_call | solution.py:44
  125.3 1.9 collective-permute-done.16
  127.3 2.9 %collective-permute-done.14 = bf16[384,384]{1,0:T(8,128)(2,1)S(1)} collective-permute-done((bf16[384,384]{1,0:T(8,128)(2,1)S(1)}, bf16[384,384]{1,0:T(8,128)(2,1)S(1)}, u32[]{:S(2)}, u32[]{:S(2)}) %collective-permute-start.14) | collective-permute-done | bytes 294944 | tf_op jit(solution)/shard_map/ppermute | solution.py:789
  132.4 1.6 collective-permute-start.23
  134.8 1.6 collective-permute-start.20
  136.4 9.7 %shard_map.302 = (f32[512,768]{1,0:T(8,128)}, f32[16,768]{1,0:T(8,128)S(1)}, f32[8,384]{1,0:T(8,128)S(1)}) custom-call(s32[8]{0:T(128)} %copy-done.14, bf16[512,768]{1,0:T(8,128)(2,1)} %hid_ref.5, bf16[16,768]{1,0:T(8,128)(2,1)} %copy-done.13, bf16[512,768]{1,0:T(8,128)(2,1)} %cot_ref.3, f32[1,768]{1,0:T(1,128)} %copy-done.16, ...), custom_call_target="tpu_custom_call" | custom-call | flops 3600000000 | bytes 2700000 | tf_op jit(solution)/shard_map/pallas_call | solution.py:44
  146.2 2.7 %collective-permute-start.21 = (bf16[384,384]{1,0:T(8,128)(2,1)S(1)}, bf16[384,384]{1,0:T(8,128)(2,1)S(1)}, u32[]{:S(2)}, u32[]{:S(2)}) collective-permute-start(bf16[384,384]{1,0:T(8,128)(2,1)S(1)} %fusion.15), channel_id=1, source_target_pairs={{0,16},{4,20},{8,24},{12,28},{16,0},{20,4},{24,8},{28,12},{1,17},{... | collective-permute-start | bytes 884744 | tf_op jit(solution)/shard_map/ppermute | solution.py:789
  149.7 1.2 collective-permute-start.25
  150.9 10.3 %collective-permute-done.21 = bf16[384,384]{1,0:T(8,128)(2,1)S(1)} collective-permute-done((bf16[384,384]{1,0:T(8,128)(2,1)S(1)}, bf16[384,384]{1,0:T(8,128)(2,1)S(1)}, u32[]{:S(2)}, u32[]{:S(2)}) %collective-permute-start.21) | collective-permute-done | bytes 294944 | tf_op jit(solution)/shard_map/ppermute | solution.py:789
  161.6 1.6 collective-permute-start.26
  163.2 2.1 collective-permute-start.29
  165.3 5.0 %shard_map.303 = bf16[512,768]{1,0:T(8,128)(2,1)} custom-call(s32[8]{0:T(128)} %copy-done.14, bf16[512,768]{1,0:T(8,128)(2,1)} %hid_ref.5, bf16[512,1536]{1,0:T(8,128)(2,1)} %get-tuple-element.191.ny_ref, bf16[384,768]{1,0:T(8,128)(2,1)} %refs_0_.3, bf16[384,768]{1,0:T(8,128)(2,1)} %copy-done.22, bf16[384,768]{1,0:T(8,128)(2,1)} %copy-done.20, ...), custom_call_target="tpu_custom_call" | custom-call | flops 1600000000 | bytes 1200000 | tf_op jit(solution)/shard_map/pallas_call | solution.py:44
  170.3 1.2 collective-permute-start.28
  171.5 4.6 %collective-permute-done.29 = bf16[384,384]{1,0:T(8,128)(2,1)S(1)} collective-permute-done((bf16[384,384]{1,0:T(8,128)(2,1)S(1)}, bf16[384,384]{1,0:T(8,128)(2,1)S(1)}, u32[]{:S(2)}, u32[]{:S(2)}) %collective-permute-start.29) | collective-permute-done | bytes 294944 | tf_op jit(solution)/shard_map/ppermute | solution.py:789
  176.9 6.8 %collective-permute-done.28 = bf16[272,384]{1,0:T(8,128)(2,1)S(1)} collective-permute-done((bf16[272,384]{1,0:T(8,128)(2,1)S(1)}, bf16[272,384]{1,0:T(8,128)(2,1)S(1)}, u32[]{:S(2)}, u32[]{:S(2)}) %collective-permute-start.28) | collective-permute-done | bytes 208928 | tf_op jit(solution)/shard_map/ppermute | solution.py:789
  183.8 1.4 add_dynamic-update-slice_fusion
  185.2 5.6 %collective-permute-done.30 = bf16[272,384]{1,0:T(8,128)(2,1)S(1)} collective-permute-done((bf16[272,384]{1,0:T(8,128)(2,1)S(1)}, bf16[272,384]{1,0:T(8,128)(2,1)S(1)}, u32[]{:S(2)}, u32[]{:S(2)}) %collective-permute-start.30) | collective-permute-done | bytes 208928 | tf_op jit(solution)/shard_map/ppermute | solution.py:789
  191.6 1.5 collective-permute-start.34
  194.4 7.4 %collective-permute-done.34 = bf16[256,384]{1,0:T(8,128)(2,1)S(1)} collective-permute-done((bf16[256,384]{1,0:T(8,128)(2,1)S(1)}, bf16[256,384]{1,0:T(8,128)(2,1)S(1)}, u32[]{:S(2)}, u32[]{:S(2)}) %collective-permute-start.34) | collective-permute-done | bytes 196640 | tf_op jit(solution)/shard_map/ppermute | solution.py:789
  205.7 1.1 collective-permute-done.33
  207.0 1.4 copy.53
  (270 shorter events, 28.5 us)
Async XLA Ops:
  0.7 10.5 %copy-start.62 = (s32[1,3]{1,0:T(1,128)S(1)}, s32[1,3]{1,0:T(1,128)}, u32[]{:S(2)}) copy-start(s32[1,3]{1,0:T(1,128)} %param.20) | copy-start | bytes 40
  0.8 10.6 %copy-start.54 = (f32[768]{0:T(1024)S(1)}, f32[768]{0:T(1024)}, u32[]{:S(2)}) copy-start(f32[768]{0:T(1024)} %param.21) | copy-start | bytes 9220
  3.7 15.8 %collective-permute-start.4 = (bf16[768,768]{1,0:T(8,128)(2,1)}, bf16[768,768]{1,0:T(8,128)(2,1)}, u32[]{:S(2)}, u32[]{:S(2)}) collective-permute-start(bf16[768,768]{1,0:T(8,128)(2,1)} %constant_dynamic-update-slice_fusion.refs_0_), channel_id=1, source_target_pairs={{0,1},{1,0},{2,3},{3,2},{4,5},{5,4},{6,7},{7,6},{8,9},{9,8},{10,11... | collective-permute-start | bytes 3538952 | tf_op jit(solution)/shard_map/ppermute | solution.py:789
  4.6 3.1 %collective-permute-start.2 = (f32[32,896]{1,0:T(8,128)S(1)}, f32[32,896]{1,0:T(8,128)S(1)}, u32[]{:S(2)}, u32[]{:S(2)}) collective-permute-start(f32[32,896]{1,0:T(8,128)S(1)} %fusion.26), channel_id=1, source_target_pairs={{0,1},{1,0},{2,3},{3,2},{4,5},{5,4},{6,7},{7,6},{8,9},{9,8},{10,11... | collective-permute-start | bytes 344072 | tf_op jit(solution)/shard_map/ppermute | solution.py:789
  4.7 6.5 %collective-permute-start = (f32[32,896]{1,0:T(8,128)S(1)}, f32[32,896]{1,0:T(8,128)S(1)}, u32[]{:S(2)}, u32[]{:S(2)}) collective-permute-start(f32[32,896]{1,0:T(8,128)S(1)} %fusion.26), channel_id=1, source_target_pairs={{0,2},{1,3},{2,0},{3,1},{4,6},{5,7},{6,4},{7,5},{8,10},{9,11},{10,... | collective-permute-start | bytes 344072 | tf_op jit(solution)/shard_map/ppermute | solution.py:789
  7.7 28.7 %collective-permute-start.3 = (bf16[768,768]{1,0:T(8,128)(2,1)}, bf16[768,768]{1,0:T(8,128)(2,1)S(1)}, u32[]{:S(2)}, u32[]{:S(2)}) collective-permute-start(bf16[768,768]{1,0:T(8,128)(2,1)} %constant_dynamic-update-slice_fusion.refs_0_), channel_id=1, source_target_pairs={{0,2},{1,3},{2,0},{3,1},{4,6},{5,7},{6,4},{7,5},{8,10},{9,11},{10,... | collective-permute-start | bytes 3538952 | tf_op jit(solution)/shard_map/ppermute | solution.py:789
  11.3 1.3 collective-permute-start.1
  11.3 71.8 %copy-start.14 = (s32[8]{0:T(128)}, s32[8]{0:T(128)S(1)}, u32[]{:S(2)}) copy-start(s32[8]{0:T(128)S(1)} %pad_add_fusion.s_ref) | copy-start | bytes 100
  16.9 22.3 %copy-start.10 = (bf16[528,768]{1,0:T(8,128)(2,1)}, bf16[528,768]{1,0:T(8,128)(2,1)S(1)}, u32[]{:S(2)}) copy-start(bf16[528,768]{1,0:T(8,128)(2,1)S(1)} %get-tuple-element.113.nx_ref) | copy-start | bytes 2433028
  16.9 48.5 %copy-start.28 = (bf16[768,512]{1,0:T(8,128)(2,1)}, bf16[768,512]{1,0:T(8,128)(2,1)S(1)}, u32[]{:S(2)}) copy-start(bf16[768,512]{1,0:T(8,128)(2,1)S(1)} %get-tuple-element.136.nt_ref) | copy-start | bytes 2359300
  16.9 48.5 %copy-start.41 = (bf16[512,128]{1,0:T(8,128)(2,1)}, bf16[512,128]{1,0:T(8,128)(2,1)S(1)}, u32[]{:S(2)}) copy-start(bf16[512,128]{1,0:T(8,128)(2,1)S(1)} %get-tuple-element.134.c_ref) | copy-start | bytes 393220
  16.9 105.4 %copy-start.12 = (f32[32,896]{1,0:T(8,128)}, f32[32,896]{1,0:T(8,128)S(1)}, u32[]{:S(2)}) copy-start(f32[32,896]{1,0:T(8,128)S(1)} %select_maximum_fusion.hp_ref) | copy-start | bytes 344068
  19.5 34.9 %copy-start.24 = (f32[12,8,512]{2,1,0:T(8,128)}, f32[12,8,512]{2,1,0:T(8,128)S(1)}, u32[]{:S(2)}) copy-start(f32[12,8,512]{2,1,0:T(8,128)S(1)} %get-tuple-element.137.rowp_ref) | copy-start | bytes 589828
  19.5 45.9 %copy-start.1 = (f32[6,512,16]{2,1,0:T(8,128)}, f32[6,512,16]{2,1,0:T(8,128)S(1)}, u32[]{:S(2)}) copy-start(f32[6,512,16]{2,1,0:T(8,128)S(1)} %get-tuple-element.115.colp_ref) | copy-start | bytes 589828
  19.5 16.9 %copy-start.19 = (bf16[384,768]{1,0:T(8,128)(2,1)S(1)}, bf16[384,768]{1,0:T(8,128)(2,1)}, u32[]{:S(2)}) copy-start(bf16[384,768]{1,0:T(8,128)(2,1)} %refs_0_.3) | copy-start | bytes 1769476
  36.4 2.8 %collective-permute-start.5 = (bf16[768,768]{1,0:T(8,128)(2,1)S(1)}, bf16[768,768]{1,0:T(8,128)(2,1)S(1)}, u32[]{:S(2)}, u32[]{:S(2)}) collective-permute-start(bf16[768,768]{1,0:T(8,128)(2,1)S(1)} %collective-permute-done.3.refs_0_.refs_2_), channel_id=1, source_target_pairs={{0,1},{1,0},{2,3},{3,2},{4,5},{5,4},{6,7},{7,6},{8,9},{9,8},{10,11... | collective-permute-start | bytes 3538952 | tf_op jit(solution)/shard_map/ppermute | solution.py:789
  36.4 15.7 %collective-permute-start.8 = (bf16[384,768]{1,0:T(8,128)(2,1)S(1)}, bf16[384,768]{1,0:T(8,128)(2,1)S(1)}, u32[]{:S(2)}, u32[]{:S(2)}) collective-permute-start(bf16[384,768]{1,0:T(8,128)(2,1)S(1)} %copy-done.19), channel_id=1, source_target_pairs={{0,2},{1,3},{2,0},{3,1},{4,6},{5,7},{6,4},{7,5},{8,10},{9,11},{10,... | collective-permute-start | bytes 1769480 | tf_op jit(solution)/shard_map/ppermute | solution.py:789
  45.5 19.9 %copy-start.6 = (bf16[512,1536]{1,0:T(8,128)(2,1)}, bf16[512,1536]{1,0:T(8,128)(2,1)S(1)}, u32[]{:S(2)}) copy-start(bf16[512,1536]{1,0:T(8,128)(2,1)S(1)} %get-tuple-element.140.x_ref) | copy-start | bytes 4718596
  45.5 1.9 collective-permute-start.6
  52.1 6.3 %collective-permute-start.9 = (bf16[384,768]{1,0:T(8,128)(2,1)S(1)}, bf16[384,768]{1,0:T(8,128)(2,1)S(1)}, u32[]{:S(2)}, u32[]{:S(2)}) collective-permute-start(bf16[384,768]{1,0:T(8,128)(2,1)S(1)} %collective-permute-done.8.refs_2_), channel_id=1, source_target_pairs={{0,1},{1,0},{2,3},{3,2},{4,5},{5,4},{6,7},{7,6},{8,9},{9,8},{10,11... | collective-permute-start | bytes 1769480 | tf_op jit(solution)/shard_map/ppermute | solution.py:789
  52.1 6.3 %collective-permute-start.7 = (bf16[384,768]{1,0:T(8,128)(2,1)S(1)}, bf16[384,768]{1,0:T(8,128)(2,1)S(1)}, u32[]{:S(2)}, u32[]{:S(2)}) collective-permute-start(bf16[384,768]{1,0:T(8,128)(2,1)S(1)} %copy-done.19), channel_id=1, source_target_pairs={{0,1},{1,0},{2,3},{3,2},{4,5},{5,4},{6,7},{7,6},{8,9},{9,8},{10,11... | collective-permute-start | bytes 1769480 | tf_op jit(solution)/shard_map/ppermute | solution.py:789
  52.6 12.1 %collective-permute-start.10 = (bf16[144,1536]{1,0:T(8,128)(2,1)S(1)}, bf16[144,1536]{1,0:T(8,128)(2,1)S(1)}, u32[]{:S(2)}, u32[]{:S(2)}) collective-permute-start(bf16[144,1536]{1,0:T(8,128)(2,1)S(1)} %shard_map.292), channel_id=1, source_target_pairs={{0,2},{1,3},{2,0},{3,1},{4,6},{5,7},{6,4},{7,5},{8,10},{9,11},{10,... | collective-permute-start | bytes 1327112 | tf_op jit(solution)/shard_map/ppermute | solution.py:789
  81.4 1.8 collective-permute-start.11
  83.9 13.3 %collective-permute-start.12 = (bf16[2,1536,384]{2,1,0:T(8,128)(2,1)}, bf16[2,1536,384]{2,1,0:T(8,128)(2,1)}, u32[]{:S(2)}, u32[]{:S(2)}) collective-permute-start(bf16[2,1536,384]{2,1,0:T(8,128)(2,1)} %get-tuple-element.148), channel_id=1, source_target_pairs={{0,1},{1,0},{2,3},{3,2},{4,5},{5,4},{6,7},{7,6},{8,9},{9,8},{10,11... | collective-permute-start | bytes 7077896 | tf_op jit(solution)/shard_map/ppermute | solution.py:789
  84.1 12.4 %collective-permute-start.17 = (bf16[144,1536]{1,0:T(8,128)(2,1)S(1)}, bf16[144,1536]{1,0:T(8,128)(2,1)S(1)}, u32[]{:S(2)}, u32[]{:S(2)}) collective-permute-start(bf16[144,1536]{1,0:T(8,128)(2,1)S(1)} %shard_map.297), channel_id=1, source_target_pairs={{0,2},{1,3},{2,0},{3,1},{4,6},{5,7},{6,4},{7,5},{8,10},{9,11},{10,... | collective-permute-start | bytes 1327112 | tf_op jit(solution)/shard_map/ppermute | solution.py:789
  86.0 10.6 %copy-start.15 = (s32[8]{0:T(128)S(1)}, s32[8]{0:T(128)}, u32[]{:S(2)}) copy-start(s32[8]{0:T(128)} %copy-done.14) | copy-start | bytes 100
  100.6 17.1 %collective-permute-start.15 = (bf16[2,384,384]{2,1,0:T(8,128)(2,1)S(1)}, bf16[2,384,384]{2,1,0:T(8,128)(2,1)S(1)}, u32[]{:S(2)}, u32[]{:S(2)}) collective-permute-start(bf16[2,384,384]{2,1,0:T(8,128)(2,1)S(1)} %fusion.13), channel_id=1, source_target_pairs={{0,4},{4,0},{8,12},{12,8},{16,20},{20,16},{24,28},{28,24},{1,5},{5... | collective-permute-start | bytes 1769480 | tf_op jit(solution)/shard_map/ppermute | solution.py:789
  102.5 18.1 %collective-permute-start.13 = (bf16[768,384]{1,0:T(8,128)(2,1)S(1)}, bf16[768,384]{1,0:T(8,128)(2,1)S(1)}, u32[]{:S(2)}, u32[]{:S(2)}) collective-permute-start(bf16[768,384]{1,0:T(8,128)(2,1)S(1)} %fusion.12), channel_id=1, source_target_pairs={{0,2},{1,3},{2,0},{3,1},{4,6},{5,7},{6,4},{7,5},{8,10},{9,11},{10,... | collective-permute-start | bytes 1769480 | tf_op jit(solution)/shard_map/ppermute | solution.py:789
  119.0 8.2 %collective-permute-start.16 = (bf16[384,384]{1,0:T(8,128)(2,1)S(1)}, bf16[384,384]{1,0:T(8,128)(2,1)S(1)}, u32[]{:S(2)}, u32[]{:S(2)}) collective-permute-start(bf16[384,384]{1,0:T(8,128)(2,1)S(1)} %fusion.22), channel_id=1, source_target_pairs={{0,2},{1,3},{2,0},{3,1},{4,6},{5,7},{6,4},{7,5},{8,10},{9,11},{10,... | collective-permute-start | bytes 884744 | tf_op jit(solution)/shard_map/ppermute | solution.py:789
  120.6 9.9 %collective-permute-start.18 = (bf16[2,768,384]{2,1,0:T(8,128)(2,1)S(1)}, bf16[2,768,384]{2,1,0:T(8,128)(2,1)S(1)}, u32[]{:S(2)}, u32[]{:S(2)}) collective-permute-start(bf16[2,768,384]{2,1,0:T(8,128)(2,1)S(1)} %copy-done.63), channel_id=1, source_target_pairs={{0,1},{1,0},{2,3},{3,2},{4,5},{5,4},{6,7},{7,6},{8,9},{9,8},{10,11... | collective-permute-start | bytes 3538952 | tf_op jit(solution)/shard_map/ppermute | solution.py:789
  120.8 9.5 %collective-permute-start.14 = (bf16[384,384]{1,0:T(8,128)(2,1)S(1)}, bf16[384,384]{1,0:T(8,128)(2,1)S(1)}, u32[]{:S(2)}, u32[]{:S(2)}) collective-permute-start(bf16[384,384]{1,0:T(8,128)(2,1)S(1)} %fusion.20), channel_id=1, source_target_pairs={{0,4},{4,0},{8,12},{12,8},{16,20},{20,16},{24,28},{28,24},{1,5},{5... | collective-permute-start | bytes 884744 | tf_op jit(solution)/shard_map/ppermute | solution.py:789
  125.1 5.4 %collective-permute-start.19 = (bf16[2,256,384]{2,1,0:T(8,128)(2,1)S(1)}, bf16[2,256,384]{2,1,0:T(8,128)(2,1)S(1)}, u32[]{:S(2)}, u32[]{:S(2)}) collective-permute-start(bf16[2,256,384]{2,1,0:T(8,128)(2,1)S(1)} %get-tuple-element.177), channel_id=1, source_target_pairs={{0,1},{1,0},{2,3},{3,2},{4,5},{5,4},{6,7},{7,6},{8,9},{9,8},{10,11... | collective-permute-start | bytes 1179656 | tf_op jit(solution)/shard_map/ppermute | solution.py:789
  132.4 16.5 %collective-permute-start.23 = (bf16[2,256,384]{2,1,0:T(8,128)(2,1)S(1)}, bf16[2,256,384]{2,1,0:T(8,128)(2,1)S(1)}, u32[]{:S(2)}, u32[]{:S(2)}) collective-permute-start(bf16[2,256,384]{2,1,0:T(8,128)(2,1)S(1)} %fusion.18), channel_id=1, source_target_pairs={{0,4},{4,0},{8,12},{12,8},{16,20},{20,16},{24,28},{28,24},{1,5},{5... | collective-permute-start | bytes 1179656 | tf_op jit(solution)/shard_map/ppermute | solution.py:789
  133.9 15.0 %collective-permute-start.22 = (bf16[512,384]{1,0:T(8,128)(2,1)S(1)}, bf16[512,384]{1,0:T(8,128)(2,1)S(1)}, u32[]{:S(2)}, u32[]{:S(2)}) collective-permute-start(bf16[512,384]{1,0:T(8,128)(2,1)S(1)} %fusion.17), channel_id=1, source_target_pairs={{0,2},{1,3},{2,0},{3,1},{4,6},{5,7},{6,4},{7,5},{8,10},{9,11},{10,... | collective-permute-start | bytes 1179656 | tf_op jit(solution)/shard_map/ppermute | solution.py:789
  134.8 11.3 %collective-permute-start.20 = (bf16[384,384]{1,0:T(8,128)(2,1)S(1)}, bf16[384,384]{1,0:T(8,128)(2,1)S(1)}, u32[]{:S(2)}, u32[]{:S(2)}) collective-permute-start(bf16[384,384]{1,0:T(8,128)(2,1)S(1)} %fusion.21), channel_id=1, source_target_pairs={{0,8},{4,12},{8,0},{12,4},{16,24},{20,28},{24,16},{28,20},{1,9},{5... | collective-permute-start | bytes 884744 | tf_op jit(solution)/shard_map/ppermute | solution.py:789
  146.2 15.0 %collective-permute-start.21 = (bf16[384,384]{1,0:T(8,128)(2,1)S(1)}, bf16[384,384]{1,0:T(8,128)(2,1)S(1)}, u32[]{:S(2)}, u32[]{:S(2)}) collective-permute-start(bf16[384,384]{1,0:T(8,128)(2,1)S(1)} %fusion.15), channel_id=1, source_target_pairs={{0,16},{4,20},{8,24},{12,28},{16,0},{20,4},{24,8},{28,12},{1,17},{... | collective-permute-start | bytes 884744 | tf_op jit(solution)/shard_map/ppermute | solution.py:789
  149.1 12.2 %collective-permute-start.24 = (bf16[256,384]{1,0:T(8,128)(2,1)S(1)}, bf16[256,384]{1,0:T(8,128)(2,1)S(1)}, u32[]{:S(2)}, u32[]{:S(2)}) collective-permute-start(bf16[256,384]{1,0:T(8,128)(2,1)S(1)} %fusion.24), channel_id=1, source_target_pairs={{0,4},{4,0},{8,12},{12,8},{16,20},{20,16},{24,28},{28,24},{1,5},{5... | collective-permute-start | bytes 589832 | tf_op jit(solution)/shard_map/ppermute | solution.py:789
  149.7 11.6 %collective-permute-start.25 = (bf16[256,384]{1,0:T(8,128)(2,1)S(1)}, bf16[256,384]{1,0:T(8,128)(2,1)S(1)}, u32[]{:S(2)}, u32[]{:S(2)}) collective-permute-start(bf16[256,384]{1,0:T(8,128)(2,1)S(1)} %fusion.25), channel_id=1, source_target_pairs={{0,2},{1,3},{2,0},{3,1},{4,6},{5,7},{6,4},{7,5},{8,10},{9,11},{10,... | collective-permute-start | bytes 589832 | tf_op jit(solution)/shard_map/ppermute | solution.py:789
  161.6 8.7 %collective-permute-start.27 = (bf16[272,384]{1,0:T(8,128)(2,1)S(1)}, bf16[272,384]{1,0:T(8,128)(2,1)S(1)}, u32[]{:S(2)}, u32[]{:S(2)}) collective-permute-start(bf16[272,384]{1,0:T(8,128)(2,1)S(1)} %fusion.23), channel_id=1, source_target_pairs={{0,8},{4,12},{8,0},{12,4},{16,24},{20,28},{24,16},{28,20},{1,9},{5... | collective-permute-start | bytes 626696 | tf_op jit(solution)/shard_map/ppermute | solution.py:789
  161.6 22.2 %collective-permute-start.26 = (f32[16,768]{1,0:T(8,128)S(1)}, f32[16,768]{1,0:T(8,128)S(1)}, u32[]{:S(2)}, u32[]{:S(2)}) collective-permute-start(f32[16,768]{1,0:T(8,128)S(1)} %get-tuple-element.185), channel_id=1, source_target_pairs={{1,0},{2,1},{3,2},{5,4},{6,5},{7,6},{9,8},{10,9},{11,10},{13,12},{... | collective-permute-start | bytes 147464 | tf_op jit(solution)/shard_map/ppermute | solution.py:1138
  163.2 12.9 %collective-permute-start.29 = (bf16[384,384]{1,0:T(8,128)(2,1)S(1)}, bf16[384,384]{1,0:T(8,128)(2,1)S(1)}, u32[]{:S(2)}, u32[]{:S(2)}) collective-permute-start(bf16[384,384]{1,0:T(8,128)(2,1)S(1)} %add_convert_fusion), channel_id=1, source_target_pairs={{0,8},{4,12},{8,0},{12,4},{16,24},{20,28},{24,16},{28,20},{1,9},{5... | collective-permute-start | bytes 884744 | tf_op jit(solution)/shard_map/ppermute | solution.py:789
  170.3 13.4 %collective-permute-start.28 = (bf16[272,384]{1,0:T(8,128)(2,1)S(1)}, bf16[272,384]{1,0:T(8,128)(2,1)S(1)}, u32[]{:S(2)}, u32[]{:S(2)}) collective-permute-start(bf16[272,384]{1,0:T(8,128)(2,1)S(1)} %fusion.16), channel_id=1, source_target_pairs={{0,16},{4,20},{8,24},{12,28},{16,0},{20,4},{24,8},{28,12},{1,17},{... | collective-permute-start | bytes 626696 | tf_op jit(solution)/shard_map/ppermute | solution.py:789
  176.3 14.7 %collective-permute-start.31 = (bf16[768,384]{1,0:T(8,128)(2,1)S(1)}, bf16[768,384]{1,0:T(8,128)(2,1)S(1)}, u32[]{:S(2)}, u32[]{:S(2)}) collective-permute-start(bf16[768,384]{1,0:T(8,128)(2,1)S(1)} %pad_maximum_fusion.3), channel_id=1, source_target_pairs={{0,4},{4,0},{8,12},{12,8},{16,20},{20,16},{24,28},{28,24},{1,5},{5... | collective-permute-start | bytes 1769480 | tf_op jit(solution)/shard_map/ppermute | solution.py:789
  183.7 7.1 %collective-permute-start.30 = (bf16[272,384]{1,0:T(8,128)(2,1)S(1)}, bf16[272,384]{1,0:T(8,128)(2,1)S(1)}, u32[]{:S(2)}, u32[]{:S(2)}) collective-permute-start(bf16[272,384]{1,0:T(8,128)(2,1)S(1)} %add_convert_fusion.1), channel_id=1, source_target_pairs={{0,8},{4,12},{8,0},{12,4},{16,24},{20,28},{24,16},{28,20},{1,9},{5... | collective-permute-start | bytes 626696 | tf_op jit(solution)/shard_map/ppermute | solution.py:789
  191.0 10.8 %collective-permute-start.32 = (bf16[288,384]{1,0:T(8,128)(2,1)S(1)}, bf16[288,384]{1,0:T(8,128)(2,1)S(1)}, u32[]{:S(2)}, u32[]{:S(2)}) collective-permute-start(bf16[288,384]{1,0:T(8,128)(2,1)S(1)} %slice.284), channel_id=1, source_target_pairs={{0,4},{4,0},{8,12},{12,8},{16,20},{20,16},{24,28},{28,24},{1,5},{5... | collective-permute-start | bytes 663560 | tf_op jit(solution)/shard_map/ppermute | solution.py:789
  191.6 10.2 %collective-permute-start.34 = (bf16[256,384]{1,0:T(8,128)(2,1)S(1)}, bf16[256,384]{1,0:T(8,128)(2,1)S(1)}, u32[]{:S(2)}, u32[]{:S(2)}) collective-permute-start(bf16[256,384]{1,0:T(8,128)(2,1)S(1)} %slice.295), channel_id=1, source_target_pairs={{0,4},{4,0},{8,12},{12,8},{16,20},{20,16},{24,28},{28,24},{1,5},{5... | collective-permute-start | bytes 589832 | tf_op jit(solution)/shard_map/ppermute | solution.py:789
  202.0 4.9 %collective-permute-start.33 = (bf16[224,256]{1,0:T(8,128)(2,1)S(1)}, bf16[224,256]{1,0:T(8,128)(2,1)S(1)}, u32[]{:S(2)}, u32[]{:S(2)}) collective-permute-start(bf16[224,256]{1,0:T(8,128)(2,1)S(1)} %pad_maximum_fusion.7), channel_id=1, source_target_pairs={{0,2},{1,3},{2,0},{3,1},{4,6},{5,7},{6,4},{7,5},{8,10},{9,11},{10,... | collective-permute-start | bytes 344072 | tf_op jit(solution)/shard_map/ppermute | solution.py:789
  206.9 1.5 collective-permute-start.35
  (54 other events, 226.4 us)

commit v5 on v4

--- a/solution.py
+++ b/solution.py
@@ -236,7 +236,8 @@
 
 def unpack_carry(ref):
     state = ref.shape[0] - HALO
-    return ref[0:state].astype(F32), ref[state : state + 1].astype(F32) + ref[state + 1 : state + 2].astype(F32)
+    fades = ref[state:].astype(F32)
+    return ref[0:state].astype(F32), fades[0:1] + fades[1:2]
 
 
 def join_kernel(forward, s_ref, own_ref, got_ref, out_ref):

time: 212 us -> 212 us (level)
  no operation moved by 1% of the time
where the time goes in v5:
time: 212 us; the launch traced here: 211 us
  Pallas kernels  82.3 us (39%)
  waiting for transfers between devices  66 us (31%)
  starting transfers between devices  34.8 us (16%)
  local copies, waits for them, and re-layouts  15.2 us (7%)
  other arithmetic  11.1 us (5%)
    pallas_call x16, Pallas kernels, call(): pl.pallas_call(kernel, grid=grid, out_shape=[kinds[at](s, d) if at in kin...  82.3 us
    ppermute x35, waiting for transfers between devices, swap(): return lax.ppermute(value, axis, [(i, i ^ mask) for i in range(size)])  66 us
    ppermute x35, starting transfers between devices, swap(): return lax.ppermute(value, axis, [(i, i ^ mask) for i in range(size)])  33.2 us
    unnamed x130, local copies, waits for them, and re-layouts  9.72 us
  transfers between devices with their start and end apart: 36, of which 18 were waited for; matrix products, arithmetic and copies ran while one was open for 5% of the time, Pallas kernels for 31%

profile of v5, /device:TPU:0, one launch (start us, length us, event | category | flops | bytes accessed | tf_op | source)
XLA Modules:
  0.0 211.4 jit_solution(3256187868058172435)
XLA Ops:
  0.8 2.0 constant_dynamic-update-slice_fusion.1
  4.7 3.0 %collective-permute-start = (f32[32,896]{1,0:T(8,128)S(1)}, f32[32,896]{1,0:T(8,128)S(1)}, u32[]{:S(2)}, u32[]{:S(2)}) collective-permute-start(f32[32,896]{1,0:T(8,128)S(1)} %fusion.26), channel_id=1, source_target_pairs={{0,2},{1,3},{2,0},{3,1},{4,6},{5,7},{6,4},{7,5},{8,10},{9,11},{10,... | collective-permute-start | bytes 344072 | tf_op jit(solution)/shard_map/ppermute | solution.py:790
  7.7 1.9 collective-permute-start.3
  9.6 1.6 collective-permute-done
  12.6 2.0 shard_map.288
  17.0 1.9 shard_map.289
  19.5 8.0 %shard_map.290 = (bf16[512,1536]{1,0:T(8,128)(2,1)}, bf16[528,1536]{1,0:T(8,128)(2,1)}, bf16[512,1536]{1,0:T(8,128)(2,1)}, f32[2,128,1536]{2,1,0:T(8,128)}, bf16...) custom-call(s32[8]{0:T(128)S(1)} %pad_add_fusion.s_ref, ...), custom_call_target="tpu_custom_call" | custom-call | flops 2400000000 | bytes 1800000 | tf_op jit(solution)/shard_map/pallas_call | solution.py:44
  27.5 8.9 %collective-permute-done.3.refs_0_.refs_2_ = bf16[768,768]{1,0:T(8,128)(2,1)S(1)} collective-permute-done((bf16[768,768]{1,0:T(8,128)(2,1)}, bf16[768,768]{1,0:T(8,128)(2,1)S(1)}, u32[]{:S(2)}, u32[]{:S(2)}) %collective-permute-start.3) | collective-permute-done | bytes 1179680 | tf_op jit(solution)/shard_map/ppermute | solution.py:790
  36.4 1.8 collective-permute-start.8
  39.2 6.2 %shard_map.291 = (bf16[512,1536]{1,0:T(8,128)(2,1)}, bf16[528,1536]{1,0:T(8,128)(2,1)}, bf16[512,1536]{1,0:T(8,128)(2,1)}, f32[2,128,1536]{2,1,0:T(8,128)}, bf16...) custom-call(s32[8]{0:T(128)S(1)} %pad_add_fusion.s_ref, ...), custom_call_target="tpu_custom_call", output_to_operand_aliasing={{0}: (8, {}), {1}: (9, {}), {2}: (10, {}), {3}: (11, {}), {... | custom-call | flops 2400000000 | bytes 1800000 | tf_op jit(solution)/shard_map/pallas_call | solution.py:44
  45.7 1.7 collective-permute-done.6.got_ref.near_ref
  48.1 4.0 %collective-permute-done.8.refs_2_ = bf16[384,768]{1,0:T(8,128)(2,1)S(1)} collective-permute-done((bf16[384,768]{1,0:T(8,128)(2,1)S(1)}, bf16[384,768]{1,0:T(8,128)(2,1)S(1)}, u32[]{:S(2)}, u32[]{:S(2)}) %collective-permute-start.8) | collective-permute-done | bytes 589856 | tf_op jit(solution)/shard_map/ppermute | solution.py:790
  52.6 1.7 collective-permute-start.10
  54.4 4.0 %shard_map.295.y_ref = f32[512,1536]{1,0:T(8,128)S(1)} custom-call(s32[8]{0:T(128)S(1)} %pad_add_fusion.s_ref, f32[12,8,512]{2,1,0:T(8,128)S(1)} %get-tuple-element.137.rowp_ref, f32[6,512,16]{2,1,0:T(8,128)S(1)} %get-tuple-element.115.colp_ref, f32[2,256,256]{2,1,0:T(8,128)S(1)} %get-tuple-element.138.cb_ref, bf16[512,1536]{1,0:T(8,128)(2,1)S(1)} %get-tuple-element.140.x_ref), custom_call_target="tpu_custom_call" | custom-call | flops 2000000000 | bytes 1500000 | tf_op jit(solution)/shard_map/pallas_call | solution.py:44
  58.5 2.4 %shard_map.293 = (bf16[512,1536]{1,0:T(8,128)(2,1)S(1)}, bf16[768,512]{1,0:T(8,128)(2,1)S(1)}) custom-call(s32[8]{0:T(128)S(1)} %pad_add_fusion.s_ref, bf16[512,768]{1,0:T(8,128)(2,1)S(1)} %copy-done.18, bf16[384,768]{1,0:T(8,128)(2,1)S(1)} %copy-done.19, bf16[384,768]{1,0:T(8,128)(2,1)S(1)} %collective-permute-done.7.refs_1_, ...), custom_call_target="tpu_custom_call" | custom-call | flops 1200000000 | bytes 900000 | tf_op jit(solution)/shard_map/pallas_call | solution.py:44
  60.9 3.8 %collective-permute-done.10.far_ref = bf16[144,1536]{1,0:T(8,128)(2,1)S(1)} collective-permute-done((bf16[144,1536]{1,0:T(8,128)(2,1)S(1)}, bf16[144,1536]{1,0:T(8,128)(2,1)S(1)}, u32[]{:S(2)}, u32[]{:S(2)}) %collective-permute-start.10) | collective-permute-done | bytes 442400 | tf_op jit(solution)/shard_map/ppermute | solution.py:790
  65.4 14.8 %shard_map.296 = (bf16[512,1536]{1,0:T(8,128)(2,1)}, bf16[512,1536]{1,0:T(8,128)(2,1)}, bf16[2,1536,384]{2,1,0:T(8,128)(2,1)}, bf16[2,1536,384]{2,1,0:T(8,128)(2...) custom-call(s32[8]{0:T(128)S(1)} %pad_add_fusion.s_ref, ...), custom_call_target="tpu_custom_call" | custom-call | flops 5600000000 | bytes 4200000 | tf_op jit(solution)/shard_map/pallas_call | solution.py:44
  81.4 1.8 collective-permute-done.11.got_ref.near_ref
  84.1 1.8 collective-permute-start.17
  86.0 9.3 %shard_map.299 = (bf16[512,1536]{1,0:T(8,128)(2,1)S(1)}, f32[32,512]{1,0:T(8,128)S(1)}, f32[512,128]{1,0:T(8,128)S(1)}, f32[512,128]{1,0:T(8,128)S(1)}) custom-call(s32[8]{0:T(128)} %copy-done.14, f32[12,8,512]{2,1,0:T(8,128)} %copy-done.24, f32[6,512,16]{2,1,0:T(8,128)} %copy-done.1, f32[2,256,256]{2,1,0:T(8,128)} %copy-done.36, ...), custom_call_target="tpu_custom_call" | custom-call | flops 3200000000 | bytes 2400000 | tf_op jit(solution)/shard_map/pallas_call | solution.py:44
  95.3 1.3 collective-permute-done.17.far_ref
  97.3 2.9 %convert_add_fusion = (f32[1,1536,384]{2,1,0:T(8,128)S(1)}, f32[1,1536,384]{2,1,0:T(8,128)S(1)}) fusion(bf16[2,1536,384]{2,1,0:T(8,128)(2,1)} %collective-permute-done.12, bf16[2,1536,384]{2,1,0:T(8,128)(2,1)} %get-tuple-element.144), kind=kLoop, calls=%fused_computation.4 | loop fusion | flops 3538944 | bytes 9437184 | tf_op jit(solution)/shard_map/add | solution.py:1031
  100.6 1.8 collective-permute-start.15
  102.5 1.6 collective-permute-start.13
  104.1 13.6 %shard_map.300 = (bf16[528,1536]{1,0:T(8,128)(2,1)S(1)}, f32[8,1536]{1,0:T(8,128)S(1)}, f32[32,512]{1,0:T(8,128)S(1)}, f32[8,1536]{1,0:T(8,128)S(1)}, f32[512,12...) custom-call(s32[8]{0:T(128)S(1)} %copy-done.15, f32[128,1536]{1,0:T(8,128)S(1)} %shard_map.298.back_in, ...), custom_call_target="tpu_custom_call" | custom-call | flops 4000000000 | bytes 3000000 | tf_op jit(solution)/shard_map/pallas_call | solution.py:44
  119.0 1.5 collective-permute-start.16
  120.8 1.6 collective-permute-start.14
  122.4 2.6 %shard_map.301 = (bf16[528,256]{1,0:T(8,128)(2,1)S(1)}, bf16[32,512]{1,0:T(8,128)(2,1)S(1)}, bf16[2,256,384]{2,1,0:T(8,128)(2,1)S(1)}, bf16[2,256,384]{2,1,0:T(8,128)(2,1)S(1)}) custom-call(s32[8]{0:T(128)S(1)} %copy-done.15, f32[512,128]{1,0:T(8,128)S(1)} %get-tuple-element.161.dbx_ref, f32[512,128]{1,0:T(8,128)S(1)} %get-tuple-element.162.dbin_ref, ...), custom_call_target="tpu_custom_call" | custom-call | flops 1600000000 | bytes 1200000 | tf_op jit(solution)/shard_map/pallas_call | solution.py:44
  125.3 1.9 collective-permute-done.16
  127.3 2.9 %collective-permute-done.14 = bf16[384,384]{1,0:T(8,128)(2,1)S(1)} collective-permute-done((bf16[384,384]{1,0:T(8,128)(2,1)S(1)}, bf16[384,384]{1,0:T(8,128)(2,1)S(1)}, u32[]{:S(2)}, u32[]{:S(2)}) %collective-permute-start.14) | collective-permute-done | bytes 294944 | tf_op jit(solution)/shard_map/ppermute | solution.py:790
  132.4 1.6 collective-permute-start.23
  134.8 1.6 collective-permute-start.20
  136.4 9.7 %shard_map.302 = (f32[512,768]{1,0:T(8,128)}, f32[16,768]{1,0:T(8,128)S(1)}, f32[8,384]{1,0:T(8,128)S(1)}) custom-call(s32[8]{0:T(128)} %copy-done.14, bf16[512,768]{1,0:T(8,128)(2,1)} %hid_ref.5, bf16[16,768]{1,0:T(8,128)(2,1)} %copy-done.13, bf16[512,768]{1,0:T(8,128)(2,1)} %cot_ref.3, f32[1,768]{1,0:T(1,128)} %copy-done.16, ...), custom_call_target="tpu_custom_call" | custom-call | flops 3600000000 | bytes 2700000 | tf_op jit(solution)/shard_map/pallas_call | solution.py:44
  146.2 2.7 %collective-permute-start.21 = (bf16[384,384]{1,0:T(8,128)(2,1)S(1)}, bf16[384,384]{1,0:T(8,128)(2,1)S(1)}, u32[]{:S(2)}, u32[]{:S(2)}) collective-permute-start(bf16[384,384]{1,0:T(8,128)(2,1)S(1)} %fusion.15), channel_id=1, source_target_pairs={{0,16},{4,20},{8,24},{12,28},{16,0},{20,4},{24,8},{28,12},{1,17},{... | collective-permute-start | bytes 884744 | tf_op jit(solution)/shard_map/ppermute | solution.py:790
  149.7 1.2 collective-permute-start.25
  150.9 10.3 %collective-permute-done.21 = bf16[384,384]{1,0:T(8,128)(2,1)S(1)} collective-permute-done((bf16[384,384]{1,0:T(8,128)(2,1)S(1)}, bf16[384,384]{1,0:T(8,128)(2,1)S(1)}, u32[]{:S(2)}, u32[]{:S(2)}) %collective-permute-start.21) | collective-permute-done | bytes 294944 | tf_op jit(solution)/shard_map/ppermute | solution.py:790
  161.6 1.6 collective-permute-start.26
  163.2 2.1 collective-permute-start.29
  165.3 5.0 %shard_map.303 = bf16[512,768]{1,0:T(8,128)(2,1)} custom-call(s32[8]{0:T(128)} %copy-done.14, bf16[512,768]{1,0:T(8,128)(2,1)} %hid_ref.5, bf16[512,1536]{1,0:T(8,128)(2,1)} %get-tuple-element.191.ny_ref, bf16[384,768]{1,0:T(8,128)(2,1)} %refs_0_.3, bf16[384,768]{1,0:T(8,128)(2,1)} %copy-done.22, bf16[384,768]{1,0:T(8,128)(2,1)} %copy-done.20, ...), custom_call_target="tpu_custom_call" | custom-call | flops 1600000000 | bytes 1200000 | tf_op jit(solution)/shard_map/pallas_call | solution.py:44
  170.3 1.2 collective-permute-start.28
  171.5 4.6 %collective-permute-done.29 = bf16[384,384]{1,0:T(8,128)(2,1)S(1)} collective-permute-done((bf16[384,384]{1,0:T(8,128)(2,1)S(1)}, bf16[384,384]{1,0:T(8,128)(2,1)S(1)}, u32[]{:S(2)}, u32[]{:S(2)}) %collective-permute-start.29) | collective-permute-done | bytes 294944 | tf_op jit(solution)/shard_map/ppermute | solution.py:790
  176.9 6.8 %collective-permute-done.28 = bf16[272,384]{1,0:T(8,128)(2,1)S(1)} collective-permute-done((bf16[272,384]{1,0:T(8,128)(2,1)S(1)}, bf16[272,384]{1,0:T(8,128)(2,1)S(1)}, u32[]{:S(2)}, u32[]{:S(2)}) %collective-permute-start.28) | collective-permute-done | bytes 208928 | tf_op jit(solution)/shard_map/ppermute | solution.py:790
  183.8 1.4 add_dynamic-update-slice_fusion
  185.2 5.6 %collective-permute-done.30 = bf16[272,384]{1,0:T(8,128)(2,1)S(1)} collective-permute-done((bf16[272,384]{1,0:T(8,128)(2,1)S(1)}, bf16[272,384]{1,0:T(8,128)(2,1)S(1)}, u32[]{:S(2)}, u32[]{:S(2)}) %collective-permute-start.30) | collective-permute-done | bytes 208928 | tf_op jit(solution)/shard_map/ppermute | solution.py:790
  191.6 1.5 collective-permute-start.34
  194.4 7.4 %collective-permute-done.34 = bf16[256,384]{1,0:T(8,128)(2,1)S(1)} collective-permute-done((bf16[256,384]{1,0:T(8,128)(2,1)S(1)}, bf16[256,384]{1,0:T(8,128)(2,1)S(1)}, u32[]{:S(2)}, u32[]{:S(2)}) %collective-permute-start.34) | collective-permute-done | bytes 196640 | tf_op jit(solution)/shard_map/ppermute | solution.py:790
  205.7 1.1 collective-permute-done.33
  207.0 1.4 copy.53
  (270 shorter events, 28.5 us)
Async XLA Ops:
  0.7 10.5 %copy-start.62 = (s32[1,3]{1,0:T(1,128)S(1)}, s32[1,3]{1,0:T(1,128)}, u32[]{:S(2)}) copy-start(s32[1,3]{1,0:T(1,128)} %param.20) | copy-start | bytes 40
  0.8 10.6 %copy-start.54 = (f32[768]{0:T(1024)S(1)}, f32[768]{0:T(1024)}, u32[]{:S(2)}) copy-start(f32[768]{0:T(1024)} %param.21) | copy-start | bytes 9220
  3.7 15.8 %collective-permute-start.4 = (bf16[768,768]{1,0:T(8,128)(2,1)}, bf16[768,768]{1,0:T(8,128)(2,1)}, u32[]{:S(2)}, u32[]{:S(2)}) collective-permute-start(bf16[768,768]{1,0:T(8,128)(2,1)} %constant_dynamic-update-slice_fusion.refs_0_), channel_id=1, source_target_pairs={{0,1},{1,0},{2,3},{3,2},{4,5},{5,4},{6,7},{7,6},{8,9},{9,8},{10,11... | collective-permute-start | bytes 3538952 | tf_op jit(solution)/shard_map/ppermute | solution.py:790
  4.6 3.1 %collective-permute-start.2 = (f32[32,896]{1,0:T(8,128)S(1)}, f32[32,896]{1,0:T(8,128)S(1)}, u32[]{:S(2)}, u32[]{:S(2)}) collective-permute-start(f32[32,896]{1,0:T(8,128)S(1)} %fusion.26), channel_id=1, source_target_pairs={{0,1},{1,0},{2,3},{3,2},{4,5},{5,4},{6,7},{7,6},{8,9},{9,8},{10,11... | collective-permute-start | bytes 344072 | tf_op jit(solution)/shard_map/ppermute | solution.py:790
  4.7 6.5 %collective-permute-start = (f32[32,896]{1,0:T(8,128)S(1)}, f32[32,896]{1,0:T(8,128)S(1)}, u32[]{:S(2)}, u32[]{:S(2)}) collective-permute-start(f32[32,896]{1,0:T(8,128)S(1)} %fusion.26), channel_id=1, source_target_pairs={{0,2},{1,3},{2,0},{3,1},{4,6},{5,7},{6,4},{7,5},{8,10},{9,11},{10,... | collective-permute-start | bytes 344072 | tf_op jit(solution)/shard_map/ppermute | solution.py:790
  7.7 28.7 %collective-permute-start.3 = (bf16[768,768]{1,0:T(8,128)(2,1)}, bf16[768,768]{1,0:T(8,128)(2,1)S(1)}, u32[]{:S(2)}, u32[]{:S(2)}) collective-permute-start(bf16[768,768]{1,0:T(8,128)(2,1)} %constant_dynamic-update-slice_fusion.refs_0_), channel_id=1, source_target_pairs={{0,2},{1,3},{2,0},{3,1},{4,6},{5,7},{6,4},{7,5},{8,10},{9,11},{10,... | collective-permute-start | bytes 3538952 | tf_op jit(solution)/shard_map/ppermute | solution.py:790
  11.3 1.3 collective-permute-start.1
  11.3 71.8 %copy-start.14 = (s32[8]{0:T(128)}, s32[8]{0:T(128)S(1)}, u32[]{:S(2)}) copy-start(s32[8]{0:T(128)S(1)} %pad_add_fusion.s_ref) | copy-start | bytes 100
  16.9 22.3 %copy-start.10 = (bf16[528,768]{1,0:T(8,128)(2,1)}, bf16[528,768]{1,0:T(8,128)(2,1)S(1)}, u32[]{:S(2)}) copy-start(bf16[528,768]{1,0:T(8,128)(2,1)S(1)} %get-tuple-element.113.nx_ref) | copy-start | bytes 2433028
  16.9 48.5 %copy-start.28 = (bf16[768,512]{1,0:T(8,128)(2,1)}, bf16[768,512]{1,0:T(8,128)(2,1)S(1)}, u32[]{:S(2)}) copy-start(bf16[768,512]{1,0:T(8,128)(2,1)S(1)} %get-tuple-element.136.nt_ref) | copy-start | bytes 2359300
  16.9 48.5 %copy-start.41 = (bf16[512,128]{1,0:T(8,128)(2,1)}, bf16[512,128]{1,0:T(8,128)(2,1)S(1)}, u32[]{:S(2)}) copy-start(bf16[512,128]{1,0:T(8,128)(2,1)S(1)} %get-tuple-element.134.c_ref) | copy-start | bytes 393220
  16.9 105.4 %copy-start.12 = (f32[32,896]{1,0:T(8,128)}, f32[32,896]{1,0:T(8,128)S(1)}, u32[]{:S(2)}) copy-start(f32[32,896]{1,0:T(8,128)S(1)} %select_maximum_fusion.hp_ref) | copy-start | bytes 344068
  19.5 34.9 %copy-start.24 = (f32[12,8,512]{2,1,0:T(8,128)}, f32[12,8,512]{2,1,0:T(8,128)S(1)}, u32[]{:S(2)}) copy-start(f32[12,8,512]{2,1,0:T(8,128)S(1)} %get-tuple-element.137.rowp_ref) | copy-start | bytes 589828
  19.5 45.9 %copy-start.1 = (f32[6,512,16]{2,1,0:T(8,128)}, f32[6,512,16]{2,1,0:T(8,128)S(1)}, u32[]{:S(2)}) copy-start(f32[6,512,16]{2,1,0:T(8,128)S(1)} %get-tuple-element.115.colp_ref) | copy-start | bytes 589828
  19.5 16.9 %copy-start.19 = (bf16[384,768]{1,0:T(8,128)(2,1)S(1)}, bf16[384,768]{1,0:T(8,128)(2,1)}, u32[]{:S(2)}) copy-start(bf16[384,768]{1,0:T(8,128)(2,1)} %refs_0_.3) | copy-start | bytes 1769476
  36.4 2.8 %collective-permute-start.5 = (bf16[768,768]{1,0:T(8,128)(2,1)S(1)}, bf16[768,768]{1,0:T(8,128)(2,1)S(1)}, u32[]{:S(2)}, u32[]{:S(2)}) collective-permute-start(bf16[768,768]{1,0:T(8,128)(2,1)S(1)} %collective-permute-done.3.refs_0_.refs_2_), channel_id=1, source_target_pairs={{0,1},{1,0},{2,3},{3,2},{4,5},{5,4},{6,7},{7,6},{8,9},{9,8},{10,11... | collective-permute-start | bytes 3538952 | tf_op jit(solution)/shard_map/ppermute | solution.py:790
  36.4 15.7 %collective-permute-start.8 = (bf16[384,768]{1,0:T(8,128)(2,1)S(1)}, bf16[384,768]{1,0:T(8,128)(2,1)S(1)}, u32[]{:S(2)}, u32[]{:S(2)}) collective-permute-start(bf16[384,768]{1,0:T(8,128)(2,1)S(1)} %copy-done.19), channel_id=1, source_target_pairs={{0,2},{1,3},{2,0},{3,1},{4,6},{5,7},{6,4},{7,5},{8,10},{9,11},{10,... | collective-permute-start | bytes 1769480 | tf_op jit(solution)/shard_map/ppermute | solution.py:790
  45.5 19.9 %copy-start.6 = (bf16[512,1536]{1,0:T(8,128)(2,1)}, bf16[512,1536]{1,0:T(8,128)(2,1)S(1)}, u32[]{:S(2)}) copy-start(bf16[512,1536]{1,0:T(8,128)(2,1)S(1)} %get-tuple-element.140.x_ref) | copy-start | bytes 4718596
  45.5 1.9 collective-permute-start.6
  52.1 6.3 %collective-permute-start.9 = (bf16[384,768]{1,0:T(8,128)(2,1)S(1)}, bf16[384,768]{1,0:T(8,128)(2,1)S(1)}, u32[]{:S(2)}, u32[]{:S(2)}) collective-permute-start(bf16[384,768]{1,0:T(8,128)(2,1)S(1)} %collective-permute-done.8.refs_2_), channel_id=1, source_target_pairs={{0,1},{1,0},{2,3},{3,2},{4,5},{5,4},{6,7},{7,6},{8,9},{9,8},{10,11... | collective-permute-start | bytes 1769480 | tf_op jit(solution)/shard_map/ppermute | solution.py:790
  52.1 6.3 %collective-permute-start.7 = (bf16[384,768]{1,0:T(8,128)(2,1)S(1)}, bf16[384,768]{1,0:T(8,128)(2,1)S(1)}, u32[]{:S(2)}, u32[]{:S(2)}) collective-permute-start(bf16[384,768]{1,0:T(8,128)(2,1)S(1)} %copy-done.19), channel_id=1, source_target_pairs={{0,1},{1,0},{2,3},{3,2},{4,5},{5,4},{6,7},{7,6},{8,9},{9,8},{10,11... | collective-permute-start | bytes 1769480 | tf_op jit(solution)/shard_map/ppermute | solution.py:790
  52.6 12.1 %collective-permute-start.10 = (bf16[144,1536]{1,0:T(8,128)(2,1)S(1)}, bf16[144,1536]{1,0:T(8,128)(2,1)S(1)}, u32[]{:S(2)}, u32[]{:S(2)}) collective-permute-start(bf16[144,1536]{1,0:T(8,128)(2,1)S(1)} %shard_map.292), channel_id=1, source_target_pairs={{0,2},{1,3},{2,0},{3,1},{4,6},{5,7},{6,4},{7,5},{8,10},{9,11},{10,... | collective-permute-start | bytes 1327112 | tf_op jit(solution)/shard_map/ppermute | solution.py:790
  81.4 1.8 collective-permute-start.11
  83.9 13.3 %collective-permute-start.12 = (bf16[2,1536,384]{2,1,0:T(8,128)(2,1)}, bf16[2,1536,384]{2,1,0:T(8,128)(2,1)}, u32[]{:S(2)}, u32[]{:S(2)}) collective-permute-start(bf16[2,1536,384]{2,1,0:T(8,128)(2,1)} %get-tuple-element.148), channel_id=1, source_target_pairs={{0,1},{1,0},{2,3},{3,2},{4,5},{5,4},{6,7},{7,6},{8,9},{9,8},{10,11... | collective-permute-start | bytes 7077896 | tf_op jit(solution)/shard_map/ppermute | solution.py:790
  84.1 12.4 %collective-permute-start.17 = (bf16[144,1536]{1,0:T(8,128)(2,1)S(1)}, bf16[144,1536]{1,0:T(8,128)(2,1)S(1)}, u32[]{:S(2)}, u32[]{:S(2)}) collective-permute-start(bf16[144,1536]{1,0:T(8,128)(2,1)S(1)} %shard_map.297), channel_id=1, source_target_pairs={{0,2},{1,3},{2,0},{3,1},{4,6},{5,7},{6,4},{7,5},{8,10},{9,11},{10,... | collective-permute-start | bytes 1327112 | tf_op jit(solution)/shard_map/ppermute | solution.py:790
  86.0 10.6 %copy-start.15 = (s32[8]{0:T(128)S(1)}, s32[8]{0:T(128)}, u32[]{:S(2)}) copy-start(s32[8]{0:T(128)} %copy-done.14) | copy-start | bytes 100
  100.6 17.1 %collective-permute-start.15 = (bf16[2,384,384]{2,1,0:T(8,128)(2,1)S(1)}, bf16[2,384,384]{2,1,0:T(8,128)(2,1)S(1)}, u32[]{:S(2)}, u32[]{:S(2)}) collective-permute-start(bf16[2,384,384]{2,1,0:T(8,128)(2,1)S(1)} %fusion.13), channel_id=1, source_target_pairs={{0,4},{4,0},{8,12},{12,8},{16,20},{20,16},{24,28},{28,24},{1,5},{5... | collective-permute-start | bytes 1769480 | tf_op jit(solution)/shard_map/ppermute | solution.py:790
  102.5 18.1 %collective-permute-start.13 = (bf16[768,384]{1,0:T(8,128)(2,1)S(1)}, bf16[768,384]{1,0:T(8,128)(2,1)S(1)}, u32[]{:S(2)}, u32[]{:S(2)}) collective-permute-start(bf16[768,384]{1,0:T(8,128)(2,1)S(1)} %fusion.12), channel_id=1, source_target_pairs={{0,2},{1,3},{2,0},{3,1},{4,6},{5,7},{6,4},{7,5},{8,10},{9,11},{10,... | collective-permute-start | bytes 1769480 | tf_op jit(solution)/shard_map/ppermute | solution.py:790
  119.0 8.2 %collective-permute-start.16 = (bf16[384,384]{1,0:T(8,128)(2,1)S(1)}, bf16[384,384]{1,0:T(8,128)(2,1)S(1)}, u32[]{:S(2)}, u32[]{:S(2)}) collective-permute-start(bf16[384,384]{1,0:T(8,128)(2,1)S(1)} %fusion.22), channel_id=1, source_target_pairs={{0,2},{1,3},{2,0},{3,1},{4,6},{5,7},{6,4},{7,5},{8,10},{9,11},{10,... | collective-permute-start | bytes 884744 | tf_op jit(solution)/shard_map/ppermute | solution.py:790
  120.7 9.9 %collective-permute-start.18 = (bf16[2,768,384]{2,1,0:T(8,128)(2,1)S(1)}, bf16[2,768,384]{2,1,0:T(8,128)(2,1)S(1)}, u32[]{:S(2)}, u32[]{:S(2)}) collective-permute-start(bf16[2,768,384]{2,1,0:T(8,128)(2,1)S(1)} %copy-done.63), channel_id=1, source_target_pairs={{0,1},{1,0},{2,3},{3,2},{4,5},{5,4},{6,7},{7,6},{8,9},{9,8},{10,11... | collective-permute-start | bytes 3538952 | tf_op jit(solution)/shard_map/ppermute | solution.py:790
  120.8 9.5 %collective-permute-start.14 = (bf16[384,384]{1,0:T(8,128)(2,1)S(1)}, bf16[384,384]{1,0:T(8,128)(2,1)S(1)}, u32[]{:S(2)}, u32[]{:S(2)}) collective-permute-start(bf16[384,384]{1,0:T(8,128)(2,1)S(1)} %fusion.20), channel_id=1, source_target_pairs={{0,4},{4,0},{8,12},{12,8},{16,20},{20,16},{24,28},{28,24},{1,5},{5... | collective-permute-start | bytes 884744 | tf_op jit(solution)/shard_map/ppermute | solution.py:790
  125.1 5.4 %collective-permute-start.19 = (bf16[2,256,384]{2,1,0:T(8,128)(2,1)S(1)}, bf16[2,256,384]{2,1,0:T(8,128)(2,1)S(1)}, u32[]{:S(2)}, u32[]{:S(2)}) collective-permute-start(bf16[2,256,384]{2,1,0:T(8,128)(2,1)S(1)} %get-tuple-element.177), channel_id=1, source_target_pairs={{0,1},{1,0},{2,3},{3,2},{4,5},{5,4},{6,7},{7,6},{8,9},{9,8},{10,11... | collective-permute-start | bytes 1179656 | tf_op jit(solution)/shard_map/ppermute | solution.py:790
  132.4 16.5 %collective-permute-start.23 = (bf16[2,256,384]{2,1,0:T(8,128)(2,1)S(1)}, bf16[2,256,384]{2,1,0:T(8,128)(2,1)S(1)}, u32[]{:S(2)}, u32[]{:S(2)}) collective-permute-start(bf16[2,256,384]{2,1,0:T(8,128)(2,1)S(1)} %fusion.18), channel_id=1, source_target_pairs={{0,4},{4,0},{8,12},{12,8},{16,20},{20,16},{24,28},{28,24},{1,5},{5... | collective-permute-start | bytes 1179656 | tf_op jit(solution)/shard_map/ppermute | solution.py:790
  133.9 15.0 %collective-permute-start.22 = (bf16[512,384]{1,0:T(8,128)(2,1)S(1)}, bf16[512,384]{1,0:T(8,128)(2,1)S(1)}, u32[]{:S(2)}, u32[]{:S(2)}) collective-permute-start(bf16[512,384]{1,0:T(8,128)(2,1)S(1)} %fusion.17), channel_id=1, source_target_pairs={{0,2},{1,3},{2,0},{3,1},{4,6},{5,7},{6,4},{7,5},{8,10},{9,11},{10,... | collective-permute-start | bytes 1179656 | tf_op jit(solution)/shard_map/ppermute | solution.py:790
  134.8 11.3 %collective-permute-start.20 = (bf16[384,384]{1,0:T(8,128)(2,1)S(1)}, bf16[384,384]{1,0:T(8,128)(2,1)S(1)}, u32[]{:S(2)}, u32[]{:S(2)}) collective-permute-start(bf16[384,384]{1,0:T(8,128)(2,1)S(1)} %fusion.21), channel_id=1, source_target_pairs={{0,8},{4,12},{8,0},{12,4},{16,24},{20,28},{24,16},{28,20},{1,9},{5... | collective-permute-start | bytes 884744 | tf_op jit(solution)/shard_map/ppermute | solution.py:790
  146.2 15.0 %collective-permute-start.21 = (bf16[384,384]{1,0:T(8,128)(2,1)S(1)}, bf16[384,384]{1,0:T(8,128)(2,1)S(1)}, u32[]{:S(2)}, u32[]{:S(2)}) collective-permute-start(bf16[384,384]{1,0:T(8,128)(2,1)S(1)} %fusion.15), channel_id=1, source_target_pairs={{0,16},{4,20},{8,24},{12,28},{16,0},{20,4},{24,8},{28,12},{1,17},{... | collective-permute-start | bytes 884744 | tf_op jit(solution)/shard_map/ppermute | solution.py:790
  149.1 12.2 %collective-permute-start.24 = (bf16[256,384]{1,0:T(8,128)(2,1)S(1)}, bf16[256,384]{1,0:T(8,128)(2,1)S(1)}, u32[]{:S(2)}, u32[]{:S(2)}) collective-permute-start(bf16[256,384]{1,0:T(8,128)(2,1)S(1)} %fusion.24), channel_id=1, source_target_pairs={{0,4},{4,0},{8,12},{12,8},{16,20},{20,16},{24,28},{28,24},{1,5},{5... | collective-permute-start | bytes 589832 | tf_op jit(solution)/shard_map/ppermute | solution.py:790
  149.7 11.6 %collective-permute-start.25 = (bf16[256,384]{1,0:T(8,128)(2,1)S(1)}, bf16[256,384]{1,0:T(8,128)(2,1)S(1)}, u32[]{:S(2)}, u32[]{:S(2)}) collective-permute-start(bf16[256,384]{1,0:T(8,128)(2,1)S(1)} %fusion.25), channel_id=1, source_target_pairs={{0,2},{1,3},{2,0},{3,1},{4,6},{5,7},{6,4},{7,5},{8,10},{9,11},{10,... | collective-permute-start | bytes 589832 | tf_op jit(solution)/shard_map/ppermute | solution.py:790
  161.6 8.7 %collective-permute-start.27 = (bf16[272,384]{1,0:T(8,128)(2,1)S(1)}, bf16[272,384]{1,0:T(8,128)(2,1)S(1)}, u32[]{:S(2)}, u32[]{:S(2)}) collective-permute-start(bf16[272,384]{1,0:T(8,128)(2,1)S(1)} %fusion.23), channel_id=1, source_target_pairs={{0,8},{4,12},{8,0},{12,4},{16,24},{20,28},{24,16},{28,20},{1,9},{5... | collective-permute-start | bytes 626696 | tf_op jit(solution)/shard_map/ppermute | solution.py:790
  161.6 22.2 %collective-permute-start.26 = (f32[16,768]{1,0:T(8,128)S(1)}, f32[16,768]{1,0:T(8,128)S(1)}, u32[]{:S(2)}, u32[]{:S(2)}) collective-permute-start(f32[16,768]{1,0:T(8,128)S(1)} %get-tuple-element.185), channel_id=1, source_target_pairs={{1,0},{2,1},{3,2},{5,4},{6,5},{7,6},{9,8},{10,9},{11,10},{13,12},{... | collective-permute-start | bytes 147464 | tf_op jit(solution)/shard_map/ppermute | solution.py:1139
  163.2 12.9 %collective-permute-start.29 = (bf16[384,384]{1,0:T(8,128)(2,1)S(1)}, bf16[384,384]{1,0:T(8,128)(2,1)S(1)}, u32[]{:S(2)}, u32[]{:S(2)}) collective-permute-start(bf16[384,384]{1,0:T(8,128)(2,1)S(1)} %add_convert_fusion), channel_id=1, source_target_pairs={{0,8},{4,12},{8,0},{12,4},{16,24},{20,28},{24,16},{28,20},{1,9},{5... | collective-permute-start | bytes 884744 | tf_op jit(solution)/shard_map/ppermute | solution.py:790
  170.3 13.4 %collective-permute-start.28 = (bf16[272,384]{1,0:T(8,128)(2,1)S(1)}, bf16[272,384]{1,0:T(8,128)(2,1)S(1)}, u32[]{:S(2)}, u32[]{:S(2)}) collective-permute-start(bf16[272,384]{1,0:T(8,128)(2,1)S(1)} %fusion.16), channel_id=1, source_target_pairs={{0,16},{4,20},{8,24},{12,28},{16,0},{20,4},{24,8},{28,12},{1,17},{... | collective-permute-start | bytes 626696 | tf_op jit(solution)/shard_map/ppermute | solution.py:790
  176.3 14.7 %collective-permute-start.31 = (bf16[768,384]{1,0:T(8,128)(2,1)S(1)}, bf16[768,384]{1,0:T(8,128)(2,1)S(1)}, u32[]{:S(2)}, u32[]{:S(2)}) collective-permute-start(bf16[768,384]{1,0:T(8,128)(2,1)S(1)} %pad_maximum_fusion.3), channel_id=1, source_target_pairs={{0,4},{4,0},{8,12},{12,8},{16,20},{20,16},{24,28},{28,24},{1,5},{5... | collective-permute-start | bytes 1769480 | tf_op jit(solution)/shard_map/ppermute | solution.py:790
  183.7 7.1 %collective-permute-start.30 = (bf16[272,384]{1,0:T(8,128)(2,1)S(1)}, bf16[272,384]{1,0:T(8,128)(2,1)S(1)}, u32[]{:S(2)}, u32[]{:S(2)}) collective-permute-start(bf16[272,384]{1,0:T(8,128)(2,1)S(1)} %add_convert_fusion.1), channel_id=1, source_target_pairs={{0,8},{4,12},{8,0},{12,4},{16,24},{20,28},{24,16},{28,20},{1,9},{5... | collective-permute-start | bytes 626696 | tf_op jit(solution)/shard_map/ppermute | solution.py:790
  191.0 10.8 %collective-permute-start.32 = (bf16[288,384]{1,0:T(8,128)(2,1)S(1)}, bf16[288,384]{1,0:T(8,128)(2,1)S(1)}, u32[]{:S(2)}, u32[]{:S(2)}) collective-permute-start(bf16[288,384]{1,0:T(8,128)(2,1)S(1)} %slice.284), channel_id=1, source_target_pairs={{0,4},{4,0},{8,12},{12,8},{16,20},{20,16},{24,28},{28,24},{1,5},{5... | collective-permute-start | bytes 663560 | tf_op jit(solution)/shard_map/ppermute | solution.py:790
  191.6 10.2 %collective-permute-start.34 = (bf16[256,384]{1,0:T(8,128)(2,1)S(1)}, bf16[256,384]{1,0:T(8,128)(2,1)S(1)}, u32[]{:S(2)}, u32[]{:S(2)}) collective-permute-start(bf16[256,384]{1,0:T(8,128)(2,1)S(1)} %slice.295), channel_id=1, source_target_pairs={{0,4},{4,0},{8,12},{12,8},{16,20},{20,16},{24,28},{28,24},{1,5},{5... | collective-permute-start | bytes 589832 | tf_op jit(solution)/shard_map/ppermute | solution.py:790
  202.0 4.9 %collective-permute-start.33 = (bf16[224,256]{1,0:T(8,128)(2,1)S(1)}, bf16[224,256]{1,0:T(8,128)(2,1)S(1)}, u32[]{:S(2)}, u32[]{:S(2)}) collective-permute-start(bf16[224,256]{1,0:T(8,128)(2,1)S(1)} %pad_maximum_fusion.7), channel_id=1, source_target_pairs={{0,2},{1,3},{2,0},{3,1},{4,6},{5,7},{6,4},{7,5},{8,10},{9,11},{10,... | collective-permute-start | bytes 344072 | tf_op jit(solution)/shard_map/ppermute | solution.py:790
  206.9 1.5 collective-permute-start.35
  (54 other events, 226.5 us)

commit v6 on v5

--- a/solution.py
+++ b/solution.py
@@ -1187,7 +1187,12 @@
     grad_gate = a_gate.astype(F32)
     cut = b_all.shape[0] - 32 - 256
     *b_rows, gain_all = unhalve(b_all[cut:], [256, 32])
-    b_rows = unhalve(b_all[:cut], [cut]) + b_rows
+    if plain:
+        begin = depth + 32 - 2 * cut
+        own_rows = b_rows[-1][begin : begin + share_rows, :side]
+        b_rows = unhalve(b_all[:cut], [cut], after(swap(b_all[:cut], "dp", 1), own_rows)) + b_rows
+    else:
+        b_rows = unhalve(b_all[:cut], [cut]) + b_rows
     if not plain:
         *b_rows, gain_all = unhalve(b_all, [cut + 256, 32])
     b_all = jnp.concatenate(b_rows, axis=0)
@@ -1197,7 +1202,7 @@
     small = b_all[depth:].astype(F32)
     grad_step = jnp.concatenate([small[8 + j * share : 8 + (j + 1) * share].T for j in range(depth // wide)], axis=0)
     if plain:
-        own = b_all[depth + 32 : depth + 32 + share_rows, :side]
+        own = own_rows
     else:
         own = b_all[depth + 32 : depth + 240].reshape(-1)[: share_rows * side].reshape(share_rows, side)
     smaller = (grad_value, grad_step, small[0:4], small[4], small[5], *[small[24 : 24 + share, at] for at in range(3)])

time: 212 us -> 209 us (0.986)
  transfers between devices with their start and end apart: 36 -> 36, of which waited for: 18 -> 19; matrix products, arithmetic and copies ran while one was open for 5% -> 4% of each run, Pallas kernels for 31% -> 32%
where the time goes in v6:
time: 209 us
  Pallas kernels  82.3 us (39%)
  waiting for transfers between devices  64.5 us (31%)
  starting transfers between devices  33.8 us (16%)
  local copies, waits for them, and re-layouts  15.2 us (7%)
  other arithmetic  11.1 us (5%)
    pallas_call x16, Pallas kernels, call(): pl.pallas_call(kernel, grid=grid, out_shape=[kinds[at](s, d) if at in kin...  82.3 us
    ppermute x35, waiting for transfers between devices, swap(): return lax.ppermute(value, axis, [(i, i ^ mask) for i in range(size)])  64.5 us
    ppermute x35, starting transfers between devices, swap(): return lax.ppermute(value, axis, [(i, i ^ mask) for i in range(size)])  32.3 us
    unnamed x130, local copies, waits for them, and re-layouts  9.72 us
  transfers between devices with their start and end apart: 36, of which 19 were waited for; matrix products, arithmetic and copies ran while one was open for 4% of the time, Pallas kernels for 32%

profile of v6, /device:TPU:0, one launch (start us, length us, event | category | flops | bytes accessed | tf_op | source)
XLA Modules:
  0.0 209.0 jit_solution(17365454653897263735)
XLA Ops:
  0.8 2.0 constant_dynamic-update-slice_fusion.1
  4.7 3.0 %collective-permute-start = (f32[32,896]{1,0:T(8,128)S(1)}, f32[32,896]{1,0:T(8,128)S(1)}, u32[]{:S(2)}, u32[]{:S(2)}) collective-permute-start(f32[32,896]{1,0:T(8,128)S(1)} %fusion.26), channel_id=1, source_target_pairs={{0,2},{1,3},{2,0},{3,1},{4,6},{5,7},{6,4},{7,5},{8,10},{9,11},{10,... | collective-permute-start | bytes 344072 | tf_op jit(solution)/shard_map/ppermute | solution.py:790
  7.7 1.9 collective-permute-start.3
  9.6 1.6 collective-permute-done
  12.6 2.0 shard_map.288
  16.9 1.9 shard_map.289
  19.5 8.0 %shard_map.290 = (bf16[512,1536]{1,0:T(8,128)(2,1)}, bf16[528,1536]{1,0:T(8,128)(2,1)}, bf16[512,1536]{1,0:T(8,128)(2,1)}, f32[2,128,1536]{2,1,0:T(8,128)}, bf16...) custom-call(s32[8]{0:T(128)S(1)} %pad_add_fusion.s_ref, ...), custom_call_target="tpu_custom_call" | custom-call | flops 2400000000 | bytes 1800000 | tf_op jit(solution)/shard_map/pallas_call | solution.py:44
  27.5 8.9 %collective-permute-done.3.refs_0_.refs_2_ = bf16[768,768]{1,0:T(8,128)(2,1)S(1)} collective-permute-done((bf16[768,768]{1,0:T(8,128)(2,1)}, bf16[768,768]{1,0:T(8,128)(2,1)S(1)}, u32[]{:S(2)}, u32[]{:S(2)}) %collective-permute-start.3) | collective-permute-done | bytes 1179680 | tf_op jit(solution)/shard_map/ppermute | solution.py:790
  36.4 1.8 collective-permute-start.8
  39.2 6.2 %shard_map.291 = (bf16[512,1536]{1,0:T(8,128)(2,1)}, bf16[528,1536]{1,0:T(8,128)(2,1)}, bf16[512,1536]{1,0:T(8,128)(2,1)}, f32[2,128,1536]{2,1,0:T(8,128)}, bf16...) custom-call(s32[8]{0:T(128)S(1)} %pad_add_fusion.s_ref, ...), custom_call_target="tpu_custom_call", output_to_operand_aliasing={{0}: (8, {}), {1}: (9, {}), {2}: (10, {}), {3}: (11, {}), {... | custom-call | flops 2400000000 | bytes 1800000 | tf_op jit(solution)/shard_map/pallas_call | solution.py:44
  45.7 1.7 collective-permute-done.6.got_ref.near_ref
  48.1 4.0 %collective-permute-done.8.refs_2_ = bf16[384,768]{1,0:T(8,128)(2,1)S(1)} collective-permute-done((bf16[384,768]{1,0:T(8,128)(2,1)S(1)}, bf16[384,768]{1,0:T(8,128)(2,1)S(1)}, u32[]{:S(2)}, u32[]{:S(2)}) %collective-permute-start.8) | collective-permute-done | bytes 589856 | tf_op jit(solution)/shard_map/ppermute | solution.py:790
  52.6 1.7 collective-permute-start.10
  54.4 4.0 %shard_map.295.y_ref = f32[512,1536]{1,0:T(8,128)S(1)} custom-call(s32[8]{0:T(128)S(1)} %pad_add_fusion.s_ref, f32[12,8,512]{2,1,0:T(8,128)S(1)} %get-tuple-element.138.rowp_ref, f32[6,512,16]{2,1,0:T(8,128)S(1)} %get-tuple-element.116.colp_ref, f32[2,256,256]{2,1,0:T(8,128)S(1)} %get-tuple-element.139.cb_ref, bf16[512,1536]{1,0:T(8,128)(2,1)S(1)} %get-tuple-element.141.x_ref), custom_call_target="tpu_custom_call" | custom-call | flops 2000000000 | bytes 1500000 | tf_op jit(solution)/shard_map/pallas_call | solution.py:44
  58.5 2.4 %shard_map.293 = (bf16[512,1536]{1,0:T(8,128)(2,1)S(1)}, bf16[768,512]{1,0:T(8,128)(2,1)S(1)}) custom-call(s32[8]{0:T(128)S(1)} %pad_add_fusion.s_ref, bf16[512,768]{1,0:T(8,128)(2,1)S(1)} %copy-done.18, bf16[384,768]{1,0:T(8,128)(2,1)S(1)} %copy-done.19, bf16[384,768]{1,0:T(8,128)(2,1)S(1)} %collective-permute-done.7.refs_1_, ...), custom_call_target="tpu_custom_call" | custom-call | flops 1200000000 | bytes 900000 | tf_op jit(solution)/shard_map/pallas_call | solution.py:44
  60.9 3.8 %collective-permute-done.10.far_ref = bf16[144,1536]{1,0:T(8,128)(2,1)S(1)} collective-permute-done((bf16[144,1536]{1,0:T(8,128)(2,1)S(1)}, bf16[144,1536]{1,0:T(8,128)(2,1)S(1)}, u32[]{:S(2)}, u32[]{:S(2)}) %collective-permute-start.10) | collective-permute-done | bytes 442400 | tf_op jit(solution)/shard_map/ppermute | solution.py:790
  65.4 14.8 %shard_map.296 = (bf16[512,1536]{1,0:T(8,128)(2,1)}, bf16[512,1536]{1,0:T(8,128)(2,1)}, bf16[2,1536,384]{2,1,0:T(8,128)(2,1)}, bf16[2,1536,384]{2,1,0:T(8,128)(2...) custom-call(s32[8]{0:T(128)S(1)} %pad_add_fusion.s_ref, ...), custom_call_target="tpu_custom_call" | custom-call | flops 5600000000 | bytes 4200000 | tf_op jit(solution)/shard_map/pallas_call | solution.py:44
  80.3 1.1 copy-done.26
  81.4 1.8 collective-permute-done.11.got_ref.near_ref
  84.2 1.8 collective-permute-start.17
  86.0 9.3 %shard_map.299 = (bf16[512,1536]{1,0:T(8,128)(2,1)S(1)}, f32[32,512]{1,0:T(8,128)S(1)}, f32[512,128]{1,0:T(8,128)S(1)}, f32[512,128]{1,0:T(8,128)S(1)}) custom-call(s32[8]{0:T(128)} %copy-done.14, f32[12,8,512]{2,1,0:T(8,128)} %copy-done.24, f32[6,512,16]{2,1,0:T(8,128)} %copy-done.1, f32[2,256,256]{2,1,0:T(8,128)} %copy-done.36, ...), custom_call_target="tpu_custom_call" | custom-call | flops 3200000000 | bytes 2400000 | tf_op jit(solution)/shard_map/pallas_call | solution.py:44
  95.3 1.3 collective-permute-done.17.far_ref
  97.3 2.9 %convert_add_fusion = (f32[1,1536,384]{2,1,0:T(8,128)S(1)}, f32[1,1536,384]{2,1,0:T(8,128)S(1)}) fusion(bf16[2,1536,384]{2,1,0:T(8,128)(2,1)} %collective-permute-done.12, bf16[2,1536,384]{2,1,0:T(8,128)(2,1)} %get-tuple-element.145), kind=kLoop, calls=%fused_computation.4 | loop fusion | flops 3538944 | bytes 9437184 | tf_op jit(solution)/shard_map/add | solution.py:1031
  100.6 1.8 collective-permute-start.15
  102.5 1.6 collective-permute-start.13
  104.1 13.6 %shard_map.300 = (bf16[528,1536]{1,0:T(8,128)(2,1)S(1)}, f32[8,1536]{1,0:T(8,128)S(1)}, f32[32,512]{1,0:T(8,128)S(1)}, f32[8,1536]{1,0:T(8,128)S(1)}, f32[512,12...) custom-call(s32[8]{0:T(128)S(1)} %copy-done.15, f32[128,1536]{1,0:T(8,128)S(1)} %shard_map.298.back_in, ...), custom_call_target="tpu_custom_call" | custom-call | flops 4000000000 | bytes 3000000 | tf_op jit(solution)/shard_map/pallas_call | solution.py:44
  119.0 1.5 collective-permute-start.16
  120.8 1.6 collective-permute-start.14
  122.4 2.6 %shard_map.301 = (bf16[528,256]{1,0:T(8,128)(2,1)S(1)}, bf16[32,512]{1,0:T(8,128)(2,1)S(1)}, bf16[2,256,384]{2,1,0:T(8,128)(2,1)S(1)}, bf16[2,256,384]{2,1,0:T(8,128)(2,1)S(1)}) custom-call(s32[8]{0:T(128)S(1)} %copy-done.15, f32[512,128]{1,0:T(8,128)S(1)} %get-tuple-element.162.dbx_ref, f32[512,128]{1,0:T(8,128)S(1)} %get-tuple-element.163.dbin_ref, ...), custom_call_target="tpu_custom_call" | custom-call | flops 1600000000 | bytes 1200000 | tf_op jit(solution)/shard_map/pallas_call | solution.py:44
  125.4 1.9 collective-permute-done.16
  127.4 2.9 %collective-permute-done.14 = bf16[384,384]{1,0:T(8,128)(2,1)S(1)} collective-permute-done((bf16[384,384]{1,0:T(8,128)(2,1)S(1)}, bf16[384,384]{1,0:T(8,128)(2,1)S(1)}, u32[]{:S(2)}, u32[]{:S(2)}) %collective-permute-start.14) | collective-permute-done | bytes 294944 | tf_op jit(solution)/shard_map/ppermute | solution.py:790
  132.4 1.6 collective-permute-start.23
  134.9 1.6 collective-permute-start.20
  136.4 9.7 %shard_map.302 = (f32[512,768]{1,0:T(8,128)}, f32[16,768]{1,0:T(8,128)S(1)}, f32[8,384]{1,0:T(8,128)S(1)}) custom-call(s32[8]{0:T(128)} %copy-done.14, bf16[512,768]{1,0:T(8,128)(2,1)} %hid_ref.5, bf16[16,768]{1,0:T(8,128)(2,1)} %copy-done.13, bf16[512,768]{1,0:T(8,128)(2,1)} %cot_ref.3, f32[1,768]{1,0:T(1,128)} %copy-done.16, ...), custom_call_target="tpu_custom_call" | custom-call | flops 3600000000 | bytes 2700000 | tf_op jit(solution)/shard_map/pallas_call | solution.py:44
  146.2 2.7 %collective-permute-start.21 = (bf16[384,384]{1,0:T(8,128)(2,1)S(1)}, bf16[384,384]{1,0:T(8,128)(2,1)S(1)}, u32[]{:S(2)}, u32[]{:S(2)}) collective-permute-start(bf16[384,384]{1,0:T(8,128)(2,1)S(1)} %fusion.15), channel_id=1, source_target_pairs={{0,16},{4,20},{8,24},{12,28},{16,0},{20,4},{24,8},{28,12},{1,17},{... | collective-permute-start | bytes 884744 | tf_op jit(solution)/shard_map/ppermute | solution.py:790
  149.7 1.2 collective-permute-start.25
  150.9 10.3 %collective-permute-done.21 = bf16[384,384]{1,0:T(8,128)(2,1)S(1)} collective-permute-done((bf16[384,384]{1,0:T(8,128)(2,1)S(1)}, bf16[384,384]{1,0:T(8,128)(2,1)S(1)}, u32[]{:S(2)}, u32[]{:S(2)}) %collective-permute-start.21) | collective-permute-done | bytes 294944 | tf_op jit(solution)/shard_map/ppermute | solution.py:790
  161.7 1.6 collective-permute-start.26
  163.2 2.1 collective-permute-start.29
  165.3 5.0 %shard_map.303 = bf16[512,768]{1,0:T(8,128)(2,1)} custom-call(s32[8]{0:T(128)} %copy-done.14, bf16[512,768]{1,0:T(8,128)(2,1)} %hid_ref.5, bf16[512,1536]{1,0:T(8,128)(2,1)} %get-tuple-element.192.ny_ref, bf16[384,768]{1,0:T(8,128)(2,1)} %refs_0_.3, bf16[384,768]{1,0:T(8,128)(2,1)} %copy-done.22, bf16[384,768]{1,0:T(8,128)(2,1)} %copy-done.20, ...), custom_call_target="tpu_custom_call" | custom-call | flops 1600000000 | bytes 1200000 | tf_op jit(solution)/shard_map/pallas_call | solution.py:44
  170.3 1.2 collective-permute-start.28
  171.6 4.6 %collective-permute-done.29 = bf16[384,384]{1,0:T(8,128)(2,1)S(1)} collective-permute-done((bf16[384,384]{1,0:T(8,128)(2,1)S(1)}, bf16[384,384]{1,0:T(8,128)(2,1)S(1)}, u32[]{:S(2)}, u32[]{:S(2)}) %collective-permute-start.29) | collective-permute-done | bytes 294944 | tf_op jit(solution)/shard_map/ppermute | solution.py:790
  176.9 6.8 %collective-permute-done.28 = bf16[272,384]{1,0:T(8,128)(2,1)S(1)} collective-permute-done((bf16[272,384]{1,0:T(8,128)(2,1)S(1)}, bf16[272,384]{1,0:T(8,128)(2,1)S(1)}, u32[]{:S(2)}, u32[]{:S(2)}) %collective-permute-start.28) | collective-permute-done | bytes 208928 | tf_op jit(solution)/shard_map/ppermute | solution.py:790
  183.8 1.4 add_dynamic-update-slice_fusion
  185.3 5.6 %collective-permute-done.30 = bf16[272,384]{1,0:T(8,128)(2,1)S(1)} collective-permute-done((bf16[272,384]{1,0:T(8,128)(2,1)S(1)}, bf16[272,384]{1,0:T(8,128)(2,1)S(1)}, u32[]{:S(2)}, u32[]{:S(2)}) %collective-permute-start.30) | collective-permute-done | bytes 208928 | tf_op jit(solution)/shard_map/ppermute | solution.py:790
  192.9 4.6 %collective-permute-done.32 = bf16[288,384]{1,0:T(8,128)(2,1)S(1)} collective-permute-done((bf16[288,384]{1,0:T(8,128)(2,1)S(1)}, bf16[288,384]{1,0:T(8,128)(2,1)S(1)}, u32[]{:S(2)}, u32[]{:S(2)}) %collective-permute-start.32) | collective-permute-done | bytes 221216 | tf_op jit(solution)/shard_map/ppermute | solution.py:790
  201.0 2.2 %collective-permute-done.33 = bf16[224,256]{1,0:T(8,128)(2,1)S(1)} collective-permute-done((bf16[224,256]{1,0:T(8,128)(2,1)S(1)}, bf16[224,256]{1,0:T(8,128)(2,1)S(1)}, u32[]{:S(2)}, u32[]{:S(2)}) %collective-permute-start.33) | collective-permute-done | bytes 114720 | tf_op jit(solution)/shard_map/ppermute | solution.py:790
  204.6 1.4 copy.53
  (270 shorter events, 28.1 us)
Async XLA Ops:
  0.7 10.5 %copy-start.62 = (s32[1,3]{1,0:T(1,128)S(1)}, s32[1,3]{1,0:T(1,128)}, u32[]{:S(2)}) copy-start(s32[1,3]{1,0:T(1,128)} %param.20) | copy-start | bytes 40
  0.8 10.6 %copy-start.54 = (f32[768]{0:T(1024)S(1)}, f32[768]{0:T(1024)}, u32[]{:S(2)}) copy-start(f32[768]{0:T(1024)} %param.21) | copy-start | bytes 9220
  3.7 15.8 %collective-permute-start.4 = (bf16[768,768]{1,0:T(8,128)(2,1)}, bf16[768,768]{1,0:T(8,128)(2,1)}, u32[]{:S(2)}, u32[]{:S(2)}) collective-permute-start(bf16[768,768]{1,0:T(8,128)(2,1)} %constant_dynamic-update-slice_fusion.refs_0_), channel_id=1, source_target_pairs={{0,1},{1,0},{2,3},{3,2},{4,5},{5,4},{6,7},{7,6},{8,9},{9,8},{10,11... | collective-permute-start | bytes 3538952 | tf_op jit(solution)/shard_map/ppermute | solution.py:790
  4.6 3.1 %collective-permute-start.2 = (f32[32,896]{1,0:T(8,128)S(1)}, f32[32,896]{1,0:T(8,128)S(1)}, u32[]{:S(2)}, u32[]{:S(2)}) collective-permute-start(f32[32,896]{1,0:T(8,128)S(1)} %fusion.26), channel_id=1, source_target_pairs={{0,1},{1,0},{2,3},{3,2},{4,5},{5,4},{6,7},{7,6},{8,9},{9,8},{10,11... | collective-permute-start | bytes 344072 | tf_op jit(solution)/shard_map/ppermute | solution.py:790
  4.7 6.5 %collective-permute-start = (f32[32,896]{1,0:T(8,128)S(1)}, f32[32,896]{1,0:T(8,128)S(1)}, u32[]{:S(2)}, u32[]{:S(2)}) collective-permute-start(f32[32,896]{1,0:T(8,128)S(1)} %fusion.26), channel_id=1, source_target_pairs={{0,2},{1,3},{2,0},{3,1},{4,6},{5,7},{6,4},{7,5},{8,10},{9,11},{10,... | collective-permute-start | bytes 344072 | tf_op jit(solution)/shard_map/ppermute | solution.py:790
  7.7 28.7 %collective-permute-start.3 = (bf16[768,768]{1,0:T(8,128)(2,1)}, bf16[768,768]{1,0:T(8,128)(2,1)S(1)}, u32[]{:S(2)}, u32[]{:S(2)}) collective-permute-start(bf16[768,768]{1,0:T(8,128)(2,1)} %constant_dynamic-update-slice_fusion.refs_0_), channel_id=1, source_target_pairs={{0,2},{1,3},{2,0},{3,1},{4,6},{5,7},{6,4},{7,5},{8,10},{9,11},{10,... | collective-permute-start | bytes 3538952 | tf_op jit(solution)/shard_map/ppermute | solution.py:790
  11.3 1.3 collective-permute-start.1
  11.3 71.8 %copy-start.14 = (s32[8]{0:T(128)}, s32[8]{0:T(128)S(1)}, u32[]{:S(2)}) copy-start(s32[8]{0:T(128)S(1)} %pad_add_fusion.s_ref) | copy-start | bytes 100
  16.9 22.3 %copy-start.10 = (bf16[528,768]{1,0:T(8,128)(2,1)}, bf16[528,768]{1,0:T(8,128)(2,1)S(1)}, u32[]{:S(2)}) copy-start(bf16[528,768]{1,0:T(8,128)(2,1)S(1)} %get-tuple-element.114.nx_ref) | copy-start | bytes 2433028
  16.9 48.5 %copy-start.28 = (bf16[768,512]{1,0:T(8,128)(2,1)}, bf16[768,512]{1,0:T(8,128)(2,1)S(1)}, u32[]{:S(2)}) copy-start(bf16[768,512]{1,0:T(8,128)(2,1)S(1)} %get-tuple-element.137.nt_ref) | copy-start | bytes 2359300
  16.9 48.5 %copy-start.41 = (bf16[512,128]{1,0:T(8,128)(2,1)}, bf16[512,128]{1,0:T(8,128)(2,1)S(1)}, u32[]{:S(2)}) copy-start(bf16[512,128]{1,0:T(8,128)(2,1)S(1)} %get-tuple-element.135.c_ref) | copy-start | bytes 393220
  16.9 105.5 %copy-start.12 = (f32[32,896]{1,0:T(8,128)}, f32[32,896]{1,0:T(8,128)S(1)}, u32[]{:S(2)}) copy-start(f32[32,896]{1,0:T(8,128)S(1)} %select_maximum_fusion.hp_ref) | copy-start | bytes 344068
  19.5 34.9 %copy-start.24 = (f32[12,8,512]{2,1,0:T(8,128)}, f32[12,8,512]{2,1,0:T(8,128)S(1)}, u32[]{:S(2)}) copy-start(f32[12,8,512]{2,1,0:T(8,128)S(1)} %get-tuple-element.138.rowp_ref) | copy-start | bytes 589828
  19.5 45.9 %copy-start.1 = (f32[6,512,16]{2,1,0:T(8,128)}, f32[6,512,16]{2,1,0:T(8,128)S(1)}, u32[]{:S(2)}) copy-start(f32[6,512,16]{2,1,0:T(8,128)S(1)} %get-tuple-element.116.colp_ref) | copy-start | bytes 589828
  19.5 16.9 %copy-start.19 = (bf16[384,768]{1,0:T(8,128)(2,1)S(1)}, bf16[384,768]{1,0:T(8,128)(2,1)}, u32[]{:S(2)}) copy-start(bf16[384,768]{1,0:T(8,128)(2,1)} %refs_0_.3) | copy-start | bytes 1769476
  36.4 2.8 %collective-permute-start.5 = (bf16[768,768]{1,0:T(8,128)(2,1)S(1)}, bf16[768,768]{1,0:T(8,128)(2,1)S(1)}, u32[]{:S(2)}, u32[]{:S(2)}) collective-permute-start(bf16[768,768]{1,0:T(8,128)(2,1)S(1)} %collective-permute-done.3.refs_0_.refs_2_), channel_id=1, source_target_pairs={{0,1},{1,0},{2,3},{3,2},{4,5},{5,4},{6,7},{7,6},{8,9},{9,8},{10,11... | collective-permute-start | bytes 3538952 | tf_op jit(solution)/shard_map/ppermute | solution.py:790
  36.4 15.7 %collective-permute-start.8 = (bf16[384,768]{1,0:T(8,128)(2,1)S(1)}, bf16[384,768]{1,0:T(8,128)(2,1)S(1)}, u32[]{:S(2)}, u32[]{:S(2)}) collective-permute-start(bf16[384,768]{1,0:T(8,128)(2,1)S(1)} %copy-done.19), channel_id=1, source_target_pairs={{0,2},{1,3},{2,0},{3,1},{4,6},{5,7},{6,4},{7,5},{8,10},{9,11},{10,... | collective-permute-start | bytes 1769480 | tf_op jit(solution)/shard_map/ppermute | solution.py:790
  45.5 20.0 %copy-start.6 = (bf16[512,1536]{1,0:T(8,128)(2,1)}, bf16[512,1536]{1,0:T(8,128)(2,1)S(1)}, u32[]{:S(2)}) copy-start(bf16[512,1536]{1,0:T(8,128)(2,1)S(1)} %get-tuple-element.141.x_ref) | copy-start | bytes 4718596
  45.5 1.9 collective-permute-start.6
  52.1 6.3 %collective-permute-start.9 = (bf16[384,768]{1,0:T(8,128)(2,1)S(1)}, bf16[384,768]{1,0:T(8,128)(2,1)S(1)}, u32[]{:S(2)}, u32[]{:S(2)}) collective-permute-start(bf16[384,768]{1,0:T(8,128)(2,1)S(1)} %collective-permute-done.8.refs_2_), channel_id=1, source_target_pairs={{0,1},{1,0},{2,3},{3,2},{4,5},{5,4},{6,7},{7,6},{8,9},{9,8},{10,11... | collective-permute-start | bytes 1769480 | tf_op jit(solution)/shard_map/ppermute | solution.py:790
  52.1 6.3 %collective-permute-start.7 = (bf16[384,768]{1,0:T(8,128)(2,1)S(1)}, bf16[384,768]{1,0:T(8,128)(2,1)S(1)}, u32[]{:S(2)}, u32[]{:S(2)}) collective-permute-start(bf16[384,768]{1,0:T(8,128)(2,1)S(1)} %copy-done.19), channel_id=1, source_target_pairs={{0,1},{1,0},{2,3},{3,2},{4,5},{5,4},{6,7},{7,6},{8,9},{9,8},{10,11... | collective-permute-start | bytes 1769480 | tf_op jit(solution)/shard_map/ppermute | solution.py:790
  52.6 12.1 %collective-permute-start.10 = (bf16[144,1536]{1,0:T(8,128)(2,1)S(1)}, bf16[144,1536]{1,0:T(8,128)(2,1)S(1)}, u32[]{:S(2)}, u32[]{:S(2)}) collective-permute-start(bf16[144,1536]{1,0:T(8,128)(2,1)S(1)} %shard_map.292), channel_id=1, source_target_pairs={{0,2},{1,3},{2,0},{3,1},{4,6},{5,7},{6,4},{7,5},{8,10},{9,11},{10,... | collective-permute-start | bytes 1327112 | tf_op jit(solution)/shard_map/ppermute | solution.py:790
  81.4 1.8 collective-permute-start.11
  84.0 13.3 %collective-permute-start.12 = (bf16[2,1536,384]{2,1,0:T(8,128)(2,1)}, bf16[2,1536,384]{2,1,0:T(8,128)(2,1)}, u32[]{:S(2)}, u32[]{:S(2)}) collective-permute-start(bf16[2,1536,384]{2,1,0:T(8,128)(2,1)} %get-tuple-element.149), channel_id=1, source_target_pairs={{0,1},{1,0},{2,3},{3,2},{4,5},{5,4},{6,7},{7,6},{8,9},{9,8},{10,11... | collective-permute-start | bytes 7077896 | tf_op jit(solution)/shard_map/ppermute | solution.py:790
  84.2 12.4 %collective-permute-start.17 = (bf16[144,1536]{1,0:T(8,128)(2,1)S(1)}, bf16[144,1536]{1,0:T(8,128)(2,1)S(1)}, u32[]{:S(2)}, u32[]{:S(2)}) collective-permute-start(bf16[144,1536]{1,0:T(8,128)(2,1)S(1)} %shard_map.297), channel_id=1, source_target_pairs={{0,2},{1,3},{2,0},{3,1},{4,6},{5,7},{6,4},{7,5},{8,10},{9,11},{10,... | collective-permute-start | bytes 1327112 | tf_op jit(solution)/shard_map/ppermute | solution.py:790
  86.0 10.6 %copy-start.15 = (s32[8]{0:T(128)S(1)}, s32[8]{0:T(128)}, u32[]{:S(2)}) copy-start(s32[8]{0:T(128)} %copy-done.14) | copy-start | bytes 100
  100.6 17.1 %collective-permute-start.15 = (bf16[2,384,384]{2,1,0:T(8,128)(2,1)S(1)}, bf16[2,384,384]{2,1,0:T(8,128)(2,1)S(1)}, u32[]{:S(2)}, u32[]{:S(2)}) collective-permute-start(bf16[2,384,384]{2,1,0:T(8,128)(2,1)S(1)} %fusion.13), channel_id=1, source_target_pairs={{0,4},{4,0},{8,12},{12,8},{16,20},{20,16},{24,28},{28,24},{1,5},{5... | collective-permute-start | bytes 1769480 | tf_op jit(solution)/shard_map/ppermute | solution.py:790
  102.5 18.1 %collective-permute-start.13 = (bf16[768,384]{1,0:T(8,128)(2,1)S(1)}, bf16[768,384]{1,0:T(8,128)(2,1)S(1)}, u32[]{:S(2)}, u32[]{:S(2)}) collective-permute-start(bf16[768,384]{1,0:T(8,128)(2,1)S(1)} %fusion.12), channel_id=1, source_target_pairs={{0,2},{1,3},{2,0},{3,1},{4,6},{5,7},{6,4},{7,5},{8,10},{9,11},{10,... | collective-permute-start | bytes 1769480 | tf_op jit(solution)/shard_map/ppermute | solution.py:790
  119.0 8.2 %collective-permute-start.16 = (bf16[384,384]{1,0:T(8,128)(2,1)S(1)}, bf16[384,384]{1,0:T(8,128)(2,1)S(1)}, u32[]{:S(2)}, u32[]{:S(2)}) collective-permute-start(bf16[384,384]{1,0:T(8,128)(2,1)S(1)} %fusion.22), channel_id=1, source_target_pairs={{0,2},{1,3},{2,0},{3,1},{4,6},{5,7},{6,4},{7,5},{8,10},{9,11},{10,... | collective-permute-start | bytes 884744 | tf_op jit(solution)/shard_map/ppermute | solution.py:790
  120.7 9.9 %collective-permute-start.18 = (bf16[2,768,384]{2,1,0:T(8,128)(2,1)S(1)}, bf16[2,768,384]{2,1,0:T(8,128)(2,1)S(1)}, u32[]{:S(2)}, u32[]{:S(2)}) collective-permute-start(bf16[2,768,384]{2,1,0:T(8,128)(2,1)S(1)} %copy-done.63), channel_id=1, source_target_pairs={{0,1},{1,0},{2,3},{3,2},{4,5},{5,4},{6,7},{7,6},{8,9},{9,8},{10,11... | collective-permute-start | bytes 3538952 | tf_op jit(solution)/shard_map/ppermute | solution.py:790
  120.8 9.5 %collective-permute-start.14 = (bf16[384,384]{1,0:T(8,128)(2,1)S(1)}, bf16[384,384]{1,0:T(8,128)(2,1)S(1)}, u32[]{:S(2)}, u32[]{:S(2)}) collective-permute-start(bf16[384,384]{1,0:T(8,128)(2,1)S(1)} %fusion.20), channel_id=1, source_target_pairs={{0,4},{4,0},{8,12},{12,8},{16,20},{20,16},{24,28},{28,24},{1,5},{5... | collective-permute-start | bytes 884744 | tf_op jit(solution)/shard_map/ppermute | solution.py:790
  125.1 5.4 %collective-permute-start.19 = (bf16[2,256,384]{2,1,0:T(8,128)(2,1)S(1)}, bf16[2,256,384]{2,1,0:T(8,128)(2,1)S(1)}, u32[]{:S(2)}, u32[]{:S(2)}) collective-permute-start(bf16[2,256,384]{2,1,0:T(8,128)(2,1)S(1)} %get-tuple-element.178), channel_id=1, source_target_pairs={{0,1},{1,0},{2,3},{3,2},{4,5},{5,4},{6,7},{7,6},{8,9},{9,8},{10,11... | collective-permute-start | bytes 1179656 | tf_op jit(solution)/shard_map/ppermute | solution.py:790
  132.4 16.5 %collective-permute-start.23 = (bf16[2,256,384]{2,1,0:T(8,128)(2,1)S(1)}, bf16[2,256,384]{2,1,0:T(8,128)(2,1)S(1)}, u32[]{:S(2)}, u32[]{:S(2)}) collective-permute-start(bf16[2,256,384]{2,1,0:T(8,128)(2,1)S(1)} %fusion.18), channel_id=1, source_target_pairs={{0,4},{4,0},{8,12},{12,8},{16,20},{20,16},{24,28},{28,24},{1,5},{5... | collective-permute-start | bytes 1179656 | tf_op jit(solution)/shard_map/ppermute | solution.py:790
  134.0 15.0 %collective-permute-start.22 = (bf16[512,384]{1,0:T(8,128)(2,1)S(1)}, bf16[512,384]{1,0:T(8,128)(2,1)S(1)}, u32[]{:S(2)}, u32[]{:S(2)}) collective-permute-start(bf16[512,384]{1,0:T(8,128)(2,1)S(1)} %fusion.17), channel_id=1, source_target_pairs={{0,2},{1,3},{2,0},{3,1},{4,6},{5,7},{6,4},{7,5},{8,10},{9,11},{10,... | collective-permute-start | bytes 1179656 | tf_op jit(solution)/shard_map/ppermute | solution.py:790
  134.9 11.3 %collective-permute-start.20 = (bf16[384,384]{1,0:T(8,128)(2,1)S(1)}, bf16[384,384]{1,0:T(8,128)(2,1)S(1)}, u32[]{:S(2)}, u32[]{:S(2)}) collective-permute-start(bf16[384,384]{1,0:T(8,128)(2,1)S(1)} %fusion.21), channel_id=1, source_target_pairs={{0,8},{4,12},{8,0},{12,4},{16,24},{20,28},{24,16},{28,20},{1,9},{5... | collective-permute-start | bytes 884744 | tf_op jit(solution)/shard_map/ppermute | solution.py:790
  146.2 15.0 %collective-permute-start.21 = (bf16[384,384]{1,0:T(8,128)(2,1)S(1)}, bf16[384,384]{1,0:T(8,128)(2,1)S(1)}, u32[]{:S(2)}, u32[]{:S(2)}) collective-permute-start(bf16[384,384]{1,0:T(8,128)(2,1)S(1)} %fusion.15), channel_id=1, source_target_pairs={{0,16},{4,20},{8,24},{12,28},{16,0},{20,4},{24,8},{28,12},{1,17},{... | collective-permute-start | bytes 884744 | tf_op jit(solution)/shard_map/ppermute | solution.py:790
  149.1 12.2 %collective-permute-start.24 = (bf16[256,384]{1,0:T(8,128)(2,1)S(1)}, bf16[256,384]{1,0:T(8,128)(2,1)S(1)}, u32[]{:S(2)}, u32[]{:S(2)}) collective-permute-start(bf16[256,384]{1,0:T(8,128)(2,1)S(1)} %fusion.24), channel_id=1, source_target_pairs={{0,4},{4,0},{8,12},{12,8},{16,20},{20,16},{24,28},{28,24},{1,5},{5... | collective-permute-start | bytes 589832 | tf_op jit(solution)/shard_map/ppermute | solution.py:790
  149.7 11.6 %collective-permute-start.25 = (bf16[256,384]{1,0:T(8,128)(2,1)S(1)}, bf16[256,384]{1,0:T(8,128)(2,1)S(1)}, u32[]{:S(2)}, u32[]{:S(2)}) collective-permute-start(bf16[256,384]{1,0:T(8,128)(2,1)S(1)} %fusion.25), channel_id=1, source_target_pairs={{0,2},{1,3},{2,0},{3,1},{4,6},{5,7},{6,4},{7,5},{8,10},{9,11},{10,... | collective-permute-start | bytes 589832 | tf_op jit(solution)/shard_map/ppermute | solution.py:790
  161.6 8.7 %collective-permute-start.27 = (bf16[272,384]{1,0:T(8,128)(2,1)S(1)}, bf16[272,384]{1,0:T(8,128)(2,1)S(1)}, u32[]{:S(2)}, u32[]{:S(2)}) collective-permute-start(bf16[272,384]{1,0:T(8,128)(2,1)S(1)} %fusion.23), channel_id=1, source_target_pairs={{0,8},{4,12},{8,0},{12,4},{16,24},{20,28},{24,16},{28,20},{1,9},{5... | collective-permute-start | bytes 626696 | tf_op jit(solution)/shard_map/ppermute | solution.py:790
  161.7 22.2 %collective-permute-start.26 = (f32[16,768]{1,0:T(8,128)S(1)}, f32[16,768]{1,0:T(8,128)S(1)}, u32[]{:S(2)}, u32[]{:S(2)}) collective-permute-start(f32[16,768]{1,0:T(8,128)S(1)} %get-tuple-element.186), channel_id=1, source_target_pairs={{1,0},{2,1},{3,2},{5,4},{6,5},{7,6},{9,8},{10,9},{11,10},{13,12},{... | collective-permute-start | bytes 147464 | tf_op jit(solution)/shard_map/ppermute | solution.py:1139
  163.2 12.9 %collective-permute-start.29 = (bf16[384,384]{1,0:T(8,128)(2,1)S(1)}, bf16[384,384]{1,0:T(8,128)(2,1)S(1)}, u32[]{:S(2)}, u32[]{:S(2)}) collective-permute-start(bf16[384,384]{1,0:T(8,128)(2,1)S(1)} %add_convert_fusion), channel_id=1, source_target_pairs={{0,8},{4,12},{8,0},{12,4},{16,24},{20,28},{24,16},{28,20},{1,9},{5... | collective-permute-start | bytes 884744 | tf_op jit(solution)/shard_map/ppermute | solution.py:790
  170.3 13.4 %collective-permute-start.28 = (bf16[272,384]{1,0:T(8,128)(2,1)S(1)}, bf16[272,384]{1,0:T(8,128)(2,1)S(1)}, u32[]{:S(2)}, u32[]{:S(2)}) collective-permute-start(bf16[272,384]{1,0:T(8,128)(2,1)S(1)} %fusion.16), channel_id=1, source_target_pairs={{0,16},{4,20},{8,24},{12,28},{16,0},{20,4},{24,8},{28,12},{1,17},{... | collective-permute-start | bytes 626696 | tf_op jit(solution)/shard_map/ppermute | solution.py:790
  176.3 14.7 %collective-permute-start.31 = (bf16[768,384]{1,0:T(8,128)(2,1)S(1)}, bf16[768,384]{1,0:T(8,128)(2,1)S(1)}, u32[]{:S(2)}, u32[]{:S(2)}) collective-permute-start(bf16[768,384]{1,0:T(8,128)(2,1)S(1)} %pad_maximum_fusion.3), channel_id=1, source_target_pairs={{0,4},{4,0},{8,12},{12,8},{16,20},{20,16},{24,28},{28,24},{1,5},{5... | collective-permute-start | bytes 1769480 | tf_op jit(solution)/shard_map/ppermute | solution.py:790
  183.8 7.1 %collective-permute-start.30 = (bf16[272,384]{1,0:T(8,128)(2,1)S(1)}, bf16[272,384]{1,0:T(8,128)(2,1)S(1)}, u32[]{:S(2)}, u32[]{:S(2)}) collective-permute-start(bf16[272,384]{1,0:T(8,128)(2,1)S(1)} %add_convert_fusion.1), channel_id=1, source_target_pairs={{0,8},{4,12},{8,0},{12,4},{16,24},{20,28},{24,16},{28,20},{1,9},{5... | collective-permute-start | bytes 626696 | tf_op jit(solution)/shard_map/ppermute | solution.py:790
  191.0 6.5 %collective-permute-start.32 = (bf16[288,384]{1,0:T(8,128)(2,1)S(1)}, bf16[288,384]{1,0:T(8,128)(2,1)S(1)}, u32[]{:S(2)}, u32[]{:S(2)}) collective-permute-start(bf16[288,384]{1,0:T(8,128)(2,1)S(1)} %slice.285), channel_id=1, source_target_pairs={{0,4},{4,0},{8,12},{12,8},{16,20},{20,16},{24,28},{28,24},{1,5},{5... | collective-permute-start | bytes 663560 | tf_op jit(solution)/shard_map/ppermute | solution.py:790
  197.7 5.7 %collective-permute-start.34 = (bf16[256,384]{1,0:T(8,128)(2,1)S(1)}, bf16[256,384]{1,0:T(8,128)(2,1)S(1)}, u32[]{:S(2)}, u32[]{:S(2)}) collective-permute-start(bf16[256,384]{1,0:T(8,128)(2,1)S(1)} %get-tuple-element.261), channel_id=1, source_target_pairs={{0,4},{4,0},{8,12},{12,8},{16,20},{20,16},{24,28},{28,24},{1,5},{5... | collective-permute-start | bytes 589832 | tf_op jit(solution)/shard_map/ppermute | solution.py:790
  198.4 4.9 %collective-permute-start.33 = (bf16[224,256]{1,0:T(8,128)(2,1)S(1)}, bf16[224,256]{1,0:T(8,128)(2,1)S(1)}, u32[]{:S(2)}, u32[]{:S(2)}) collective-permute-start(bf16[224,256]{1,0:T(8,128)(2,1)S(1)} %pad_maximum_fusion.7), channel_id=1, source_target_pairs={{0,2},{1,3},{2,0},{3,1},{4,6},{5,7},{6,4},{7,5},{8,10},{9,11},{10,... | collective-permute-start | bytes 344072 | tf_op jit(solution)/shard_map/ppermute | solution.py:790
  204.6 1.5 collective-permute-start.35
  (54 other events, 226.4 us)

commit v7 on v6

--- a/solution.py
+++ b/solution.py
@@ -952,7 +952,7 @@
             near = swap(own_turned, "head", 1)
             (run,) = call(functools.partial(join_kernel, forward), [(own.shape, BF16)], [scalars, own, near], mib=8)
             far = swap(run, "head", 2)
-            between = beside(run)
+            between = beside(run if forward else near)
             far = after(far, between[1]) if between else far
             (result,) = call(functools.partial(arrive_kernel, forward), [((state, total), F32)], [scalars, near, far], mib=8)
             return result, between

time: 209 us -> 209 us (level)
  no operation moved by 1% of the time
where the time goes in v7:
time: 209 us
  Pallas kernels  82.3 us (39%)
  waiting for transfers between devices  64.5 us (31%)
  starting transfers between devices  33.8 us (16%)
  local copies, waits for them, and re-layouts  15.2 us (7%)
  other arithmetic  11.1 us (5%)
    pallas_call x16, Pallas kernels, call(): pl.pallas_call(kernel, grid=grid, out_shape=[kinds[at](s, d) if at in kin...  82.3 us
    ppermute x35, waiting for transfers between devices, swap(): return lax.ppermute(value, axis, [(i, i ^ mask) for i in range(size)])  64.5 us
    ppermute x35, starting transfers between devices, swap(): return lax.ppermute(value, axis, [(i, i ^ mask) for i in range(size)])  32.3 us
    unnamed x130, local copies, waits for them, and re-layouts  9.72 us
  transfers between devices with their start and end apart: 36, of which 19 were waited for; matrix products, arithmetic and copies ran while one was open for 4% of the time, Pallas kernels for 32%

profile of v7, /device:TPU:0, one launch (start us, length us, event | category | flops | bytes accessed | tf_op | source)
XLA Modules:
  0.0 209.0 jit_solution(3537063846649360348)
XLA Ops:
  0.8 2.0 constant_dynamic-update-slice_fusion.1
  4.7 3.0 %collective-permute-start = (f32[32,896]{1,0:T(8,128)S(1)}, f32[32,896]{1,0:T(8,128)S(1)}, u32[]{:S(2)}, u32[]{:S(2)}) collective-permute-start(f32[32,896]{1,0:T(8,128)S(1)} %fusion.26), channel_id=1, source_target_pairs={{0,2},{1,3},{2,0},{3,1},{4,6},{5,7},{6,4},{7,5},{8,10},{9,11},{10,... | collective-permute-start | bytes 344072 | tf_op jit(solution)/shard_map/ppermute | solution.py:790
  7.7 1.9 collective-permute-start.3
  9.6 1.6 collective-permute-done
  12.6 2.0 shard_map.288
  16.9 1.9 shard_map.289
  19.5 8.0 %shard_map.290 = (bf16[512,1536]{1,0:T(8,128)(2,1)}, bf16[528,1536]{1,0:T(8,128)(2,1)}, bf16[512,1536]{1,0:T(8,128)(2,1)}, f32[2,128,1536]{2,1,0:T(8,128)}, bf16...) custom-call(s32[8]{0:T(128)S(1)} %pad_add_fusion.s_ref, ...), custom_call_target="tpu_custom_call" | custom-call | flops 2400000000 | bytes 1800000 | tf_op jit(solution)/shard_map/pallas_call | solution.py:44
  27.5 8.9 %collective-permute-done.3.refs_0_.refs_2_ = bf16[768,768]{1,0:T(8,128)(2,1)S(1)} collective-permute-done((bf16[768,768]{1,0:T(8,128)(2,1)}, bf16[768,768]{1,0:T(8,128)(2,1)S(1)}, u32[]{:S(2)}, u32[]{:S(2)}) %collective-permute-start.3) | collective-permute-done | bytes 1179680 | tf_op jit(solution)/shard_map/ppermute | solution.py:790
  36.4 1.8 collective-permute-start.8
  39.2 6.2 %shard_map.291 = (bf16[512,1536]{1,0:T(8,128)(2,1)}, bf16[528,1536]{1,0:T(8,128)(2,1)}, bf16[512,1536]{1,0:T(8,128)(2,1)}, f32[2,128,1536]{2,1,0:T(8,128)}, bf16...) custom-call(s32[8]{0:T(128)S(1)} %pad_add_fusion.s_ref, ...), custom_call_target="tpu_custom_call", output_to_operand_aliasing={{0}: (8, {}), {1}: (9, {}), {2}: (10, {}), {3}: (11, {}), {... | custom-call | flops 2400000000 | bytes 1800000 | tf_op jit(solution)/shard_map/pallas_call | solution.py:44
  45.7 1.7 collective-permute-done.6.got_ref.near_ref
  48.1 4.0 %collective-permute-done.8.refs_2_ = bf16[384,768]{1,0:T(8,128)(2,1)S(1)} collective-permute-done((bf16[384,768]{1,0:T(8,128)(2,1)S(1)}, bf16[384,768]{1,0:T(8,128)(2,1)S(1)}, u32[]{:S(2)}, u32[]{:S(2)}) %collective-permute-start.8) | collective-permute-done | bytes 589856 | tf_op jit(solution)/shard_map/ppermute | solution.py:790
  52.6 1.7 collective-permute-start.10
  54.4 4.0 %shard_map.295.y_ref = f32[512,1536]{1,0:T(8,128)S(1)} custom-call(s32[8]{0:T(128)S(1)} %pad_add_fusion.s_ref, f32[12,8,512]{2,1,0:T(8,128)S(1)} %get-tuple-element.138.rowp_ref, f32[6,512,16]{2,1,0:T(8,128)S(1)} %get-tuple-element.116.colp_ref, f32[2,256,256]{2,1,0:T(8,128)S(1)} %get-tuple-element.139.cb_ref, bf16[512,1536]{1,0:T(8,128)(2,1)S(1)} %get-tuple-element.141.x_ref), custom_call_target="tpu_custom_call" | custom-call | flops 2000000000 | bytes 1500000 | tf_op jit(solution)/shard_map/pallas_call | solution.py:44
  58.5 2.4 %shard_map.293 = (bf16[512,1536]{1,0:T(8,128)(2,1)S(1)}, bf16[768,512]{1,0:T(8,128)(2,1)S(1)}) custom-call(s32[8]{0:T(128)S(1)} %pad_add_fusion.s_ref, bf16[512,768]{1,0:T(8,128)(2,1)S(1)} %copy-done.18, bf16[384,768]{1,0:T(8,128)(2,1)S(1)} %copy-done.19, bf16[384,768]{1,0:T(8,128)(2,1)S(1)} %collective-permute-done.7.refs_1_, ...), custom_call_target="tpu_custom_call" | custom-call | flops 1200000000 | bytes 900000 | tf_op jit(solution)/shard_map/pallas_call | solution.py:44
  60.9 3.8 %collective-permute-done.10.far_ref = bf16[144,1536]{1,0:T(8,128)(2,1)S(1)} collective-permute-done((bf16[144,1536]{1,0:T(8,128)(2,1)S(1)}, bf16[144,1536]{1,0:T(8,128)(2,1)S(1)}, u32[]{:S(2)}, u32[]{:S(2)}) %collective-permute-start.10) | collective-permute-done | bytes 442400 | tf_op jit(solution)/shard_map/ppermute | solution.py:790
  65.4 14.8 %shard_map.296 = (bf16[512,1536]{1,0:T(8,128)(2,1)}, bf16[512,1536]{1,0:T(8,128)(2,1)}, bf16[2,1536,384]{2,1,0:T(8,128)(2,1)}, bf16[2,1536,384]{2,1,0:T(8,128)(2...) custom-call(s32[8]{0:T(128)S(1)} %pad_add_fusion.s_ref, ...), custom_call_target="tpu_custom_call" | custom-call | flops 5600000000 | bytes 4200000 | tf_op jit(solution)/shard_map/pallas_call | solution.py:44
  80.3 1.1 copy-done.26
  81.4 1.8 collective-permute-done.11.got_ref.near_ref
  84.1 1.8 collective-permute-start.17
  86.0 9.3 %shard_map.299 = (bf16[512,1536]{1,0:T(8,128)(2,1)S(1)}, f32[32,512]{1,0:T(8,128)S(1)}, f32[512,128]{1,0:T(8,128)S(1)}, f32[512,128]{1,0:T(8,128)S(1)}) custom-call(s32[8]{0:T(128)} %copy-done.14, f32[12,8,512]{2,1,0:T(8,128)} %copy-done.24, f32[6,512,16]{2,1,0:T(8,128)} %copy-done.1, f32[2,256,256]{2,1,0:T(8,128)} %copy-done.36, ...), custom_call_target="tpu_custom_call" | custom-call | flops 3200000000 | bytes 2400000 | tf_op jit(solution)/shard_map/pallas_call | solution.py:44
  95.3 1.3 collective-permute-done.17.far_ref
  97.3 2.9 %convert_add_fusion = (f32[1,1536,384]{2,1,0:T(8,128)S(1)}, f32[1,1536,384]{2,1,0:T(8,128)S(1)}) fusion(bf16[2,1536,384]{2,1,0:T(8,128)(2,1)} %collective-permute-done.12, bf16[2,1536,384]{2,1,0:T(8,128)(2,1)} %get-tuple-element.145), kind=kLoop, calls=%fused_computation.4 | loop fusion | flops 3538944 | bytes 9437184 | tf_op jit(solution)/shard_map/add | solution.py:1031
  100.6 1.8 collective-permute-start.15
  102.5 1.6 collective-permute-start.13
  104.1 13.6 %shard_map.300 = (bf16[528,1536]{1,0:T(8,128)(2,1)S(1)}, f32[8,1536]{1,0:T(8,128)S(1)}, f32[32,512]{1,0:T(8,128)S(1)}, f32[8,1536]{1,0:T(8,128)S(1)}, f32[512,12...) custom-call(s32[8]{0:T(128)S(1)} %copy-done.15, f32[128,1536]{1,0:T(8,128)S(1)} %shard_map.298.back_in, ...), custom_call_target="tpu_custom_call" | custom-call | flops 4000000000 | bytes 3000000 | tf_op jit(solution)/shard_map/pallas_call | solution.py:44
  119.0 1.5 collective-permute-start.16
  120.8 1.6 collective-permute-start.14
  122.4 2.6 %shard_map.301 = (bf16[528,256]{1,0:T(8,128)(2,1)S(1)}, bf16[32,512]{1,0:T(8,128)(2,1)S(1)}, bf16[2,256,384]{2,1,0:T(8,128)(2,1)S(1)}, bf16[2,256,384]{2,1,0:T(8,128)(2,1)S(1)}) custom-call(s32[8]{0:T(128)S(1)} %copy-done.15, f32[512,128]{1,0:T(8,128)S(1)} %get-tuple-element.162.dbx_ref, f32[512,128]{1,0:T(8,128)S(1)} %get-tuple-element.163.dbin_ref, ...), custom_call_target="tpu_custom_call" | custom-call | flops 1600000000 | bytes 1200000 | tf_op jit(solution)/shard_map/pallas_call | solution.py:44
  125.4 1.9 collective-permute-done.16
  127.4 2.9 %collective-permute-done.14 = bf16[384,384]{1,0:T(8,128)(2,1)S(1)} collective-permute-done((bf16[384,384]{1,0:T(8,128)(2,1)S(1)}, bf16[384,384]{1,0:T(8,128)(2,1)S(1)}, u32[]{:S(2)}, u32[]{:S(2)}) %collective-permute-start.14) | collective-permute-done | bytes 294944 | tf_op jit(solution)/shard_map/ppermute | solution.py:790
  132.4 1.6 collective-permute-start.23
  134.9 1.6 collective-permute-start.20
  136.4 9.7 %shard_map.302 = (f32[512,768]{1,0:T(8,128)}, f32[16,768]{1,0:T(8,128)S(1)}, f32[8,384]{1,0:T(8,128)S(1)}) custom-call(s32[8]{0:T(128)} %copy-done.14, bf16[512,768]{1,0:T(8,128)(2,1)} %hid_ref.5, bf16[16,768]{1,0:T(8,128)(2,1)} %copy-done.13, bf16[512,768]{1,0:T(8,128)(2,1)} %cot_ref.3, f32[1,768]{1,0:T(1,128)} %copy-done.16, ...), custom_call_target="tpu_custom_call" | custom-call | flops 3600000000 | bytes 2700000 | tf_op jit(solution)/shard_map/pallas_call | solution.py:44
  146.2 2.7 %collective-permute-start.21 = (bf16[384,384]{1,0:T(8,128)(2,1)S(1)}, bf16[384,384]{1,0:T(8,128)(2,1)S(1)}, u32[]{:S(2)}, u32[]{:S(2)}) collective-permute-start(bf16[384,384]{1,0:T(8,128)(2,1)S(1)} %fusion.15), channel_id=1, source_target_pairs={{0,16},{4,20},{8,24},{12,28},{16,0},{20,4},{24,8},{28,12},{1,17},{... | collective-permute-start | bytes 884744 | tf_op jit(solution)/shard_map/ppermute | solution.py:790
  149.7 1.2 collective-permute-start.25
  150.9 10.3 %collective-permute-done.21 = bf16[384,384]{1,0:T(8,128)(2,1)S(1)} collective-permute-done((bf16[384,384]{1,0:T(8,128)(2,1)S(1)}, bf16[384,384]{1,0:T(8,128)(2,1)S(1)}, u32[]{:S(2)}, u32[]{:S(2)}) %collective-permute-start.21) | collective-permute-done | bytes 294944 | tf_op jit(solution)/shard_map/ppermute | solution.py:790
  161.7 1.6 collective-permute-start.26
  163.2 2.1 collective-permute-start.29
  165.3 5.0 %shard_map.303 = bf16[512,768]{1,0:T(8,128)(2,1)} custom-call(s32[8]{0:T(128)} %copy-done.14, bf16[512,768]{1,0:T(8,128)(2,1)} %hid_ref.5, bf16[512,1536]{1,0:T(8,128)(2,1)} %get-tuple-element.192.ny_ref, bf16[384,768]{1,0:T(8,128)(2,1)} %refs_0_.3, bf16[384,768]{1,0:T(8,128)(2,1)} %copy-done.22, bf16[384,768]{1,0:T(8,128)(2,1)} %copy-done.20, ...), custom_call_target="tpu_custom_call" | custom-call | flops 1600000000 | bytes 1200000 | tf_op jit(solution)/shard_map/pallas_call | solution.py:44
  170.3 1.2 collective-permute-start.28
  171.6 4.6 %collective-permute-done.29 = bf16[384,384]{1,0:T(8,128)(2,1)S(1)} collective-permute-done((bf16[384,384]{1,0:T(8,128)(2,1)S(1)}, bf16[384,384]{1,0:T(8,128)(2,1)S(1)}, u32[]{:S(2)}, u32[]{:S(2)}) %collective-permute-start.29) | collective-permute-done | bytes 294944 | tf_op jit(solution)/shard_map/ppermute | solution.py:790
  176.9 6.8 %collective-permute-done.28 = bf16[272,384]{1,0:T(8,128)(2,1)S(1)} collective-permute-done((bf16[272,384]{1,0:T(8,128)(2,1)S(1)}, bf16[272,384]{1,0:T(8,128)(2,1)S(1)}, u32[]{:S(2)}, u32[]{:S(2)}) %collective-permute-start.28) | collective-permute-done | bytes 208928 | tf_op jit(solution)/shard_map/ppermute | solution.py:790
  183.8 1.4 add_dynamic-update-slice_fusion
  185.3 5.6 %collective-permute-done.30 = bf16[272,384]{1,0:T(8,128)(2,1)S(1)} collective-permute-done((bf16[272,384]{1,0:T(8,128)(2,1)S(1)}, bf16[272,384]{1,0:T(8,128)(2,1)S(1)}, u32[]{:S(2)}, u32[]{:S(2)}) %collective-permute-start.30) | collective-permute-done | bytes 208928 | tf_op jit(solution)/shard_map/ppermute | solution.py:790
  192.9 4.6 %collective-permute-done.32 = bf16[288,384]{1,0:T(8,128)(2,1)S(1)} collective-permute-done((bf16[288,384]{1,0:T(8,128)(2,1)S(1)}, bf16[288,384]{1,0:T(8,128)(2,1)S(1)}, u32[]{:S(2)}, u32[]{:S(2)}) %collective-permute-start.32) | collective-permute-done | bytes 221216 | tf_op jit(solution)/shard_map/ppermute | solution.py:790
  201.0 2.2 %collective-permute-done.33 = bf16[224,256]{1,0:T(8,128)(2,1)S(1)} collective-permute-done((bf16[224,256]{1,0:T(8,128)(2,1)S(1)}, bf16[224,256]{1,0:T(8,128)(2,1)S(1)}, u32[]{:S(2)}, u32[]{:S(2)}) %collective-permute-start.33) | collective-permute-done | bytes 114720 | tf_op jit(solution)/shard_map/ppermute | solution.py:790
  204.6 1.4 copy.53
  (270 shorter events, 28.0 us)
Async XLA Ops:
  0.7 10.5 %copy-start.62 = (s32[1,3]{1,0:T(1,128)S(1)}, s32[1,3]{1,0:T(1,128)}, u32[]{:S(2)}) copy-start(s32[1,3]{1,0:T(1,128)} %param.20) | copy-start | bytes 40
  0.8 10.6 %copy-start.54 = (f32[768]{0:T(1024)S(1)}, f32[768]{0:T(1024)}, u32[]{:S(2)}) copy-start(f32[768]{0:T(1024)} %param.21) | copy-start | bytes 9220
  3.7 15.8 %collective-permute-start.4 = (bf16[768,768]{1,0:T(8,128)(2,1)}, bf16[768,768]{1,0:T(8,128)(2,1)}, u32[]{:S(2)}, u32[]{:S(2)}) collective-permute-start(bf16[768,768]{1,0:T(8,128)(2,1)} %constant_dynamic-update-slice_fusion.refs_0_), channel_id=1, source_target_pairs={{0,1},{1,0},{2,3},{3,2},{4,5},{5,4},{6,7},{7,6},{8,9},{9,8},{10,11... | collective-permute-start | bytes 3538952 | tf_op jit(solution)/shard_map/ppermute | solution.py:790
  4.6 3.1 %collective-permute-start.2 = (f32[32,896]{1,0:T(8,128)S(1)}, f32[32,896]{1,0:T(8,128)S(1)}, u32[]{:S(2)}, u32[]{:S(2)}) collective-permute-start(f32[32,896]{1,0:T(8,128)S(1)} %fusion.26), channel_id=1, source_target_pairs={{0,1},{1,0},{2,3},{3,2},{4,5},{5,4},{6,7},{7,6},{8,9},{9,8},{10,11... | collective-permute-start | bytes 344072 | tf_op jit(solution)/shard_map/ppermute | solution.py:790
  4.7 6.5 %collective-permute-start = (f32[32,896]{1,0:T(8,128)S(1)}, f32[32,896]{1,0:T(8,128)S(1)}, u32[]{:S(2)}, u32[]{:S(2)}) collective-permute-start(f32[32,896]{1,0:T(8,128)S(1)} %fusion.26), channel_id=1, source_target_pairs={{0,2},{1,3},{2,0},{3,1},{4,6},{5,7},{6,4},{7,5},{8,10},{9,11},{10,... | collective-permute-start | bytes 344072 | tf_op jit(solution)/shard_map/ppermute | solution.py:790
  7.7 28.7 %collective-permute-start.3 = (bf16[768,768]{1,0:T(8,128)(2,1)}, bf16[768,768]{1,0:T(8,128)(2,1)S(1)}, u32[]{:S(2)}, u32[]{:S(2)}) collective-permute-start(bf16[768,768]{1,0:T(8,128)(2,1)} %constant_dynamic-update-slice_fusion.refs_0_), channel_id=1, source_target_pairs={{0,2},{1,3},{2,0},{3,1},{4,6},{5,7},{6,4},{7,5},{8,10},{9,11},{10,... | collective-permute-start | bytes 3538952 | tf_op jit(solution)/shard_map/ppermute | solution.py:790
  11.3 1.3 collective-permute-start.1
  11.3 72.0 %copy-start.14 = (s32[8]{0:T(128)}, s32[8]{0:T(128)S(1)}, u32[]{:S(2)}) copy-start(s32[8]{0:T(128)S(1)} %pad_add_fusion.s_ref) | copy-start | bytes 100
  16.9 22.3 %copy-start.10 = (bf16[528,768]{1,0:T(8,128)(2,1)}, bf16[528,768]{1,0:T(8,128)(2,1)S(1)}, u32[]{:S(2)}) copy-start(bf16[528,768]{1,0:T(8,128)(2,1)S(1)} %get-tuple-element.114.nx_ref) | copy-start | bytes 2433028
  16.9 48.5 %copy-start.28 = (bf16[768,512]{1,0:T(8,128)(2,1)}, bf16[768,512]{1,0:T(8,128)(2,1)S(1)}, u32[]{:S(2)}) copy-start(bf16[768,512]{1,0:T(8,128)(2,1)S(1)} %get-tuple-element.137.nt_ref) | copy-start | bytes 2359300
  16.9 48.5 %copy-start.41 = (bf16[512,128]{1,0:T(8,128)(2,1)}, bf16[512,128]{1,0:T(8,128)(2,1)S(1)}, u32[]{:S(2)}) copy-start(bf16[512,128]{1,0:T(8,128)(2,1)S(1)} %get-tuple-element.135.c_ref) | copy-start | bytes 393220
  16.9 105.5 %copy-start.12 = (f32[32,896]{1,0:T(8,128)}, f32[32,896]{1,0:T(8,128)S(1)}, u32[]{:S(2)}) copy-start(f32[32,896]{1,0:T(8,128)S(1)} %select_maximum_fusion.hp_ref) | copy-start | bytes 344068
  19.5 34.9 %copy-start.24 = (f32[12,8,512]{2,1,0:T(8,128)}, f32[12,8,512]{2,1,0:T(8,128)S(1)}, u32[]{:S(2)}) copy-start(f32[12,8,512]{2,1,0:T(8,128)S(1)} %get-tuple-element.138.rowp_ref) | copy-start | bytes 589828
  19.5 45.9 %copy-start.1 = (f32[6,512,16]{2,1,0:T(8,128)}, f32[6,512,16]{2,1,0:T(8,128)S(1)}, u32[]{:S(2)}) copy-start(f32[6,512,16]{2,1,0:T(8,128)S(1)} %get-tuple-element.116.colp_ref) | copy-start | bytes 589828
  19.5 16.9 %copy-start.19 = (bf16[384,768]{1,0:T(8,128)(2,1)S(1)}, bf16[384,768]{1,0:T(8,128)(2,1)}, u32[]{:S(2)}) copy-start(bf16[384,768]{1,0:T(8,128)(2,1)} %refs_0_.3) | copy-start | bytes 1769476
  36.4 2.8 %collective-permute-start.5 = (bf16[768,768]{1,0:T(8,128)(2,1)S(1)}, bf16[768,768]{1,0:T(8,128)(2,1)S(1)}, u32[]{:S(2)}, u32[]{:S(2)}) collective-permute-start(bf16[768,768]{1,0:T(8,128)(2,1)S(1)} %collective-permute-done.3.refs_0_.refs_2_), channel_id=1, source_target_pairs={{0,1},{1,0},{2,3},{3,2},{4,5},{5,4},{6,7},{7,6},{8,9},{9,8},{10,11... | collective-permute-start | bytes 3538952 | tf_op jit(solution)/shard_map/ppermute | solution.py:790
  36.4 15.7 %collective-permute-start.8 = (bf16[384,768]{1,0:T(8,128)(2,1)S(1)}, bf16[384,768]{1,0:T(8,128)(2,1)S(1)}, u32[]{:S(2)}, u32[]{:S(2)}) collective-permute-start(bf16[384,768]{1,0:T(8,128)(2,1)S(1)} %copy-done.19), channel_id=1, source_target_pairs={{0,2},{1,3},{2,0},{3,1},{4,6},{5,7},{6,4},{7,5},{8,10},{9,11},{10,... | collective-permute-start | bytes 1769480 | tf_op jit(solution)/shard_map/ppermute | solution.py:790
  45.5 20.0 %copy-start.6 = (bf16[512,1536]{1,0:T(8,128)(2,1)}, bf16[512,1536]{1,0:T(8,128)(2,1)S(1)}, u32[]{:S(2)}) copy-start(bf16[512,1536]{1,0:T(8,128)(2,1)S(1)} %get-tuple-element.141.x_ref) | copy-start | bytes 4718596
  45.5 1.9 collective-permute-start.6
  52.1 6.3 %collective-permute-start.9 = (bf16[384,768]{1,0:T(8,128)(2,1)S(1)}, bf16[384,768]{1,0:T(8,128)(2,1)S(1)}, u32[]{:S(2)}, u32[]{:S(2)}) collective-permute-start(bf16[384,768]{1,0:T(8,128)(2,1)S(1)} %collective-permute-done.8.refs_2_), channel_id=1, source_target_pairs={{0,1},{1,0},{2,3},{3,2},{4,5},{5,4},{6,7},{7,6},{8,9},{9,8},{10,11... | collective-permute-start | bytes 1769480 | tf_op jit(solution)/shard_map/ppermute | solution.py:790
  52.1 6.3 %collective-permute-start.7 = (bf16[384,768]{1,0:T(8,128)(2,1)S(1)}, bf16[384,768]{1,0:T(8,128)(2,1)S(1)}, u32[]{:S(2)}, u32[]{:S(2)}) collective-permute-start(bf16[384,768]{1,0:T(8,128)(2,1)S(1)} %copy-done.19), channel_id=1, source_target_pairs={{0,1},{1,0},{2,3},{3,2},{4,5},{5,4},{6,7},{7,6},{8,9},{9,8},{10,11... | collective-permute-start | bytes 1769480 | tf_op jit(solution)/shard_map/ppermute | solution.py:790
  52.6 12.1 %collective-permute-start.10 = (bf16[144,1536]{1,0:T(8,128)(2,1)S(1)}, bf16[144,1536]{1,0:T(8,128)(2,1)S(1)}, u32[]{:S(2)}, u32[]{:S(2)}) collective-permute-start(bf16[144,1536]{1,0:T(8,128)(2,1)S(1)} %shard_map.292), channel_id=1, source_target_pairs={{0,2},{1,3},{2,0},{3,1},{4,6},{5,7},{6,4},{7,5},{8,10},{9,11},{10,... | collective-permute-start | bytes 1327112 | tf_op jit(solution)/shard_map/ppermute | solution.py:790
  81.4 1.8 collective-permute-start.11
  83.2 14.1 %collective-permute-start.12 = (bf16[2,1536,384]{2,1,0:T(8,128)(2,1)}, bf16[2,1536,384]{2,1,0:T(8,128)(2,1)}, u32[]{:S(2)}, u32[]{:S(2)}) collective-permute-start(bf16[2,1536,384]{2,1,0:T(8,128)(2,1)} %get-tuple-element.148), channel_id=1, source_target_pairs={{0,1},{1,0},{2,3},{3,2},{4,5},{5,4},{6,7},{7,6},{8,9},{9,8},{10,11... | collective-permute-start | bytes 7077896 | tf_op jit(solution)/shard_map/ppermute | solution.py:790
  84.1 12.5 %collective-permute-start.17 = (bf16[144,1536]{1,0:T(8,128)(2,1)S(1)}, bf16[144,1536]{1,0:T(8,128)(2,1)S(1)}, u32[]{:S(2)}, u32[]{:S(2)}) collective-permute-start(bf16[144,1536]{1,0:T(8,128)(2,1)S(1)} %shard_map.297), channel_id=1, source_target_pairs={{0,2},{1,3},{2,0},{3,1},{4,6},{5,7},{6,4},{7,5},{8,10},{9,11},{10,... | collective-permute-start | bytes 1327112 | tf_op jit(solution)/shard_map/ppermute | solution.py:790
  86.0 10.6 %copy-start.15 = (s32[8]{0:T(128)S(1)}, s32[8]{0:T(128)}, u32[]{:S(2)}) copy-start(s32[8]{0:T(128)} %copy-done.14) | copy-start | bytes 100
  100.6 17.1 %collective-permute-start.15 = (bf16[2,384,384]{2,1,0:T(8,128)(2,1)S(1)}, bf16[2,384,384]{2,1,0:T(8,128)(2,1)S(1)}, u32[]{:S(2)}, u32[]{:S(2)}) collective-permute-start(bf16[2,384,384]{2,1,0:T(8,128)(2,1)S(1)} %fusion.13), channel_id=1, source_target_pairs={{0,4},{4,0},{8,12},{12,8},{16,20},{20,16},{24,28},{28,24},{1,5},{5... | collective-permute-start | bytes 1769480 | tf_op jit(solution)/shard_map/ppermute | solution.py:790
  102.5 18.1 %collective-permute-start.13 = (bf16[768,384]{1,0:T(8,128)(2,1)S(1)}, bf16[768,384]{1,0:T(8,128)(2,1)S(1)}, u32[]{:S(2)}, u32[]{:S(2)}) collective-permute-start(bf16[768,384]{1,0:T(8,128)(2,1)S(1)} %fusion.12), channel_id=1, source_target_pairs={{0,2},{1,3},{2,0},{3,1},{4,6},{5,7},{6,4},{7,5},{8,10},{9,11},{10,... | collective-permute-start | bytes 1769480 | tf_op jit(solution)/shard_map/ppermute | solution.py:790
  119.0 8.2 %collective-permute-start.16 = (bf16[384,384]{1,0:T(8,128)(2,1)S(1)}, bf16[384,384]{1,0:T(8,128)(2,1)S(1)}, u32[]{:S(2)}, u32[]{:S(2)}) collective-permute-start(bf16[384,384]{1,0:T(8,128)(2,1)S(1)} %fusion.22), channel_id=1, source_target_pairs={{0,2},{1,3},{2,0},{3,1},{4,6},{5,7},{6,4},{7,5},{8,10},{9,11},{10,... | collective-permute-start | bytes 884744 | tf_op jit(solution)/shard_map/ppermute | solution.py:790
  120.7 9.9 %collective-permute-start.18 = (bf16[2,768,384]{2,1,0:T(8,128)(2,1)S(1)}, bf16[2,768,384]{2,1,0:T(8,128)(2,1)S(1)}, u32[]{:S(2)}, u32[]{:S(2)}) collective-permute-start(bf16[2,768,384]{2,1,0:T(8,128)(2,1)S(1)} %copy-done.63), channel_id=1, source_target_pairs={{0,1},{1,0},{2,3},{3,2},{4,5},{5,4},{6,7},{7,6},{8,9},{9,8},{10,11... | collective-permute-start | bytes 3538952 | tf_op jit(solution)/shard_map/ppermute | solution.py:790
  120.8 9.5 %collective-permute-start.14 = (bf16[384,384]{1,0:T(8,128)(2,1)S(1)}, bf16[384,384]{1,0:T(8,128)(2,1)S(1)}, u32[]{:S(2)}, u32[]{:S(2)}) collective-permute-start(bf16[384,384]{1,0:T(8,128)(2,1)S(1)} %fusion.20), channel_id=1, source_target_pairs={{0,4},{4,0},{8,12},{12,8},{16,20},{20,16},{24,28},{28,24},{1,5},{5... | collective-permute-start | bytes 884744 | tf_op jit(solution)/shard_map/ppermute | solution.py:790
  125.1 5.4 %collective-permute-start.19 = (bf16[2,256,384]{2,1,0:T(8,128)(2,1)S(1)}, bf16[2,256,384]{2,1,0:T(8,128)(2,1)S(1)}, u32[]{:S(2)}, u32[]{:S(2)}) collective-permute-start(bf16[2,256,384]{2,1,0:T(8,128)(2,1)S(1)} %get-tuple-element.178), channel_id=1, source_target_pairs={{0,1},{1,0},{2,3},{3,2},{4,5},{5,4},{6,7},{7,6},{8,9},{9,8},{10,11... | collective-permute-start | bytes 1179656 | tf_op jit(solution)/shard_map/ppermute | solution.py:790
  132.4 16.5 %collective-permute-start.23 = (bf16[2,256,384]{2,1,0:T(8,128)(2,1)S(1)}, bf16[2,256,384]{2,1,0:T(8,128)(2,1)S(1)}, u32[]{:S(2)}, u32[]{:S(2)}) collective-permute-start(bf16[2,256,384]{2,1,0:T(8,128)(2,1)S(1)} %fusion.18), channel_id=1, source_target_pairs={{0,4},{4,0},{8,12},{12,8},{16,20},{20,16},{24,28},{28,24},{1,5},{5... | collective-permute-start | bytes 1179656 | tf_op jit(solution)/shard_map/ppermute | solution.py:790
  133.9 15.0 %collective-permute-start.22 = (bf16[512,384]{1,0:T(8,128)(2,1)S(1)}, bf16[512,384]{1,0:T(8,128)(2,1)S(1)}, u32[]{:S(2)}, u32[]{:S(2)}) collective-permute-start(bf16[512,384]{1,0:T(8,128)(2,1)S(1)} %fusion.17), channel_id=1, source_target_pairs={{0,2},{1,3},{2,0},{3,1},{4,6},{5,7},{6,4},{7,5},{8,10},{9,11},{10,... | collective-permute-start | bytes 1179656 | tf_op jit(solution)/shard_map/ppermute | solution.py:790
  134.9 11.3 %collective-permute-start.20 = (bf16[384,384]{1,0:T(8,128)(2,1)S(1)}, bf16[384,384]{1,0:T(8,128)(2,1)S(1)}, u32[]{:S(2)}, u32[]{:S(2)}) collective-permute-start(bf16[384,384]{1,0:T(8,128)(2,1)S(1)} %fusion.21), channel_id=1, source_target_pairs={{0,8},{4,12},{8,0},{12,4},{16,24},{20,28},{24,16},{28,20},{1,9},{5... | collective-permute-start | bytes 884744 | tf_op jit(solution)/shard_map/ppermute | solution.py:790
  146.2 15.0 %collective-permute-start.21 = (bf16[384,384]{1,0:T(8,128)(2,1)S(1)}, bf16[384,384]{1,0:T(8,128)(2,1)S(1)}, u32[]{:S(2)}, u32[]{:S(2)}) collective-permute-start(bf16[384,384]{1,0:T(8,128)(2,1)S(1)} %fusion.15), channel_id=1, source_target_pairs={{0,16},{4,20},{8,24},{12,28},{16,0},{20,4},{24,8},{28,12},{1,17},{... | collective-permute-start | bytes 884744 | tf_op jit(solution)/shard_map/ppermute | solution.py:790
  149.1 12.2 %collective-permute-start.24 = (bf16[256,384]{1,0:T(8,128)(2,1)S(1)}, bf16[256,384]{1,0:T(8,128)(2,1)S(1)}, u32[]{:S(2)}, u32[]{:S(2)}) collective-permute-start(bf16[256,384]{1,0:T(8,128)(2,1)S(1)} %fusion.24), channel_id=1, source_target_pairs={{0,4},{4,0},{8,12},{12,8},{16,20},{20,16},{24,28},{28,24},{1,5},{5... | collective-permute-start | bytes 589832 | tf_op jit(solution)/shard_map/ppermute | solution.py:790
  149.7 11.6 %collective-permute-start.25 = (bf16[256,384]{1,0:T(8,128)(2,1)S(1)}, bf16[256,384]{1,0:T(8,128)(2,1)S(1)}, u32[]{:S(2)}, u32[]{:S(2)}) collective-permute-start(bf16[256,384]{1,0:T(8,128)(2,1)S(1)} %fusion.25), channel_id=1, source_target_pairs={{0,2},{1,3},{2,0},{3,1},{4,6},{5,7},{6,4},{7,5},{8,10},{9,11},{10,... | collective-permute-start | bytes 589832 | tf_op jit(solution)/shard_map/ppermute | solution.py:790
  161.6 8.7 %collective-permute-start.27 = (bf16[272,384]{1,0:T(8,128)(2,1)S(1)}, bf16[272,384]{1,0:T(8,128)(2,1)S(1)}, u32[]{:S(2)}, u32[]{:S(2)}) collective-permute-start(bf16[272,384]{1,0:T(8,128)(2,1)S(1)} %fusion.23), channel_id=1, source_target_pairs={{0,8},{4,12},{8,0},{12,4},{16,24},{20,28},{24,16},{28,20},{1,9},{5... | collective-permute-start | bytes 626696 | tf_op jit(solution)/shard_map/ppermute | solution.py:790
  161.7 22.2 %collective-permute-start.26 = (f32[16,768]{1,0:T(8,128)S(1)}, f32[16,768]{1,0:T(8,128)S(1)}, u32[]{:S(2)}, u32[]{:S(2)}) collective-permute-start(f32[16,768]{1,0:T(8,128)S(1)} %get-tuple-element.186), channel_id=1, source_target_pairs={{1,0},{2,1},{3,2},{5,4},{6,5},{7,6},{9,8},{10,9},{11,10},{13,12},{... | collective-permute-start | bytes 147464 | tf_op jit(solution)/shard_map/ppermute | solution.py:1139
  163.2 12.9 %collective-permute-start.29 = (bf16[384,384]{1,0:T(8,128)(2,1)S(1)}, bf16[384,384]{1,0:T(8,128)(2,1)S(1)}, u32[]{:S(2)}, u32[]{:S(2)}) collective-permute-start(bf16[384,384]{1,0:T(8,128)(2,1)S(1)} %add_convert_fusion), channel_id=1, source_target_pairs={{0,8},{4,12},{8,0},{12,4},{16,24},{20,28},{24,16},{28,20},{1,9},{5... | collective-permute-start | bytes 884744 | tf_op jit(solution)/shard_map/ppermute | solution.py:790
  170.3 13.4 %collective-permute-start.28 = (bf16[272,384]{1,0:T(8,128)(2,1)S(1)}, bf16[272,384]{1,0:T(8,128)(2,1)S(1)}, u32[]{:S(2)}, u32[]{:S(2)}) collective-permute-start(bf16[272,384]{1,0:T(8,128)(2,1)S(1)} %fusion.16), channel_id=1, source_target_pairs={{0,16},{4,20},{8,24},{12,28},{16,0},{20,4},{24,8},{28,12},{1,17},{... | collective-permute-start | bytes 626696 | tf_op jit(solution)/shard_map/ppermute | solution.py:790
  176.3 14.7 %collective-permute-start.31 = (bf16[768,384]{1,0:T(8,128)(2,1)S(1)}, bf16[768,384]{1,0:T(8,128)(2,1)S(1)}, u32[]{:S(2)}, u32[]{:S(2)}) collective-permute-start(bf16[768,384]{1,0:T(8,128)(2,1)S(1)} %pad_maximum_fusion.3), channel_id=1, source_target_pairs={{0,4},{4,0},{8,12},{12,8},{16,20},{20,16},{24,28},{28,24},{1,5},{5... | collective-permute-start | bytes 1769480 | tf_op jit(solution)/shard_map/ppermute | solution.py:790
  183.8 7.1 %collective-permute-start.30 = (bf16[272,384]{1,0:T(8,128)(2,1)S(1)}, bf16[272,384]{1,0:T(8,128)(2,1)S(1)}, u32[]{:S(2)}, u32[]{:S(2)}) collective-permute-start(bf16[272,384]{1,0:T(8,128)(2,1)S(1)} %add_convert_fusion.1), channel_id=1, source_target_pairs={{0,8},{4,12},{8,0},{12,4},{16,24},{20,28},{24,16},{28,20},{1,9},{5... | collective-permute-start | bytes 626696 | tf_op jit(solution)/shard_map/ppermute | solution.py:790
  191.0 6.5 %collective-permute-start.32 = (bf16[288,384]{1,0:T(8,128)(2,1)S(1)}, bf16[288,384]{1,0:T(8,128)(2,1)S(1)}, u32[]{:S(2)}, u32[]{:S(2)}) collective-permute-start(bf16[288,384]{1,0:T(8,128)(2,1)S(1)} %slice.285), channel_id=1, source_target_pairs={{0,4},{4,0},{8,12},{12,8},{16,20},{20,16},{24,28},{28,24},{1,5},{5... | collective-permute-start | bytes 663560 | tf_op jit(solution)/shard_map/ppermute | solution.py:790
  197.7 5.7 %collective-permute-start.34 = (bf16[256,384]{1,0:T(8,128)(2,1)S(1)}, bf16[256,384]{1,0:T(8,128)(2,1)S(1)}, u32[]{:S(2)}, u32[]{:S(2)}) collective-permute-start(bf16[256,384]{1,0:T(8,128)(2,1)S(1)} %get-tuple-element.261), channel_id=1, source_target_pairs={{0,4},{4,0},{8,12},{12,8},{16,20},{20,16},{24,28},{28,24},{1,5},{5... | collective-permute-start | bytes 589832 | tf_op jit(solution)/shard_map/ppermute | solution.py:790
  198.4 4.9 %collective-permute-start.33 = (bf16[224,256]{1,0:T(8,128)(2,1)S(1)}, bf16[224,256]{1,0:T(8,128)(2,1)S(1)}, u32[]{:S(2)}, u32[]{:S(2)}) collective-permute-start(bf16[224,256]{1,0:T(8,128)(2,1)S(1)} %pad_maximum_fusion.7), channel_id=1, source_target_pairs={{0,2},{1,3},{2,0},{3,1},{4,6},{5,7},{6,4},{7,5},{8,10},{9,11},{10,... | collective-permute-start | bytes 344072 | tf_op jit(solution)/shard_map/ppermute | solution.py:790
  204.6 1.5 collective-permute-start.35
  (54 other events, 226.3 us)
